TPU v7x, 32 devices: a whole 2x2x4 slice. The times are simulated.
32 devices in a mesh: harm: 2 (over y), gx: 4 (over z), gz: 4 (over x, core).
Axes of the slice: x: 2, y: 2, z: 4, core: 2. Of those that a mesh axis runs over, the one named last changes fastest.
Arguments:
- perturbation: bfloat16 [8, 2, 4, 128, 24, 128], P('harm', None, None, 'gx', 'gz'), may hold values from -6 to 6
- base_mean: bfloat16 [3, 128, 24, 128], P(None, 'gx', 'gz'), may hold values from -6 to 6
- base_modes: bfloat16 [2, 2, 3, 128, 24, 128], P(None, None, None, 'gx', 'gz'), may hold values from -3 to 3
- solid_mask: int32 [128, 24, 128], P('gx', 'gz'), may hold values from 0 to 1, as said below
Outputs:
- residual_harmonics: float32 [8, 2, 4, 128, 24, 128], P('harm', None, None, 'gx', 'gz')
Inputs may be any that keep to these rules, and one draw needn't show every extreme that they name: `solid_mask`: 1 on the cells of one circular cylinder of radius 2 or more cells in the x-y plane, the same at every spanwise position, 0 elsewhere.
All inputs are finite; a program needn't handle non-finite values.
Results may differ from a plain program's by a relative error of at most 0.0003.
Values may be sent and summed in bfloat16 or wider, within the bound.
No kernel may reach another device: no remote copies, remote signals or barrier semaphores. Data moves between devices by JAX's collectives and lax.ppermute only.
A program may use at most 128 MiB of HBM per device.

v0:
```python
import jax
import jax.numpy as jnp
import numpy as np
from jax import lax
from jax.experimental import pallas as pl
from jax.experimental.pallas import tpu as pltpu
from jax.sharding import PartitionSpec as P

FREQUENCY_STEP = 0.2
VISCOSITY = 0.05
PENALTY = 4.0
FIRST = {-2: 1.0, -1: -8.0, 1: 8.0, 2: -1.0}
SECOND = {-2: -1.0, -1: 16.0, 0: -30.0, 1: 16.0, 2: -1.0}
HALO_X = 16
VMEM_BYTES = 56 * 1024 * 1024
ANY = pl.BlockSpec(memory_space=pl.ANY)
VMEM = pl.BlockSpec(memory_space=pltpu.VMEM)
SMEM = pl.BlockSpec(memory_space=pltpu.SMEM)


def stencil_rows(nz, nx, odd):
    own = nz * nx
    at_xb, at_xa = own, own + HALO_X
    at_cross = own + 2 * HALO_X
    at_near = at_cross + 2 * nx
    depth = at_near + 2 * nx
    at_zb, at_za = (at_near, at_cross) if odd else (at_cross, at_near)
    rows = np.zeros((3, own, depth), np.float32)
    for z in range(nz):
        for x in range(nx):
            row = z * nx + x
            for table, parts in ((FIRST, (0, 1)), (SECOND, (2, 2))):
                for step, weight in table.items():
                    sx = x + step
                    if sx < 0:
                        column = at_xb + 2 * z + sx + 2
                    elif sx >= nx:
                        column = at_xa + 2 * z + sx - nx
                    else:
                        column = z * nx + sx
                    rows[parts[0], row, column] += weight
                    sz = z + step
                    if sz < 0:
                        column = at_zb + (sz + 2) * nx + x
                    elif sz >= nz:
                        column = at_za + (sz - nz) * nx + x
                    else:
                        column = sz * nx + x
                    rows[parts[1], row, column] += weight
    return rows.reshape(3 * own, depth)


def wall_columns(ny):
    out = np.zeros((ny, 2 * ny), np.float32)
    for part, table in enumerate((FIRST, SECOND)):
        for y in range(ny):
            for step, weight in table.items():
                if 0 <= y + step < ny:
                    out[y + step, part * ny + y] = weight
    return out


def edge_rows(nz, nx):
    pick = np.zeros((2 * HALO_X, nz * nx), np.float32)
    for z in range(nz):
        for j in range(2):
            pick[2 * z + j, z * nx + j] = 1.0
            pick[HALO_X + 2 * z + j, z * nx + nx - 2 + j] = 1.0
    return pick


def run_copies(copies, sems):
    started = [pltpu.make_async_copy(src, dst, sems.at[i]) for i, (src, dst) in enumerate(copies)]
    for copy in started:
        copy.start()
    for copy in started:
        copy.wait()


def shards(perturbation, base_mean, base_modes, solid_mask):
    per, modes = perturbation.shape[0], base_modes.shape[0]
    nx, nz, ny = perturbation.shape[3], perturbation.shape[4], perturbation.shape[5]
    own = nz * nx
    bf16, f32 = jnp.bfloat16, jnp.float32
    harms, size_x, size_z = (lax.axis_size(a) for a in ("harm", "gx", "gz"))
    me_h, me_z = lax.axis_index("harm"), lax.axis_index("gz")
    swap = harms == 2
    sides = 1 if swap else 2
    n_pert, n_mean, n_modes = per * 8, 3, modes * 6
    n_base = n_mean + n_modes
    n_res = n_pert + n_base
    n_nb = modes * 6
    n_all = n_res + sides * n_nb

    pert = jnp.swapaxes(perturbation, 3, 4).reshape(n_pert, nz, nx, ny)
    mean = jnp.swapaxes(base_mean, 1, 2)
    mode = jnp.swapaxes(base_modes, 3, 4).reshape(n_modes, nz, nx, ny)
    mask = jnp.swapaxes(solid_mask, 0, 1).reshape(own, ny)

    odd = lax.rem(me_z, 2)
    cross_z = odd * (nz - 2)
    near_z = (1 - odd) * (nz - 2)
    shared = jnp.where(me_h == 0, per - modes, 0) if swap else jnp.int32(0)
    scalars = jnp.stack([me_h, odd, cross_z, near_z, shared]).astype(jnp.int32)

    cross_pairs = [(i, (i + 1) % size_z if i % 2 else (i - 1) % size_z) for i in range(size_z)]
    near_pairs = [(i, i + 1 if i % 2 == 0 else i - 1) for i in range(size_z)]
    up_x = [(i, (i + 1) % size_x) for i in range(size_x)]
    down_x = [(j, i) for i, j in up_x]
    if swap:
        harm_perms = [[(0, 1), (1, 0)]]
    else:
        up_h = [(i, i + 1) for i in range(harms - 1)]
        harm_perms = [up_h, [(j, i) for i, j in up_h]]
    n_first = modes * 8 if swap else n_pert
    n_second = n_res - n_first

    def sent(s, scal):
        return scal[4] if swap else (per - modes if s == 0 else 0)

    def plan_first(refs):
        scal, pert_ref, first_ref, *nb_refs = refs
        copies = []
        at = scal[4] * 8 if swap else 0
        copies.append((pert_ref.at[pl.ds(at, n_first), pl.ds(scal[2], 2)], first_ref))
        for s, nb_ref in enumerate(nb_refs):
            for i in range(modes * 2):
                copies.append((pert_ref.at[pl.ds(sent(s, scal) * 8 + 4 * i, 3)], nb_ref.at[pl.ds(3 * i, 3)]))
        return copies

    face = lambda n: jax.ShapeDtypeStruct((n, 2, nx, ny), bf16)

    def copies_of(plan, count, outs, *args):
        def body(*refs):
            run_copies(plan(refs[:-1]), refs[-1])

        return pl.pallas_call(
            body,
            out_shape=outs,
            in_specs=[SMEM] + [ANY] * (len(args) - 1),
            out_specs=tuple(ANY for _ in outs),
            scratch_shapes=[pltpu.SemaphoreType.DMA((count,))],
        )(*args)

    with jax.named_scope("pack_first"):
        first, *nb_send = copies_of(
            plan_first,
            1 + sides * modes * 2,
            (face(n_first),) + tuple(jax.ShapeDtypeStruct((n_nb, nz, nx, ny), bf16) for _ in range(sides)),
            scalars,
            pert,
        )
    first_got = lax.ppermute(first, "gz", cross_pairs)
    nb_got = [lax.ppermute(b, "harm", p) for b, p in zip(nb_send, harm_perms)]

    def pack_second(scal, pick_ref, pert_any, mean_any, mode_any, pert_ref, mean_ref, mode_ref, second_ref, lo_ref, hi_ref, sems):
        z = pl.ds(scal[2], 2)
        copies = []
        if swap:
            rest = per - modes - scal[4]
            copies.append((pert_any.at[pl.ds(rest * 8, n_pert - n_first), z], second_ref.at[pl.ds(0, n_pert - n_first)]))
        at = n_pert - n_first
        copies.append((mean_any.at[:, z], second_ref.at[pl.ds(at, n_mean)]))
        copies.append((mode_any.at[:, z], second_ref.at[pl.ds(at + n_mean, n_modes)]))
        started = [pltpu.make_async_copy(src, dst, sems.at[i]) for i, (src, dst) in enumerate(copies)]
        for copy in started:
            copy.start()
        pick = pick_ref[...]
        at = 0
        for ref, count in ((pert_ref, n_pert), (mean_ref, n_mean), (mode_ref, n_modes)):
            for f in range(0, count, 2):
                wide = min(2, count - f)
                rows = [ref[f + i].reshape(own, ny) for i in range(wide)]
                both = jnp.concatenate(rows, axis=1) if wide == 2 else rows[0]
                got = jnp.dot(pick, both, preferred_element_type=f32).astype(bf16)
                for i in range(wide):
                    lo_ref[at + f + i] = got[:HALO_X, i * ny : (i + 1) * ny]
                    hi_ref[at + f + i] = got[HALO_X:, i * ny : (i + 1) * ny]
            at += count
        for copy in started:
            copy.wait()

    edge = jax.ShapeDtypeStruct((n_res, HALO_X, ny), bf16)
    with jax.named_scope("pack_second"):
        second, edge_lo, edge_hi = pl.pallas_call(
            pack_second,
            out_shape=(face(n_second), edge, edge),
            in_specs=[SMEM, VMEM, ANY, ANY, ANY, VMEM, VMEM, VMEM],
            out_specs=(ANY, VMEM, VMEM),
            scratch_shapes=[pltpu.SemaphoreType.DMA((3,))],
            compiler_params=pltpu.CompilerParams(vmem_limit_bytes=VMEM_BYTES // 2),
        )(scalars, jnp.asarray(edge_rows(nz, nx), bf16), pert, mean, mode, pert, mean, mode)
    second_got = lax.ppermute(second, "gz", cross_pairs)
    xb_got = lax.ppermute(edge_hi, "gx", up_x)
    xa_got = lax.ppermute(edge_lo, "gx", down_x)

    deep = 2 * nx + 2 * HALO_X
    first_rows = first_got.reshape(n_first, 2 * nx, ny)

    def plan_relay(refs):
        scal, first_ref, xb_ref, xa_ref, *outs = refs
        copies = []
        for s, out in enumerate(outs):
            for i in range(modes * 2):
                field = sent(s, scal) * 8 + 4 * i
                to = pl.ds(3 * i, 3)
                near = 4 * i if swap else field
                copies.append((first_ref.at[pl.ds(near, 3)], out.at[to, pl.ds(0, 2 * nx)]))
                copies.append((xb_ref.at[pl.ds(field, 3)], out.at[to, pl.ds(2 * nx, HALO_X)]))
                copies.append((xa_ref.at[pl.ds(field, 3)], out.at[to, pl.ds(2 * nx + HALO_X, HALO_X)]))
        return copies

    with jax.named_scope("pack_relay"):
        relay = copies_of(
            plan_relay,
            sides * modes * 6,
            tuple(jax.ShapeDtypeStruct((n_nb, deep, ny), bf16) for _ in range(sides)),
            scalars,
            first_rows,
            xb_got,
            xa_got,
        )
    relay_got = [lax.ppermute(b, "harm", p) for b, p in zip(relay, harm_perms)]

    def plan_near(refs):
        scal, pert_ref, mean_ref, mode_ref, *rest = refs
        z = pl.ds(scal[3], 2)
        out = rest[-1]
        copies = [
            (pert_ref.at[:, z], out.at[pl.ds(0, n_pert)]),
            (mean_ref.at[:, z], out.at[pl.ds(n_pert, n_mean)]),
            (mode_ref.at[:, z], out.at[pl.ds(n_pert + n_mean, n_modes)]),
        ]
        for s in range(sides):
            copies.append((rest[s].at[:, z], out.at[pl.ds(n_res + s * n_nb, n_nb)]))
        return copies

    with jax.named_scope("pack_near"):
        (near,) = copies_of(plan_near, 3 + sides, (face(n_all),), scalars, pert, mean, mode, *nb_got)
    near_got = lax.ppermute(near, "gz", near_pairs)

    at_xb, at_xa = own, own + HALO_X
    at_cross = own + 2 * HALO_X
    at_near = at_cross + 2 * nx
    depth = at_near + 2 * nx
    stencil = jnp.asarray(np.stack([stencil_rows(nz, nx, False), stencil_rows(nz, nx, True)]), bf16)
    walls = jnp.asarray(wall_columns(ny), bf16)
    n_even = n_all + n_all % 2

    def operator(scal, stencil_any, walls_ref, mask_ref, pert_ref, mean_ref, mode_ref, first_ref, second_ref, near_ref, xb_ref, xa_ref, *rest):
        nb_refs, relay_refs = rest[:sides], rest[sides : 2 * sides]
        out_ref, fields, grads, laps, plain, weights, sems = rest[2 * sides :]
        base_at = n_pert
        copies = [(stencil_any.at[scal[1]], weights)]
        copies.append((pert_ref, fields.at[pl.ds(0, n_pert), pl.ds(0, own)]))
        copies.append((mean_ref, fields.at[pl.ds(base_at, n_mean), pl.ds(0, own)]))
        copies.append((mode_ref, fields.at[pl.ds(base_at + n_mean, n_modes), pl.ds(0, own)]))
        cross = pl.ds(at_cross, 2 * nx)
        if swap:
            rest_at = per - modes - scal[4]
            copies.append((first_ref, fields.at[pl.ds(scal[4] * 8, n_first), cross]))
            copies.append((second_ref.at[pl.ds(0, n_pert - n_first)], fields.at[pl.ds(rest_at * 8, n_pert - n_first), cross]))
        else:
            copies.append((first_ref, fields.at[pl.ds(0, n_pert), cross]))
        copies.append((second_ref.at[pl.ds(n_pert - n_first, n_base)], fields.at[pl.ds(base_at, n_base), cross]))
        copies.append((near_ref, fields.at[pl.ds(0, n_all), pl.ds(at_near, 2 * nx)]))
        copies.append((xb_ref, fields.at[pl.ds(0, n_res), pl.ds(at_xb, HALO_X)]))
        copies.append((xa_ref, fields.at[pl.ds(0, n_res), pl.ds(at_xa, HALO_X)]))
        for s in range(sides):
            mine = pl.ds(n_res + s * n_nb, n_nb)
            copies.append((nb_refs[s], fields.at[mine, pl.ds(0, own)]))
            copies.append((relay_refs[s].at[:, pl.ds(0, 2 * nx)], fields.at[mine, cross]))
            copies.append((relay_refs[s].at[:, pl.ds(2 * nx, 2 * HALO_X)], fields.at[mine, pl.ds(at_xb, 2 * HALO_X)]))
        run_copies(copies, sems)
        if n_even != n_all:
            fields[n_all] = jnp.zeros((depth, ny), bf16)

        def slopes(pair, carry):
            f = 2 * pair
            both = jnp.concatenate([fields[f], fields[f + 1]], axis=1)
            got = jnp.dot(weights[...], both, preferred_element_type=f32)
            for i in range(2):
                lanes = slice(i * ny, (i + 1) * ny)
                grads[f + i, 0] = got[:own, lanes]
                grads[f + i, 2] = got[own : 2 * own, lanes]
                mine = fields[f + i, pl.ds(0, own)]
                wall = jnp.dot(mine, walls_ref[...], preferred_element_type=f32)
                grads[f + i, 1] = wall[:, :ny]
                laps[f + i] = got[2 * own :, lanes] + wall[:, ny:]
                plain[f + i] = mine.astype(f32)
            return carry

        lax.fori_loop(0, n_even // 2, slopes, 0)

        def base_at_mode(m, c):
            if m == 0:
                return base_at + c, None, 1.0
            at = base_at + n_mean + (abs(m) - 1) * 6 + c
            return at, at + 3, (1.0 if m > 0 else -1.0)

        def product(acc, flow, value):
            (fr, fi, sign), (vr, vi) = flow, value
            re, im = acc[0] + fr * vr, acc[1] + fr * vi
            if fi is not None:
                if sign > 0:
                    re, im = re - fi * vi, im + fi * vr
                else:
                    re, im = re + fi * vi, im - fi * vr
            return re, im

        def contribution(acc, pairs, rows):
            for d in range(3):
                for k, m, at in pairs:
                    fr, fi, sign = base_at_mode(m, d)
                    flow = (plain[fr, rows], None if fi is None else plain[fi, rows], sign)
                    along = (plain[at + d, rows], plain[at + d + nb_step(at), rows])
                    for c in range(3):
                        sr, si, _ = base_at_mode(m, c)
                        slope = (grads[sr, d, rows], None if si is None else grads[si, d, rows], sign)
                        grad = (grads[at + c, d, rows], grads[at + c + nb_step(at), d, rows])
                        acc[k, c] = product(acc[k, c], flow, grad)
                        acc[k, c] = product(acc[k, c], slope, along)
            return acc

        def nb_step(at):
            return 4 if at < n_pert else 3

        resident, below, above = [], [], []
        for k in range(per):
            for m in range(-modes, modes + 1):
                l = k - m
                if l < 0:
                    below.append((k, m, n_res + (l + modes) * 6))
                elif l >= per:
                    above.append((k, m, n_res + (sides - 1) * n_nb + (l - per) * 6))
                else:
                    resident.append((k, m, l * 8))
        half = per * harms // 2

        def block(b, carry):
            rows = pl.ds(pl.multiple_of(b * 8, 8), 8)
            zero = jnp.zeros((8, ny), f32)
            acc = {(k, c): (zero, zero) for k in range(per) for c in range(3)}
            acc = contribution(acc, resident, rows)
            solid = PENALTY * mask_ref[rows].astype(f32)
            for k in range(per):
                freq = FREQUENCY_STEP * (scal[0] * per + k - half).astype(f32)
                for c in range(3):
                    ur, ui = plain[k * 8 + c, rows], plain[k * 8 + 4 + c, rows]
                    re = acc[k, c][0] + grads[k * 8 + 3, c, rows] - VISCOSITY * laps[k * 8 + c, rows]
                    im = acc[k, c][1] + grads[k * 8 + 7, c, rows] - VISCOSITY * laps[k * 8 + 4 + c, rows]
                    out_ref[k * 8 + c, rows] = re * (1.0 / 12.0) + (solid * ur - freq * ui)
                    out_ref[k * 8 + 4 + c, rows] = im * (1.0 / 12.0) + (solid * ui + freq * ur)
                for i in range(2):
                    at = k * 8 + 4 * i
                    out_ref[at + 3, rows] = (grads[at, 0, rows] + grads[at + 1, 1, rows] + grads[at + 2, 2, rows]) * (1.0 / 12.0)
            return carry

        lax.fori_loop(0, own // 8, block, 0)

        def neighbours(pairs):
            def nb_block(b, carry):
                rows = pl.ds(pl.multiple_of(b * 8, 8), 8)
                zero = jnp.zeros((8, ny), f32)
                keys = sorted({k for k, _, _ in pairs})
                acc = {(k, c): (zero, zero) for k in keys for c in range(3)}
                acc = contribution(acc, pairs, rows)
                for k in keys:
                    for c in range(3):
                        for i in range(2):
                            at = k * 8 + 4 * i + c
                            out_ref[at, rows] = out_ref[at, rows] + acc[k, c][i] * (1.0 / 12.0)
                return carry

            lax.fori_loop(0, own // 8, nb_block, 0)

        pl.when(scal[0] > 0)(lambda: neighbours(below))
        pl.when(scal[0] < harms - 1)(lambda: neighbours(above))

    n_copies = 10 + 3 * sides + (1 if swap else 0)
    flat = lambda a: a.reshape(a.shape[0], -1, ny)
    with jax.named_scope("operator"):
        out = pl.pallas_call(
            operator,
            out_shape=jax.ShapeDtypeStruct((n_pert, own, ny), f32),
            in_specs=[SMEM, ANY, VMEM, VMEM] + [ANY] * (8 + 2 * sides),
            out_specs=VMEM,
            scratch_shapes=[
                pltpu.VMEM((n_even, depth, ny), bf16),
                pltpu.VMEM((n_even, 3, own, ny), f32),
                pltpu.VMEM((n_even, own, ny), f32),
                pltpu.VMEM((n_even, own, ny), f32),
                pltpu.VMEM((3 * own, depth), bf16),
                pltpu.SemaphoreType.DMA((n_copies,)),
            ],
            compiler_params=pltpu.CompilerParams(vmem_limit_bytes=VMEM_BYTES),
        )(
            scalars, stencil, walls, mask, flat(pert), flat(mean), flat(mode), flat(first_got), flat(second_got), flat(near_got),
            xb_got, xa_got, *[flat(b) for b in nb_got], *relay_got,
        )
    return jnp.swapaxes(out.reshape(per, 2, 4, nz, nx, ny), 3, 4)


def solution(mesh):
    return jax.shard_map(
        shards,
        mesh=mesh,
        in_specs=(
            P("harm", None, None, "gx", "gz", None),
            P(None, "gx", "gz", None),
            P(None, None, None, "gx", "gz", None),
            P("gx", "gz", None),
        ),
        out_specs=P("harm", None, None, "gx", "gz", None),
        check_vma=False,
    )
```

profile of v0, /device:TPU:0, one launch (start us, length us, event | category | flops | bytes accessed | tf_op | source)
XLA Modules:
  0.0 140.9 jit_solution(16483024644055152680)
XLA Ops:
  0.0 0.6 stack.23.refs_0_.scal
  0.6 27.8 %pack_first.1 = (bf16[16,2,32,128]{3,2,1,0:T(8,128)(2,1)}, bf16[12,6,32,128]{3,2,1,0:T(8,128)(2,1)}) custom-call(s32[5]{0:T(128)} %stack.23.refs_0_.scal, bf16[32,6,32,128]{3,2,1,0:T(8,128)(2,1)} %bitcast.28), custom_call_target="tpu_custom_call" | custom-call | tf_op jit(solution)/shard_map/pack_first/pallas_call | solution.py:137
  28.4 0.0 copy-start.11
  28.4 3.1 %collective-permute-start.2 = (bf16[12,6,32,128]{3,2,1,0:T(8,128)(2,1)}, bf16[12,6,32,128]{3,2,1,0:T(8,128)(2,1)S(1)}, u32[]{:S(2)}, u32[]{:S(2)}) collective-permute-start(bf16[12,6,32,128]{3,2,1,0:T(8,128)(2,1)} %get-tuple-element.12), channel_id=1, source_target_pairs={{0,16},{16,0},{1,17},{17,1},{2,18},{18,2},{3,19},{19,3},{4,20},{20... | collective-permute-start | bytes 1769480 | tf_op jit(solution)/shard_map/ppermute | solution.py:154
  31.5 13.5 %collective-permute-done.2.refs_4_ = bf16[12,6,32,128]{3,2,1,0:T(8,128)(2,1)S(1)} collective-permute-done((bf16[12,6,32,128]{3,2,1,0:T(8,128)(2,1)}, bf16[12,6,32,128]{3,2,1,0:T(8,128)(2,1)S(1)}, u32[]{:S(2)}, u32[]{:S(2)}) %collective-permute-start.2) | collective-permute-done | bytes 589856 | tf_op jit(solution)/shard_map/ppermute | solution.py:154
  45.0 0.8 copy-done.5
  45.8 31.1 %pack_near.1 = bf16[59,2,32,128]{3,2,1,0:T(8,128)(2,1)} custom-call(s32[5]{0:T(128)} %stack.23.refs_0_.scal, bf16[32,6,32,128]{3,2,1,0:T(8,128)(2,1)} %bitcast.29, bf16[3,6,32,128]{3,2,1,0:T(8,128)(2,1)} %bitcast.37, bf16[12,6,32,128]{3,2,1,0:T(8,128)(2,1)} %bitcast.33, bf16[12,6,32,128]{3,2,1,0:T(8,128)(2,1)} %copy-done.5), custom_call_target="tpu_custom_call" | custom-call | tf_op jit(solution)/shard_map/pack_near/pallas_call | solution.py:137
  76.9 0.1 collective-permute-start.3
  77.0 0.0 copy-done.11
  77.0 1.8 %collective-permute-start = (bf16[16,2,32,128]{3,2,1,0:T(8,128)(2,1)S(1)}, bf16[16,2,32,128]{3,2,1,0:T(8,128)(2,1)S(1)}, u32[]{:S(2)}, u32[]{:S(2)}) collective-permute-start(bf16[16,2,32,128]{3,2,1,0:T(8,128)(2,1)S(1)} %copy-done.11), channel_id=1, source_target_pairs={{0,3},{1,2},{2,1},{3,0},{4,7},{5,6},{6,5},{7,4},{8,11},{9,10},{10,... | collective-permute-start | bytes 786440 | tf_op jit(solution)/shard_map/ppermute | solution.py:153
  78.8 0.0 copy-done.4
  78.8 0.0 copy-done
  78.8 0.0 copy-done.1
  78.9 0.0 copy-done.2
  78.9 0.0 copy-done.3
  78.9 1.2 pack_second.1
  80.1 0.1 collective-permute-start.1
  80.2 1.8 %collective-permute-start.4 = (bf16[47,16,128]{2,1,0:T(8,128)(2,1)S(1)}, bf16[47,16,128]{2,1,0:T(8,128)(2,1)S(1)}, u32[]{:S(2)}, u32[]{:S(2)}) collective-permute-start(bf16[47,16,128]{2,1,0:T(8,128)(2,1)S(1)} %get-tuple-element.13), channel_id=1, source_target_pairs={{0,4},{4,8},{8,12},{12,0},{1,5},{5,9},{9,13},{13,1},{2,6},{6,10},{... | collective-permute-start | bytes 577544 | tf_op jit(solution)/shard_map/ppermute | solution.py:194
  81.9 2.1 %collective-permute-start.5 = (bf16[47,16,128]{2,1,0:T(8,128)(2,1)S(1)}, bf16[47,16,128]{2,1,0:T(8,128)(2,1)S(1)}, u32[]{:S(2)}, u32[]{:S(2)}) collective-permute-start(bf16[47,16,128]{2,1,0:T(8,128)(2,1)S(1)} %get-tuple-element.14), channel_id=1, source_target_pairs={{4,0},{8,4},{12,8},{0,12},{5,1},{9,5},{13,9},{1,13},{6,2},{10,6},{... | collective-permute-start | bytes 577544 | tf_op jit(solution)/shard_map/ppermute | solution.py:195
  84.0 5.7 %collective-permute-done.4.refs_2_.xb_ref = bf16[47,16,128]{2,1,0:T(8,128)(2,1)S(1)} collective-permute-done((bf16[47,16,128]{2,1,0:T(8,128)(2,1)S(1)}, bf16[47,16,128]{2,1,0:T(8,128)(2,1)S(1)}, u32[]{:S(2)}, u32[]{:S(2)}) %collective-permute-start.4) | collective-permute-done | bytes 192544 | tf_op jit(solution)/shard_map/ppermute | solution.py:194
  89.8 3.2 %collective-permute-done.5.refs_3_.xa_ref = bf16[47,16,128]{2,1,0:T(8,128)(2,1)S(1)} collective-permute-done((bf16[47,16,128]{2,1,0:T(8,128)(2,1)S(1)}, bf16[47,16,128]{2,1,0:T(8,128)(2,1)S(1)}, u32[]{:S(2)}, u32[]{:S(2)}) %collective-permute-start.5) | collective-permute-done | bytes 192544 | tf_op jit(solution)/shard_map/ppermute | solution.py:195
  92.9 0.0 collective-permute-done
  92.9 0.0 copy-done.7
  92.9 0.7 copy-done.8
  93.6 0.1 copy-done.6
  93.7 10.8 %pack_relay.1 = bf16[12,96,128]{2,1,0:T(8,128)(2,1)} custom-call(s32[5]{0:T(128)} %stack.23.refs_0_.scal, bf16[16,64,128]{2,1,0:T(8,128)(2,1)} %bitcast.42, bf16[47,16,128]{2,1,0:T(8,128)(2,1)} %copy-done.7, bf16[47,16,128]{2,1,0:T(8,128)(2,1)} %copy-done.8), custom_call_target="tpu_custom_call" | custom-call | tf_op jit(solution)/shard_map/pack_relay/pallas_call | solution.py:137
  104.5 1.6 %collective-permute-start.6 = (bf16[12,96,128]{2,1,0:T(8,128)(2,1)}, bf16[12,96,128]{2,1,0:T(8,128)(2,1)S(1)}, u32[]{:S(2)}, u32[]{:S(2)}) collective-permute-start(bf16[12,96,128]{2,1,0:T(8,128)(2,1)} %pack_relay.1), channel_id=1, source_target_pairs={{0,16},{16,0},{1,17},{17,1},{2,18},{18,2},{3,19},{19,3},{4,20},{20... | collective-permute-start | bytes 884744 | tf_op jit(solution)/shard_map/ppermute | solution.py:223
  106.1 0.0 collective-permute-done.1
  106.1 7.1 %collective-permute-done.6.rest_1_ = bf16[12,96,128]{2,1,0:T(8,128)(2,1)S(1)} collective-permute-done((bf16[12,96,128]{2,1,0:T(8,128)(2,1)}, bf16[12,96,128]{2,1,0:T(8,128)(2,1)S(1)}, u32[]{:S(2)}, u32[]{:S(2)}) %collective-permute-start.6) | collective-permute-done | bytes 294944 | tf_op jit(solution)/shard_map/ppermute | solution.py:223
  113.2 0.0 collective-permute-done.3
  113.2 0.7 copy-done.10
  113.9 27.0 %operator.1 = f32[32,192,128]{2,1,0:T(8,128)} custom-call(s32[5]{0:T(128)} %stack.23.refs_0_.scal, bf16[2,576,352]{2,1,0:T(8,128)(2,1)} %constant.27.clone.stencil_any, bf16[128,256]{1,0:T(8,128)(2,1)} %constant.28.clone.walls_ref, s32[192,128]{1,0:T(8,128)} %bitcast.45, bf16[32,192,128]{2,1,0:T(8,128)(2,1)} %bitcast.30, bf16[3,192,128]{2,1,0:T(8,128)(2,1)} %bitcast.38, ...), custom_call_target="tpu_custom_call" | custom-call | tf_op jit(solution)/shard_map/operator/pallas_call | solution.py:383
  (12 shorter events, 0.0 us)
Async XLA Ops:
  0.0 78.8 %copy-start.4 = (bf16[32,192]{1,0:T(8,128)(2,1)S(1)}, bf16[32,192]{1,0:T(8,128)(2,1)}, u32[]{:S(2)}) copy-start(bf16[32,192]{1,0:T(8,128)(2,1)} %constant.26.clone.pick_ref) | copy-start | bytes 36868
  0.0 78.8 %copy-start = (bf16[4,2,4,32,6,128]{5,3,4,2,1,0:T(8,128)(2,1)S(1)}, bf16[4,2,4,32,6,128]{5,3,4,2,1,0:T(8,128)(2,1)}, u32[]{:S(2)}) copy-start(bf16[4,2,4,32,6,128]{5,3,4,2,1,0:T(8,128)(2,1)} %param.7) | copy-start | bytes 4718596
  0.0 78.8 %copy-start.1 = (bf16[2,2,3,32,6,128]{5,3,4,2,1,0:T(8,128)(2,1)S(1)}, bf16[2,2,3,32,6,128]{5,3,4,2,1,0:T(8,128)(2,1)}, u32[]{:S(2)}) copy-start(bf16[2,2,3,32,6,128]{5,3,4,2,1,0:T(8,128)(2,1)} %param.9) | copy-start | bytes 1769476
  0.0 78.8 %copy-start.2 = (bf16[3,32,6,128]{3,1,2,0:T(8,128)(2,1)S(1)}, bf16[3,32,6,128]{3,1,2,0:T(8,128)(2,1)}, u32[]{:S(2)}) copy-start(bf16[3,32,6,128]{3,1,2,0:T(8,128)(2,1)} %param.8) | copy-start | bytes 442372
  0.6 78.2 %copy-start.3 = (s32[5]{0:T(128)S(1)}, s32[5]{0:T(128)}, u32[]{:S(2)}) copy-start(s32[5]{0:T(128)} %stack.23.refs_0_.scal) | copy-start | bytes 64
  28.4 48.6 %copy-start.11 = (bf16[16,2,32,128]{3,2,1,0:T(8,128)(2,1)S(1)}, bf16[16,2,32,128]{3,2,1,0:T(8,128)(2,1)}, u32[]{:S(2)}) copy-start(bf16[16,2,32,128]{3,2,1,0:T(8,128)(2,1)} %get-tuple-element.10) | copy-start | bytes 786436
  28.4 16.6 %collective-permute-start.2 = (bf16[12,6,32,128]{3,2,1,0:T(8,128)(2,1)}, bf16[12,6,32,128]{3,2,1,0:T(8,128)(2,1)S(1)}, u32[]{:S(2)}, u32[]{:S(2)}) collective-permute-start(bf16[12,6,32,128]{3,2,1,0:T(8,128)(2,1)} %get-tuple-element.12), channel_id=1, source_target_pairs={{0,16},{16,0},{1,17},{17,1},{2,18},{18,2},{3,19},{19,3},{4,20},{20... | collective-permute-start | bytes 1769480 | tf_op jit(solution)/shard_map/ppermute | solution.py:154
  45.0 0.8 copy-start.5
  76.9 36.3 %collective-permute-start.3 = (bf16[59,2,32,128]{3,2,1,0:T(8,128)(2,1)}, bf16[59,2,32,128]{3,2,1,0:T(8,128)(2,1)}, u32[]{:S(2)}, u32[]{:S(2)}) collective-permute-start(bf16[59,2,32,128]{3,2,1,0:T(8,128)(2,1)} %pack_near.1), channel_id=1, source_target_pairs={{0,1},{1,0},{2,3},{3,2},{4,5},{5,4},{6,7},{7,6},{8,9},{9,8},{10,11... | collective-permute-start | bytes 2899976 | tf_op jit(solution)/shard_map/ppermute | solution.py:240
  77.0 15.9 %collective-permute-start = (bf16[16,2,32,128]{3,2,1,0:T(8,128)(2,1)S(1)}, bf16[16,2,32,128]{3,2,1,0:T(8,128)(2,1)S(1)}, u32[]{:S(2)}, u32[]{:S(2)}) collective-permute-start(bf16[16,2,32,128]{3,2,1,0:T(8,128)(2,1)S(1)} %copy-done.11), channel_id=1, source_target_pairs={{0,3},{1,2},{2,1},{3,0},{4,7},{5,6},{6,5},{7,4},{8,11},{9,10},{10,... | collective-permute-start | bytes 786440 | tf_op jit(solution)/shard_map/ppermute | solution.py:153
  80.1 26.0 %collective-permute-start.1 = (bf16[31,2,32,128]{3,2,1,0:T(8,128)(2,1)S(1)}, bf16[31,2,32,128]{3,2,1,0:T(8,128)(2,1)S(1)}, u32[]{:S(2)}, u32[]{:S(2)}) collective-permute-start(bf16[31,2,32,128]{3,2,1,0:T(8,128)(2,1)S(1)} %get-tuple-element.11), channel_id=1, source_target_pairs={{0,3},{1,2},{2,1},{3,0},{4,7},{5,6},{6,5},{7,4},{8,11},{9,10},{10,... | collective-permute-start | bytes 1523720 | tf_op jit(solution)/shard_map/ppermute | solution.py:193
  80.2 9.6 %collective-permute-start.4 = (bf16[47,16,128]{2,1,0:T(8,128)(2,1)S(1)}, bf16[47,16,128]{2,1,0:T(8,128)(2,1)S(1)}, u32[]{:S(2)}, u32[]{:S(2)}) collective-permute-start(bf16[47,16,128]{2,1,0:T(8,128)(2,1)S(1)} %get-tuple-element.13), channel_id=1, source_target_pairs={{0,4},{4,8},{8,12},{12,0},{1,5},{5,9},{9,13},{13,1},{2,6},{6,10},{... | collective-permute-start | bytes 577544 | tf_op jit(solution)/shard_map/ppermute | solution.py:194
  81.9 11.0 %collective-permute-start.5 = (bf16[47,16,128]{2,1,0:T(8,128)(2,1)S(1)}, bf16[47,16,128]{2,1,0:T(8,128)(2,1)S(1)}, u32[]{:S(2)}, u32[]{:S(2)}) collective-permute-start(bf16[47,16,128]{2,1,0:T(8,128)(2,1)S(1)} %get-tuple-element.14), channel_id=1, source_target_pairs={{4,0},{8,4},{12,8},{0,12},{5,1},{9,5},{13,9},{1,13},{6,2},{10,6},{... | collective-permute-start | bytes 577544 | tf_op jit(solution)/shard_map/ppermute | solution.py:195
  89.7 3.2 %copy-start.7 = (bf16[47,16,128]{2,1,0:T(8,128)(2,1)}, bf16[47,16,128]{2,1,0:T(8,128)(2,1)S(1)}, u32[]{:S(2)}) copy-start(bf16[47,16,128]{2,1,0:T(8,128)(2,1)S(1)} %collective-permute-done.4.refs_2_.xb_ref) | copy-start | bytes 577540
  92.9 0.7 copy-start.8
  92.9 0.8 copy-start.6
  104.5 8.7 %collective-permute-start.6 = (bf16[12,96,128]{2,1,0:T(8,128)(2,1)}, bf16[12,96,128]{2,1,0:T(8,128)(2,1)S(1)}, u32[]{:S(2)}, u32[]{:S(2)}) collective-permute-start(bf16[12,96,128]{2,1,0:T(8,128)(2,1)} %pack_relay.1), channel_id=1, source_target_pairs={{0,16},{16,0},{1,17},{17,1},{2,18},{18,2},{3,19},{19,3},{4,20},{20... | collective-permute-start | bytes 884744 | tf_op jit(solution)/shard_map/ppermute | solution.py:223
  106.1 7.1 %copy-start.9 = (bf16[31,2,32,128]{3,2,1,0:T(8,128)(2,1)}, bf16[31,2,32,128]{3,2,1,0:T(8,128)(2,1)S(1)}, u32[]{:S(2)}) copy-start(bf16[31,2,32,128]{3,2,1,0:T(8,128)(2,1)S(1)} %collective-permute-done.1) | copy-start | bytes 1523716
  113.2 0.7 copy-start.10
where the time goes:
time: 141 us
  Pallas kernels  97.9 us (69%)
  waiting for transfers between devices  29.5 us (21%)
  starting transfers between devices  10.5 us (7%)
  local copies, waits for them, and re-layouts  2.96 us (2%)
    pallas_call x3, Pallas kernels, copies_of(): pl.pallas_call(body, out_shape=outs, in_specs=[SMEM] + [ANY] * (len(args)...  69.6 us
    pallas_call x1, Pallas kernels, shards(): pl.pallas_call(operator, out_shape=jax.ShapeDtypeStruct((n_pert, own, ny)...  27 us
    ppermute x1, waiting for transfers between devices, shards(): nb_got = [lax.ppermute(b, 'harm', p) for b, p in zip(nb_send, harm_perms)]  13.5 us
    ppermute x1, waiting for transfers between devices, shards(): relay_got = [lax.ppermute(b, 'harm', p) for b, p in zip(relay, harm_perms)]  7.08 us
    ppermute x1, waiting for transfers between devices, shards(): xb_got = lax.ppermute(edge_hi, 'gx', up_x)  5.7 us
    ppermute x1, waiting for transfers between devices, shards(): xa_got = lax.ppermute(edge_lo, 'gx', down_x)  3.18 us
    ppermute x1, starting transfers between devices, shards(): nb_got = [lax.ppermute(b, 'harm', p) for b, p in zip(nb_send, harm_perms)]  3.06 us
  transfers between devices with their start and end apart: 7, of which 4 were waited for; matrix products, arithmetic and copies ran while one was open for 0% of the time, Pallas kernels for 9%

commit v1 on v0

--- a/solution.py
+++ b/solution.py
@@ -15,7 +15,6 @@
 VMEM_BYTES = 56 * 1024 * 1024
 ANY = pl.BlockSpec(memory_space=pl.ANY)
 VMEM = pl.BlockSpec(memory_space=pltpu.VMEM)
-SMEM = pl.BlockSpec(memory_space=pltpu.SMEM)
 
 
 def stencil_rows(nz, nx, odd):
@@ -83,7 +82,6 @@
     own = nz * nx
     bf16, f32 = jnp.bfloat16, jnp.float32
     harms, size_x, size_z = (lax.axis_size(a) for a in ("harm", "gx", "gz"))
-    me_h, me_z = lax.axis_index("harm"), lax.axis_index("gz")
     swap = harms == 2
     sides = 1 if swap else 2
     n_pert, n_mean, n_modes = per * 8, 3, modes * 6
@@ -97,11 +95,10 @@
     mode = jnp.swapaxes(base_modes, 3, 4).reshape(n_modes, nz, nx, ny)
     mask = jnp.swapaxes(solid_mask, 0, 1).reshape(own, ny)
 
-    odd = lax.rem(me_z, 2)
-    cross_z = odd * (nz - 2)
-    near_z = (1 - odd) * (nz - 2)
-    shared = jnp.where(me_h == 0, per - modes, 0) if swap else jnp.int32(0)
-    scalars = jnp.stack([me_h, odd, cross_z, near_z, shared]).astype(jnp.int32)
+    def place():
+        me_h, odd = lax.axis_index("harm"), lax.rem(lax.axis_index("gz"), 2)
+        shared = jnp.where(me_h == 0, per - modes, 0) if swap else 0
+        return me_h, odd, odd * (nz - 2), (1 - odd) * (nz - 2), shared
 
     cross_pairs = [(i, (i + 1) % size_z if i % 2 else (i - 1) % size_z) for i in range(size_z)]
     near_pairs = [(i, i + 1 if i % 2 == 0 else i - 1) for i in range(size_z)]
@@ -118,53 +115,38 @@
     def sent(s, scal):
         return scal[4] if swap else (per - modes if s == 0 else 0)
 
-    def plan_first(refs):
-        scal, pert_ref, first_ref, *nb_refs = refs
-        copies = []
+    face = lambda n: jax.ShapeDtypeStruct((n, 2, nx, ny), bf16)
+    roomy = pltpu.CompilerParams(vmem_limit_bytes=VMEM_BYTES // 2)
+
+    def pack_first(pert_ref, first_ref, *nb_refs):
+        scal = place()
         at = scal[4] * 8 if swap else 0
-        copies.append((pert_ref.at[pl.ds(at, n_first), pl.ds(scal[2], 2)], first_ref))
+        for f in range(n_first):
+            first_ref[f] = pert_ref[at + f, pl.ds(scal[2], 2)]
         for s, nb_ref in enumerate(nb_refs):
             for i in range(modes * 2):
-                copies.append((pert_ref.at[pl.ds(sent(s, scal) * 8 + 4 * i, 3)], nb_ref.at[pl.ds(3 * i, 3)]))
-        return copies
-
-    face = lambda n: jax.ShapeDtypeStruct((n, 2, nx, ny), bf16)
-
-    def copies_of(plan, count, outs, *args):
-        def body(*refs):
-            run_copies(plan(refs[:-1]), refs[-1])
-
-        return pl.pallas_call(
-            body,
-            out_shape=outs,
-            in_specs=[SMEM] + [ANY] * (len(args) - 1),
-            out_specs=tuple(ANY for _ in outs),
-            scratch_shapes=[pltpu.SemaphoreType.DMA((count,))],
-        )(*args)
+                for c in range(3):
+                    nb_ref[3 * i + c] = pert_ref[sent(s, scal) * 8 + 4 * i + c]
 
     with jax.named_scope("pack_first"):
-        first, *nb_send = copies_of(
-            plan_first,
-            1 + sides * modes * 2,
-            (face(n_first),) + tuple(jax.ShapeDtypeStruct((n_nb, nz, nx, ny), bf16) for _ in range(sides)),
-            scalars,
-            pert,
-        )
+        first, *nb_send = pl.pallas_call(
+            pack_first,
+            out_shape=(face(n_first),) + tuple(jax.ShapeDtypeStruct((n_nb, nz, nx, ny), bf16) for _ in range(sides)),
+            compiler_params=roomy,
+        )(pert)
     first_got = lax.ppermute(first, "gz", cross_pairs)
     nb_got = [lax.ppermute(b, "harm", p) for b, p in zip(nb_send, harm_perms)]
 
-    def pack_second(scal, pick_ref, pert_any, mean_any, mode_any, pert_ref, mean_ref, mode_ref, second_ref, lo_ref, hi_ref, sems):
+    def pack_second(pick_ref, pert_ref, mean_ref, mode_ref, second_ref, lo_ref, hi_ref):
+        scal = place()
         z = pl.ds(scal[2], 2)
-        copies = []
+        at = n_pert - n_first
         if swap:
-            rest = per - modes - scal[4]
-            copies.append((pert_any.at[pl.ds(rest * 8, n_pert - n_first), z], second_ref.at[pl.ds(0, n_pert - n_first)]))
-        at = n_pert - n_first
-        copies.append((mean_any.at[:, z], second_ref.at[pl.ds(at, n_mean)]))
-        copies.append((mode_any.at[:, z], second_ref.at[pl.ds(at + n_mean, n_modes)]))
-        started = [pltpu.make_async_copy(src, dst, sems.at[i]) for i, (src, dst) in enumerate(copies)]
-        for copy in started:
-            copy.start()
+            rest = (per - modes - scal[4]) * 8
+            for f in range(at):
+                second_ref[f] = pert_ref[rest + f, z]
+        second_ref[at : at + n_mean] = mean_ref[:, z]
+        second_ref[at + n_mean :] = mode_ref[:, z]
         pick = pick_ref[...]
         at = 0
         for ref, count in ((pert_ref, n_pert), (mean_ref, n_mean), (mode_ref, n_modes)):
@@ -177,66 +159,53 @@
                     lo_ref[at + f + i] = got[:HALO_X, i * ny : (i + 1) * ny]
                     hi_ref[at + f + i] = got[HALO_X:, i * ny : (i + 1) * ny]
             at += count
-        for copy in started:
-            copy.wait()
 
     edge = jax.ShapeDtypeStruct((n_res, HALO_X, ny), bf16)
     with jax.named_scope("pack_second"):
         second, edge_lo, edge_hi = pl.pallas_call(
-            pack_second,
-            out_shape=(face(n_second), edge, edge),
-            in_specs=[SMEM, VMEM, ANY, ANY, ANY, VMEM, VMEM, VMEM],
-            out_specs=(ANY, VMEM, VMEM),
-            scratch_shapes=[pltpu.SemaphoreType.DMA((3,))],
-            compiler_params=pltpu.CompilerParams(vmem_limit_bytes=VMEM_BYTES // 2),
-        )(scalars, jnp.asarray(edge_rows(nz, nx), bf16), pert, mean, mode, pert, mean, mode)
+            pack_second, out_shape=(face(n_second), edge, edge), compiler_params=roomy
+        )(jnp.asarray(edge_rows(nz, nx), bf16), pert, mean, mode)
     second_got = lax.ppermute(second, "gz", cross_pairs)
     xb_got = lax.ppermute(edge_hi, "gx", up_x)
     xa_got = lax.ppermute(edge_lo, "gx", down_x)
 
     deep = 2 * nx + 2 * HALO_X
-    first_rows = first_got.reshape(n_first, 2 * nx, ny)
-
-    def plan_relay(refs):
-        scal, first_ref, xb_ref, xa_ref, *outs = refs
-        copies = []
+
+    def pack_relay(first_ref, xb_ref, xa_ref, *outs):
+        scal = place()
         for s, out in enumerate(outs):
             for i in range(modes * 2):
                 field = sent(s, scal) * 8 + 4 * i
-                to = pl.ds(3 * i, 3)
                 near = 4 * i if swap else field
-                copies.append((first_ref.at[pl.ds(near, 3)], out.at[to, pl.ds(0, 2 * nx)]))
-                copies.append((xb_ref.at[pl.ds(field, 3)], out.at[to, pl.ds(2 * nx, HALO_X)]))
-                copies.append((xa_ref.at[pl.ds(field, 3)], out.at[to, pl.ds(2 * nx + HALO_X, HALO_X)]))
-        return copies
+                for c in range(3):
+                    out[3 * i + c, : 2 * nx] = first_ref[near + c].reshape(2 * nx, ny)
+                    out[3 * i + c, 2 * nx : 2 * nx + HALO_X] = xb_ref[field + c]
+                    out[3 * i + c, 2 * nx + HALO_X :] = xa_ref[field + c]
 
     with jax.named_scope("pack_relay"):
-        relay = copies_of(
-            plan_relay,
-            sides * modes * 6,
-            tuple(jax.ShapeDtypeStruct((n_nb, deep, ny), bf16) for _ in range(sides)),
-            scalars,
-            first_rows,
-            xb_got,
-            xa_got,
-        )
+        relay = pl.pallas_call(
+            pack_relay,
+            out_shape=tuple(jax.ShapeDtypeStruct((n_nb, deep, ny), bf16) for _ in range(sides)),
+            compiler_params=roomy,
+        )(first_got, xb_got, xa_got)
     relay_got = [lax.ppermute(b, "harm", p) for b, p in zip(relay, harm_perms)]
 
-    def plan_near(refs):
-        scal, pert_ref, mean_ref, mode_ref, *rest = refs
-        z = pl.ds(scal[3], 2)
+    def pack_near(pert_ref, mean_ref, mode_ref, *rest):
         out = rest[-1]
-        copies = [
-            (pert_ref.at[:, z], out.at[pl.ds(0, n_pert)]),
-            (mean_ref.at[:, z], out.at[pl.ds(n_pert, n_mean)]),
-            (mode_ref.at[:, z], out.at[pl.ds(n_pert + n_mean, n_modes)]),
-        ]
+        z = pl.ds(place()[3], 2)
+        out[:n_pert] = pert_ref[:, z]
+        out[n_pert : n_pert + n_mean] = mean_ref[:, z]
+        out[n_pert + n_mean : n_res] = mode_ref[:, z]
         for s in range(sides):
-            copies.append((rest[s].at[:, z], out.at[pl.ds(n_res + s * n_nb, n_nb)]))
-        return copies
+            out[n_res + s * n_nb : n_res + (s + 1) * n_nb] = rest[s][:, z]
 
     with jax.named_scope("pack_near"):
-        (near,) = copies_of(plan_near, 3 + sides, (face(n_all),), scalars, pert, mean, mode, *nb_got)
+        near = pl.pallas_call(
+            pack_near,
+            out_shape=face(n_all),
+            in_specs=[VMEM] * (3 + sides) + [ANY],
+            compiler_params=roomy,
+        )(pert, mean, mode, *nb_got, relay[0])
     near_got = lax.ppermute(near, "gz", near_pairs)
 
     at_xb, at_xa = own, own + HALO_X
@@ -247,7 +216,8 @@
     walls = jnp.asarray(wall_columns(ny), bf16)
     n_even = n_all + n_all % 2
 
-    def operator(scal, stencil_any, walls_ref, mask_ref, pert_ref, mean_ref, mode_ref, first_ref, second_ref, near_ref, xb_ref, xa_ref, *rest):
+    def operator(stencil_any, walls_ref, mask_ref, pert_ref, mean_ref, mode_ref, first_ref, second_ref, near_ref, xb_ref, xa_ref, *rest):
+        scal = place()
         nb_refs, relay_refs = rest[:sides], rest[sides : 2 * sides]
         out_ref, fields, grads, laps, plain, weights, sems = rest[2 * sides :]
         base_at = n_pert
@@ -383,7 +353,7 @@
         out = pl.pallas_call(
             operator,
             out_shape=jax.ShapeDtypeStruct((n_pert, own, ny), f32),
-            in_specs=[SMEM, ANY, VMEM, VMEM] + [ANY] * (8 + 2 * sides),
+            in_specs=[ANY, VMEM, VMEM] + [ANY] * (8 + 2 * sides),
             out_specs=VMEM,
             scratch_shapes=[
                 pltpu.VMEM((n_even, depth, ny), bf16),
@@ -395,7 +365,7 @@
             ],
             compiler_params=pltpu.CompilerParams(vmem_limit_bytes=VMEM_BYTES),
         )(
-            scalars, stencil, walls, mask, flat(pert), flat(mean), flat(mode), flat(first_got), flat(second_got), flat(near_got),
+            stencil, walls, mask, flat(pert), flat(mean), flat(mode), flat(first_got), flat(second_got), flat(near_got),
             xb_got, xa_got, *[flat(b) for b in nb_got], *relay_got,
         )
     return jnp.swapaxes(out.reshape(per, 2, 4, nz, nx, ny), 3, 4)

time: 141 us -> 63.7 us (0.45)
  Pallas kernels: 97.9 us -> 27.7 us
  waiting for transfers between devices: 29.5 us -> 21.5 us
  local copies, waits for them, and re-layouts: 2.96 us -> 5.28 us
  starting transfers between devices: 10.5 us -> 8.77 us
    pallas_call x4, Pallas kernels: 70.8 us -> 0.71 us  [the longest x1 0.55 us: shards(): pl.pallas_call(pack_second, out_shape=(face(n_second), edge, edge), compi...]
    ppermute x1, waiting for transfers between devices: 13.5 us -> 0.01 us  [shards(): nb_got = [lax.ppermute(b, 'harm', p) for b, p in zip(nb_send, harm_perms)]]
    ppermute x1, waiting for transfers between devices: 0.01 us -> 12.2 us  [shards(): second_got = lax.ppermute(second, 'gz', cross_pairs)]
    ppermute x1, waiting for transfers between devices: 7.08 us -> 0.01 us  [shards(): relay_got = [lax.ppermute(b, 'harm', p) for b, p in zip(relay, harm_perms)]]
    unnamed x24 -> x26, local copies, waits for them, and re-layouts: 2.33 us -> 5.28 us
  transfers between devices with their start and end apart: 7 -> 7, of which waited for: 4 -> 3; matrix products, arithmetic and copies ran while one was open for 0% -> 0% of each run, Pallas kernels for 9% -> 1%
where the time goes in v1:
time: 63.7 us; the launch traced here: 63.4 us
  Pallas kernels  27.7 us (43%)
  waiting for transfers between devices  21.5 us (34%)
  starting transfers between devices  8.77 us (14%)
  local copies, waits for them, and re-layouts  5.28 us (8%)
    pallas_call x1, Pallas kernels, shards(): pl.pallas_call(operator, out_shape=jax.ShapeDtypeStruct((n_pert, own, ny)...  27 us
    ppermute x1, waiting for transfers between devices, shards(): second_got = lax.ppermute(second, 'gz', cross_pairs)  12.2 us
    ppermute x1, waiting for transfers between devices, shards(): xb_got = lax.ppermute(edge_hi, 'gx', up_x)  5.76 us
    unnamed x26, local copies, waits for them, and re-layouts  5.28 us
    ppermute x1, waiting for transfers between devices, shards(): xa_got = lax.ppermute(edge_lo, 'gx', down_x)  3.51 us
    ppermute x1, starting transfers between devices, shards(): nb_got = [lax.ppermute(b, 'harm', p) for b, p in zip(nb_send, harm_perms)]  3.03 us
    ppermute x1, starting transfers between devices, shards(): xa_got = lax.ppermute(edge_lo, 'gx', down_x)  2.25 us
    ppermute x1, starting transfers between devices, shards(): xb_got = lax.ppermute(edge_hi, 'gx', up_x)  1.62 us
  transfers between devices with their start and end apart: 7, of which 3 were waited for; matrix products, arithmetic and copies ran while one was open for 0% of the time, Pallas kernels for 1%

profile of v1, /device:TPU:0, one launch (start us, length us, event | category | flops | bytes accessed | tf_op | source)
XLA Modules:
  0.0 63.4 jit_solution(10238955675151220956)
XLA Ops:
  0.0 1.4 %copy-done = bf16[4,2,4,32,6,128]{5,3,4,2,1,0:T(8,128)(2,1)S(1)} copy-done((bf16[4,2,4,32,6,128]{5,3,4,2,1,0:T(8,128)(2,1)S(1)}, bf16[4,2,4,32,6,128]{5,3,4,2,1,0:T(8,128)(2,1)}, u32[]{:S(2)}) %copy-start) | copy-done | bytes 1572888
  1.4 0.1 pack_first.1
  1.5 3.0 %collective-permute-start.2 = (bf16[12,6,32,128]{3,2,1,0:T(8,128)(2,1)S(1)}, bf16[12,6,32,128]{3,2,1,0:T(8,128)(2,1)S(1)}, u32[]{:S(2)}, u32[]{:S(2)}) collective-permute-start(bf16[12,6,32,128]{3,2,1,0:T(8,128)(2,1)S(1)} %get-tuple-element.12), channel_id=1, source_target_pairs={{0,16},{16,0},{1,17},{17,1},{2,18},{18,2},{3,19},{19,3},{4,20},{20... | collective-permute-start | bytes 1769480 | tf_op jit(solution)/shard_map/ppermute | solution.py:138
  4.5 0.7 %collective-permute-start = (bf16[16,2,32,128]{3,2,1,0:T(8,128)(2,1)S(1)}, bf16[16,2,32,128]{3,2,1,0:T(8,128)(2,1)S(1)}, u32[]{:S(2)}, u32[]{:S(2)}) collective-permute-start(bf16[16,2,32,128]{3,2,1,0:T(8,128)(2,1)S(1)} %get-tuple-element.10), channel_id=1, source_target_pairs={{0,3},{1,2},{2,1},{3,0},{4,7},{5,6},{6,5},{7,4},{8,11},{9,10},{10,... | collective-permute-start | bytes 786440 | tf_op jit(solution)/shard_map/ppermute | solution.py:137
  5.2 1.1 %copy-done.2 = bf16[2,2,3,32,6,128]{5,3,4,2,1,0:T(8,128)(2,1)S(1)} copy-done((bf16[2,2,3,32,6,128]{5,3,4,2,1,0:T(8,128)(2,1)S(1)}, bf16[2,2,3,32,6,128]{5,3,4,2,1,0:T(8,128)(2,1)}, u32[]{:S(2)}) %copy-start.2) | copy-done | bytes 589848
  6.2 0.9 %copy-done.5 = bf16[3,32,6,128]{3,1,2,0:T(8,128)(2,1)S(1)} copy-done((bf16[3,32,6,128]{3,1,2,0:T(8,128)(2,1)S(1)}, bf16[3,32,6,128]{3,1,2,0:T(8,128)(2,1)}, u32[]{:S(2)}) %copy-start.5) | copy-done | bytes 147480
  7.1 0.7 %copy-done.9 = bf16[32,192]{1,0:T(8,128)(2,1)S(1)} copy-done((bf16[32,192]{1,0:T(8,128)(2,1)S(1)}, bf16[32,192]{1,0:T(8,128)(2,1)}, u32[]{:S(2)}) %copy-start.9) | copy-done | bytes 12312
  7.8 0.6 pack_second.1
  8.4 1.6 %collective-permute-start.3 = (bf16[47,16,128]{2,1,0:T(8,128)(2,1)S(1)}, bf16[47,16,128]{2,1,0:T(8,128)(2,1)S(1)}, u32[]{:S(2)}, u32[]{:S(2)}) collective-permute-start(bf16[47,16,128]{2,1,0:T(8,128)(2,1)S(1)} %get-tuple-element.13), channel_id=1, source_target_pairs={{0,4},{4,8},{8,12},{12,0},{1,5},{5,9},{9,13},{13,1},{2,6},{6,10},{... | collective-permute-start | bytes 577544 | tf_op jit(solution)/shard_map/ppermute | solution.py:169
  10.0 2.2 %collective-permute-start.4 = (bf16[47,16,128]{2,1,0:T(8,128)(2,1)S(1)}, bf16[47,16,128]{2,1,0:T(8,128)(2,1)S(1)}, u32[]{:S(2)}, u32[]{:S(2)}) collective-permute-start(bf16[47,16,128]{2,1,0:T(8,128)(2,1)S(1)} %get-tuple-element.14), channel_id=1, source_target_pairs={{4,0},{8,4},{12,8},{0,12},{5,1},{9,5},{13,9},{1,13},{6,2},{10,6},{... | collective-permute-start | bytes 577544 | tf_op jit(solution)/shard_map/ppermute | solution.py:170
  12.3 5.8 %collective-permute-done.3.xb_ref = bf16[47,16,128]{2,1,0:T(8,128)(2,1)S(1)} collective-permute-done((bf16[47,16,128]{2,1,0:T(8,128)(2,1)S(1)}, bf16[47,16,128]{2,1,0:T(8,128)(2,1)S(1)}, u32[]{:S(2)}, u32[]{:S(2)}) %collective-permute-start.3) | collective-permute-done | bytes 192544 | tf_op jit(solution)/shard_map/ppermute | solution.py:169
  18.0 3.5 %collective-permute-done.4.xa_ref = bf16[47,16,128]{2,1,0:T(8,128)(2,1)S(1)} collective-permute-done((bf16[47,16,128]{2,1,0:T(8,128)(2,1)S(1)}, bf16[47,16,128]{2,1,0:T(8,128)(2,1)S(1)}, u32[]{:S(2)}, u32[]{:S(2)}) %collective-permute-start.4) | collective-permute-done | bytes 192544 | tf_op jit(solution)/shard_map/ppermute | solution.py:170
  21.5 0.0 collective-permute-done.first_ref
  21.6 0.0 collective-permute-done.2.rest_0_
  21.6 0.0 copy-done.1
  21.6 0.0 copy-done.3
  21.6 0.0 copy-start.4
  21.6 0.1 pack_near.1
  21.7 0.1 collective-permute-start.5
  21.8 0.6 %collective-permute-start.1 = (bf16[31,2,32,128]{3,2,1,0:T(8,128)(2,1)S(1)}, bf16[31,2,32,128]{3,2,1,0:T(8,128)(2,1)S(1)}, u32[]{:S(2)}, u32[]{:S(2)}) collective-permute-start(bf16[31,2,32,128]{3,2,1,0:T(8,128)(2,1)S(1)} %get-tuple-element.11), channel_id=1, source_target_pairs={{0,3},{1,2},{2,1},{3,0},{4,7},{5,6},{6,5},{7,4},{8,11},{9,10},{10,... | collective-permute-start | bytes 1523720 | tf_op jit(solution)/shard_map/ppermute | solution.py:168
  22.4 0.5 collective-permute-start.6
  22.9 12.2 %collective-permute-done.1 = bf16[31,2,32,128]{3,2,1,0:T(8,128)(2,1)S(1)} collective-permute-done((bf16[31,2,32,128]{3,2,1,0:T(8,128)(2,1)S(1)}, bf16[31,2,32,128]{3,2,1,0:T(8,128)(2,1)S(1)}, u32[]{:S(2)}, u32[]{:S(2)}) %collective-permute-start.1) | collective-permute-done | bytes 507936 | tf_op jit(solution)/shard_map/ppermute | solution.py:168
  35.1 0.0 collective-permute-done.6.rest_1_
  35.2 0.0 collective-permute-done.5
  35.2 0.0 copy-start.10
  35.2 0.0 copy-done.7
  35.2 0.0 copy-done.8
  35.2 0.0 copy-done.6
  35.2 0.8 %copy-done.11 = bf16[31,2,32,128]{3,2,1,0:T(8,128)(2,1)} copy-done((bf16[31,2,32,128]{3,2,1,0:T(8,128)(2,1)}, bf16[31,2,32,128]{3,2,1,0:T(8,128)(2,1)S(1)}, u32[]{:S(2)}) %copy-start.11) | copy-done | bytes 507928
  36.0 0.1 copy-done.12
  36.0 0.3 copy-done.10
  36.4 27.0 %operator.1 = f32[32,192,128]{2,1,0:T(8,128)} custom-call(bf16[2,576,352]{2,1,0:T(8,128)(2,1)} %constant.7.clone.stencil_any, bf16[128,256]{1,0:T(8,128)(2,1)} %constant.8.clone.walls_ref, s32[192,128]{1,0:T(8,128)} %bitcast.37, bf16[32,192,128]{2,1,0:T(8,128)(2,1)} %bitcast.23, bf16[3,192,128]{2,1,0:T(8,128)(2,1)} %bitcast.31, ...), custom_call_target="tpu_custom_call" | custom-call | tf_op jit(solution)/shard_map/operator/pallas_call | solution.py:353
  (13 shorter events, 0.0 us)
Async XLA Ops:
  0.0 1.4 %copy-start = (bf16[4,2,4,32,6,128]{5,3,4,2,1,0:T(8,128)(2,1)S(1)}, bf16[4,2,4,32,6,128]{5,3,4,2,1,0:T(8,128)(2,1)}, u32[]{:S(2)}) copy-start(bf16[4,2,4,32,6,128]{5,3,4,2,1,0:T(8,128)(2,1)} %param.7) | copy-start | bytes 4718596
  1.4 20.2 %copy-start.1 = (bf16[4,2,4,32,6,128]{5,3,4,2,1,0:T(8,128)(2,1)S(1)}, bf16[4,2,4,32,6,128]{5,3,4,2,1,0:T(8,128)(2,1)}, u32[]{:S(2)}) copy-start(bf16[4,2,4,32,6,128]{5,3,4,2,1,0:T(8,128)(2,1)} %param.7) | copy-start | bytes 4718596
  1.5 20.1 %collective-permute-start.2 = (bf16[12,6,32,128]{3,2,1,0:T(8,128)(2,1)S(1)}, bf16[12,6,32,128]{3,2,1,0:T(8,128)(2,1)S(1)}, u32[]{:S(2)}, u32[]{:S(2)}) collective-permute-start(bf16[12,6,32,128]{3,2,1,0:T(8,128)(2,1)S(1)} %get-tuple-element.12), channel_id=1, source_target_pairs={{0,16},{16,0},{1,17},{17,1},{2,18},{18,2},{3,19},{19,3},{4,20},{20... | collective-permute-start | bytes 1769480 | tf_op jit(solution)/shard_map/ppermute | solution.py:138
  4.5 17.0 %collective-permute-start = (bf16[16,2,32,128]{3,2,1,0:T(8,128)(2,1)S(1)}, bf16[16,2,32,128]{3,2,1,0:T(8,128)(2,1)S(1)}, u32[]{:S(2)}, u32[]{:S(2)}) collective-permute-start(bf16[16,2,32,128]{3,2,1,0:T(8,128)(2,1)S(1)} %get-tuple-element.10), channel_id=1, source_target_pairs={{0,3},{1,2},{2,1},{3,0},{4,7},{5,6},{6,5},{7,4},{8,11},{9,10},{10,... | collective-permute-start | bytes 786440 | tf_op jit(solution)/shard_map/ppermute | solution.py:137
  5.2 1.1 %copy-start.2 = (bf16[2,2,3,32,6,128]{5,3,4,2,1,0:T(8,128)(2,1)S(1)}, bf16[2,2,3,32,6,128]{5,3,4,2,1,0:T(8,128)(2,1)}, u32[]{:S(2)}) copy-start(bf16[2,2,3,32,6,128]{5,3,4,2,1,0:T(8,128)(2,1)} %param.9) | copy-start | bytes 1769476
  6.2 0.9 %copy-start.5 = (bf16[3,32,6,128]{3,1,2,0:T(8,128)(2,1)S(1)}, bf16[3,32,6,128]{3,1,2,0:T(8,128)(2,1)}, u32[]{:S(2)}) copy-start(bf16[3,32,6,128]{3,1,2,0:T(8,128)(2,1)} %param.8) | copy-start | bytes 442372
  7.1 0.7 %copy-start.9 = (bf16[32,192]{1,0:T(8,128)(2,1)S(1)}, bf16[32,192]{1,0:T(8,128)(2,1)}, u32[]{:S(2)}) copy-start(bf16[32,192]{1,0:T(8,128)(2,1)} %constant.6.clone.pick_ref) | copy-start | bytes 36868
  7.8 13.7 %copy-start.3 = (bf16[2,2,3,32,6,128]{5,3,4,2,1,0:T(8,128)(2,1)S(1)}, bf16[2,2,3,32,6,128]{5,3,4,2,1,0:T(8,128)(2,1)}, u32[]{:S(2)}) copy-start(bf16[2,2,3,32,6,128]{5,3,4,2,1,0:T(8,128)(2,1)} %param.9) | copy-start | bytes 1769476
  8.4 9.6 %collective-permute-start.3 = (bf16[47,16,128]{2,1,0:T(8,128)(2,1)S(1)}, bf16[47,16,128]{2,1,0:T(8,128)(2,1)S(1)}, u32[]{:S(2)}, u32[]{:S(2)}) collective-permute-start(bf16[47,16,128]{2,1,0:T(8,128)(2,1)S(1)} %get-tuple-element.13), channel_id=1, source_target_pairs={{0,4},{4,8},{8,12},{12,0},{1,5},{5,9},{9,13},{13,1},{2,6},{6,10},{... | collective-permute-start | bytes 577544 | tf_op jit(solution)/shard_map/ppermute | solution.py:169
  10.0 11.5 %collective-permute-start.4 = (bf16[47,16,128]{2,1,0:T(8,128)(2,1)S(1)}, bf16[47,16,128]{2,1,0:T(8,128)(2,1)S(1)}, u32[]{:S(2)}, u32[]{:S(2)}) collective-permute-start(bf16[47,16,128]{2,1,0:T(8,128)(2,1)S(1)} %get-tuple-element.14), channel_id=1, source_target_pairs={{4,0},{8,4},{12,8},{0,12},{5,1},{9,5},{13,9},{1,13},{6,2},{10,6},{... | collective-permute-start | bytes 577544 | tf_op jit(solution)/shard_map/ppermute | solution.py:170
  18.0 17.1 %copy-start.7 = (bf16[47,16,128]{2,1,0:T(8,128)(2,1)}, bf16[47,16,128]{2,1,0:T(8,128)(2,1)S(1)}, u32[]{:S(2)}) copy-start(bf16[47,16,128]{2,1,0:T(8,128)(2,1)S(1)} %collective-permute-done.3.xb_ref) | copy-start | bytes 577540
  21.5 13.6 %copy-start.8 = (bf16[47,16,128]{2,1,0:T(8,128)(2,1)}, bf16[47,16,128]{2,1,0:T(8,128)(2,1)S(1)}, u32[]{:S(2)}) copy-start(bf16[47,16,128]{2,1,0:T(8,128)(2,1)S(1)} %collective-permute-done.4.xa_ref) | copy-start | bytes 577540
  21.5 13.6 %copy-start.6 = (bf16[16,2,32,128]{3,2,1,0:T(8,128)(2,1)}, bf16[16,2,32,128]{3,2,1,0:T(8,128)(2,1)S(1)}, u32[]{:S(2)}) copy-start(bf16[16,2,32,128]{3,2,1,0:T(8,128)(2,1)S(1)} %collective-permute-done.first_ref) | copy-start | bytes 786436
  21.6 13.6 %copy-start.4 = (bf16[12,6,32,128]{3,2,1,0:T(8,128)(2,1)}, bf16[12,6,32,128]{3,2,1,0:T(8,128)(2,1)S(1)}, u32[]{:S(2)}) copy-start(bf16[12,6,32,128]{3,2,1,0:T(8,128)(2,1)S(1)} %collective-permute-done.2.rest_0_) | copy-start | bytes 1769476
  21.7 13.5 %collective-permute-start.5 = (bf16[59,2,32,128]{3,2,1,0:T(8,128)(2,1)S(1)}, bf16[59,2,32,128]{3,2,1,0:T(8,128)(2,1)S(1)}, u32[]{:S(2)}, u32[]{:S(2)}) collective-permute-start(bf16[59,2,32,128]{3,2,1,0:T(8,128)(2,1)S(1)} %pack_near.1), channel_id=1, source_target_pairs={{0,1},{1,0},{2,3},{3,2},{4,5},{5,4},{6,7},{7,6},{8,9},{9,8},{10,11... | collective-permute-start | bytes 2899976 | tf_op jit(solution)/shard_map/ppermute | solution.py:209
  21.8 13.4 %collective-permute-start.1 = (bf16[31,2,32,128]{3,2,1,0:T(8,128)(2,1)S(1)}, bf16[31,2,32,128]{3,2,1,0:T(8,128)(2,1)S(1)}, u32[]{:S(2)}, u32[]{:S(2)}) collective-permute-start(bf16[31,2,32,128]{3,2,1,0:T(8,128)(2,1)S(1)} %get-tuple-element.11), channel_id=1, source_target_pairs={{0,3},{1,2},{2,1},{3,0},{4,7},{5,6},{6,5},{7,4},{8,11},{9,10},{10,... | collective-permute-start | bytes 1523720 | tf_op jit(solution)/shard_map/ppermute | solution.py:168
  22.4 12.7 %collective-permute-start.6 = (bf16[12,96,128]{2,1,0:T(8,128)(2,1)S(1)}, bf16[12,96,128]{2,1,0:T(8,128)(2,1)S(1)}, u32[]{:S(2)}, u32[]{:S(2)}) collective-permute-start(bf16[12,96,128]{2,1,0:T(8,128)(2,1)S(1)} %pack_relay.1.rest_1_), channel_id=1, source_target_pairs={{0,16},{16,0},{1,17},{17,1},{2,18},{18,2},{3,19},{19,3},{4,20},{20... | collective-permute-start | bytes 884744 | tf_op jit(solution)/shard_map/ppermute | solution.py:191
  35.1 0.8 %copy-start.11 = (bf16[31,2,32,128]{3,2,1,0:T(8,128)(2,1)}, bf16[31,2,32,128]{3,2,1,0:T(8,128)(2,1)S(1)}, u32[]{:S(2)}) copy-start(bf16[31,2,32,128]{3,2,1,0:T(8,128)(2,1)S(1)} %collective-permute-done.1) | copy-start | bytes 1523716
  35.2 0.9 %copy-start.12 = (bf16[12,96,128]{2,1,0:T(8,128)(2,1)}, bf16[12,96,128]{2,1,0:T(8,128)(2,1)S(1)}, u32[]{:S(2)}) copy-start(bf16[12,96,128]{2,1,0:T(8,128)(2,1)S(1)} %collective-permute-done.6.rest_1_) | copy-start | bytes 884740
  35.2 1.2 %copy-start.10 = (bf16[59,2,32,128]{3,2,1,0:T(8,128)(2,1)}, bf16[59,2,32,128]{3,2,1,0:T(8,128)(2,1)S(1)}, u32[]{:S(2)}) copy-start(bf16[59,2,32,128]{3,2,1,0:T(8,128)(2,1)S(1)} %collective-permute-done.5) | copy-start | bytes 2899972

commit v2 on v1

--- a/solution.py
+++ b/solution.py
@@ -59,6 +59,11 @@
     return out
 
 
+def wall_pairs(ny):
+    first, second = np.split(wall_columns(ny), 2, axis=1)
+    return np.block([[first, first, second, second], [first, -first, second, -second]])
+
+
 def edge_rows(nz, nx):
     pick = np.zeros((2 * HALO_X, nz * nx), np.float32)
     for z in range(nz):
@@ -169,9 +174,191 @@
     xb_got = lax.ppermute(edge_hi, "gx", up_x)
     xa_got = lax.ppermute(edge_lo, "gx", down_x)
 
+    quarter = nx // 4
+    part = own // 2
+    walls_pair = jnp.asarray(wall_pairs(ny), bf16)
+    table = stencil_rows(nz, nx, False).reshape(3, nz, nx, -1)
+    PAIRS = ((0, 3), (1, 2))
+    DRIFT = (-1.5 * FREQUENCY_STEP, -0.5 * FREQUENCY_STEP)
+
+    def entries(t, p, q, r, s):
+        return t, q, p + r, p - r, q + s, s - q, t + p, t - p
+
+    def couple(acc, ent, vec):
+        t, q, pr, pmr, qs, sq, tp, tmp = ent
+        out = []
+        for i in range(2):
+            a, e, b, g = (vec[j][i] for j in range(4))
+            out.append(
+                (
+                    acc[0][i] + t * a + pr * b + sq * g,
+                    acc[1][i] + t * e + qs * b + pmr * g,
+                    acc[2][i] + pr * a + qs * e + tp * b + q * g,
+                    acc[3][i] + sq * a + pmr * e + q * b + tmp * g,
+                )
+            )
+        return [(out[0][j], out[1][j]) for j in range(4)]
+
+    def harmonics_of(acc, scale):
+        out = [None] * 4
+        for at, (lo, hi) in enumerate(PAIRS):
+            (ar, ai), (er, ei) = acc[2 * at], acc[2 * at + 1]
+            out[lo] = ((ar + ei) * scale, (ai - er) * scale)
+            out[hi] = ((ar - ei) * scale, (ai + er) * scale)
+        return out
+
+    def basis_of(values):
+        out = []
+        for lo, hi in PAIRS:
+            (lr, li), (hr, hi_) = values[lo], values[hi]
+            out += [(lr + hr, li + hi_), (hi_ - li, lr - hr)]
+        return out
+
+    def resident_kernel(edge):
+        def pick(x):
+            x = x.reshape(nz, nx, ny)
+            if edge:
+                x = jnp.concatenate([x[:, :quarter], x[:, nx - quarter :]], axis=1)
+            else:
+                x = x[:, quarter : nx - quarter]
+            return x.reshape(part, ny)
+
+        cells = table[:, :, [*range(quarter), *range(nx - quarter, nx)]] if edge else table[:, :, quarter : nx - quarter]
+        depth = own + 2 * HALO_X if edge else own
+        rows_of = jnp.asarray(cells[..., :depth].reshape(3 * part, depth), bf16)
+
+        def body(rows_ref, walls_ref, mask_ref, pert_ref, mean_ref, mode_ref, *rest):
+            if edge:
+                xb_ref, xa_ref = rest[:2]
+            out_ref, grads, plain, ents, lin = rest[-5:]
+            me_h = place()[0]
+            mean_freq = 12.0 * FREQUENCY_STEP * (me_h * per + 1.5 - per * harms / 2).astype(f32)
+
+            def rhs(ref, at, fields):
+                cols = []
+                for f in fields:
+                    mine = ref[f]
+                    if edge:
+                        mine = jnp.concatenate([mine, xb_ref[at + f], xa_ref[at + f]], axis=0)
+                    cols.append(mine)
+                return cols[0] if len(cols) == 1 else jnp.concatenate(cols, axis=1)
+
+            def dot(a, b):
+                return jnp.dot(a, b, preferred_element_type=f32)
+
+            for at, (lo, hi) in enumerate(PAIRS):
+                for i in range(2):
+                    fl, fr = lo * 8 + i * 4 + 3, hi * 8 + i * 4 + 3
+                    got = dot(rows_ref[: 2 * part], rhs(pert_ref, 0, (fl, fr)))
+                    wall = dot(jnp.concatenate([pick(pert_ref[fl].astype(f32)), pick(pert_ref[fr].astype(f32))], axis=1).astype(bf16), walls_ref[:, : 2 * ny])
+                    for d in range(3):
+                        if d == 1:
+                            total, diff = wall[:, :ny], wall[:, ny:]
+                        else:
+                            span = slice(0, part) if d == 0 else slice(part, 2 * part)
+                            total, diff = got[span, :ny] + got[span, ny:], got[span, :ny] - got[span, ny:]
+                        lin[2 * at, i, d] = total
+                        lin[2 * at + 1, 1 - i, d] = diff if i == 0 else -diff
+            for at, (lo, hi) in enumerate(PAIRS):
+                for c in range(3):
+                    for i in range(2):
+                        sign = 1.0 if i == 0 else -1.0
+                        fl, fr = lo * 8 + i * 4 + c, hi * 8 + i * 4 + c
+                        got = dot(rows_ref[...], rhs(pert_ref, 0, (fl, fr)))
+                        xl, xr = pick(pert_ref[fl].astype(f32)), pick(pert_ref[fr].astype(f32))
+                        wall = dot(jnp.concatenate([xl, xr], axis=1).astype(bf16), walls_ref[...])
+                        total, diff = xl + xr, xl - xr
+                        plain[2 * at, i, c] = total
+                        plain[2 * at + 1, 1 - i, c] = sign * diff
+                        for d in range(3):
+                            if d == 1:
+                                gt, gd = wall[:, :ny], wall[:, ny : 2 * ny]
+                            else:
+                                span = slice(0, part) if d == 0 else slice(part, 2 * part)
+                                gt, gd = got[span, :ny] + got[span, ny:], got[span, :ny] - got[span, ny:]
+                            gd = sign * gd
+                            grads[2 * at, i, c, d] = gt
+                            grads[2 * at + 1, 1 - i, c, d] = gd
+                            if d == c:
+                                if c == 0:
+                                    lin[2 * at, i, 3] = gt
+                                    lin[2 * at + 1, 1 - i, 3] = gd
+                                else:
+                                    lin[2 * at, i, 3] = lin[2 * at, i, 3] + gt
+                                    lin[2 * at + 1, 1 - i, 3] = lin[2 * at + 1, 1 - i, 3] + gd
+                        lt = got[2 * part :, :ny] + got[2 * part :, ny:] + wall[:, 2 * ny : 3 * ny]
+                        ld = got[2 * part :, :ny] - got[2 * part :, ny:] + wall[:, 3 * ny :]
+                        solid = (12.0 * PENALTY) * pick(mask_ref[...].astype(f32))
+                        drift = 12.0 * DRIFT[at]
+                        lin[2 * at, i, c] = lin[2 * at, i, c] - VISCOSITY * lt + solid * total
+                        lin[2 * at + 1, 1 - i, c] = lin[2 * at + 1, 1 - i, c] + sign * (solid * diff - VISCOSITY * ld)
+                        lin[2 * at, 1 - i, c] = lin[2 * at, 1 - i, c] + sign * (mean_freq * total + drift * diff)
+                        lin[2 * at + 1, i, c] = lin[2 * at + 1, i, c] - (mean_freq * diff + drift * total)
+            for c in range(3):
+                picked = [pick(mean_ref[c].astype(f32))] + [pick(mode_ref[3 * i + c].astype(f32)) for i in range(4)]
+                for n, ent in enumerate(entries(*picked)):
+                    ents[c, n] = ent
+                mean_at = dot(rows_ref[: 2 * part], rhs(mean_ref, n_pert, (c,)))
+                mean_wall = dot(picked[0].astype(bf16), walls_ref[:ny, :ny])
+                at = n_pert + n_mean
+                real = dot(rows_ref[: 2 * part], rhs(mode_ref, at, (c, 6 + c)))
+                imag = dot(rows_ref[: 2 * part], rhs(mode_ref, at, (3 + c, 9 + c)))
+                wall_real = dot(jnp.concatenate([picked[1], picked[3]], axis=1).astype(bf16), walls_ref[:, : 2 * ny])
+                wall_imag = dot(jnp.concatenate([picked[2], picked[4]], axis=1).astype(bf16), walls_ref[:, : 2 * ny])
+                for d in range(3):
+                    if d == 1:
+                        pr, pmr = wall_real[:, :ny], wall_real[:, ny:]
+                        qs, qms = wall_imag[:, :ny], wall_imag[:, ny:]
+                        t, p, q = mean_wall, 0.5 * (pr + pmr), 0.5 * (qs + qms)
+                        values = (t, q, pr, pmr, qs, -qms, t + p, t - p)
+                    else:
+                        span = slice(0, part) if d == 0 else slice(part, 2 * part)
+                        values = entries(mean_at[span], real[span, :ny], imag[span, :ny], real[span, ny:], imag[span, ny:])
+                    for n, ent in enumerate(values):
+                        ents[3 + 3 * d + c, n] = ent
+
+            def block(b, carry):
+                rows = pl.ds(pl.multiple_of(b * 8, 8), 8)
+                for c in range(4):
+                    acc = [(lin[j, 0, c, rows], lin[j, 1, c, rows]) for j in range(4)]
+                    if c < 3:
+                        for d in range(3):
+                            flow = [ents[d, n, rows] for n in range(8)]
+                            acc = couple(acc, flow, [(grads[j, 0, c, d, rows], grads[j, 1, c, d, rows]) for j in range(4)])
+                            slope = [ents[3 + 3 * d + c, n, rows] for n in range(8)]
+                            acc = couple(acc, slope, [(plain[j, 0, d, rows], plain[j, 1, d, rows]) for j in range(4)])
+                    for k, (re, im) in enumerate(harmonics_of(acc, 1.0 / 24.0)):
+                        out_ref[k * 8 + c, rows] = re
+                        out_ref[k * 8 + 4 + c, rows] = im
+                return carry
+
+            lax.fori_loop(0, part // 8, block, 0)
+
+        def call(*extra):
+            return pl.pallas_call(
+                body,
+                out_shape=jax.ShapeDtypeStruct((n_pert, part, ny), f32),
+                in_specs=[VMEM] * 6 + ([VMEM, VMEM] if edge else [ANY]) + [ANY] * (len(extra) - (2 if edge else 1)),
+                out_specs=VMEM,
+                scratch_shapes=[
+                    pltpu.VMEM((4, 2, 3, 3, part, ny), f32),
+                    pltpu.VMEM((4, 2, 3, part, ny), f32),
+                    pltpu.VMEM((12, 8, part, ny), f32),
+                    pltpu.VMEM((4, 2, 4, part, ny), f32),
+                ],
+                compiler_params=roomy,
+                cost_estimate=pl.CostEstimate(flops=40_000_000, bytes_accessed=20_000_000, transcendentals=0),
+            )(rows_of, walls_pair, mask, flat(pert), flat(mean), flat(mode), *extra)
+
+        return call
+
+    flat = lambda a: a.reshape(a.shape[0], -1, ny)
+    with jax.named_scope("resident_middle"):
+        middle = resident_kernel(False)(edge_lo)
+
     deep = 2 * nx + 2 * HALO_X
 
-    def pack_relay(first_ref, xb_ref, xa_ref, *outs):
+    def pack_relay(first_ref, xb_ref, xa_ref, _, *outs):
         scal = place()
         for s, out in enumerate(outs):
             for i in range(modes * 2):
@@ -186,8 +373,9 @@
         relay = pl.pallas_call(
             pack_relay,
             out_shape=tuple(jax.ShapeDtypeStruct((n_nb, deep, ny), bf16) for _ in range(sides)),
+            in_specs=[VMEM] * 3 + [ANY],
             compiler_params=roomy,
-        )(first_got, xb_got, xa_got)
+        )(first_got, xb_got, xa_got, middle)
     relay_got = [lax.ppermute(b, "harm", p) for b, p in zip(relay, harm_perms)]
 
     def pack_near(pert_ref, mean_ref, mode_ref, *rest):
@@ -208,42 +396,49 @@
         )(pert, mean, mode, *nb_got, relay[0])
     near_got = lax.ppermute(near, "gz", near_pairs)
 
-    at_xb, at_xa = own, own + HALO_X
-    at_cross = own + 2 * HALO_X
+    with jax.named_scope("resident_edge"):
+        edges = resident_kernel(True)(xb_got, xa_got, relay[0], near)
+
+    at_xb, at_cross = own, own + 2 * HALO_X
     at_near = at_cross + 2 * nx
     depth = at_near + 2 * nx
-    stencil = jnp.asarray(np.stack([stencil_rows(nz, nx, False), stencil_rows(nz, nx, True)]), bf16)
-    walls = jnp.asarray(wall_columns(ny), bf16)
-    n_even = n_all + n_all % 2
-
-    def operator(stencil_any, walls_ref, mask_ref, pert_ref, mean_ref, mode_ref, first_ref, second_ref, near_ref, xb_ref, xa_ref, *rest):
+    both_stencils = np.stack([stencil_rows(nz, nx, odd)[: 2 * own] for odd in (False, True)])
+    n_ext = n_modes + sides * n_nb
+
+    def finish(stencil_any, walls_ref, pert_ref, mean_ref, mode_ref, middle_any, edges_any, mode_any, first_any, second_any, near_any, second_flat, near_flat, xb_any, xa_any, *rest):
         scal = place()
-        nb_refs, relay_refs = rest[:sides], rest[sides : 2 * sides]
-        out_ref, fields, grads, laps, plain, weights, sems = rest[2 * sides :]
-        base_at = n_pert
+        nb_any, relay_any = rest[:sides], rest[sides : 2 * sides]
+        out_ref, fields, halo, grads, plain, weights, sems = rest[2 * sides :]
         copies = [(stencil_any.at[scal[1]], weights)]
-        copies.append((pert_ref, fields.at[pl.ds(0, n_pert), pl.ds(0, own)]))
-        copies.append((mean_ref, fields.at[pl.ds(base_at, n_mean), pl.ds(0, own)]))
-        copies.append((mode_ref, fields.at[pl.ds(base_at + n_mean, n_modes), pl.ds(0, own)]))
-        cross = pl.ds(at_cross, 2 * nx)
+        cross, close = pl.ds(at_cross, 2 * nx), pl.ds(at_near, 2 * nx)
+        mine = pl.ds(0, n_modes)
+        base_modes_at = n_pert + n_mean
+        second_at = n_pert - n_first
+        copies.append((mode_any, fields.at[mine, pl.ds(0, own)]))
+        copies.append((second_flat.at[pl.ds(second_at + n_mean, n_modes)], fields.at[mine, cross]))
+        copies.append((near_flat.at[pl.ds(base_modes_at, n_modes)], fields.at[mine, close]))
+        copies.append((xb_any.at[pl.ds(base_modes_at, n_modes)], fields.at[mine, pl.ds(at_xb, HALO_X)]))
+        copies.append((xa_any.at[pl.ds(base_modes_at, n_modes)], fields.at[mine, pl.ds(at_xb + HALO_X, HALO_X)]))
+        for s in range(sides):
+            mine = pl.ds(n_modes + s * n_nb, n_nb)
+            copies.append((nb_any[s], fields.at[mine, pl.ds(0, own)]))
+            copies.append((relay_any[s].at[:, pl.ds(0, 2 * nx)], fields.at[mine, cross]))
+            copies.append((relay_any[s].at[:, pl.ds(2 * nx, 2 * HALO_X)], fields.at[mine, pl.ds(at_xb, 2 * HALO_X)]))
+            copies.append((near_flat.at[pl.ds(n_res + s * n_nb, n_nb)], fields.at[mine, close]))
         if swap:
             rest_at = per - modes - scal[4]
-            copies.append((first_ref, fields.at[pl.ds(scal[4] * 8, n_first), cross]))
-            copies.append((second_ref.at[pl.ds(0, n_pert - n_first)], fields.at[pl.ds(rest_at * 8, n_pert - n_first), cross]))
+            copies.append((first_any, halo.at[0, pl.ds(scal[4] * 8, n_first)]))
+            copies.append((second_any.at[pl.ds(0, second_at)], halo.at[0, pl.ds(rest_at * 8, second_at)]))
         else:
-            copies.append((first_ref, fields.at[pl.ds(0, n_pert), cross]))
-        copies.append((second_ref.at[pl.ds(n_pert - n_first, n_base)], fields.at[pl.ds(base_at, n_base), cross]))
-        copies.append((near_ref, fields.at[pl.ds(0, n_all), pl.ds(at_near, 2 * nx)]))
-        copies.append((xb_ref, fields.at[pl.ds(0, n_res), pl.ds(at_xb, HALO_X)]))
-        copies.append((xa_ref, fields.at[pl.ds(0, n_res), pl.ds(at_xa, HALO_X)]))
-        for s in range(sides):
-            mine = pl.ds(n_res + s * n_nb, n_nb)
-            copies.append((nb_refs[s], fields.at[mine, pl.ds(0, own)]))
-            copies.append((relay_refs[s].at[:, pl.ds(0, 2 * nx)], fields.at[mine, cross]))
-            copies.append((relay_refs[s].at[:, pl.ds(2 * nx, 2 * HALO_X)], fields.at[mine, pl.ds(at_xb, 2 * HALO_X)]))
+            copies.append((first_any, halo.at[0, pl.ds(0, n_pert)]))
+        copies.append((second_any.at[pl.ds(second_at, n_base)], halo.at[0, pl.ds(n_pert, n_base)]))
+        copies.append((near_any.at[pl.ds(0, n_res)], halo.at[1]))
+        for z in range(nz):
+            half = nx // 2
+            copies.append((middle_any.at[:, pl.ds(z * half, half)], out_ref.at[:, pl.ds(z * nx + quarter, half)]))
+            copies.append((edges_any.at[:, pl.ds(z * half, quarter)], out_ref.at[:, pl.ds(z * nx, quarter)]))
+            copies.append((edges_any.at[:, pl.ds(z * half + quarter, quarter)], out_ref.at[:, pl.ds(z * nx + nx - quarter, quarter)]))
         run_copies(copies, sems)
-        if n_even != n_all:
-            fields[n_all] = jnp.zeros((depth, ny), bf16)
 
         def slopes(pair, carry):
             f = 2 * pair
@@ -252,121 +447,123 @@
             for i in range(2):
                 lanes = slice(i * ny, (i + 1) * ny)
                 grads[f + i, 0] = got[:own, lanes]
-                grads[f + i, 2] = got[own : 2 * own, lanes]
-                mine = fields[f + i, pl.ds(0, own)]
-                wall = jnp.dot(mine, walls_ref[...], preferred_element_type=f32)
-                grads[f + i, 1] = wall[:, :ny]
-                laps[f + i] = got[2 * own :, lanes] + wall[:, ny:]
-                plain[f + i] = mine.astype(f32)
+                grads[f + i, 2] = got[own:, lanes]
+                own_rows = fields[f + i, pl.ds(0, own)]
+                grads[f + i, 1] = jnp.dot(own_rows, walls_ref[:ny, :ny], preferred_element_type=f32)
+                plain[f + i] = own_rows.astype(f32)
             return carry
 
-        lax.fori_loop(0, n_even // 2, slopes, 0)
-
-        def base_at_mode(m, c):
-            if m == 0:
-                return base_at + c, None, 1.0
-            at = base_at + n_mean + (abs(m) - 1) * 6 + c
-            return at, at + 3, (1.0 if m > 0 else -1.0)
-
-        def product(acc, flow, value):
-            (fr, fi, sign), (vr, vi) = flow, value
-            re, im = acc[0] + fr * vr, acc[1] + fr * vi
-            if fi is not None:
-                if sign > 0:
-                    re, im = re - fi * vi, im + fi * vr
-                else:
-                    re, im = re + fi * vi, im - fi * vr
-            return re, im
-
-        def contribution(acc, pairs, rows):
-            for d in range(3):
-                for k, m, at in pairs:
-                    fr, fi, sign = base_at_mode(m, d)
-                    flow = (plain[fr, rows], None if fi is None else plain[fi, rows], sign)
-                    along = (plain[at + d, rows], plain[at + d + nb_step(at), rows])
-                    for c in range(3):
-                        sr, si, _ = base_at_mode(m, c)
-                        slope = (grads[sr, d, rows], None if si is None else grads[si, d, rows], sign)
-                        grad = (grads[at + c, d, rows], grads[at + c + nb_step(at), d, rows])
-                        acc[k, c] = product(acc[k, c], flow, grad)
-                        acc[k, c] = product(acc[k, c], slope, along)
-            return acc
-
-        def nb_step(at):
-            return 4 if at < n_pert else 3
-
-        resident, below, above = [], [], []
+        lax.fori_loop(0, n_ext // 2, slopes, 0)
+
+        def product(acc, flow, value, sign):
+            (fr, fi), (vr, vi) = flow, value
+            if sign > 0:
+                return acc[0] + fr * vr - fi * vi, acc[1] + fr * vi + fi * vr
+            return acc[0] + fr * vr + fi * vi, acc[1] + fr * vi - fi * vr
+
+        below, above = [], []
         for k in range(per):
             for m in range(-modes, modes + 1):
                 l = k - m
                 if l < 0:
-                    below.append((k, m, n_res + (l + modes) * 6))
+                    below.append((k, m, n_modes + (l + modes) * 6))
                 elif l >= per:
-                    above.append((k, m, n_res + (sides - 1) * n_nb + (l - per) * 6))
-                else:
-                    resident.append((k, m, l * 8))
-        half = per * harms // 2
-
-        def block(b, carry):
-            rows = pl.ds(pl.multiple_of(b * 8, 8), 8)
-            zero = jnp.zeros((8, ny), f32)
-            acc = {(k, c): (zero, zero) for k in range(per) for c in range(3)}
-            acc = contribution(acc, resident, rows)
-            solid = PENALTY * mask_ref[rows].astype(f32)
-            for k in range(per):
-                freq = FREQUENCY_STEP * (scal[0] * per + k - half).astype(f32)
-                for c in range(3):
-                    ur, ui = plain[k * 8 + c, rows], plain[k * 8 + 4 + c, rows]
-                    re = acc[k, c][0] + grads[k * 8 + 3, c, rows] - VISCOSITY * laps[k * 8 + c, rows]
-                    im = acc[k, c][1] + grads[k * 8 + 7, c, rows] - VISCOSITY * laps[k * 8 + 4 + c, rows]
-                    out_ref[k * 8 + c, rows] = re * (1.0 / 12.0) + (solid * ur - freq * ui)
-                    out_ref[k * 8 + 4 + c, rows] = im * (1.0 / 12.0) + (solid * ui + freq * ur)
-                for i in range(2):
-                    at = k * 8 + 4 * i
-                    out_ref[at + 3, rows] = (grads[at, 0, rows] + grads[at + 1, 1, rows] + grads[at + 2, 2, rows]) * (1.0 / 12.0)
-            return carry
-
-        lax.fori_loop(0, own // 8, block, 0)
+                    above.append((k, m, n_modes + (sides - 1) * n_nb + (l - per) * 6))
 
         def neighbours(pairs):
-            def nb_block(b, carry):
+            def block(b, carry):
                 rows = pl.ds(pl.multiple_of(b * 8, 8), 8)
-                zero = jnp.zeros((8, ny), f32)
-                keys = sorted({k for k, _, _ in pairs})
-                acc = {(k, c): (zero, zero) for k in keys for c in range(3)}
-                acc = contribution(acc, pairs, rows)
-                for k in keys:
+                for k in sorted({p[0] for p in pairs}):
+                    zero = jnp.zeros((8, ny), f32)
+                    acc = [(zero, zero)] * 3
+                    for _, m, at in [p for p in pairs if p[0] == k]:
+                        base = (abs(m) - 1) * 6
+                        for d in range(3):
+                            flow = plain[base + d, rows], plain[base + 3 + d, rows]
+                            along = plain[at + d, rows], plain[at + 3 + d, rows]
+                            for c in range(3):
+                                slope = grads[base + c, d, rows], grads[base + 3 + c, d, rows]
+                                grad = grads[at + c, d, rows], grads[at + 3 + c, d, rows]
+                                acc[c] = product(acc[c], flow, grad, m)
+                                acc[c] = product(acc[c], slope, along, m)
                     for c in range(3):
                         for i in range(2):
                             at = k * 8 + 4 * i + c
-                            out_ref[at, rows] = out_ref[at, rows] + acc[k, c][i] * (1.0 / 12.0)
+                            out_ref[at, rows] = out_ref[at, rows] + acc[c][i] * (1.0 / 12.0)
                 return carry
 
-            lax.fori_loop(0, own // 8, nb_block, 0)
+            lax.fori_loop(0, own // 8, block, 0)
 
         pl.when(scal[0] > 0)(lambda: neighbours(below))
         pl.when(scal[0] < harms - 1)(lambda: neighbours(above))
 
-    n_copies = 10 + 3 * sides + (1 if swap else 0)
-    flat = lambda a: a.reshape(a.shape[0], -1, ny)
-    with jax.named_scope("operator"):
+        def face_block(n, carry):
+            side, step, chunk = n // 4, (n // 2) % 2, n % 2
+            before = side == scal[1]
+            near_at = jnp.where(before, 1, 0)
+            layer = jnp.where(before, step, nz - 1 - step)
+            turn = jnp.where(before, 1.0, -1.0)
+            first_step = step == 0
+            cn, cf = turn * jnp.where(first_step, -8.0, 1.0), turn * jnp.where(first_step, 1.0, 0.0)
+            ln, lf = jnp.where(first_step, 16.0, -1.0), jnp.where(first_step, -1.0, 0.0)
+            rows = pl.ds(pl.multiple_of(layer * nx + chunk * 16, 16), 16)
+            strip = pl.ds(pl.multiple_of(chunk * 16, 16), 16)
+
+            def halos(f):
+                return halo[side, f, near_at, strip].astype(f32), halo[side, f, 1 - near_at, strip].astype(f32)
+
+            def slope(f):
+                a, b = halos(f)
+                return cn * a + cf * b
+
+            def slope_lap(f):
+                a, b = halos(f)
+                return cn * a + cf * b, ln * a + lf * b
+
+            flow = entries(mean_ref[2, rows].astype(f32), *[mode_ref[3 * i + 2, rows].astype(f32) for i in range(4)])
+            along = basis_of([(pert_ref[l * 8 + 2, rows].astype(f32), pert_ref[l * 8 + 6, rows].astype(f32)) for l in range(per)])
+            for c in range(4):
+                if c < 3:
+                    got = [[slope_lap(l * 8 + 4 * i + c) for i in range(2)] for l in range(per)]
+                    vec = basis_of([(g[0][0], g[1][0]) for g in got])
+                    lap = basis_of([(g[0][1], g[1][1]) for g in got])
+                    acc = [tuple(-VISCOSITY * v for v in pair) for pair in lap]
+                    if c == 2:
+                        press = basis_of([(slope(l * 8 + 3), slope(l * 8 + 7)) for l in range(per)])
+                        acc = [(a[0] + p[0], a[1] + p[1]) for a, p in zip(acc, press)]
+                    acc = couple(acc, flow, vec)
+                    bend = entries(slope(n_pert + c), *[slope(n_pert + n_mean + 3 * i + c) for i in range(4)])
+                    acc = couple(acc, bend, along)
+                else:
+                    acc = vec
+                for k, parts in enumerate(harmonics_of(acc, 1.0 / 24.0)):
+                    for i in range(2):
+                        at = k * 8 + 4 * i + c
+                        out_ref[at, rows] = out_ref[at, rows] + parts[i]
+            return carry
+
+        lax.fori_loop(0, 8, face_block, 0)
+
+    n_copies = 6 + 4 * sides + (2 if swap else 1) + 2 + 3 * nz
+    with jax.named_scope("finish"):
         out = pl.pallas_call(
-            operator,
+            finish,
             out_shape=jax.ShapeDtypeStruct((n_pert, own, ny), f32),
-            in_specs=[ANY, VMEM, VMEM] + [ANY] * (8 + 2 * sides),
+            in_specs=[ANY] + [VMEM] * 4 + [ANY] * (10 + 2 * sides),
             out_specs=VMEM,
             scratch_shapes=[
-                pltpu.VMEM((n_even, depth, ny), bf16),
-                pltpu.VMEM((n_even, 3, own, ny), f32),
-                pltpu.VMEM((n_even, own, ny), f32),
-                pltpu.VMEM((n_even, own, ny), f32),
-                pltpu.VMEM((3 * own, depth), bf16),
+                pltpu.VMEM((n_ext, depth, ny), bf16),
+                pltpu.VMEM((2, n_res, 2, nx, ny), bf16),
+                pltpu.VMEM((n_ext, 3, own, ny), f32),
+                pltpu.VMEM((n_ext, own, ny), f32),
+                pltpu.VMEM((2 * own, depth), bf16),
                 pltpu.SemaphoreType.DMA((n_copies,)),
             ],
-            compiler_params=pltpu.CompilerParams(vmem_limit_bytes=VMEM_BYTES),
+            compiler_params=roomy,
+            cost_estimate=pl.CostEstimate(flops=40_000_000, bytes_accessed=20_000_000, transcendentals=0),
         )(
-            stencil, walls, mask, flat(pert), flat(mean), flat(mode), flat(first_got), flat(second_got), flat(near_got),
-            xb_got, xa_got, *[flat(b) for b in nb_got], *relay_got,
+            jnp.asarray(both_stencils, bf16), walls_pair, flat(pert), flat(mean), flat(mode), middle, edges, flat(mode),
+            first_got, second_got, near_got, flat(second_got), flat(near_got), xb_got, xa_got, *[flat(b) for b in nb_got], *relay_got,
         )
     return jnp.swapaxes(out.reshape(per, 2, 4, nz, nx, ny), 3, 4)
 

time: 63.7 us -> 46.5 us (0.73)
  waiting for transfers between devices: 21.5 us -> 12.4 us
  Pallas kernels: 27.7 us -> 20.8 us
  local copies, waits for them, and re-layouts: 5.28 us -> 4.14 us
    pallas_call x1 -> x3, Pallas kernels: 27 us -> 20.1 us  [the longest x1 11 us: shards(): pl.pallas_call(finish, out_shape=jax.ShapeDtypeStruct((n_pert, own, ny),...]
    ppermute x1, waiting for transfers between devices: 12.2 us -> 7.64 us  [shards(): second_got = lax.ppermute(second, 'gz', cross_pairs)]
    ppermute x1, waiting for transfers between devices: 5.76 us -> 1.26 us  [shards(): xb_got = lax.ppermute(edge_hi, 'gx', up_x)]
    unnamed x26 -> x24, local copies, waits for them, and re-layouts: 5.28 us -> 4.14 us
  transfers between devices with their start and end apart: 7 -> 7, of which waited for: 3 -> 3; matrix products, arithmetic and copies ran while one was open for 0% -> 0% of each run, Pallas kernels for 1% -> 21%
where the time goes in v2:
time: 46.5 us; the launch traced here: 46.2 us
  Pallas kernels  20.8 us (45%)
  waiting for transfers between devices  12.4 us (27%)
  starting transfers between devices  8.76 us (19%)
  local copies, waits for them, and re-layouts  4.14 us (9%)
    pallas_call x1, Pallas kernels, shards(): pl.pallas_call(finish, out_shape=jax.ShapeDtypeStruct((n_pert, own, ny),...  11 us
    pallas_call x2, Pallas kernels, call(): pl.pallas_call(body, out_shape=jax.ShapeDtypeStruct((n_pert, part, ny), f...  9.05 us
    ppermute x1, waiting for transfers between devices, shards(): second_got = lax.ppermute(second, 'gz', cross_pairs)  7.64 us
    unnamed x24, local copies, waits for them, and re-layouts  4.14 us
    ppermute x1, waiting for transfers between devices, shards(): xa_got = lax.ppermute(edge_lo, 'gx', down_x)  3.51 us
    ppermute x1, starting transfers between devices, shards(): nb_got = [lax.ppermute(b, 'harm', p) for b, p in zip(nb_send, harm_perms)]  3.03 us
    ppermute x1, starting transfers between devices, shards(): xa_got = lax.ppermute(edge_lo, 'gx', down_x)  2.25 us
    ppermute x1, starting transfers between devices, shards(): xb_got = lax.ppermute(edge_hi, 'gx', up_x)  1.61 us
  transfers between devices with their start and end apart: 7, of which 3 were waited for; matrix products, arithmetic and copies ran while one was open for 0% of the time, Pallas kernels for 21%

profile of v2, /device:TPU:0, one launch (start us, length us, event | category | flops | bytes accessed | tf_op | source)
XLA Modules:
  0.0 46.2 jit_solution(12850285745792537858)
XLA Ops:
  0.0 1.4 %copy-done = bf16[4,2,4,32,6,128]{5,3,4,2,1,0:T(8,128)(2,1)S(1)} copy-done((bf16[4,2,4,32,6,128]{5,3,4,2,1,0:T(8,128)(2,1)S(1)}, bf16[4,2,4,32,6,128]{5,3,4,2,1,0:T(8,128)(2,1)}, u32[]{:S(2)}) %copy-start) | copy-done | bytes 1572888
  1.4 0.1 pack_first.1
  1.5 3.0 %collective-permute-start.3 = (bf16[12,6,32,128]{3,2,1,0:T(8,128)(2,1)S(1)}, bf16[12,6,32,128]{3,2,1,0:T(8,128)(2,1)S(1)}, u32[]{:S(2)}, u32[]{:S(2)}) collective-permute-start(bf16[12,6,32,128]{3,2,1,0:T(8,128)(2,1)S(1)} %get-tuple-element.13), channel_id=1, source_target_pairs={{0,16},{16,0},{1,17},{17,1},{2,18},{18,2},{3,19},{19,3},{4,20},{20... | collective-permute-start | bytes 1769480 | tf_op jit(solution)/shard_map/ppermute | solution.py:143
  4.5 0.7 %collective-permute-start.2 = (bf16[16,2,32,128]{3,2,1,0:T(8,128)(2,1)S(1)}, bf16[16,2,32,128]{3,2,1,0:T(8,128)(2,1)S(1)}, u32[]{:S(2)}, u32[]{:S(2)}) collective-permute-start(bf16[16,2,32,128]{3,2,1,0:T(8,128)(2,1)S(1)} %get-tuple-element.12), channel_id=1, source_target_pairs={{0,3},{1,2},{2,1},{3,0},{4,7},{5,6},{6,5},{7,4},{8,11},{9,10},{10,... | collective-permute-start | bytes 786440 | tf_op jit(solution)/shard_map/ppermute | solution.py:142
  5.2 0.0 copy-done.1
  5.2 1.1 %copy-done.2 = bf16[2,2,3,32,6,128]{5,3,4,2,1,0:T(8,128)(2,1)S(1)} copy-done((bf16[2,2,3,32,6,128]{5,3,4,2,1,0:T(8,128)(2,1)S(1)}, bf16[2,2,3,32,6,128]{5,3,4,2,1,0:T(8,128)(2,1)}, u32[]{:S(2)}) %copy-start.2) | copy-done | bytes 589848
  6.2 0.9 %copy-done.4 = bf16[3,32,6,128]{3,1,2,0:T(8,128)(2,1)S(1)} copy-done((bf16[3,32,6,128]{3,1,2,0:T(8,128)(2,1)S(1)}, bf16[3,32,6,128]{3,1,2,0:T(8,128)(2,1)}, u32[]{:S(2)}) %copy-start.4) | copy-done | bytes 147480
  7.1 0.7 %copy-done.11 = bf16[32,192]{1,0:T(8,128)(2,1)S(1)} copy-done((bf16[32,192]{1,0:T(8,128)(2,1)S(1)}, bf16[32,192]{1,0:T(8,128)(2,1)}, u32[]{:S(2)}) %copy-start.11) | copy-done | bytes 12312
  7.9 0.0 copy-start.10
  7.9 0.6 %pack_second.1 = (bf16[31,2,32,128]{3,2,1,0:T(8,128)(2,1)S(1)}, bf16[47,16,128]{2,1,0:T(8,128)(2,1)S(1)}, bf16[47,16,128]{2,1,0:T(8,128)(2,1)S(1)}) custom-call(bf16[32,192]{1,0:T(8,128)(2,1)S(1)} %copy-done.11, bf16[32,6,32,128]{3,2,1,0:T(8,128)(2,1)S(1)} %bitcast.23, bf16[3,6,32,128]{3,2,1,0:T(8,128)(2,1)S(1)} %bitcast.35, ...), custom_call_target="tpu_custom_call" | custom-call | tf_op jit(solution)/shard_map/pack_second/pallas_call | solution.py:170
  8.4 1.6 %collective-permute-start = (bf16[47,16,128]{2,1,0:T(8,128)(2,1)S(1)}, bf16[47,16,128]{2,1,0:T(8,128)(2,1)S(1)}, u32[]{:S(2)}, u32[]{:S(2)}) collective-permute-start(bf16[47,16,128]{2,1,0:T(8,128)(2,1)S(1)} %get-tuple-element.11), channel_id=1, source_target_pairs={{0,4},{4,8},{8,12},{12,0},{1,5},{5,9},{9,13},{13,1},{2,6},{6,10},{... | collective-permute-start | bytes 577544 | tf_op jit(solution)/shard_map/ppermute | solution.py:174
  10.0 2.2 %collective-permute-start.1 = (bf16[47,16,128]{2,1,0:T(8,128)(2,1)S(1)}, bf16[47,16,128]{2,1,0:T(8,128)(2,1)S(1)}, u32[]{:S(2)}, u32[]{:S(2)}) collective-permute-start(bf16[47,16,128]{2,1,0:T(8,128)(2,1)S(1)} %get-tuple-element.10.rest_0_), channel_id=1, source_target_pairs={{4,0},{8,4},{12,8},{0,12},{5,1},{9,5},{13,9},{1,13},{6,2},{10,6},{... | collective-permute-start | bytes 577544 | tf_op jit(solution)/shard_map/ppermute | solution.py:175
  12.3 0.0 copy-done.3
  12.3 0.0 copy-done.5
  12.3 0.0 copy-done.6
  12.3 0.0 copy-done.8
  12.3 4.5 %resident_middle.1._.middle_any = f32[32,96,128]{2,1,0:T(8,128)S(1)} custom-call(bf16[288,192]{1,0:T(8,128)(2,1)S(1)} %copy-done.10, bf16[256,512]{1,0:T(8,128)(2,1)S(1)} %copy-done.6, s32[192,128]{1,0:T(8,128)S(1)} %bitcast.42, bf16[32,192,128]{2,1,0:T(8,128)(2,1)S(1)} %bitcast.24, bf16[3,192,128]{2,1,0:T(8,128)(2,1)S(1)} %bitcast.36, ...), custom_call_target="tpu_custom_call" | custom-call | flops 40000000 | bytes 20000000 | tf_op jit(solution)/shard_map/resident_middle/pallas_call | solution.py:338
  16.8 1.3 %collective-permute-done.xb_ref.rest_0_.xb_any = bf16[47,16,128]{2,1,0:T(8,128)(2,1)S(1)} collective-permute-done((bf16[47,16,128]{2,1,0:T(8,128)(2,1)S(1)}, bf16[47,16,128]{2,1,0:T(8,128)(2,1)S(1)}, u32[]{:S(2)}, u32[]{:S(2)}) %collective-permute-start) | collective-permute-done | bytes 192544 | tf_op jit(solution)/shard_map/ppermute | solution.py:174
  18.1 3.5 %collective-permute-done.1.xa_ref.rest_1_.xa_any = bf16[47,16,128]{2,1,0:T(8,128)(2,1)S(1)} collective-permute-done((bf16[47,16,128]{2,1,0:T(8,128)(2,1)S(1)}, bf16[47,16,128]{2,1,0:T(8,128)(2,1)S(1)}, u32[]{:S(2)}, u32[]{:S(2)}) %collective-permute-start.1) | collective-permute-done | bytes 192544 | tf_op jit(solution)/shard_map/ppermute | solution.py:175
  21.6 0.0 collective-permute-done.2.first_ref.first_any
  21.6 0.0 copy-start.9
  21.6 0.0 collective-permute-done.3.rest_0_
  21.6 0.1 pack_near.1.rest_3_
  21.7 0.1 collective-permute-start.5
  21.8 0.0 copy-start.7
  21.8 0.6 %collective-permute-start.4 = (bf16[31,2,32,128]{3,2,1,0:T(8,128)(2,1)S(1)}, bf16[31,2,32,128]{3,2,1,0:T(8,128)(2,1)S(1)}, u32[]{:S(2)}, u32[]{:S(2)}) collective-permute-start(bf16[31,2,32,128]{3,2,1,0:T(8,128)(2,1)S(1)} %get-tuple-element.14), channel_id=1, source_target_pairs={{0,3},{1,2},{2,1},{3,0},{4,7},{5,6},{6,5},{7,4},{8,11},{9,10},{10,... | collective-permute-start | bytes 1523720 | tf_op jit(solution)/shard_map/ppermute | solution.py:173
  22.4 0.5 %collective-permute-start.6 = (bf16[12,96,128]{2,1,0:T(8,128)(2,1)S(1)}, bf16[12,96,128]{2,1,0:T(8,128)(2,1)S(1)}, u32[]{:S(2)}, u32[]{:S(2)}) collective-permute-start(bf16[12,96,128]{2,1,0:T(8,128)(2,1)S(1)} %pack_relay.1.rest_1_.rest_2_), channel_id=1, source_target_pairs={{0,16},{16,0},{1,17},{17,1},{2,18},{18,2},{3,19},{19,3},{4,20},{20... | collective-permute-start | bytes 884744 | tf_op jit(solution)/shard_map/ppermute | solution.py:379
  22.9 4.6 %resident_edge.1.edges_any = f32[32,96,128]{2,1,0:T(8,128)S(1)} custom-call(bf16[288,224]{1,0:T(8,128)(2,1)S(1)} %copy-done.9, bf16[256,512]{1,0:T(8,128)(2,1)S(1)} %copy-done.6, s32[192,128]{1,0:T(8,128)S(1)} %bitcast.43, bf16[32,192,128]{2,1,0:T(8,128)(2,1)S(1)} %bitcast.26, bf16[3,192,128]{2,1,0:T(8,128)(2,1)S(1)} %bitcast.38, ...), custom_call_target="tpu_custom_call" | custom-call | flops 40000000 | bytes 20000000 | tf_op jit(solution)/shard_map/resident_edge/pallas_call | solution.py:338
  27.5 7.6 %collective-permute-done.4.second_any = bf16[31,2,32,128]{3,2,1,0:T(8,128)(2,1)S(1)} collective-permute-done((bf16[31,2,32,128]{3,2,1,0:T(8,128)(2,1)S(1)}, bf16[31,2,32,128]{3,2,1,0:T(8,128)(2,1)S(1)}, u32[]{:S(2)}, u32[]{:S(2)}) %collective-permute-start.4) | collective-permute-done | bytes 507936 | tf_op jit(solution)/shard_map/ppermute | solution.py:173
  35.2 0.0 collective-permute-done.6.rest_1_
  35.2 0.0 collective-permute-done.5.near_any
  35.2 11.0 %finish.1 = f32[32,192,128]{2,1,0:T(8,128)} custom-call(bf16[2,384,352]{2,1,0:T(8,128)(2,1)S(1)} %copy-done.7, bf16[256,512]{1,0:T(8,128)(2,1)S(1)} %copy-done.6, bf16[32,192,128]{2,1,0:T(8,128)(2,1)S(1)} %bitcast.27, bf16[3,192,128]{2,1,0:T(8,128)(2,1)S(1)} %bitcast.39, bf16[12,192,128]{2,1,0:T(8,128)(2,1)S(1)} %bitcast.32, ...), custom_call_target="tpu_custom_call" | custom-call | flops 40000000 | bytes 20000000 | tf_op jit(solution)/shard_map/finish/pallas_call | solution.py:549
  (13 shorter events, 0.0 us)
Async XLA Ops:
  0.0 1.4 %copy-start = (bf16[4,2,4,32,6,128]{5,3,4,2,1,0:T(8,128)(2,1)S(1)}, bf16[4,2,4,32,6,128]{5,3,4,2,1,0:T(8,128)(2,1)}, u32[]{:S(2)}) copy-start(bf16[4,2,4,32,6,128]{5,3,4,2,1,0:T(8,128)(2,1)} %param.9) | copy-start | bytes 4718596
  1.4 3.7 %copy-start.1 = (bf16[4,2,4,32,6,128]{5,3,4,2,1,0:T(8,128)(2,1)S(1)}, bf16[4,2,4,32,6,128]{5,3,4,2,1,0:T(8,128)(2,1)}, u32[]{:S(2)}) copy-start(bf16[4,2,4,32,6,128]{5,3,4,2,1,0:T(8,128)(2,1)} %param.9) | copy-start | bytes 4718596
  1.5 20.1 %collective-permute-start.3 = (bf16[12,6,32,128]{3,2,1,0:T(8,128)(2,1)S(1)}, bf16[12,6,32,128]{3,2,1,0:T(8,128)(2,1)S(1)}, u32[]{:S(2)}, u32[]{:S(2)}) collective-permute-start(bf16[12,6,32,128]{3,2,1,0:T(8,128)(2,1)S(1)} %get-tuple-element.13), channel_id=1, source_target_pairs={{0,16},{16,0},{1,17},{17,1},{2,18},{18,2},{3,19},{19,3},{4,20},{20... | collective-permute-start | bytes 1769480 | tf_op jit(solution)/shard_map/ppermute | solution.py:143
  4.5 17.1 %collective-permute-start.2 = (bf16[16,2,32,128]{3,2,1,0:T(8,128)(2,1)S(1)}, bf16[16,2,32,128]{3,2,1,0:T(8,128)(2,1)S(1)}, u32[]{:S(2)}, u32[]{:S(2)}) collective-permute-start(bf16[16,2,32,128]{3,2,1,0:T(8,128)(2,1)S(1)} %get-tuple-element.12), channel_id=1, source_target_pairs={{0,3},{1,2},{2,1},{3,0},{4,7},{5,6},{6,5},{7,4},{8,11},{9,10},{10,... | collective-permute-start | bytes 786440 | tf_op jit(solution)/shard_map/ppermute | solution.py:142
  5.2 1.1 %copy-start.2 = (bf16[2,2,3,32,6,128]{5,3,4,2,1,0:T(8,128)(2,1)S(1)}, bf16[2,2,3,32,6,128]{5,3,4,2,1,0:T(8,128)(2,1)}, u32[]{:S(2)}) copy-start(bf16[2,2,3,32,6,128]{5,3,4,2,1,0:T(8,128)(2,1)} %param.11) | copy-start | bytes 1769476
  6.2 0.9 %copy-start.4 = (bf16[3,32,6,128]{3,1,2,0:T(8,128)(2,1)S(1)}, bf16[3,32,6,128]{3,1,2,0:T(8,128)(2,1)}, u32[]{:S(2)}) copy-start(bf16[3,32,6,128]{3,1,2,0:T(8,128)(2,1)} %param.10) | copy-start | bytes 442372
  7.1 0.7 %copy-start.11 = (bf16[32,192]{1,0:T(8,128)(2,1)S(1)}, bf16[32,192]{1,0:T(8,128)(2,1)}, u32[]{:S(2)}) copy-start(bf16[32,192]{1,0:T(8,128)(2,1)} %constant.10.clone.pick_ref) | copy-start | bytes 36868
  7.9 4.5 %copy-start.3 = (bf16[2,2,3,32,6,128]{5,3,4,2,1,0:T(8,128)(2,1)S(1)}, bf16[2,2,3,32,6,128]{5,3,4,2,1,0:T(8,128)(2,1)}, u32[]{:S(2)}) copy-start(bf16[2,2,3,32,6,128]{5,3,4,2,1,0:T(8,128)(2,1)} %param.11) | copy-start | bytes 1769476
  7.9 4.5 %copy-start.5 = (bf16[3,32,6,128]{3,1,2,0:T(8,128)(2,1)S(1)}, bf16[3,32,6,128]{3,1,2,0:T(8,128)(2,1)}, u32[]{:S(2)}) copy-start(bf16[3,32,6,128]{3,1,2,0:T(8,128)(2,1)} %param.10) | copy-start | bytes 442372
  7.9 4.5 %copy-start.6 = (bf16[256,512]{1,0:T(8,128)(2,1)S(1)}, bf16[256,512]{1,0:T(8,128)(2,1)}, u32[]{:S(2)}) copy-start(bf16[256,512]{1,0:T(8,128)(2,1)} %constant.11.clone.walls_ref) | copy-start | bytes 786436
  7.9 4.5 %copy-start.8 = (s32[32,6,128]{2,0,1:T(8,128)S(1)}, s32[32,6,128]{2,0,1:T(8,128)}, u32[]{:S(2)}) copy-start(s32[32,6,128]{2,0,1:T(8,128)} %param.12) | copy-start | bytes 294916
  7.9 4.5 %copy-start.10 = (bf16[288,192]{1,0:T(8,128)(2,1)S(1)}, bf16[288,192]{1,0:T(8,128)(2,1)}, u32[]{:S(2)}) copy-start(bf16[288,192]{1,0:T(8,128)(2,1)} %constant.12.clone.rows_ref) | copy-start | bytes 331780
  8.4 9.6 %collective-permute-start = (bf16[47,16,128]{2,1,0:T(8,128)(2,1)S(1)}, bf16[47,16,128]{2,1,0:T(8,128)(2,1)S(1)}, u32[]{:S(2)}, u32[]{:S(2)}) collective-permute-start(bf16[47,16,128]{2,1,0:T(8,128)(2,1)S(1)} %get-tuple-element.11), channel_id=1, source_target_pairs={{0,4},{4,8},{8,12},{12,0},{1,5},{5,9},{9,13},{13,1},{2,6},{6,10},{... | collective-permute-start | bytes 577544 | tf_op jit(solution)/shard_map/ppermute | solution.py:174
  10.0 11.5 %collective-permute-start.1 = (bf16[47,16,128]{2,1,0:T(8,128)(2,1)S(1)}, bf16[47,16,128]{2,1,0:T(8,128)(2,1)S(1)}, u32[]{:S(2)}, u32[]{:S(2)}) collective-permute-start(bf16[47,16,128]{2,1,0:T(8,128)(2,1)S(1)} %get-tuple-element.10.rest_0_), channel_id=1, source_target_pairs={{4,0},{8,4},{12,8},{0,12},{5,1},{9,5},{13,9},{1,13},{6,2},{10,6},{... | collective-permute-start | bytes 577544 | tf_op jit(solution)/shard_map/ppermute | solution.py:175
  21.6 1.3 %copy-start.9 = (bf16[288,224]{1,0:T(8,128)(2,1)S(1)}, bf16[288,224]{1,0:T(8,128)(2,1)}, u32[]{:S(2)}) copy-start(bf16[288,224]{1,0:T(8,128)(2,1)} %constant.13.clone.rows_ref) | copy-start | bytes 387076
  21.7 13.5 %collective-permute-start.5 = (bf16[59,2,32,128]{3,2,1,0:T(8,128)(2,1)S(1)}, bf16[59,2,32,128]{3,2,1,0:T(8,128)(2,1)S(1)}, u32[]{:S(2)}, u32[]{:S(2)}) collective-permute-start(bf16[59,2,32,128]{3,2,1,0:T(8,128)(2,1)S(1)} %pack_near.1.rest_3_), channel_id=1, source_target_pairs={{0,1},{1,0},{2,3},{3,2},{4,5},{5,4},{6,7},{7,6},{8,9},{9,8},{10,11... | collective-permute-start | bytes 2899976 | tf_op jit(solution)/shard_map/ppermute | solution.py:397
  21.8 13.4 %copy-start.7 = (bf16[2,384,352]{2,1,0:T(8,128)(2,1)S(1)}, bf16[2,384,352]{2,1,0:T(8,128)(2,1)}, u32[]{:S(2)}) copy-start(bf16[2,384,352]{2,1,0:T(8,128)(2,1)} %constant.14.clone.stencil_any) | copy-start | bytes 1622020
  21.8 13.4 %collective-permute-start.4 = (bf16[31,2,32,128]{3,2,1,0:T(8,128)(2,1)S(1)}, bf16[31,2,32,128]{3,2,1,0:T(8,128)(2,1)S(1)}, u32[]{:S(2)}, u32[]{:S(2)}) collective-permute-start(bf16[31,2,32,128]{3,2,1,0:T(8,128)(2,1)S(1)} %get-tuple-element.14), channel_id=1, source_target_pairs={{0,3},{1,2},{2,1},{3,0},{4,7},{5,6},{6,5},{7,4},{8,11},{9,10},{10,... | collective-permute-start | bytes 1523720 | tf_op jit(solution)/shard_map/ppermute | solution.py:173
  22.4 12.7 %collective-permute-start.6 = (bf16[12,96,128]{2,1,0:T(8,128)(2,1)S(1)}, bf16[12,96,128]{2,1,0:T(8,128)(2,1)S(1)}, u32[]{:S(2)}, u32[]{:S(2)}) collective-permute-start(bf16[12,96,128]{2,1,0:T(8,128)(2,1)S(1)} %pack_relay.1.rest_1_.rest_2_), channel_id=1, source_target_pairs={{0,16},{16,0},{1,17},{17,1},{2,18},{18,2},{3,19},{19,3},{4,20},{20... | collective-permute-start | bytes 884744 | tf_op jit(solution)/shard_map/ppermute | solution.py:379

commit v3 on v2

--- a/solution.py
+++ b/solution.py
@@ -12,9 +12,10 @@
 FIRST = {-2: 1.0, -1: -8.0, 1: 8.0, 2: -1.0}
 SECOND = {-2: -1.0, -1: 16.0, 0: -30.0, 1: 16.0, 2: -1.0}
 HALO_X = 16
-VMEM_BYTES = 56 * 1024 * 1024
+VMEM_BYTES = 58 * 1024 * 1024
 ANY = pl.BlockSpec(memory_space=pl.ANY)
 VMEM = pl.BlockSpec(memory_space=pltpu.VMEM)
+HBM = pl.BlockSpec(memory_space=pltpu.HBM)
 
 
 def stencil_rows(nz, nx, odd):
@@ -64,6 +65,15 @@
     return np.block([[first, first, second, second], [first, -first, second, -second]])
 
 
+def edge_stencil(nz):
+    out = np.zeros((2, nz, 8, 2 * HALO_X), np.float32)
+    for z in range(nz):
+        xb, xa = 2 * z, HALO_X + 2 * z
+        out[0, z, 0, xb], out[0, z, 0, xb + 1], out[0, z, 1, xb + 1] = 1.0, -8.0, 1.0
+        out[1, z, 6, xa], out[1, z, 7, xa], out[1, z, 7, xa + 1] = -1.0, 8.0, -1.0
+    return out.reshape(16 * nz, 2 * HALO_X)
+
+
 def edge_rows(nz, nx):
     pick = np.zeros((2 * HALO_X, nz * nx), np.float32)
     for z in range(nz):
@@ -114,44 +124,32 @@
     else:
         up_h = [(i, i + 1) for i in range(harms - 1)]
         harm_perms = [up_h, [(j, i) for i, j in up_h]]
-    n_first = modes * 8 if swap else n_pert
-    n_second = n_res - n_first
-
     def sent(s, scal):
         return scal[4] if swap else (per - modes if s == 0 else 0)
 
     face = lambda n: jax.ShapeDtypeStruct((n, 2, nx, ny), bf16)
-    roomy = pltpu.CompilerParams(vmem_limit_bytes=VMEM_BYTES // 2)
-
-    def pack_first(pert_ref, first_ref, *nb_refs):
+    roomy = pltpu.CompilerParams(vmem_limit_bytes=28 * 1024 * 1024)
+
+    chunks = [(at, 8) for at in range(0, n_pert, 8)]
+
+    def pack(pick_any, pert_any, mean_any, mode_any, first_ref, second_ref, lo_ref, hi_ref, *rest):
+        nb_refs = rest[:sides]
+        pick_ref, pert_ref, mean_ref, mode_ref, sems = rest[sides:]
         scal = place()
-        at = scal[4] * 8 if swap else 0
-        for f in range(n_first):
-            first_ref[f] = pert_ref[at + f, pl.ds(scal[2], 2)]
+        loads = [(pert_any.at[pl.ds(*c)], pert_ref.at[pl.ds(*c)]) for c in chunks]
+        loads += [(mean_any, mean_ref), (mode_any, mode_ref), (pick_any, pick_ref)]
+        run_copies(loads, sems)
+        z = pl.ds(scal[2], 2)
+        for f in range(n_pert):
+            first_ref[f] = pert_ref[f, z]
+        for f in range(n_mean):
+            second_ref[f] = mean_ref[f, z]
+        for f in range(n_modes):
+            second_ref[n_mean + f] = mode_ref[f, z]
         for s, nb_ref in enumerate(nb_refs):
             for i in range(modes * 2):
                 for c in range(3):
                     nb_ref[3 * i + c] = pert_ref[sent(s, scal) * 8 + 4 * i + c]
-
-    with jax.named_scope("pack_first"):
-        first, *nb_send = pl.pallas_call(
-            pack_first,
-            out_shape=(face(n_first),) + tuple(jax.ShapeDtypeStruct((n_nb, nz, nx, ny), bf16) for _ in range(sides)),
-            compiler_params=roomy,
-        )(pert)
-    first_got = lax.ppermute(first, "gz", cross_pairs)
-    nb_got = [lax.ppermute(b, "harm", p) for b, p in zip(nb_send, harm_perms)]
-
-    def pack_second(pick_ref, pert_ref, mean_ref, mode_ref, second_ref, lo_ref, hi_ref):
-        scal = place()
-        z = pl.ds(scal[2], 2)
-        at = n_pert - n_first
-        if swap:
-            rest = (per - modes - scal[4]) * 8
-            for f in range(at):
-                second_ref[f] = pert_ref[rest + f, z]
-        second_ref[at : at + n_mean] = mean_ref[:, z]
-        second_ref[at + n_mean :] = mode_ref[:, z]
         pick = pick_ref[...]
         at = 0
         for ref, count in ((pert_ref, n_pert), (mean_ref, n_mean), (mode_ref, n_modes)):
@@ -166,13 +164,25 @@
             at += count
 
     edge = jax.ShapeDtypeStruct((n_res, HALO_X, ny), bf16)
-    with jax.named_scope("pack_second"):
-        second, edge_lo, edge_hi = pl.pallas_call(
-            pack_second, out_shape=(face(n_second), edge, edge), compiler_params=roomy
+    with jax.named_scope("pack"):
+        first, second, edge_lo, edge_hi, *nb_send = pl.pallas_call(
+            pack,
+            out_shape=(face(n_pert), face(n_base), edge, edge) + tuple(jax.ShapeDtypeStruct((n_nb, nz, nx, ny), bf16) for _ in range(sides)),
+            in_specs=[HBM] * 4,
+            scratch_shapes=[
+                pltpu.VMEM((2 * HALO_X, own), bf16),
+                pltpu.VMEM((n_pert, nz, nx, ny), bf16),
+                pltpu.VMEM((n_mean, nz, nx, ny), bf16),
+                pltpu.VMEM((n_modes, nz, nx, ny), bf16),
+                pltpu.SemaphoreType.DMA((len(chunks) + 3,)),
+            ],
+            compiler_params=pltpu.CompilerParams(vmem_limit_bytes=VMEM_BYTES),
         )(jnp.asarray(edge_rows(nz, nx), bf16), pert, mean, mode)
-    second_got = lax.ppermute(second, "gz", cross_pairs)
+    first_got = lax.ppermute(first, "gz", cross_pairs)
+    nb_got = [lax.ppermute(b, "harm", p) for b, p in zip(nb_send, harm_perms)]
     xb_got = lax.ppermute(edge_hi, "gx", up_x)
     xa_got = lax.ppermute(edge_lo, "gx", down_x)
+    second_got = lax.ppermute(second, "gz", cross_pairs)
 
     quarter = nx // 4
     part = own // 2
@@ -363,9 +373,8 @@
         for s, out in enumerate(outs):
             for i in range(modes * 2):
                 field = sent(s, scal) * 8 + 4 * i
-                near = 4 * i if swap else field
                 for c in range(3):
-                    out[3 * i + c, : 2 * nx] = first_ref[near + c].reshape(2 * nx, ny)
+                    out[3 * i + c, : 2 * nx] = first_ref[field + c].reshape(2 * nx, ny)
                     out[3 * i + c, 2 * nx : 2 * nx + HALO_X] = xb_ref[field + c]
                     out[3 * i + c, 2 * nx + HALO_X :] = xa_ref[field + c]
 
@@ -399,85 +408,67 @@
     with jax.named_scope("resident_edge"):
         edges = resident_kernel(True)(xb_got, xa_got, relay[0], near)
 
-    at_xb, at_cross = own, own + 2 * HALO_X
-    at_near = at_cross + 2 * nx
-    depth = at_near + 2 * nx
-    both_stencils = np.stack([stencil_rows(nz, nx, odd)[: 2 * own] for odd in (False, True)])
-    n_ext = n_modes + sides * n_nb
-
-    def finish(stencil_any, walls_ref, pert_ref, mean_ref, mode_ref, middle_any, edges_any, mode_any, first_any, second_any, near_any, second_flat, near_flat, xb_any, xa_any, *rest):
-        scal = place()
-        nb_any, relay_any = rest[:sides], rest[sides : 2 * sides]
-        out_ref, fields, halo, grads, plain, weights, sems = rest[2 * sides :]
-        copies = [(stencil_any.at[scal[1]], weights)]
-        cross, close = pl.ds(at_cross, 2 * nx), pl.ds(at_near, 2 * nx)
-        mine = pl.ds(0, n_modes)
-        base_modes_at = n_pert + n_mean
-        second_at = n_pert - n_first
-        copies.append((mode_any, fields.at[mine, pl.ds(0, own)]))
-        copies.append((second_flat.at[pl.ds(second_at + n_mean, n_modes)], fields.at[mine, cross]))
-        copies.append((near_flat.at[pl.ds(base_modes_at, n_modes)], fields.at[mine, close]))
-        copies.append((xb_any.at[pl.ds(base_modes_at, n_modes)], fields.at[mine, pl.ds(at_xb, HALO_X)]))
-        copies.append((xa_any.at[pl.ds(base_modes_at, n_modes)], fields.at[mine, pl.ds(at_xb + HALO_X, HALO_X)]))
-        for s in range(sides):
-            mine = pl.ds(n_modes + s * n_nb, n_nb)
-            copies.append((nb_any[s], fields.at[mine, pl.ds(0, own)]))
-            copies.append((relay_any[s].at[:, pl.ds(0, 2 * nx)], fields.at[mine, cross]))
-            copies.append((relay_any[s].at[:, pl.ds(2 * nx, 2 * HALO_X)], fields.at[mine, pl.ds(at_xb, 2 * HALO_X)]))
-            copies.append((near_flat.at[pl.ds(n_res + s * n_nb, n_nb)], fields.at[mine, close]))
-        if swap:
-            rest_at = per - modes - scal[4]
-            copies.append((first_any, halo.at[0, pl.ds(scal[4] * 8, n_first)]))
-            copies.append((second_any.at[pl.ds(0, second_at)], halo.at[0, pl.ds(rest_at * 8, second_at)]))
-        else:
-            copies.append((first_any, halo.at[0, pl.ds(0, n_pert)]))
-        copies.append((second_any.at[pl.ds(second_at, n_base)], halo.at[0, pl.ds(n_pert, n_base)]))
-        copies.append((near_any.at[pl.ds(0, n_res)], halo.at[1]))
-        for z in range(nz):
-            half = nx // 2
-            copies.append((middle_any.at[:, pl.ds(z * half, half)], out_ref.at[:, pl.ds(z * nx + quarter, half)]))
-            copies.append((edges_any.at[:, pl.ds(z * half, quarter)], out_ref.at[:, pl.ds(z * nx, quarter)]))
-            copies.append((edges_any.at[:, pl.ds(z * half + quarter, quarter)], out_ref.at[:, pl.ds(z * nx + nx - quarter, quarter)]))
-        run_copies(copies, sems)
-
-        def slopes(pair, carry):
-            f = 2 * pair
-            both = jnp.concatenate([fields[f], fields[f + 1]], axis=1)
-            got = jnp.dot(weights[...], both, preferred_element_type=f32)
+    below, above = [], []
+    for k in range(per):
+        for m in range(-modes, modes + 1):
+            l = k - m
+            if l < 0:
+                below.append((k, m, 0, (l + modes) * 6))
+            elif l >= per:
+                above.append((k, m, sides - 1, (l - per) * 6))
+
+    def on_sides(work):
+        me_h = lax.axis_index("harm")
+        pl.when(me_h > 0)(lambda: work(below))
+        pl.when(me_h < harms - 1)(lambda: work(above))
+
+    def product(acc, flow, value, m):
+        (fr, fi), (vr, vi) = flow, value
+        if m > 0:
+            return acc[0] + fr * vr - fi * vi, acc[1] + fr * vi + fi * vr
+        return acc[0] + fr * vr + fi * vi, acc[1] + fr * vi - fi * vr
+
+    own_stencil = stencil_rows(nz, nx, False)[: 2 * own, : own + 2 * HALO_X]
+    base_modes_at = n_pert + n_mean
+
+    def neighbours(stencil_ref, walls_ref, mode_ref, xb_ref, xa_ref, middle_ref, edges_ref, *rest):
+        nb_refs = rest[:sides]
+        out_ref, grads, plain = rest[-3:]
+
+        def slopes(at, mine, halo):
+            both = jnp.concatenate(mine, axis=1)
+            rows = both if halo is None else jnp.concatenate([both, halo], axis=0)
+            got = jnp.dot(stencil_ref[:, : rows.shape[0]], rows, preferred_element_type=f32)
+            wall = [jnp.dot(x, walls_ref[:ny, :ny], preferred_element_type=f32) for x in mine]
             for i in range(2):
                 lanes = slice(i * ny, (i + 1) * ny)
-                grads[f + i, 0] = got[:own, lanes]
-                grads[f + i, 2] = got[own:, lanes]
-                own_rows = fields[f + i, pl.ds(0, own)]
-                grads[f + i, 1] = jnp.dot(own_rows, walls_ref[:ny, :ny], preferred_element_type=f32)
-                plain[f + i] = own_rows.astype(f32)
-            return carry
-
-        lax.fori_loop(0, n_ext // 2, slopes, 0)
-
-        def product(acc, flow, value, sign):
-            (fr, fi), (vr, vi) = flow, value
-            if sign > 0:
-                return acc[0] + fr * vr - fi * vi, acc[1] + fr * vi + fi * vr
-            return acc[0] + fr * vr + fi * vi, acc[1] + fr * vi - fi * vr
-
-        below, above = [], []
-        for k in range(per):
-            for m in range(-modes, modes + 1):
-                l = k - m
-                if l < 0:
-                    below.append((k, m, n_modes + (l + modes) * 6))
-                elif l >= per:
-                    above.append((k, m, n_modes + (sides - 1) * n_nb + (l - per) * 6))
-
-        def neighbours(pairs):
+                grads[at + i, 0] = got[:own, lanes]
+                grads[at + i, 2] = got[own:, lanes]
+                grads[at + i, 1] = wall[i]
+                plain[at + i] = mine[i].astype(f32)
+
+        for f in range(0, n_modes, 2):
+            at = base_modes_at + f
+            halo = [jnp.concatenate([ref[at], ref[at + 1]], axis=1) for ref in (xb_ref, xa_ref)]
+            slopes(f, [mode_ref[f], mode_ref[f + 1]], jnp.concatenate(halo, axis=0))
+        for s in range(sides):
+            for f in range(0, n_nb, 2):
+                slopes(n_modes + s * n_nb + f, [nb_refs[s][f], nb_refs[s][f + 1]], None)
+
+        for z in range(nz):
+            half, at = nx // 2, z * nx
+            out_ref[:, at : at + quarter] = edges_ref[:, z * half : z * half + quarter]
+            out_ref[:, at + quarter : at + quarter + half] = middle_ref[:, z * half : (z + 1) * half]
+            out_ref[:, at + quarter + half : at + nx] = edges_ref[:, z * half + quarter : (z + 1) * half]
+
+        def work(pairs):
             def block(b, carry):
                 rows = pl.ds(pl.multiple_of(b * 8, 8), 8)
                 for k in sorted({p[0] for p in pairs}):
                     zero = jnp.zeros((8, ny), f32)
                     acc = [(zero, zero)] * 3
-                    for _, m, at in [p for p in pairs if p[0] == k]:
-                        base = (abs(m) - 1) * 6
+                    for _, m, s, f in [p for p in pairs if p[0] == k]:
+                        at, base = n_modes + s * n_nb + f, (abs(m) - 1) * 6
                         for d in range(3):
                             flow = plain[base + d, rows], plain[base + 3 + d, rows]
                             along = plain[at + d, rows], plain[at + 3 + d, rows]
@@ -494,76 +485,161 @@
 
             lax.fori_loop(0, own // 8, block, 0)
 
-        pl.when(scal[0] > 0)(lambda: neighbours(below))
-        pl.when(scal[0] < harms - 1)(lambda: neighbours(above))
-
-        def face_block(n, carry):
-            side, step, chunk = n // 4, (n // 2) % 2, n % 2
-            before = side == scal[1]
+        on_sides(work)
+
+    n_ext = n_modes + sides * n_nb
+    with jax.named_scope("neighbours"):
+        inner = pl.pallas_call(
+            neighbours,
+            out_shape=jax.ShapeDtypeStruct((n_pert, own, ny), f32),
+            scratch_shapes=[pltpu.VMEM((n_ext, 3, own, ny), f32), pltpu.VMEM((n_ext, own, ny), f32)],
+            compiler_params=roomy,
+        )(jnp.asarray(own_stencil, bf16), walls_pair, flat(mode), xb_got, xa_got, middle, edges, *[flat(b) for b in nb_got])
+
+    def finish(edge_ref, pert_ref, mean_ref, mode_ref, inner_ref, first_ref, second_ref, near_ref, *rest):
+        relay_refs, nb_refs = rest[:sides], rest[sides : 2 * sides]
+        out_any, done, bends, sems = rest[2 * sides :]
+        odd = place()[1]
+        half = nx // 2
+        done[...] = inner_ref[...]
+
+        def send(layer):
+            rows = pl.ds(pl.multiple_of(layer * nx, nx), nx)
+            return pltpu.make_async_copy(done.at[:, rows], out_any.at[:, rows], sems.at[layer])
+
+        for s in range(sides):
+            for f in range(0, n_nb, 2):
+                both = jnp.concatenate([relay_refs[s][f + i, 2 * nx :] for i in range(2)], axis=1)
+                got = jnp.dot(edge_ref[...], both, preferred_element_type=f32)
+                for i in range(2):
+                    bends[s * n_nb + f + i] = got[:, i * ny : (i + 1) * ny]
+
+        def edge_work(pairs):
+            def layer_edges(z, carry):
+                for end in range(2):
+                    strip = pl.ds(pl.multiple_of(z * nx + end * half, 16), 16)
+                    keep = slice(8 * end, 8 * end + 8)
+                    rows = pl.ds(pl.multiple_of(z * nx + end * (nx - 8), 8), 8)
+                    bent = pl.ds(pl.multiple_of((end * nz + z) * 8, 8), 8)
+                    for k in sorted({p[0] for p in pairs}):
+                        zero = jnp.zeros((8, ny), f32)
+                        acc = [(zero, zero)] * 3
+                        for _, m, s, f in [p for p in pairs if p[0] == k]:
+                            base = (abs(m) - 1) * 6
+                            flow = tuple(mode_ref[base + 3 * i, strip].astype(f32)[keep] for i in range(2))
+                            for c in range(3):
+                                at = s * n_nb + f + c
+                                acc[c] = product(acc[c], flow, (bends[at, bent], bends[at + 3, bent]), m)
+                        for c in range(3):
+                            for i in range(2):
+                                at = k * 8 + 4 * i + c
+                                done[at, rows] = done[at, rows] + acc[c][i] * (1.0 / 12.0)
+                return carry
+
+            lax.fori_loop(0, nz, layer_edges, 0)
+
+        on_sides(edge_work)
+        for layer in range(2, nz - 2):
+            send(layer).start()
+
+        def face_layer(cross, step):
+            before = (odd == 0) if cross else (odd == 1)
             near_at = jnp.where(before, 1, 0)
             layer = jnp.where(before, step, nz - 1 - step)
             turn = jnp.where(before, 1.0, -1.0)
             first_step = step == 0
             cn, cf = turn * jnp.where(first_step, -8.0, 1.0), turn * jnp.where(first_step, 1.0, 0.0)
             ln, lf = jnp.where(first_step, 16.0, -1.0), jnp.where(first_step, -1.0, 0.0)
-            rows = pl.ds(pl.multiple_of(layer * nx + chunk * 16, 16), 16)
-            strip = pl.ds(pl.multiple_of(chunk * 16, 16), 16)
-
-            def halos(f):
-                return halo[side, f, near_at, strip].astype(f32), halo[side, f, 1 - near_at, strip].astype(f32)
-
-            def slope(f):
-                a, b = halos(f)
-                return cn * a + cf * b
-
-            def slope_lap(f):
-                a, b = halos(f)
-                return cn * a + cf * b, ln * a + lf * b
-
-            flow = entries(mean_ref[2, rows].astype(f32), *[mode_ref[3 * i + 2, rows].astype(f32) for i in range(4)])
-            along = basis_of([(pert_ref[l * 8 + 2, rows].astype(f32), pert_ref[l * 8 + 6, rows].astype(f32)) for l in range(per)])
-            for c in range(4):
-                if c < 3:
-                    got = [[slope_lap(l * 8 + 4 * i + c) for i in range(2)] for l in range(per)]
-                    vec = basis_of([(g[0][0], g[1][0]) for g in got])
-                    lap = basis_of([(g[0][1], g[1][1]) for g in got])
-                    acc = [tuple(-VISCOSITY * v for v in pair) for pair in lap]
-                    if c == 2:
-                        press = basis_of([(slope(l * 8 + 3), slope(l * 8 + 7)) for l in range(per)])
-                        acc = [(a[0] + p[0], a[1] + p[1]) for a, p in zip(acc, press)]
-                    acc = couple(acc, flow, vec)
-                    bend = entries(slope(n_pert + c), *[slope(n_pert + n_mean + 3 * i + c) for i in range(4)])
-                    acc = couple(acc, bend, along)
-                else:
-                    acc = vec
-                for k, parts in enumerate(harmonics_of(acc, 1.0 / 24.0)):
-                    for i in range(2):
-                        at = k * 8 + 4 * i + c
-                        out_ref[at, rows] = out_ref[at, rows] + parts[i]
-            return carry
-
-        lax.fori_loop(0, 8, face_block, 0)
-
-    n_copies = 6 + 4 * sides + (2 if swap else 1) + 2 + 3 * nz
+
+            def chunk_work(chunk):
+                rows = pl.ds(pl.multiple_of(layer * nx + chunk * 16, 16), 16)
+                strip = pl.ds(chunk * 16, 16)
+
+                def halos(f):
+                    if not cross:
+                        ref, at = near_ref, f
+                    elif f < n_pert:
+                        ref, at = first_ref, f
+                    else:
+                        ref, at = second_ref, f - n_pert
+                    return ref[at, near_at, strip].astype(f32), ref[at, 1 - near_at, strip].astype(f32)
+
+                def nb_halos(s, f):
+                    if not cross:
+                        return halos(n_res + s * n_nb + f)
+                    at = [pl.ds(pl.multiple_of(j * nx + chunk * 16, 16), 16) for j in (near_at, 1 - near_at)]
+                    return tuple(relay_refs[s][f, r].astype(f32) for r in at)
+
+                def mix(pair):
+                    return cn * pair[0] + cf * pair[1]
+
+                def slope_lap(f):
+                    a, b = halos(f)
+                    return cn * a + cf * b, ln * a + lf * b
+
+                flows = [mean_ref[2, rows].astype(f32)] + [mode_ref[3 * i + 2, rows].astype(f32) for i in range(4)]
+                flow = entries(*flows)
+                along = basis_of([(pert_ref[l * 8 + 2, rows].astype(f32), pert_ref[l * 8 + 6, rows].astype(f32)) for l in range(per)])
+                for c in range(4):
+                    if c < 3:
+                        got = [[slope_lap(l * 8 + 4 * i + c) for i in range(2)] for l in range(per)]
+                        vec = basis_of([(g[0][0], g[1][0]) for g in got])
+                        lap = basis_of([(g[0][1], g[1][1]) for g in got])
+                        acc = [tuple(-VISCOSITY * v for v in pair) for pair in lap]
+                        if c == 2:
+                            press = basis_of([(mix(halos(l * 8 + 3)), mix(halos(l * 8 + 7))) for l in range(per)])
+                            acc = [(a[0] + p[0], a[1] + p[1]) for a, p in zip(acc, press)]
+                        acc = couple(acc, flow, vec)
+                        bend = entries(mix(halos(n_pert + c)), *[mix(halos(base_modes_at + 3 * i + c)) for i in range(4)])
+                        acc = couple(acc, bend, along)
+                    else:
+                        acc = vec
+                    for k, parts in enumerate(harmonics_of(acc, 1.0 / 24.0)):
+                        for i in range(2):
+                            at = k * 8 + 4 * i + c
+                            done[at, rows] = done[at, rows] + parts[i]
+
+                def nb_work(pairs):
+                    for k in sorted({p[0] for p in pairs}):
+                        zero = jnp.zeros((16, ny), f32)
+                        for c in range(3):
+                            acc = (zero, zero)
+                            for _, m, s, f in [p for p in pairs if p[0] == k]:
+                                base = (abs(m) - 1) * 6
+                                mine = tuple(mode_ref[base + 3 * i + 2, rows].astype(f32) for i in range(2))
+                                acc = product(acc, mine, tuple(mix(nb_halos(s, f + 3 * i + c)) for i in range(2)), m)
+                                bent = tuple(mix(halos(base_modes_at + base + 3 * i + c)) for i in range(2))
+                                carried = tuple(nb_refs[s][f + 3 * i + 2, rows].astype(f32) for i in range(2))
+                                acc = product(acc, bent, carried, m)
+                            for i in range(2):
+                                at = k * 8 + 4 * i + c
+                                done[at, rows] = done[at, rows] + acc[i] * (1.0 / 12.0)
+
+                on_sides(nb_work)
+
+            for chunk in range(nx // 16):
+                chunk_work(chunk)
+            send(layer).start()
+
+        for cross in (False, True):
+            lax.fori_loop(0, 2, lambda step, carry: (face_layer(cross, step), carry)[1], 0)
+        for layer in range(nz):
+            send(layer).wait()
+
     with jax.named_scope("finish"):
         out = pl.pallas_call(
             finish,
             out_shape=jax.ShapeDtypeStruct((n_pert, own, ny), f32),
-            in_specs=[ANY] + [VMEM] * 4 + [ANY] * (10 + 2 * sides),
-            out_specs=VMEM,
+            out_specs=HBM,
             scratch_shapes=[
-                pltpu.VMEM((n_ext, depth, ny), bf16),
-                pltpu.VMEM((2, n_res, 2, nx, ny), bf16),
-                pltpu.VMEM((n_ext, 3, own, ny), f32),
-                pltpu.VMEM((n_ext, own, ny), f32),
-                pltpu.VMEM((2 * own, depth), bf16),
-                pltpu.SemaphoreType.DMA((n_copies,)),
+                pltpu.VMEM((n_pert, own, ny), f32),
+                pltpu.VMEM((sides * n_nb, 16 * nz, ny), f32),
+                pltpu.SemaphoreType.DMA((nz,)),
             ],
             compiler_params=roomy,
-            cost_estimate=pl.CostEstimate(flops=40_000_000, bytes_accessed=20_000_000, transcendentals=0),
         )(
-            jnp.asarray(both_stencils, bf16), walls_pair, flat(pert), flat(mean), flat(mode), middle, edges, flat(mode),
-            first_got, second_got, near_got, flat(second_got), flat(near_got), xb_got, xa_got, *[flat(b) for b in nb_got], *relay_got,
+            jnp.asarray(edge_stencil(nz), bf16), flat(pert), flat(mean), flat(mode), inner, first_got, second_got, near_got,
+            *relay_got, *[flat(b) for b in nb_got],
         )
     return jnp.swapaxes(out.reshape(per, 2, 4, nz, nx, ny), 3, 4)
 

time: 46.5 us -> 35.7 us (0.77)
  waiting for transfers between devices: 12.4 us -> 1.69 us
  starting transfers between devices: 8.76 us -> 9.72 us
  Pallas kernels: 20.8 us -> 20.2 us
    ppermute x1, waiting for transfers between devices: 7.64 us -> 0.01 us  [shards(): second_got = lax.ppermute(second, 'gz', cross_pairs)]
    pallas_call x1, Pallas kernels: 11 us -> 4.21 us  [shards(): pl.pallas_call(finish, out_shape=jax.ShapeDtypeStruct((n_pert, own, ny),...]
    pallas_call x2, Pallas kernels: 0.62 us -> 6.94 us  [the longest x1 3.48 us: shards(): pl.pallas_call(neighbours, out_shape=jax.ShapeDtypeStruct((n_pert, own, n...]
    ppermute x1, waiting for transfers between devices: 3.51 us -> 1.25 us  [shards(): xa_got = lax.ppermute(edge_lo, 'gx', down_x)]
    ppermute x1, waiting for transfers between devices: 1.26 us -> 0.01 us  [shards(): xb_got = lax.ppermute(edge_hi, 'gx', up_x)]
    ppermute x1, starting transfers between devices: 0.64 us -> 1.26 us  [shards(): second_got = lax.ppermute(second, 'gz', cross_pairs)]
  transfers between devices with their start and end apart: 7 -> 7, of which waited for: 3 -> 2; matrix products, arithmetic and copies ran while one was open for 0% -> 0% of each run, Pallas kernels for 21% -> 35%
where the time goes in v3:
time: 35.7 us; the launch traced here: 35.5 us
  Pallas kernels  20.2 us (57%)
  starting transfers between devices  9.72 us (27%)
  local copies, waits for them, and re-layouts  3.71 us (10%)
  waiting for transfers between devices  1.69 us (5%)
    pallas_call x2, Pallas kernels, call(): pl.pallas_call(body, out_shape=jax.ShapeDtypeStruct((n_pert, part, ny), f...  8.99 us
    pallas_call x1, Pallas kernels, shards(): pl.pallas_call(finish, out_shape=jax.ShapeDtypeStruct((n_pert, own, ny),...  4.21 us
    unnamed x24, local copies, waits for them, and re-layouts  3.71 us
    pallas_call x1, Pallas kernels, shards(): pl.pallas_call(neighbours, out_shape=jax.ShapeDtypeStruct((n_pert, own, n...  3.48 us
    pallas_call x1, Pallas kernels, shards(): pl.pallas_call(pack, out_shape=(face(n_pert), face(n_base), edge, edge) +...  3.46 us
    ppermute x1, starting transfers between devices, shards(): nb_got = [lax.ppermute(b, 'harm', p) for b, p in zip(nb_send, harm_perms)]  3.04 us
    ppermute x1, starting transfers between devices, shards(): xa_got = lax.ppermute(edge_lo, 'gx', down_x)  2.25 us
    ppermute x1, starting transfers between devices, shards(): xb_got = lax.ppermute(edge_hi, 'gx', up_x)  1.58 us
  transfers between devices with their start and end apart: 7, of which 2 were waited for; matrix products, arithmetic and copies ran while one was open for 0% of the time, Pallas kernels for 35%

profile of v3, /device:TPU:0, one launch (start us, length us, event | category | flops | bytes accessed | tf_op | source)
XLA Modules:
  0.0 35.5 jit_solution(12631232328221577419)
XLA Ops:
  0.0 3.5 %pack.1 = (bf16[32,2,32,128]{3,2,1,0:T(8,128)(2,1)}, bf16[15,2,32,128]{3,2,1,0:T(8,128)(2,1)}, bf16[47,16,128]{2,1,0:T(8,128)(2,1)}, bf16[47,16,128]{2,1,0:T(8,128)(2,1)}, bf16[12,6,32,128]{3,2,1,0:T(8,128)(2,1)}) custom-call(bf16[32,192]{1,0:T(8,128)(2,1)} %constant.12.clone.pick_any, bf16[32,6,32,128]{3,2,1,0:T(8,128)(2,1)} %bitcast.20, ...), custom_call_target="tpu_custom_call" | custom-call | tf_op jit(solution)/shard_map/pack/pallas_call | solution.py:168
  3.5 3.0 %collective-permute-start.3 = (bf16[12,6,32,128]{3,2,1,0:T(8,128)(2,1)}, bf16[12,6,32,128]{3,2,1,0:T(8,128)(2,1)S(1)}, u32[]{:S(2)}, u32[]{:S(2)}) collective-permute-start(bf16[12,6,32,128]{3,2,1,0:T(8,128)(2,1)} %get-tuple-element.13), channel_id=1, source_target_pairs={{0,16},{16,0},{1,17},{17,1},{2,18},{18,2},{3,19},{19,3},{4,20},{20... | collective-permute-start | bytes 1769480 | tf_op jit(solution)/shard_map/ppermute | solution.py:182
  6.5 0.7 %collective-permute-start.2 = (bf16[32,2,32,128]{3,2,1,0:T(8,128)(2,1)}, bf16[32,2,32,128]{3,2,1,0:T(8,128)(2,1)S(1)}, u32[]{:S(2)}, u32[]{:S(2)}) collective-permute-start(bf16[32,2,32,128]{3,2,1,0:T(8,128)(2,1)} %get-tuple-element.12), channel_id=1, source_target_pairs={{0,3},{1,2},{2,1},{3,0},{4,7},{5,6},{6,5},{7,4},{8,11},{9,10},{10,... | collective-permute-start | bytes 1572872 | tf_op jit(solution)/shard_map/ppermute | solution.py:181
  7.2 1.6 %collective-permute-start = (bf16[47,16,128]{2,1,0:T(8,128)(2,1)}, bf16[47,16,128]{2,1,0:T(8,128)(2,1)S(1)}, u32[]{:S(2)}, u32[]{:S(2)}) collective-permute-start(bf16[47,16,128]{2,1,0:T(8,128)(2,1)} %get-tuple-element.10), channel_id=1, source_target_pairs={{0,4},{4,8},{8,12},{12,0},{1,5},{5,9},{9,13},{13,1},{2,6},{6,10},{... | collective-permute-start | bytes 577544 | tf_op jit(solution)/shard_map/ppermute | solution.py:183
  8.7 2.2 %collective-permute-start.1 = (bf16[47,16,128]{2,1,0:T(8,128)(2,1)}, bf16[47,16,128]{2,1,0:T(8,128)(2,1)S(1)}, u32[]{:S(2)}, u32[]{:S(2)}) collective-permute-start(bf16[47,16,128]{2,1,0:T(8,128)(2,1)} %get-tuple-element.11.rest_0_), channel_id=1, source_target_pairs={{4,0},{8,4},{12,8},{0,12},{5,1},{9,5},{13,9},{1,13},{6,2},{10,6},{... | collective-permute-start | bytes 577544 | tf_op jit(solution)/shard_map/ppermute | solution.py:184
  11.0 0.0 copy-done.1
  11.0 0.0 copy-done.2
  11.0 0.0 copy-done
  11.0 0.9 %copy-done.3 = bf16[256,512]{1,0:T(8,128)(2,1)S(1)} copy-done((bf16[256,512]{1,0:T(8,128)(2,1)S(1)}, bf16[256,512]{1,0:T(8,128)(2,1)}, u32[]{:S(2)}) %copy-start.3) | copy-done | bytes 262168
  12.0 0.9 %copy-done.5 = s32[32,6,128]{2,0,1:T(8,128)S(1)} copy-done((s32[32,6,128]{2,0,1:T(8,128)S(1)}, s32[32,6,128]{2,0,1:T(8,128)}, u32[]{:S(2)}) %copy-start.5) | copy-done | bytes 98328
  12.8 0.9 %copy-done.7 = bf16[47,16,128]{2,1,0:T(8,128)(2,1)S(1)} copy-done((bf16[47,16,128]{2,1,0:T(8,128)(2,1)S(1)}, bf16[47,16,128]{2,1,0:T(8,128)(2,1)}, u32[]{:S(2)}) %copy-start.7) | copy-done | bytes 192536
  13.8 0.9 %copy-done.9 = bf16[288,192]{1,0:T(8,128)(2,1)S(1)} copy-done((bf16[288,192]{1,0:T(8,128)(2,1)S(1)}, bf16[288,192]{1,0:T(8,128)(2,1)}, u32[]{:S(2)}) %copy-start.9) | copy-done | bytes 110616
  14.7 4.5 %resident_middle.1._.middle_ref = f32[32,96,128]{2,1,0:T(8,128)S(1)} custom-call(bf16[288,192]{1,0:T(8,128)(2,1)S(1)} %copy-done.9, bf16[256,512]{1,0:T(8,128)(2,1)S(1)} %copy-done.3, s32[192,128]{1,0:T(8,128)S(1)} %bitcast.38, bf16[32,192,128]{2,1,0:T(8,128)(2,1)S(1)} %bitcast.21, bf16[3,192,128]{2,1,0:T(8,128)(2,1)S(1)} %bitcast.34, ...), custom_call_target="tpu_custom_call" | custom-call | flops 40000000 | bytes 20000000 | tf_op jit(solution)/shard_map/resident_middle/pallas_call | solution.py:348
  19.2 0.0 collective-permute-done.xb_ref.rest_0_
  19.2 1.2 %collective-permute-done.1.xa_ref.rest_1_ = bf16[47,16,128]{2,1,0:T(8,128)(2,1)S(1)} collective-permute-done((bf16[47,16,128]{2,1,0:T(8,128)(2,1)}, bf16[47,16,128]{2,1,0:T(8,128)(2,1)S(1)}, u32[]{:S(2)}, u32[]{:S(2)}) %collective-permute-start.1) | collective-permute-done | bytes 192544 | tf_op jit(solution)/shard_map/ppermute | solution.py:184
  20.5 0.4 %collective-permute-done.2.first_ref = bf16[32,2,32,128]{3,2,1,0:T(8,128)(2,1)S(1)} collective-permute-done((bf16[32,2,32,128]{3,2,1,0:T(8,128)(2,1)}, bf16[32,2,32,128]{3,2,1,0:T(8,128)(2,1)S(1)}, u32[]{:S(2)}, u32[]{:S(2)}) %collective-permute-start.2) | collective-permute-done | bytes 524320 | tf_op jit(solution)/shard_map/ppermute | solution.py:181
  20.9 0.0 copy-start.11
  20.9 0.0 copy-start.4
  21.0 0.0 copy-start.8
  21.0 0.0 collective-permute-done.3.rest_0_
  21.0 0.1 pack_near.1.rest_3_
  21.1 0.2 collective-permute-start.5
  21.2 0.8 %collective-permute-start.6 = (bf16[12,96,128]{2,1,0:T(8,128)(2,1)S(1)}, bf16[12,96,128]{2,1,0:T(8,128)(2,1)S(1)}, u32[]{:S(2)}, u32[]{:S(2)}) collective-permute-start(bf16[12,96,128]{2,1,0:T(8,128)(2,1)S(1)} %pack_relay.1.rest_1_.rest_2_), channel_id=1, source_target_pairs={{0,16},{16,0},{1,17},{17,1},{2,18},{18,2},{3,19},{19,3},{4,20},{20... | collective-permute-start | bytes 884744 | tf_op jit(solution)/shard_map/ppermute | solution.py:388
  22.0 1.3 %collective-permute-start.4 = (bf16[15,2,32,128]{3,2,1,0:T(8,128)(2,1)S(1)}, bf16[15,2,32,128]{3,2,1,0:T(8,128)(2,1)S(1)}, u32[]{:S(2)}, u32[]{:S(2)}) collective-permute-start(bf16[15,2,32,128]{3,2,1,0:T(8,128)(2,1)S(1)} %copy-done.11), channel_id=1, source_target_pairs={{0,3},{1,2},{2,1},{3,0},{4,7},{5,6},{6,5},{7,4},{8,11},{9,10},{10,... | collective-permute-start | bytes 737288 | tf_op jit(solution)/shard_map/ppermute | solution.py:185
  23.3 0.0 copy-done.8
  23.3 4.5 %resident_edge.1.edges_ref = f32[32,96,128]{2,1,0:T(8,128)S(1)} custom-call(bf16[288,224]{1,0:T(8,128)(2,1)S(1)} %copy-done.8, bf16[256,512]{1,0:T(8,128)(2,1)S(1)} %copy-done.4, s32[192,128]{1,0:T(8,128)S(1)} %bitcast.39, bf16[32,192,128]{2,1,0:T(8,128)(2,1)S(1)} %bitcast.23, bf16[3,192,128]{2,1,0:T(8,128)(2,1)S(1)} %bitcast.36, ...), custom_call_target="tpu_custom_call" | custom-call | flops 40000000 | bytes 20000000 | tf_op jit(solution)/shard_map/resident_edge/pallas_call | solution.py:348
  27.8 0.0 copy-start.10
  27.8 3.5 %neighbours.1.inner_ref = f32[32,192,128]{2,1,0:T(8,128)S(1)} custom-call(bf16[384,224]{1,0:T(8,128)(2,1)S(1)} %copy-done.6, bf16[256,512]{1,0:T(8,128)(2,1)S(1)} %copy-done.4, bf16[12,192,128]{2,1,0:T(8,128)(2,1)S(1)} %bitcast.29, bf16[47,16,128]{2,1,0:T(8,128)(2,1)S(1)} %collective-permute-done.xb_ref.rest_0_, ...), custom_call_target="tpu_custom_call" | custom-call | tf_op jit(solution)/shard_map/neighbours/pallas_call | solution.py:492
  31.2 0.0 collective-permute-done.4.second_ref
  31.3 0.0 collective-permute-done.6.rest_0_
  31.3 0.0 collective-permute-done.5.near_ref
  31.3 4.2 %finish.1 = f32[32,192,128]{2,1,0:T(8,128)} custom-call(bf16[96,32]{1,0:T(8,128)(2,1)S(1)} %copy-done.10, bf16[32,192,128]{2,1,0:T(8,128)(2,1)S(1)} %bitcast.24, bf16[3,192,128]{2,1,0:T(8,128)(2,1)S(1)} %bitcast.37, bf16[12,192,128]{2,1,0:T(8,128)(2,1)S(1)} %bitcast.30, f32[32,192,128]{2,1,0:T(8,128)S(1)} %neighbours.1.inner_ref, ...), custom_call_target="tpu_custom_call" | custom-call | tf_op jit(solution)/shard_map/finish/pallas_call | solution.py:630
  (13 shorter events, 0.0 us)
Async XLA Ops:
  0.0 11.0 %copy-start.1 = (bf16[2,2,3,32,6,128]{5,3,4,2,1,0:T(8,128)(2,1)S(1)}, bf16[2,2,3,32,6,128]{5,3,4,2,1,0:T(8,128)(2,1)}, u32[]{:S(2)}) copy-start(bf16[2,2,3,32,6,128]{5,3,4,2,1,0:T(8,128)(2,1)} %param.12) | copy-start | bytes 1769476
  0.0 11.0 %copy-start.2 = (bf16[3,32,6,128]{3,1,2,0:T(8,128)(2,1)S(1)}, bf16[3,32,6,128]{3,1,2,0:T(8,128)(2,1)}, u32[]{:S(2)}) copy-start(bf16[3,32,6,128]{3,1,2,0:T(8,128)(2,1)} %param.11) | copy-start | bytes 442372
  0.0 11.0 %copy-start = (bf16[4,2,4,32,6,128]{5,3,4,2,1,0:T(8,128)(2,1)S(1)}, bf16[4,2,4,32,6,128]{5,3,4,2,1,0:T(8,128)(2,1)}, u32[]{:S(2)}) copy-start(bf16[4,2,4,32,6,128]{5,3,4,2,1,0:T(8,128)(2,1)} %param.10) | copy-start | bytes 4718596
  3.5 17.5 %collective-permute-start.3 = (bf16[12,6,32,128]{3,2,1,0:T(8,128)(2,1)}, bf16[12,6,32,128]{3,2,1,0:T(8,128)(2,1)S(1)}, u32[]{:S(2)}, u32[]{:S(2)}) collective-permute-start(bf16[12,6,32,128]{3,2,1,0:T(8,128)(2,1)} %get-tuple-element.13), channel_id=1, source_target_pairs={{0,16},{16,0},{1,17},{17,1},{2,18},{18,2},{3,19},{19,3},{4,20},{20... | collective-permute-start | bytes 1769480 | tf_op jit(solution)/shard_map/ppermute | solution.py:182
  6.5 14.4 %collective-permute-start.2 = (bf16[32,2,32,128]{3,2,1,0:T(8,128)(2,1)}, bf16[32,2,32,128]{3,2,1,0:T(8,128)(2,1)S(1)}, u32[]{:S(2)}, u32[]{:S(2)}) collective-permute-start(bf16[32,2,32,128]{3,2,1,0:T(8,128)(2,1)} %get-tuple-element.12), channel_id=1, source_target_pairs={{0,3},{1,2},{2,1},{3,0},{4,7},{5,6},{6,5},{7,4},{8,11},{9,10},{10,... | collective-permute-start | bytes 1572872 | tf_op jit(solution)/shard_map/ppermute | solution.py:181
  7.2 12.1 %collective-permute-start = (bf16[47,16,128]{2,1,0:T(8,128)(2,1)}, bf16[47,16,128]{2,1,0:T(8,128)(2,1)S(1)}, u32[]{:S(2)}, u32[]{:S(2)}) collective-permute-start(bf16[47,16,128]{2,1,0:T(8,128)(2,1)} %get-tuple-element.10), channel_id=1, source_target_pairs={{0,4},{4,8},{8,12},{12,0},{1,5},{5,9},{9,13},{13,1},{2,6},{6,10},{... | collective-permute-start | bytes 577544 | tf_op jit(solution)/shard_map/ppermute | solution.py:183
  8.7 11.7 %collective-permute-start.1 = (bf16[47,16,128]{2,1,0:T(8,128)(2,1)}, bf16[47,16,128]{2,1,0:T(8,128)(2,1)S(1)}, u32[]{:S(2)}, u32[]{:S(2)}) collective-permute-start(bf16[47,16,128]{2,1,0:T(8,128)(2,1)} %get-tuple-element.11.rest_0_), channel_id=1, source_target_pairs={{4,0},{8,4},{12,8},{0,12},{5,1},{9,5},{13,9},{1,13},{6,2},{10,6},{... | collective-permute-start | bytes 577544 | tf_op jit(solution)/shard_map/ppermute | solution.py:184
  11.0 1.0 %copy-start.3 = (bf16[256,512]{1,0:T(8,128)(2,1)S(1)}, bf16[256,512]{1,0:T(8,128)(2,1)}, u32[]{:S(2)}) copy-start(bf16[256,512]{1,0:T(8,128)(2,1)} %constant.13.clone.walls_ref) | copy-start | bytes 786436
  12.0 0.9 %copy-start.5 = (s32[32,6,128]{2,0,1:T(8,128)S(1)}, s32[32,6,128]{2,0,1:T(8,128)}, u32[]{:S(2)}) copy-start(s32[32,6,128]{2,0,1:T(8,128)} %param.13) | copy-start | bytes 294916
  12.8 0.9 %copy-start.7 = (bf16[47,16,128]{2,1,0:T(8,128)(2,1)S(1)}, bf16[47,16,128]{2,1,0:T(8,128)(2,1)}, u32[]{:S(2)}) copy-start(bf16[47,16,128]{2,1,0:T(8,128)(2,1)} %get-tuple-element.11.rest_0_) | copy-start | bytes 577540
  13.8 0.9 %copy-start.9 = (bf16[288,192]{1,0:T(8,128)(2,1)S(1)}, bf16[288,192]{1,0:T(8,128)(2,1)}, u32[]{:S(2)}) copy-start(bf16[288,192]{1,0:T(8,128)(2,1)} %constant.14.clone.rows_ref) | copy-start | bytes 331780
  20.9 1.1 %copy-start.11 = (bf16[15,2,32,128]{3,2,1,0:T(8,128)(2,1)S(1)}, bf16[15,2,32,128]{3,2,1,0:T(8,128)(2,1)}, u32[]{:S(2)}) copy-start(bf16[15,2,32,128]{3,2,1,0:T(8,128)(2,1)} %get-tuple-element.14) | copy-start | bytes 737284
  20.9 2.3 %copy-start.4 = (bf16[256,512]{1,0:T(8,128)(2,1)S(1)}, bf16[256,512]{1,0:T(8,128)(2,1)}, u32[]{:S(2)}) copy-start(bf16[256,512]{1,0:T(8,128)(2,1)} %constant.13.clone.walls_ref) | copy-start | bytes 786436
  21.0 2.3 %copy-start.8 = (bf16[288,224]{1,0:T(8,128)(2,1)S(1)}, bf16[288,224]{1,0:T(8,128)(2,1)}, u32[]{:S(2)}) copy-start(bf16[288,224]{1,0:T(8,128)(2,1)} %constant.15.clone.rows_ref) | copy-start | bytes 387076
  21.1 10.2 %collective-permute-start.5 = (bf16[59,2,32,128]{3,2,1,0:T(8,128)(2,1)S(1)}, bf16[59,2,32,128]{3,2,1,0:T(8,128)(2,1)S(1)}, u32[]{:S(2)}, u32[]{:S(2)}) collective-permute-start(bf16[59,2,32,128]{3,2,1,0:T(8,128)(2,1)S(1)} %pack_near.1.rest_3_), channel_id=1, source_target_pairs={{0,1},{1,0},{2,3},{3,2},{4,5},{5,4},{6,7},{7,6},{8,9},{9,8},{10,11... | collective-permute-start | bytes 2899976 | tf_op jit(solution)/shard_map/ppermute | solution.py:406
  21.2 10.0 %collective-permute-start.6 = (bf16[12,96,128]{2,1,0:T(8,128)(2,1)S(1)}, bf16[12,96,128]{2,1,0:T(8,128)(2,1)S(1)}, u32[]{:S(2)}, u32[]{:S(2)}) collective-permute-start(bf16[12,96,128]{2,1,0:T(8,128)(2,1)S(1)} %pack_relay.1.rest_1_.rest_2_), channel_id=1, source_target_pairs={{0,16},{16,0},{1,17},{17,1},{2,18},{18,2},{3,19},{19,3},{4,20},{20... | collective-permute-start | bytes 884744 | tf_op jit(solution)/shard_map/ppermute | solution.py:388
  22.0 5.7 %copy-start.6 = (bf16[384,224]{1,0:T(8,128)(2,1)S(1)}, bf16[384,224]{1,0:T(8,128)(2,1)}, u32[]{:S(2)}) copy-start(bf16[384,224]{1,0:T(8,128)(2,1)} %constant.16.clone.stencil_ref) | copy-start | bytes 516100
  22.0 9.2 %collective-permute-start.4 = (bf16[15,2,32,128]{3,2,1,0:T(8,128)(2,1)S(1)}, bf16[15,2,32,128]{3,2,1,0:T(8,128)(2,1)S(1)}, u32[]{:S(2)}, u32[]{:S(2)}) collective-permute-start(bf16[15,2,32,128]{3,2,1,0:T(8,128)(2,1)S(1)} %copy-done.11), channel_id=1, source_target_pairs={{0,3},{1,2},{2,1},{3,0},{4,7},{5,6},{6,5},{7,4},{8,11},{9,10},{10,... | collective-permute-start | bytes 737288 | tf_op jit(solution)/shard_map/ppermute | solution.py:185
  27.8 3.5 %copy-start.10 = (bf16[96,32]{1,0:T(8,128)(2,1)S(1)}, bf16[96,32]{1,0:T(8,128)(2,1)}, u32[]{:S(2)}) copy-start(bf16[96,32]{1,0:T(8,128)(2,1)} %constant.17.clone.edge_ref) | copy-start | bytes 18436

commit v4 on v3

v4 whole, which is shorter than its diff:
```python
import jax
import jax.numpy as jnp
from jax import lax
from jax.experimental import pallas as pl
from jax.experimental.pallas import tpu as pltpu
from jax.sharding import PartitionSpec as P

FREQUENCY_STEP = 0.2
VISCOSITY = 0.05
PENALTY = 4.0
FIRST = {-2: 1.0, -1: -8.0, 1: 8.0, 2: -1.0}
SECOND = {-2: -1.0, -1: 16.0, 0: -30.0, 1: 16.0, 2: -1.0}
HALO_X = 16
VMEM_BYTES = 58 * 1024 * 1024
ANY = pl.BlockSpec(memory_space=pl.ANY)
VMEM = pl.BlockSpec(memory_space=pltpu.VMEM)
HBM = pl.BlockSpec(memory_space=pltpu.HBM)


def taps(delta, table):
    out = jnp.zeros(delta.shape, jnp.float32)
    for step, weight in table.items():
        out = jnp.where(delta == step, weight, out)
    return out


def iotas(rows, columns):
    return lax.broadcasted_iota(jnp.int32, (rows, 1), 0), lax.broadcasted_iota(jnp.int32, (1, columns), 1)


def column_cells(column, nz, nx):
    shift, own = nx.bit_length() - 1, nz * nx
    halo = column - own
    after = halo >= HALO_X
    edge = jnp.where(after, halo - HALO_X, halo)
    inside = column < own
    z = jnp.where(inside, column >> shift, edge >> 1)
    x = jnp.where(inside, column & (nx - 1), (edge & 1) + jnp.where(after, nx, -2))
    return z, x


def slope_matrix(part, z, x, to_z, to_x):
    dz, dx = to_z - z, to_x - x
    if part == 0:
        return jnp.where(dz == 0, taps(dx, FIRST), 0.0)
    if part == 1:
        return jnp.where(dx == 0, taps(dz, FIRST), 0.0)
    return jnp.where(dz == 0, taps(dx, SECOND), 0.0) + jnp.where(dx == 0, taps(dz, SECOND), 0.0)


def store_walls(walls_ref, ny):
    row, column = iotas(ny, ny)
    first, second = (taps(row - column, table).astype(jnp.bfloat16) for table in (FIRST, SECOND))
    for i, (block, sign) in enumerate(((first, 1), (first, -1), (second, 1), (second, -1))):
        if i * ny < walls_ref.shape[1]:
            walls_ref[:ny, i * ny : (i + 1) * ny] = block
            if walls_ref.shape[0] > ny:
                walls_ref[ny:, i * ny : (i + 1) * ny] = block if sign > 0 else -block


def run_copies(copies, sems):
    started = [pltpu.make_async_copy(src, dst, sems.at[i]) for i, (src, dst) in enumerate(copies)]
    for copy in started:
        copy.start()
    for copy in started:
        copy.wait()


def shards(perturbation, base_mean, base_modes, solid_mask):
    per, modes = perturbation.shape[0], base_modes.shape[0]
    nx, nz, ny = perturbation.shape[3], perturbation.shape[4], perturbation.shape[5]
    own = nz * nx
    bf16, f32 = jnp.bfloat16, jnp.float32
    harms, size_x, size_z = (lax.axis_size(a) for a in ("harm", "gx", "gz"))
    swap = harms == 2
    sides = 1 if swap else 2
    n_pert, n_mean, n_modes = per * 8, 3, modes * 6
    n_base = n_mean + n_modes
    n_res = n_pert + n_base
    n_nb = modes * 6
    n_all = n_res + sides * n_nb

    pert = jnp.swapaxes(perturbation, 3, 4).reshape(n_pert, nz, nx, ny)
    mean = jnp.swapaxes(base_mean, 1, 2)
    mode = jnp.swapaxes(base_modes, 3, 4).reshape(n_modes, nz, nx, ny)
    mask = jnp.swapaxes(solid_mask, 0, 1).reshape(own, ny)

    def place():
        me_h, odd = lax.axis_index("harm"), lax.rem(lax.axis_index("gz"), 2)
        shared = jnp.where(me_h == 0, per - modes, 0) if swap else 0
        return me_h, odd, odd * (nz - 2), (1 - odd) * (nz - 2), shared

    cross_pairs = [(i, (i + 1) % size_z if i % 2 else (i - 1) % size_z) for i in range(size_z)]
    near_pairs = [(i, i + 1 if i % 2 == 0 else i - 1) for i in range(size_z)]
    up_x = [(i, (i + 1) % size_x) for i in range(size_x)]
    down_x = [(j, i) for i, j in up_x]
    if swap:
        harm_perms = [[(0, 1), (1, 0)]]
    else:
        up_h = [(i, i + 1) for i in range(harms - 1)]
        harm_perms = [up_h, [(j, i) for i, j in up_h]]
    def sent(s, scal):
        return scal[4] if swap else (per - modes if s == 0 else 0)

    face = lambda n: jax.ShapeDtypeStruct((n, 2, nx, ny), bf16)
    roomy = pltpu.CompilerParams(vmem_limit_bytes=32 * 1024 * 1024)

    used = 2 * nz
    spare = HALO_X - used
    tiles = 3 * (-(-n_res // 4))

    def edge_tile(ref, f):
        group, i = divmod(f, 4)
        if i < 3:
            return ref[3 * group + i]
        parts = [ref[3 * group + j].astype(f32)[used:] for j in range(3)]
        return jnp.concatenate(parts + [jnp.zeros((spare, ny), f32)], axis=0).astype(bf16)

    def pack(pert_any, mean_any, mode_any, first_any, second_any, lo_any, hi_any, *rest):
        nb_anys = rest[:sides]
        pert_ref, mean_ref, mode_ref, lo_ref, hi_ref, in_sems, out_sems = rest[sides:]
        scal = place()
        z = pl.ds(scal[2], 2)
        loads = [(pert_any.at[pl.ds(8 * l, 8)], pert_ref.at[pl.ds(8 * l, 8)]) for l in range(per)]
        loads += [(mean_any, mean_ref), (mode_any, mode_ref)]
        loads = [pltpu.make_async_copy(src, dst, in_sems.at[i]) for i, (src, dst) in enumerate(loads)]
        for copy in loads:
            copy.start()
        out = []

        def send(src, dst):
            out.append(pltpu.make_async_copy(src, dst, out_sems.at[len(out)]))
            out[-1].start()

        row, column = iotas(2 * HALO_X, own)
        low = row < HALO_X
        row = jnp.where(low, row, row - HALO_X)
        target = (row >> 1) * nx + (row & 1) + jnp.where(low, 0, nx - 2)
        pick = jnp.where(column == target, 1.0, 0.0).astype(bf16)
        where = [(pert_ref, f) for f in range(n_pert)] + [(mean_ref, f) for f in range(n_mean)] + [(mode_ref, f) for f in range(n_modes)]

        def edges(group):
            got = []
            for f in range(4 * group, min(4 * group + 4, n_res), 2):
                mine = [ref[i].reshape(own, ny) for ref, i in where[f : min(f + 2, n_res)]]
                both = jnp.concatenate(mine, axis=1) if len(mine) == 2 else mine[0]
                both = jnp.dot(pick, both, preferred_element_type=f32)
                got += [both[:, i * ny : (i + 1) * ny] for i in range(len(mine))]
            if len(got) == 3:
                got.append(jnp.zeros((2 * HALO_X, ny), f32))
            for i in range(3):
                for ref, at in ((lo_ref, 0), (hi_ref, HALO_X)):
                    extra = got[3][at + spare * i : at + spare * (i + 1)]
                    ref[3 * group + i] = jnp.concatenate([got[i][at : at + used], extra], axis=0).astype(bf16)

        for l in range(per):
            loads[l].wait()
            mine = pl.ds(8 * l, 8)
            send(pert_ref.at[mine, z], first_any.at[mine])
        for s, nb_any in enumerate(nb_anys):
            for i in range(modes * 2):
                send(pert_ref.at[pl.ds(sent(s, scal) * 8 + 4 * i, 3)], nb_any.at[pl.ds(3 * i, 3)])
        for group in range(n_pert // 4):
            edges(group)
        loads[per].wait()
        loads[per + 1].wait()
        send(mean_ref.at[:, z], second_any.at[pl.ds(0, n_mean)])
        send(mode_ref.at[:, z], second_any.at[pl.ds(n_mean, n_modes)])
        for group in range(n_pert // 4, tiles // 3):
            edges(group)
        send(lo_ref, lo_any)
        send(hi_ref, hi_any)
        for copy in out:
            copy.wait()

    edge = jax.ShapeDtypeStruct((tiles, HALO_X, ny), bf16)
    with jax.named_scope("pack"):
        first, second, edge_lo, edge_hi, *nb_send = pl.pallas_call(
            pack,
            out_shape=(face(n_pert), face(n_base), edge, edge) + tuple(jax.ShapeDtypeStruct((n_nb, nz, nx, ny), bf16) for _ in range(sides)),
            in_specs=[HBM] * 3,
            out_specs=(ANY,) * (4 + sides),
            scratch_shapes=[
                pltpu.VMEM((n_pert, nz, nx, ny), bf16),
                pltpu.VMEM((n_mean, nz, nx, ny), bf16),
                pltpu.VMEM((n_modes, nz, nx, ny), bf16),
                pltpu.VMEM((tiles, HALO_X, ny), bf16),
                pltpu.VMEM((tiles, HALO_X, ny), bf16),
                pltpu.SemaphoreType.DMA((per + 2,)),
                pltpu.SemaphoreType.DMA((per + sides * modes * 2 + 4,)),
            ],
            compiler_params=pltpu.CompilerParams(vmem_limit_bytes=VMEM_BYTES),
        )(pert, mean, mode)
    first_got = lax.ppermute(first, "gz", cross_pairs)
    nb_got = [lax.ppermute(b, "harm", p) for b, p in zip(nb_send, harm_perms)]
    xb_got = lax.ppermute(edge_hi, "gx", up_x)
    xa_got = lax.ppermute(edge_lo, "gx", down_x)
    second_got = lax.ppermute(second, "gz", cross_pairs)

    PAIRS = ((0, 3), (1, 2))
    DRIFT = (-1.5 * FREQUENCY_STEP, -0.5 * FREQUENCY_STEP)

    def entries(t, p, q, r, s):
        return t, q, p + r, p - r, q + s, s - q, t + p, t - p

    def couple(acc, ent, vec):
        t, q, pr, pmr, qs, sq, tp, tmp = ent
        out = []
        for i in range(2):
            a, e, b, g = (vec[j][i] for j in range(4))
            out.append(
                (
                    acc[0][i] + t * a + pr * b + sq * g,
                    acc[1][i] + t * e + qs * b + pmr * g,
                    acc[2][i] + pr * a + qs * e + tp * b + q * g,
                    acc[3][i] + sq * a + pmr * e + q * b + tmp * g,
                )
            )
        return [(out[0][j], out[1][j]) for j in range(4)]

    def harmonics_of(acc, scale):
        out = [None] * 4
        for at, (lo, hi) in enumerate(PAIRS):
            (ar, ai), (er, ei) = acc[2 * at], acc[2 * at + 1]
            out[lo] = ((ar + ei) * scale, (ai - er) * scale)
            out[hi] = ((ar - ei) * scale, (ai + er) * scale)
        return out

    def basis_of(values):
        out = []
        for lo, hi in PAIRS:
            (lr, li), (hr, hi_) = values[lo], values[hi]
            out += [(lr + hr, li + hi_), (hi_ - li, lr - hr)]
        return out

    def resident(pert_ref, mean_ref, mode_ref, out_ref, grads, plain, ents, lin, rows_ref, walls_ref):
        me_h = place()[0]
        row, column = iotas(own, own)
        to_z, to_x = column_cells(column, nz, nx)
        for i in range(3):
            rows_ref[i * own : (i + 1) * own] = slope_matrix(i, row >> nx.bit_length() - 1, row & (nx - 1), to_z, to_x).astype(bf16)
        store_walls(walls_ref, ny)
        mean_freq = 12.0 * FREQUENCY_STEP * (me_h * per + 1.5 - per * harms / 2).astype(f32)

        def rhs(ref, fields):
            cols = [ref[f] for f in fields]
            return cols[0] if len(cols) == 1 else jnp.concatenate(cols, axis=1)

        def dot(a, b):
            return jnp.dot(a, b, preferred_element_type=f32)

        for at, (lo, hi) in enumerate(PAIRS):
            for i in range(2):
                fl, fr = lo * 8 + i * 4 + 3, hi * 8 + i * 4 + 3
                got = dot(rows_ref[: 2 * own], rhs(pert_ref, (fl, fr)))
                wall = dot(rhs(pert_ref, (fl, fr)), walls_ref[:, : 2 * ny])
                for d in range(3):
                    if d == 1:
                        total, diff = wall[:, :ny], wall[:, ny:]
                    else:
                        span = slice(0, own) if d == 0 else slice(own, 2 * own)
                        total, diff = got[span, :ny] + got[span, ny:], got[span, :ny] - got[span, ny:]
                    lin[2 * at, i, d] = total
                    lin[2 * at + 1, 1 - i, d] = diff if i == 0 else -diff
        for at, (lo, hi) in enumerate(PAIRS):
            for c in range(3):
                for i in range(2):
                    sign = 1.0 if i == 0 else -1.0
                    fl, fr = lo * 8 + i * 4 + c, hi * 8 + i * 4 + c
                    got = dot(rows_ref[...], rhs(pert_ref, (fl, fr)))
                    xl, xr = pert_ref[fl].astype(f32), pert_ref[fr].astype(f32)
                    wall = dot(rhs(pert_ref, (fl, fr)), walls_ref[...])
                    total, diff = xl + xr, xl - xr
                    plain[2 * at, i, c] = total
                    plain[2 * at + 1, 1 - i, c] = sign * diff
                    for d in range(3):
                        if d == 1:
                            gt, gd = wall[:, :ny], wall[:, ny : 2 * ny]
                        else:
                            span = slice(0, own) if d == 0 else slice(own, 2 * own)
                            gt, gd = got[span, :ny] + got[span, ny:], got[span, :ny] - got[span, ny:]
                        gd = sign * gd
                        grads[2 * at, i, c, d] = gt
                        grads[2 * at + 1, 1 - i, c, d] = gd
                        if d == c:
                            if c == 0:
                                lin[2 * at, i, 3] = gt
                                lin[2 * at + 1, 1 - i, 3] = gd
                            else:
                                lin[2 * at, i, 3] = lin[2 * at, i, 3] + gt
                                lin[2 * at + 1, 1 - i, 3] = lin[2 * at + 1, 1 - i, 3] + gd
                    lt = got[2 * own :, :ny] + got[2 * own :, ny:] + wall[:, 2 * ny : 3 * ny]
                    ld = got[2 * own :, :ny] - got[2 * own :, ny:] + wall[:, 3 * ny :]
                    drift = 12.0 * DRIFT[at]
                    lin[2 * at, i, c] = lin[2 * at, i, c] - VISCOSITY * lt
                    lin[2 * at + 1, 1 - i, c] = lin[2 * at + 1, 1 - i, c] - sign * VISCOSITY * ld
                    lin[2 * at, 1 - i, c] = lin[2 * at, 1 - i, c] + sign * (mean_freq * total + drift * diff)
                    lin[2 * at + 1, i, c] = lin[2 * at + 1, i, c] - (mean_freq * diff + drift * total)
        for c in range(3):
            picked = [mean_ref[c].astype(f32)] + [mode_ref[3 * i + c].astype(f32) for i in range(4)]
            for n, ent in enumerate(entries(*picked)):
                ents[c, n] = ent
            mean_at = dot(rows_ref[: 2 * own], rhs(mean_ref, (c,)))
            mean_wall = dot(mean_ref[c], walls_ref[:ny, :ny])
            real = dot(rows_ref[: 2 * own], rhs(mode_ref, (c, 6 + c)))
            imag = dot(rows_ref[: 2 * own], rhs(mode_ref, (3 + c, 9 + c)))
            wall_real = dot(rhs(mode_ref, (c, 6 + c)), walls_ref[:, : 2 * ny])
            wall_imag = dot(rhs(mode_ref, (3 + c, 9 + c)), walls_ref[:, : 2 * ny])
            for d in range(3):
                if d == 1:
                    pr, pmr = wall_real[:, :ny], wall_real[:, ny:]
                    qs, qms = wall_imag[:, :ny], wall_imag[:, ny:]
                    t, p, q = mean_wall, 0.5 * (pr + pmr), 0.5 * (qs + qms)
                    values = (t, q, pr, pmr, qs, -qms, t + p, t - p)
                else:
                    span = slice(0, own) if d == 0 else slice(own, 2 * own)
                    values = entries(mean_at[span], real[span, :ny], imag[span, :ny], real[span, ny:], imag[span, ny:])
                for n, ent in enumerate(values):
                    ents[3 + 3 * d + c, n] = ent

        def block(b, carry):
            rows = pl.ds(pl.multiple_of(b * 8, 8), 8)
            accs = [[(lin[j, 0, c, rows], lin[j, 1, c, rows]) for j in range(4)] for c in range(4)]
            for d in range(3):
                flow = [ents[d, n, rows] for n in range(8)]
                for c in range(3):
                    accs[c] = couple(accs[c], flow, [(grads[j, 0, c, d, rows], grads[j, 1, c, d, rows]) for j in range(4)])
                along = [(plain[j, 0, d, rows], plain[j, 1, d, rows]) for j in range(4)]
                for c in range(3):
                    slope = [ents[3 + 3 * d + c, n, rows] for n in range(8)]
                    accs[c] = couple(accs[c], slope, along)
            for c in range(4):
                for k, (re, im) in enumerate(harmonics_of(accs[c], 1.0 / 24.0)):
                    out_ref[k * 8 + c, rows] = re
                    out_ref[k * 8 + 4 + c, rows] = im
            return carry

        lax.fori_loop(0, own // 8, block, 0, unroll=2)

    flat = lambda a: a.reshape(a.shape[0], -1, ny)
    with jax.named_scope("resident"):
        whole = pl.pallas_call(
            resident,
            out_shape=jax.ShapeDtypeStruct((n_pert, own, ny), f32),
            scratch_shapes=[
                pltpu.VMEM((4, 2, 3, 3, own, ny), f32),
                pltpu.VMEM((4, 2, 3, own, ny), f32),
                pltpu.VMEM((12, 8, own, ny), f32),
                pltpu.VMEM((4, 2, 4, own, ny), f32),
                pltpu.VMEM((3 * own, own), bf16),
                pltpu.VMEM((2 * ny, 4 * ny), bf16),
            ],
            compiler_params=roomy,
        )(flat(pert), flat(mean), flat(mode))

    deep = 2 * nx + 2 * HALO_X

    def pack_relay(first_ref, xb_ref, xa_ref, _, *outs):
        scal = place()
        for s, out in enumerate(outs):
            for i in range(modes * 2):
                group = sent(s, scal) * 2 + i
                for c in range(3):
                    out[3 * i + c, : 2 * nx] = first_ref[group * 4 + c].reshape(2 * nx, ny)
                    out[3 * i + c, 2 * nx : 2 * nx + HALO_X] = xb_ref[group * 3 + c]
                    out[3 * i + c, 2 * nx + HALO_X :] = xa_ref[group * 3 + c]

    with jax.named_scope("pack_relay"):
        relay = pl.pallas_call(
            pack_relay,
            out_shape=tuple(jax.ShapeDtypeStruct((n_nb, deep, ny), bf16) for _ in range(sides)),
            in_specs=[VMEM] * 3 + [ANY],
            compiler_params=roomy,
        )(first_got, xb_got, xa_got, whole)
    relay_got = [lax.ppermute(b, "harm", p) for b, p in zip(relay, harm_perms)]

    def pack_near(pert_ref, mean_ref, mode_ref, *rest):
        out = rest[-1]
        z = pl.ds(place()[3], 2)
        out[:n_pert] = pert_ref[:, z]
        out[n_pert : n_pert + n_mean] = mean_ref[:, z]
        out[n_pert + n_mean : n_res] = mode_ref[:, z]
        for s in range(sides):
            out[n_res + s * n_nb : n_res + (s + 1) * n_nb] = rest[s][:, z]

    with jax.named_scope("pack_near"):
        near = pl.pallas_call(
            pack_near,
            out_shape=face(n_all),
            in_specs=[VMEM] * (3 + sides) + [ANY],
            compiler_params=roomy,
        )(pert, mean, mode, *nb_got, relay[0])
    near_got = lax.ppermute(near, "gz", near_pairs)

    below, above = [], []
    for k in range(per):
        for m in range(-modes, modes + 1):
            l = k - m
            if l < 0:
                below.append((k, m, 0, (l + modes) * 6))
            elif l >= per:
                above.append((k, m, sides - 1, (l - per) * 6))

    ends = 16 * nz

    def edge_taps(tables):
        row, column = iotas(ends, own + 2 * HALO_X)
        last = row >= 8 * nz
        row = jnp.where(last, row - 8 * nz, row)
        to_z, to_x = column_cells(column, nz, nx)
        dz, dx = to_z - (row >> 3), to_x - (row & 7) - jnp.where(last, nx - 8, 0)
        return jnp.concatenate([jnp.where(dz == 0, taps(dx, table), 0.0)[:, own:] for table in tables], axis=0).astype(bf16)

    def on_sides(work):
        me_h = lax.axis_index("harm")
        pl.when(me_h > 0)(lambda: work(below))
        pl.when(me_h < harms - 1)(lambda: work(above))

    def product(acc, flow, value, m):
        (fr, fi), (vr, vi) = flow, value
        if m > 0:
            return acc[0] + fr * vr - fi * vi, acc[1] + fr * vi + fi * vr
        return acc[0] + fr * vr + fi * vi, acc[1] + fr * vi - fi * vr

    base_modes_at = n_pert + n_mean

    def neighbours(mask_ref, pert_ref, mean_ref, mode_ref, xb_ref, xa_ref, whole_ref, *rest):
        nb_refs = rest[:sides]
        out_ref, grads, plain, stencil_ref, walls_ref, vecs, lins, bends = rest[-8:]
        row, column = iotas(own, own + 2 * HALO_X)
        to_z, to_x = column_cells(column, nz, nx)
        for i in range(2):
            stencil_ref[i * own : (i + 1) * own] = slope_matrix(i, row >> nx.bit_length() - 1, row & (nx - 1), to_z, to_x).astype(bf16)
        store_walls(walls_ref, ny)

        def slopes(at, mine, halo):
            both = jnp.concatenate(mine, axis=1)
            rows = both if halo is None else jnp.concatenate([both, halo], axis=0)
            got = jnp.dot(stencil_ref[:, : rows.shape[0]], rows, preferred_element_type=f32)
            wall = [jnp.dot(x, walls_ref[:ny, :ny], preferred_element_type=f32) for x in mine]
            for i in range(2):
                lanes = slice(i * ny, (i + 1) * ny)
                grads[at + i, 0] = got[:own, lanes]
                grads[at + i, 2] = got[own:, lanes]
                grads[at + i, 1] = wall[i]
                plain[at + i] = mine[i].astype(f32)

        for f in range(0, n_modes, 2):
            at = base_modes_at + f
            halo = [jnp.concatenate([edge_tile(ref, at), edge_tile(ref, at + 1)], axis=1) for ref in (xb_ref, xa_ref)]
            slopes(f, [mode_ref[f], mode_ref[f + 1]], jnp.concatenate(halo, axis=0))
        for s in range(sides):
            for f in range(0, n_nb, 2):
                slopes(n_modes + s * n_nb + f, [nb_refs[s][f], nb_refs[s][f + 1]], None)

        taps_of = edge_taps((FIRST, SECOND))

        def bent(fields, lap):
            cols = [jnp.concatenate([edge_tile(xb_ref, f), edge_tile(xa_ref, f)], axis=0) for f in fields]
            both = cols[0] if len(cols) == 1 else jnp.concatenate(cols, axis=1)
            got = jnp.dot(taps_of if lap else taps_of[:ends], both, preferred_element_type=f32)
            return [(got[:ends, i * ny : (i + 1) * ny], got[ends:, i * ny : (i + 1) * ny]) for i in range(len(fields))]

        for at, (lo, hi) in enumerate(PAIRS):
            for i in range(2):
                sign = 1.0 if i == 0 else -1.0
                for c in range(4):
                    (gl, ll), (gr, lr) = bent((lo * 8 + 4 * i + c, hi * 8 + 4 * i + c), c < 3)
                    if c < 3:
                        vecs[2 * at, i, c] = gl + gr
                        vecs[2 * at + 1, 1 - i, c] = sign * (gl - gr)
                        lins[2 * at, i, c] = -VISCOSITY * (ll + lr)
                        lins[2 * at + 1, 1 - i, c] = (-VISCOSITY * sign) * (ll - lr)
                    else:
                        lins[2 * at, i, 0] = lins[2 * at, i, 0] + (gl + gr)
                        lins[2 * at + 1, 1 - i, 0] = lins[2 * at + 1, 1 - i, 0] + sign * (gl - gr)
        for c in range(3):
            at = base_modes_at + c
            (t, _), = bent((n_pert + c,), False)
            (p, _), (r, _) = bent((at, at + 6), False)
            (q, _), (s_, _) = bent((at + 3, at + 9), False)
            for n, ent in enumerate(entries(t, p, q, r, s_)):
                bends[c, n] = ent

        for z in range(nz):
            rows = slice(z * nx, (z + 1) * nx)
            solid = PENALTY * mask_ref[rows].astype(f32)
            for f in range(n_pert):
                if f % 4 < 3:
                    out_ref[f, rows] = whole_ref[f, rows] + solid * pert_ref[f, rows].astype(f32)
                else:
                    out_ref[f, rows] = whole_ref[f, rows]

        def layer_ends(z, carry):
            for end in range(2):
                strip = pl.ds(pl.multiple_of(z * nx + end * (nx // 2), 16), 16)
                keep = slice(8 * end, 8 * end + 8)
                rows = pl.ds(pl.multiple_of(z * nx + end * (nx - 8), 8), 8)
                mine = pl.ds(pl.multiple_of((end * nz + z) * 8, 8), 8)

                def read(ref, f):
                    return ref[f, strip].astype(f32)[keep]

                flow = entries(read(mean_ref, 0), *[read(mode_ref, 3 * i) for i in range(4)])
                along = basis_of([(read(pert_ref, l * 8), read(pert_ref, l * 8 + 4)) for l in range(per)])
                for c in range(4):
                    if c < 3:
                        acc = [(lins[j, 0, c, mine], lins[j, 1, c, mine]) for j in range(4)]
                        acc = couple(acc, flow, [(vecs[j, 0, c, mine], vecs[j, 1, c, mine]) for j in range(4)])
                        acc = couple(acc, [bends[c, n, mine] for n in range(8)], along)
                    else:
                        acc = [(vecs[j, 0, 0, mine], vecs[j, 1, 0, mine]) for j in range(4)]
                    for k, parts in enumerate(harmonics_of(acc, 1.0 / 24.0)):
                        for i in range(2):
                            at = k * 8 + 4 * i + c
                            out_ref[at, rows] = out_ref[at, rows] + parts[i]
            return carry

        lax.fori_loop(0, nz, layer_ends, 0)

        def work(pairs):
            def block(b, carry):
                rows = pl.ds(pl.multiple_of(b * 8, 8), 8)
                for k in sorted({p[0] for p in pairs}):
                    zero = jnp.zeros((8, ny), f32)
                    acc = [(zero, zero)] * 3
                    for _, m, s, f in [p for p in pairs if p[0] == k]:
                        at, base = n_modes + s * n_nb + f, (abs(m) - 1) * 6
                        for d in range(3):
                            flow = plain[base + d, rows], plain[base + 3 + d, rows]
                            along = plain[at + d, rows], plain[at + 3 + d, rows]
                            for c in range(3):
                                slope = grads[base + c, d, rows], grads[base + 3 + c, d, rows]
                                grad = grads[at + c, d, rows], grads[at + 3 + c, d, rows]
                                acc[c] = product(acc[c], flow, grad, m)
                                acc[c] = product(acc[c], slope, along, m)
                    for c in range(3):
                        for i in range(2):
                            at = k * 8 + 4 * i + c
                            out_ref[at, rows] = out_ref[at, rows] + acc[c][i] * (1.0 / 12.0)
                return carry

            lax.fori_loop(0, own // 8, block, 0)

        on_sides(work)

    n_ext = n_modes + sides * n_nb
    with jax.named_scope("neighbours"):
        inner = pl.pallas_call(
            neighbours,
            out_shape=jax.ShapeDtypeStruct((n_pert, own, ny), f32),
            scratch_shapes=[
                pltpu.VMEM((n_ext, 3, own, ny), f32),
                pltpu.VMEM((n_ext, own, ny), f32),
                pltpu.VMEM((2 * own, own + 2 * HALO_X), bf16),
                pltpu.VMEM((ny, ny), bf16),
                pltpu.VMEM((4, 2, 3, ends, ny), f32),
                pltpu.VMEM((4, 2, 3, ends, ny), f32),
                pltpu.VMEM((3, 8, ends, ny), f32),
            ],
            compiler_params=roomy,
        )(mask, flat(pert), flat(mean), flat(mode), xb_got, xa_got, whole, *[flat(b) for b in nb_got])

    def finish(pert_ref, mean_ref, mode_ref, inner_ref, first_ref, second_ref, near_ref, *rest):
        relay_refs, nb_refs = rest[:sides], rest[sides : 2 * sides]
        out_any, done, bends, sems = rest[2 * sides :]
        odd = place()[1]
        half = nx // 2
        done[...] = inner_ref[...]
        taps_of = edge_taps((FIRST,))

        def send(layer):
            rows = pl.ds(pl.multiple_of(layer * nx, nx), nx)
            return pltpu.make_async_copy(done.at[:, rows], out_any.at[:, rows], sems.at[layer])

        for s in range(sides):
            for f in range(0, n_nb, 2):
                both = jnp.concatenate([relay_refs[s][f + i, 2 * nx :] for i in range(2)], axis=1)
                got = jnp.dot(taps_of, both, preferred_element_type=f32)
                for i in range(2):
                    bends[s * n_nb + f + i] = got[:, i * ny : (i + 1) * ny]

        def edge_work(pairs):
            def layer_edges(z, carry):
                for end in range(2):
                    strip = pl.ds(pl.multiple_of(z * nx + end * half, 16), 16)
                    keep = slice(8 * end, 8 * end + 8)
                    rows = pl.ds(pl.multiple_of(z * nx + end * (nx - 8), 8), 8)
                    bent = pl.ds(pl.multiple_of((end * nz + z) * 8, 8), 8)
                    for k in sorted({p[0] for p in pairs}):
                        zero = jnp.zeros((8, ny), f32)
                        acc = [(zero, zero)] * 3
                        for _, m, s, f in [p for p in pairs if p[0] == k]:
                            base = (abs(m) - 1) * 6
                            flow = tuple(mode_ref[base + 3 * i, strip].astype(f32)[keep] for i in range(2))
                            for c in range(3):
                                at = s * n_nb + f + c
                                acc[c] = product(acc[c], flow, (bends[at, bent], bends[at + 3, bent]), m)
                        for c in range(3):
                            for i in range(2):
                                at = k * 8 + 4 * i + c
                                done[at, rows] = done[at, rows] + acc[c][i] * (1.0 / 12.0)
                return carry

            lax.fori_loop(0, nz, layer_edges, 0)

        on_sides(edge_work)
        for layer in range(2, nz - 2):
            send(layer).start()

        def face_layer(cross, step):
            before = (odd == 0) if cross else (odd == 1)
            near_at = jnp.where(before, 1, 0)
            layer = jnp.where(before, step, nz - 1 - step)
            turn = jnp.where(before, 1.0, -1.0)

            def mix(pair):
                return pair[1] - 8.0 * pair[0] if step == 0 else pair[0]

            def mix_lap(pair):
                return pair[1] - 16.0 * pair[0] if step == 0 else pair[0]

            def chunk_work(chunk):
                rows = pl.ds(pl.multiple_of(layer * nx + chunk * 16, 16), 16)
                strip = pl.ds(pl.multiple_of(chunk * 16, 16), 16)

                def halos(f):
                    if not cross:
                        ref, at = near_ref, f
                    elif f < n_pert:
                        ref, at = first_ref, f
                    else:
                        ref, at = second_ref, f - n_pert
                    return ref[at, near_at, strip].astype(f32), (ref[at, 1 - near_at, strip].astype(f32) if step == 0 else None)

                def nb_halos(s, f):
                    if not cross:
                        return halos(n_res + s * n_nb + f)
                    at = [pl.ds(pl.multiple_of(j * nx + chunk * 16, 16), 16) for j in (near_at, 1 - near_at)]
                    return tuple(relay_refs[s][f, r].astype(f32) for r in at)

                flows = [mean_ref[2, rows].astype(f32)] + [mode_ref[3 * i + 2, rows].astype(f32) for i in range(4)]
                flow = entries(*flows)
                along = basis_of([(pert_ref[l * 8 + 2, rows].astype(f32), pert_ref[l * 8 + 6, rows].astype(f32)) for l in range(per)])
                for c in range(4):
                    if c < 3:
                        got = [[halos(l * 8 + 4 * i + c) for i in range(2)] for l in range(per)]
                        vec = basis_of([(mix(g[0]), mix(g[1])) for g in got])
                        lap = basis_of([(mix_lap(g[0]), mix_lap(g[1])) for g in got])
                        if c == 2:
                            acc = basis_of([(mix(halos(l * 8 + 3)), mix(halos(l * 8 + 7))) for l in range(per)])
                        else:
                            acc = [(0.0, 0.0)] * 4
                        acc = couple(acc, flow, vec)
                        bend = entries(mix(halos(n_pert + c)), *[mix(halos(base_modes_at + 3 * i + c)) for i in range(4)])
                        acc = couple(acc, bend, along)
                        acc = [tuple(turn * a + VISCOSITY * v for a, v in zip(*pair)) for pair in zip(acc, lap)]
                    else:
                        acc = [tuple(turn * v for v in pair) for pair in vec]
                    for k, parts in enumerate(harmonics_of(acc, 1.0 / 24.0)):
                        for i in range(2):
                            at = k * 8 + 4 * i + c
                            done[at, rows] = done[at, rows] + parts[i]

                def nb_work(pairs):
                    for k in sorted({p[0] for p in pairs}):
                        zero = jnp.zeros((16, ny), f32)
                        for c in range(3):
                            acc = (zero, zero)
                            for _, m, s, f in [p for p in pairs if p[0] == k]:
                                base = (abs(m) - 1) * 6
                                mine = tuple(mode_ref[base + 3 * i + 2, rows].astype(f32) for i in range(2))
                                acc = product(acc, mine, tuple(mix(nb_halos(s, f + 3 * i + c)) for i in range(2)), m)
                                bent = tuple(mix(halos(base_modes_at + base + 3 * i + c)) for i in range(2))
                                carried = tuple(nb_refs[s][f + 3 * i + 2, rows].astype(f32) for i in range(2))
                                acc = product(acc, bent, carried, m)
                            for i in range(2):
                                at = k * 8 + 4 * i + c
                                done[at, rows] = done[at, rows] + (turn * (1.0 / 12.0)) * acc[i]

                on_sides(nb_work)

            lax.fori_loop(0, nx // 16, lambda chunk, carry: (chunk_work(chunk), carry)[1], 0)
            send(layer).start()

        for cross in (False, True):
            for step in range(2):
                face_layer(cross, step)
        for layer in range(nz):
            send(layer).wait()

    with jax.named_scope("finish"):
        out = pl.pallas_call(
            finish,
            out_shape=jax.ShapeDtypeStruct((n_pert, own, ny), f32),
            out_specs=HBM,
            scratch_shapes=[
                pltpu.VMEM((n_pert, own, ny), f32),
                pltpu.VMEM((sides * n_nb, ends, ny), f32),
                pltpu.SemaphoreType.DMA((nz,)),
            ],
            compiler_params=roomy,
        )(
            flat(pert), flat(mean), flat(mode), inner, first_got, second_got, near_got,
            *relay_got, *[flat(b) for b in nb_got],
        )
    return jnp.swapaxes(out.reshape(per, 2, 4, nz, nx, ny), 3, 4)


def solution(mesh):
    return jax.shard_map(
        shards,
        mesh=mesh,
        in_specs=(
            P("harm", None, None, "gx", "gz", None),
            P(None, "gx", "gz", None),
            P(None, None, None, "gx", "gz", None),
            P("gx", "gz", None),
        ),
        out_specs=P("harm", None, None, "gx", "gz", None),
        check_vma=False,
    )
```

time: 35.7 us -> 34.1 us (0.955)
  local copies, waits for them, and re-layouts: 3.71 us -> 1.99 us
  waiting for transfers between devices: 1.69 us -> 2.56 us
  Pallas kernels: 20.2 us -> 19.7 us
    ppermute x1, waiting for transfers between devices: 0.01 us -> 1.97 us  [shards(): second_got = lax.ppermute(second, 'gz', cross_pairs)]
    unnamed x24 -> x10, local copies, waits for them, and re-layouts: 3.71 us -> 1.99 us
    pallas_call x1, Pallas kernels: 3.48 us -> 4.87 us  [shards(): pl.pallas_call(neighbours, out_shape=jax.ShapeDtypeStruct((n_pert, own, n...]
    ppermute x1, waiting for transfers between devices: 1.25 us -> 0.01 us  [shards(): xa_got = lax.ppermute(edge_lo, 'gx', down_x)]
    pallas_call x2 -> x1, Pallas kernels: 8.99 us -> 8.02 us  [shards(): pl.pallas_call(resident, out_shape=jax.ShapeDtypeStruct((n_pert, own, ny)...]
    ppermute x1, waiting for transfers between devices: 0.01 us -> 0.58 us  [shards(): relay_got = [lax.ppermute(b, 'harm', p) for b, p in zip(relay, harm_perms)]]
    pallas_call x1, Pallas kernels: 4.21 us -> 3.68 us  [shards(): pl.pallas_call(finish, out_shape=jax.ShapeDtypeStruct((n_pert, own, ny),...]
    pallas_call x1, Pallas kernels: 3.46 us -> 2.98 us  [shards(): pl.pallas_call(pack, out_shape=(face(n_pert), face(n_base), edge, edge) +...]
  transfers between devices with their start and end apart: 7 -> 7, of which waited for: 2 -> 2; matrix products, arithmetic and copies ran while one was open for 0% -> 0% of each run, Pallas kernels for 35% -> 38%
where the time goes in v4:
time: 34.1 us; the launch traced here: 33.9 us
  Pallas kernels  19.7 us (58%)
  starting transfers between devices  9.59 us (28%)
  waiting for transfers between devices  2.56 us (8%)
  local copies, waits for them, and re-layouts  1.99 us (6%)
    pallas_call x1, Pallas kernels, shards(): pl.pallas_call(resident, out_shape=jax.ShapeDtypeStruct((n_pert, own, ny)...  8.02 us
    pallas_call x1, Pallas kernels, shards(): pl.pallas_call(neighbours, out_shape=jax.ShapeDtypeStruct((n_pert, own, n...  4.87 us
    pallas_call x1, Pallas kernels, shards(): pl.pallas_call(finish, out_shape=jax.ShapeDtypeStruct((n_pert, own, ny),...  3.68 us
    ppermute x1, starting transfers between devices, shards(): nb_got = [lax.ppermute(b, 'harm', p) for b, p in zip(nb_send, harm_perms)]  3.03 us
    pallas_call x1, Pallas kernels, shards(): pl.pallas_call(pack, out_shape=(face(n_pert), face(n_base), edge, edge) +...  2.98 us
    ppermute x1, starting transfers between devices, shards(): xa_got = lax.ppermute(edge_lo, 'gx', down_x)  2.25 us
    unnamed x10, local copies, waits for them, and re-layouts  1.99 us
    ppermute x1, waiting for transfers between devices, shards(): second_got = lax.ppermute(second, 'gz', cross_pairs)  1.97 us
  transfers between devices with their start and end apart: 7, of which 2 were waited for; matrix products, arithmetic and copies ran while one was open for 0% of the time, Pallas kernels for 38%

profile of v4, /device:TPU:0, one launch (start us, length us, event | category | flops | bytes accessed | tf_op | source)
XLA Modules:
  0.0 33.9 jit_solution(15131809153233094592)
XLA Ops:
  0.0 0.0 copy-start
  0.0 3.0 %pack.1 = (bf16[32,2,32,128]{3,2,1,0:T(8,128)(2,1)}, bf16[15,2,32,128]{3,2,1,0:T(8,128)(2,1)}, bf16[36,16,128]{2,1,0:T(8,128)(2,1)}, bf16[36,16,128]{2,1,0:T(8,128)(2,1)}, bf16[12,6,32,128]{3,2,1,0:T(8,128)(2,1)}) custom-call(bf16[32,6,32,128]{3,2,1,0:T(8,128)(2,1)} %bitcast.20, bf16[3,6,32,128]{3,2,1,0:T(8,128)(2,1)} %bitcast.32, ...), custom_call_target="tpu_custom_call" | custom-call | tf_op jit(solution)/shard_map/pack/pallas_call | solution.py:178
  3.0 3.0 %collective-permute-start.2 = (bf16[12,6,32,128]{3,2,1,0:T(8,128)(2,1)}, bf16[12,6,32,128]{3,2,1,0:T(8,128)(2,1)S(1)}, u32[]{:S(2)}, u32[]{:S(2)}) collective-permute-start(bf16[12,6,32,128]{3,2,1,0:T(8,128)(2,1)} %get-tuple-element.12), channel_id=1, source_target_pairs={{0,16},{16,0},{1,17},{17,1},{2,18},{18,2},{3,19},{19,3},{4,20},{20... | collective-permute-start | bytes 1769480 | tf_op jit(solution)/shard_map/ppermute | solution.py:195
  6.0 0.7 %collective-permute-start.3 = (bf16[32,2,32,128]{3,2,1,0:T(8,128)(2,1)}, bf16[32,2,32,128]{3,2,1,0:T(8,128)(2,1)S(1)}, u32[]{:S(2)}, u32[]{:S(2)}) collective-permute-start(bf16[32,2,32,128]{3,2,1,0:T(8,128)(2,1)} %get-tuple-element.13), channel_id=1, source_target_pairs={{0,3},{1,2},{2,1},{3,0},{4,7},{5,6},{6,5},{7,4},{8,11},{9,10},{10,... | collective-permute-start | bytes 1572872 | tf_op jit(solution)/shard_map/ppermute | solution.py:194
  6.7 1.6 %collective-permute-start = (bf16[36,16,128]{2,1,0:T(8,128)(2,1)}, bf16[36,16,128]{2,1,0:T(8,128)(2,1)S(1)}, u32[]{:S(2)}, u32[]{:S(2)}) collective-permute-start(bf16[36,16,128]{2,1,0:T(8,128)(2,1)} %get-tuple-element.10), channel_id=1, source_target_pairs={{0,4},{4,8},{8,12},{12,0},{1,5},{5,9},{9,13},{13,1},{2,6},{6,10},{... | collective-permute-start | bytes 442376 | tf_op jit(solution)/shard_map/ppermute | solution.py:196
  8.3 2.2 %collective-permute-start.1 = (bf16[36,16,128]{2,1,0:T(8,128)(2,1)}, bf16[36,16,128]{2,1,0:T(8,128)(2,1)S(1)}, u32[]{:S(2)}, u32[]{:S(2)}) collective-permute-start(bf16[36,16,128]{2,1,0:T(8,128)(2,1)} %get-tuple-element.11), channel_id=1, source_target_pairs={{4,0},{8,4},{12,8},{0,12},{5,1},{9,5},{13,9},{1,13},{6,2},{10,6},{... | collective-permute-start | bytes 442376 | tf_op jit(solution)/shard_map/ppermute | solution.py:197
  10.5 0.0 copy-done
  10.5 0.0 copy-start.1
  10.5 1.1 %copy-done.1 = bf16[2,2,3,32,6,128]{5,3,4,2,1,0:T(8,128)(2,1)S(1)} copy-done((bf16[2,2,3,32,6,128]{5,3,4,2,1,0:T(8,128)(2,1)S(1)}, bf16[2,2,3,32,6,128]{5,3,4,2,1,0:T(8,128)(2,1)}, u32[]{:S(2)}) %copy-start.1) | copy-done | bytes 589848
  11.6 0.0 copy-start.2
  11.6 0.9 %copy-done.2 = bf16[3,32,6,128]{3,1,2,0:T(8,128)(2,1)S(1)} copy-done((bf16[3,32,6,128]{3,1,2,0:T(8,128)(2,1)S(1)}, bf16[3,32,6,128]{3,1,2,0:T(8,128)(2,1)}, u32[]{:S(2)}) %copy-start.2) | copy-done | bytes 147480
  12.5 8.0 %resident.1.whole_ref._ = f32[32,192,128]{2,1,0:T(8,128)S(1)} custom-call(bf16[32,192,128]{2,1,0:T(8,128)(2,1)S(1)} %bitcast.21, bf16[3,192,128]{2,1,0:T(8,128)(2,1)S(1)} %bitcast.33, bf16[12,192,128]{2,1,0:T(8,128)(2,1)S(1)} %bitcast.26), custom_call_target="tpu_custom_call" | custom-call | tf_op jit(solution)/shard_map/resident/pallas_call | solution.py:342
  20.5 0.0 collective-permute-done.xb_ref
  20.5 0.0 collective-permute-done.1.xa_ref
  20.5 0.0 collective-permute-done.3.first_ref
  20.6 0.0 copy-start.4
  20.6 0.0 copy-start.3
  20.6 0.0 collective-permute-done.2.rest_0_
  20.6 0.1 pack_near.1
  20.7 0.5 %collective-permute-start.5 = (bf16[59,2,32,128]{3,2,1,0:T(8,128)(2,1)S(1)}, bf16[59,2,32,128]{3,2,1,0:T(8,128)(2,1)S(1)}, u32[]{:S(2)}, u32[]{:S(2)}) collective-permute-start(bf16[59,2,32,128]{3,2,1,0:T(8,128)(2,1)S(1)} %pack_near.1), channel_id=1, source_target_pairs={{0,1},{1,0},{2,3},{3,2},{4,5},{5,4},{6,7},{7,6},{8,9},{9,8},{10,11... | collective-permute-start | bytes 2899976 | tf_op jit(solution)/shard_map/ppermute | solution.py:393
  21.2 0.5 %collective-permute-start.6 = (bf16[12,96,128]{2,1,0:T(8,128)(2,1)S(1)}, bf16[12,96,128]{2,1,0:T(8,128)(2,1)S(1)}, u32[]{:S(2)}, u32[]{:S(2)}) collective-permute-start(bf16[12,96,128]{2,1,0:T(8,128)(2,1)S(1)} %pack_relay.1.rest_1_), channel_id=1, source_target_pairs={{0,16},{16,0},{1,17},{17,1},{2,18},{18,2},{3,19},{19,3},{4,20},{20... | collective-permute-start | bytes 884744 | tf_op jit(solution)/shard_map/ppermute | solution.py:375
  21.7 0.0 copy-done.4
  21.7 1.1 %collective-permute-start.4 = (bf16[15,2,32,128]{3,2,1,0:T(8,128)(2,1)S(1)}, bf16[15,2,32,128]{3,2,1,0:T(8,128)(2,1)S(1)}, u32[]{:S(2)}, u32[]{:S(2)}) collective-permute-start(bf16[15,2,32,128]{3,2,1,0:T(8,128)(2,1)S(1)} %copy-done.4), channel_id=1, source_target_pairs={{0,3},{1,2},{2,1},{3,0},{4,7},{5,6},{6,5},{7,4},{8,11},{9,10},{10,... | collective-permute-start | bytes 737288 | tf_op jit(solution)/shard_map/ppermute | solution.py:198
  22.8 0.0 copy-done.3
  22.8 4.9 %neighbours.1.inner_ref = f32[32,192,128]{2,1,0:T(8,128)S(1)} custom-call(s32[192,128]{1,0:T(8,128)S(1)} %bitcast.37, bf16[32,192,128]{2,1,0:T(8,128)(2,1)S(1)} %bitcast.23, bf16[3,192,128]{2,1,0:T(8,128)(2,1)S(1)} %bitcast.35, bf16[12,192,128]{2,1,0:T(8,128)(2,1)S(1)} %bitcast.28, bf16[36,16,128]{2,1,0:T(8,128)(2,1)S(1)} %collective-permute-done.xb_ref, ...), custom_call_target="tpu_custom_call" | custom-call | tf_op jit(solution)/shard_map/neighbours/pallas_call | solution.py:549
  27.7 2.0 %collective-permute-done.4.second_ref = bf16[15,2,32,128]{3,2,1,0:T(8,128)(2,1)S(1)} collective-permute-done((bf16[15,2,32,128]{3,2,1,0:T(8,128)(2,1)S(1)}, bf16[15,2,32,128]{3,2,1,0:T(8,128)(2,1)S(1)}, u32[]{:S(2)}, u32[]{:S(2)}) %collective-permute-start.4) | collective-permute-done | bytes 245792 | tf_op jit(solution)/shard_map/ppermute | solution.py:198
  29.6 0.6 %collective-permute-done.6.rest_0_ = bf16[12,96,128]{2,1,0:T(8,128)(2,1)S(1)} collective-permute-done((bf16[12,96,128]{2,1,0:T(8,128)(2,1)S(1)}, bf16[12,96,128]{2,1,0:T(8,128)(2,1)S(1)}, u32[]{:S(2)}, u32[]{:S(2)}) %collective-permute-start.6) | collective-permute-done | bytes 294944 | tf_op jit(solution)/shard_map/ppermute | solution.py:375
  30.2 0.0 collective-permute-done.5.near_ref
  30.2 3.7 %finish.1 = f32[32,192,128]{2,1,0:T(8,128)} custom-call(bf16[32,192,128]{2,1,0:T(8,128)(2,1)S(1)} %bitcast.24, bf16[3,192,128]{2,1,0:T(8,128)(2,1)S(1)} %bitcast.36, bf16[12,192,128]{2,1,0:T(8,128)(2,1)S(1)} %bitcast.29, f32[32,192,128]{2,1,0:T(8,128)S(1)} %neighbours.1.inner_ref, bf16[32,2,32,128]{3,2,1,0:T(8,128)(2,1)S(1)} %collective-permute-done.3.first_ref, ...), custom_call_target="tpu_custom_call" | custom-call | tf_op jit(solution)/shard_map/finish/pallas_call | solution.py:693
  (1 shorter events, 0.0 us)
Async XLA Ops:
  0.0 10.5 %copy-start = (bf16[4,2,4,32,6,128]{5,3,4,2,1,0:T(8,128)(2,1)S(1)}, bf16[4,2,4,32,6,128]{5,3,4,2,1,0:T(8,128)(2,1)}, u32[]{:S(2)}) copy-start(bf16[4,2,4,32,6,128]{5,3,4,2,1,0:T(8,128)(2,1)} %param.4) | copy-start | bytes 4718596
  3.0 17.6 %collective-permute-start.2 = (bf16[12,6,32,128]{3,2,1,0:T(8,128)(2,1)}, bf16[12,6,32,128]{3,2,1,0:T(8,128)(2,1)S(1)}, u32[]{:S(2)}, u32[]{:S(2)}) collective-permute-start(bf16[12,6,32,128]{3,2,1,0:T(8,128)(2,1)} %get-tuple-element.12), channel_id=1, source_target_pairs={{0,16},{16,0},{1,17},{17,1},{2,18},{18,2},{3,19},{19,3},{4,20},{20... | collective-permute-start | bytes 1769480 | tf_op jit(solution)/shard_map/ppermute | solution.py:195
  6.0 14.5 %collective-permute-start.3 = (bf16[32,2,32,128]{3,2,1,0:T(8,128)(2,1)}, bf16[32,2,32,128]{3,2,1,0:T(8,128)(2,1)S(1)}, u32[]{:S(2)}, u32[]{:S(2)}) collective-permute-start(bf16[32,2,32,128]{3,2,1,0:T(8,128)(2,1)} %get-tuple-element.13), channel_id=1, source_target_pairs={{0,3},{1,2},{2,1},{3,0},{4,7},{5,6},{6,5},{7,4},{8,11},{9,10},{10,... | collective-permute-start | bytes 1572872 | tf_op jit(solution)/shard_map/ppermute | solution.py:194
  6.7 13.8 %collective-permute-start = (bf16[36,16,128]{2,1,0:T(8,128)(2,1)}, bf16[36,16,128]{2,1,0:T(8,128)(2,1)S(1)}, u32[]{:S(2)}, u32[]{:S(2)}) collective-permute-start(bf16[36,16,128]{2,1,0:T(8,128)(2,1)} %get-tuple-element.10), channel_id=1, source_target_pairs={{0,4},{4,8},{8,12},{12,0},{1,5},{5,9},{9,13},{13,1},{2,6},{6,10},{... | collective-permute-start | bytes 442376 | tf_op jit(solution)/shard_map/ppermute | solution.py:196
  8.3 12.3 %collective-permute-start.1 = (bf16[36,16,128]{2,1,0:T(8,128)(2,1)}, bf16[36,16,128]{2,1,0:T(8,128)(2,1)S(1)}, u32[]{:S(2)}, u32[]{:S(2)}) collective-permute-start(bf16[36,16,128]{2,1,0:T(8,128)(2,1)} %get-tuple-element.11), channel_id=1, source_target_pairs={{4,0},{8,4},{12,8},{0,12},{5,1},{9,5},{13,9},{1,13},{6,2},{10,6},{... | collective-permute-start | bytes 442376 | tf_op jit(solution)/shard_map/ppermute | solution.py:197
  10.5 1.1 %copy-start.1 = (bf16[2,2,3,32,6,128]{5,3,4,2,1,0:T(8,128)(2,1)S(1)}, bf16[2,2,3,32,6,128]{5,3,4,2,1,0:T(8,128)(2,1)}, u32[]{:S(2)}) copy-start(bf16[2,2,3,32,6,128]{5,3,4,2,1,0:T(8,128)(2,1)} %param.6) | copy-start | bytes 1769476
  11.6 0.9 %copy-start.2 = (bf16[3,32,6,128]{3,1,2,0:T(8,128)(2,1)S(1)}, bf16[3,32,6,128]{3,1,2,0:T(8,128)(2,1)}, u32[]{:S(2)}) copy-start(bf16[3,32,6,128]{3,1,2,0:T(8,128)(2,1)} %param.5) | copy-start | bytes 442372
  20.6 1.1 %copy-start.4 = (bf16[15,2,32,128]{3,2,1,0:T(8,128)(2,1)S(1)}, bf16[15,2,32,128]{3,2,1,0:T(8,128)(2,1)}, u32[]{:S(2)}) copy-start(bf16[15,2,32,128]{3,2,1,0:T(8,128)(2,1)} %get-tuple-element.14) | copy-start | bytes 737284
  20.6 2.2 %copy-start.3 = (s32[32,6,128]{2,0,1:T(8,128)S(1)}, s32[32,6,128]{2,0,1:T(8,128)}, u32[]{:S(2)}) copy-start(s32[32,6,128]{2,0,1:T(8,128)} %param.7) | copy-start | bytes 294916
  20.7 9.5 %collective-permute-start.5 = (bf16[59,2,32,128]{3,2,1,0:T(8,128)(2,1)S(1)}, bf16[59,2,32,128]{3,2,1,0:T(8,128)(2,1)S(1)}, u32[]{:S(2)}, u32[]{:S(2)}) collective-permute-start(bf16[59,2,32,128]{3,2,1,0:T(8,128)(2,1)S(1)} %pack_near.1), channel_id=1, source_target_pairs={{0,1},{1,0},{2,3},{3,2},{4,5},{5,4},{6,7},{7,6},{8,9},{9,8},{10,11... | collective-permute-start | bytes 2899976 | tf_op jit(solution)/shard_map/ppermute | solution.py:393
  21.2 9.0 %collective-permute-start.6 = (bf16[12,96,128]{2,1,0:T(8,128)(2,1)S(1)}, bf16[12,96,128]{2,1,0:T(8,128)(2,1)S(1)}, u32[]{:S(2)}, u32[]{:S(2)}) collective-permute-start(bf16[12,96,128]{2,1,0:T(8,128)(2,1)S(1)} %pack_relay.1.rest_1_), channel_id=1, source_target_pairs={{0,16},{16,0},{1,17},{17,1},{2,18},{18,2},{3,19},{19,3},{4,20},{20... | collective-permute-start | bytes 884744 | tf_op jit(solution)/shard_map/ppermute | solution.py:375
  21.7 7.9 %collective-permute-start.4 = (bf16[15,2,32,128]{3,2,1,0:T(8,128)(2,1)S(1)}, bf16[15,2,32,128]{3,2,1,0:T(8,128)(2,1)S(1)}, u32[]{:S(2)}, u32[]{:S(2)}) collective-permute-start(bf16[15,2,32,128]{3,2,1,0:T(8,128)(2,1)S(1)} %copy-done.4), channel_id=1, source_target_pairs={{0,3},{1,2},{2,1},{3,0},{4,7},{5,6},{6,5},{7,4},{8,11},{9,10},{10,... | collective-permute-start | bytes 737288 | tf_op jit(solution)/shard_map/ppermute | solution.py:198

commit v5 on v4

--- a/solution.py
+++ b/solution.py
@@ -424,7 +424,92 @@
 
     base_modes_at = n_pert + n_mean
 
-    def neighbours(mask_ref, pert_ref, mean_ref, mode_ref, xb_ref, xa_ref, whole_ref, *rest):
+    def face_place(cross, step):
+        odd = place()[1]
+        before = (odd == 0) if cross else (odd == 1)
+        return before, jnp.where(before, step, nz - 1 - step), jnp.where(before, 1, 0)
+
+    def faces(out_ref, mean_ref, mode_ref, pert_ref, nb_refs, first_ref, second_ref, near_ref, relay_refs, step):
+        cross = near_ref is None
+        before, layer, near_at = face_place(cross, step)
+        turn = jnp.where(before, 1.0, -1.0)
+
+        def mix(pair):
+            return pair[1] - 8.0 * pair[0] if step == 0 else pair[0]
+
+        def mix_lap(pair):
+            return pair[1] - 16.0 * pair[0] if step == 0 else pair[0]
+
+        def chunk_work(chunk, carry):
+            rows = pl.ds(pl.multiple_of(layer * nx + chunk * 16, 16), 16)
+            strip = pl.ds(pl.multiple_of(chunk * 16, 16), 16)
+
+            def halos(f):
+                if not cross:
+                    ref, at = near_ref, f
+                elif f < n_pert:
+                    ref, at = first_ref, f
+                else:
+                    ref, at = second_ref, f - n_pert
+                return ref[at, near_at, strip].astype(f32), (ref[at, 1 - near_at, strip].astype(f32) if step == 0 else None)
+
+            def nb_halos(s, f):
+                if not cross:
+                    return halos(n_res + s * n_nb + f)
+                at = [pl.ds(pl.multiple_of(j * nx + chunk * 16, 16), 16) for j in (near_at, 1 - near_at)]
+                return tuple(relay_refs[s][f, r].astype(f32) for r in at)
+
+            velocity, base = first_ref is not None or not cross, second_ref is not None or not cross
+            if velocity:
+                flow = entries(mean_ref[2, rows].astype(f32), *[mode_ref[3 * i + 2, rows].astype(f32) for i in range(4)])
+            if base:
+                along = basis_of([(pert_ref[l * 8 + 2, rows].astype(f32), pert_ref[l * 8 + 6, rows].astype(f32)) for l in range(per)])
+            for c in range(4 if velocity else 3):
+                acc = [(0.0, 0.0)] * 4
+                if velocity and c < 3:
+                    got = [[halos(l * 8 + 4 * i + c) for i in range(2)] for l in range(per)]
+                    vec = basis_of([(mix(g[0]), mix(g[1])) for g in got])
+                    lap = basis_of([(mix_lap(g[0]), mix_lap(g[1])) for g in got])
+                    if c == 2:
+                        acc = basis_of([(mix(halos(l * 8 + 3)), mix(halos(l * 8 + 7))) for l in range(per)])
+                    acc = couple(acc, flow, vec)
+                if base and c < 3:
+                    bend = entries(mix(halos(n_pert + c)), *[mix(halos(base_modes_at + 3 * i + c)) for i in range(4)])
+                    acc = couple(acc, bend, along)
+                if c == 3:
+                    acc = vec
+                if velocity and c < 3:
+                    acc = [tuple(turn * a + VISCOSITY * v for a, v in zip(*pair)) for pair in zip(acc, lap)]
+                else:
+                    acc = [tuple(turn * a for a in pair) for pair in acc]
+                for k, parts in enumerate(harmonics_of(acc, 1.0 / 24.0)):
+                    for i in range(2):
+                        at = k * 8 + 4 * i + c
+                        out_ref[at, rows] = out_ref[at, rows] + parts[i]
+
+            def nb_work(pairs):
+                for k in sorted({p[0] for p in pairs}):
+                    zero = jnp.zeros((16, ny), f32)
+                    for c in range(3):
+                        acc = (zero, zero)
+                        for _, m, s, f in [p for p in pairs if p[0] == k]:
+                            at = (abs(m) - 1) * 6
+                            mine = tuple(mode_ref[at + 3 * i + 2, rows].astype(f32) for i in range(2))
+                            acc = product(acc, mine, tuple(mix(nb_halos(s, f + 3 * i + c)) for i in range(2)), m)
+                            bent = tuple(mix(halos(base_modes_at + at + 3 * i + c)) for i in range(2))
+                            carried = tuple(nb_refs[s][f + 3 * i + 2, rows].astype(f32) for i in range(2))
+                            acc = product(acc, bent, carried, m)
+                        for i in range(2):
+                            at = k * 8 + 4 * i + c
+                            out_ref[at, rows] = out_ref[at, rows] + (turn * (1.0 / 12.0)) * acc[i]
+
+            if base:
+                on_sides(nb_work)
+            return carry
+
+        lax.fori_loop(0, nx // 16, chunk_work, 0)
+
+    def neighbours(mask_ref, pert_ref, mean_ref, mode_ref, xb_ref, xa_ref, whole_ref, first_ref, near_ref, *rest):
         nb_refs = rest[:sides]
         out_ref, grads, plain, stencil_ref, walls_ref, vecs, lins, bends = rest[-8:]
         row, column = iotas(own, own + 2 * HALO_X)
@@ -543,6 +628,9 @@
             lax.fori_loop(0, own // 8, block, 0)
 
         on_sides(work)
+        for step in range(2):
+            faces(out_ref, mean_ref, mode_ref, pert_ref, nb_refs, first_ref, None, None, None, step)
+            faces(out_ref, mean_ref, mode_ref, pert_ref, nb_refs, None, None, near_ref, None, step)
 
     n_ext = n_modes + sides * n_nb
     with jax.named_scope("neighbours"):
@@ -559,12 +647,11 @@
                 pltpu.VMEM((3, 8, ends, ny), f32),
             ],
             compiler_params=roomy,
-        )(mask, flat(pert), flat(mean), flat(mode), xb_got, xa_got, whole, *[flat(b) for b in nb_got])
-
-    def finish(pert_ref, mean_ref, mode_ref, inner_ref, first_ref, second_ref, near_ref, *rest):
+        )(mask, flat(pert), flat(mean), flat(mode), xb_got, xa_got, whole, first_got, near_got, *[flat(b) for b in nb_got])
+
+    def finish(pert_ref, mean_ref, mode_ref, inner_ref, second_ref, *rest):
         relay_refs, nb_refs = rest[:sides], rest[sides : 2 * sides]
         out_any, done, bends, sems = rest[2 * sides :]
-        odd = place()[1]
         half = nx // 2
         done[...] = inner_ref[...]
         taps_of = edge_taps((FIRST,))
@@ -607,85 +694,12 @@
         on_sides(edge_work)
         for layer in range(2, nz - 2):
             send(layer).start()
-
-        def face_layer(cross, step):
-            before = (odd == 0) if cross else (odd == 1)
-            near_at = jnp.where(before, 1, 0)
-            layer = jnp.where(before, step, nz - 1 - step)
-            turn = jnp.where(before, 1.0, -1.0)
-
-            def mix(pair):
-                return pair[1] - 8.0 * pair[0] if step == 0 else pair[0]
-
-            def mix_lap(pair):
-                return pair[1] - 16.0 * pair[0] if step == 0 else pair[0]
-
-            def chunk_work(chunk):
-                rows = pl.ds(pl.multiple_of(layer * nx + chunk * 16, 16), 16)
-                strip = pl.ds(pl.multiple_of(chunk * 16, 16), 16)
-
-                def halos(f):
-                    if not cross:
-                        ref, at = near_ref, f
-                    elif f < n_pert:
-                        ref, at = first_ref, f
-                    else:
-                        ref, at = second_ref, f - n_pert
-                    return ref[at, near_at, strip].astype(f32), (ref[at, 1 - near_at, strip].astype(f32) if step == 0 else None)
-
-                def nb_halos(s, f):
-                    if not cross:
-                        return halos(n_res + s * n_nb + f)
-                    at = [pl.ds(pl.multiple_of(j * nx + chunk * 16, 16), 16) for j in (near_at, 1 - near_at)]
-                    return tuple(relay_refs[s][f, r].astype(f32) for r in at)
-
-                flows = [mean_ref[2, rows].astype(f32)] + [mode_ref[3 * i + 2, rows].astype(f32) for i in range(4)]
-                flow = entries(*flows)
-                along = basis_of([(pert_ref[l * 8 + 2, rows].astype(f32), pert_ref[l * 8 + 6, rows].astype(f32)) for l in range(per)])
-                for c in range(4):
-                    if c < 3:
-                        got = [[halos(l * 8 + 4 * i + c) for i in range(2)] for l in range(per)]
-                        vec = basis_of([(mix(g[0]), mix(g[1])) for g in got])
-                        lap = basis_of([(mix_lap(g[0]), mix_lap(g[1])) for g in got])
-                        if c == 2:
-                            acc = basis_of([(mix(halos(l * 8 + 3)), mix(halos(l * 8 + 7))) for l in range(per)])
-                        else:
-                            acc = [(0.0, 0.0)] * 4
-                        acc = couple(acc, flow, vec)
-                        bend = entries(mix(halos(n_pert + c)), *[mix(halos(base_modes_at + 3 * i + c)) for i in range(4)])
-                        acc = couple(acc, bend, along)
-                        acc = [tuple(turn * a + VISCOSITY * v for a, v in zip(*pair)) for pair in zip(acc, lap)]
-                    else:
-                        acc = [tuple(turn * v for v in pair) for pair in vec]
-                    for k, parts in enumerate(harmonics_of(acc, 1.0 / 24.0)):
-                        for i in range(2):
-                            at = k * 8 + 4 * i + c
-                            done[at, rows] = done[at, rows] + parts[i]
-
-                def nb_work(pairs):
-                    for k in sorted({p[0] for p in pairs}):
-                        zero = jnp.zeros((16, ny), f32)
-                        for c in range(3):
-                            acc = (zero, zero)
-                            for _, m, s, f in [p for p in pairs if p[0] == k]:
-                                base = (abs(m) - 1) * 6
-                                mine = tuple(mode_ref[base + 3 * i + 2, rows].astype(f32) for i in range(2))
-                                acc = product(acc, mine, tuple(mix(nb_halos(s, f + 3 * i + c)) for i in range(2)), m)
-                                bent = tuple(mix(halos(base_modes_at + base + 3 * i + c)) for i in range(2))
-                                carried = tuple(nb_refs[s][f + 3 * i + 2, rows].astype(f32) for i in range(2))
-                                acc = product(acc, bent, carried, m)
-                            for i in range(2):
-                                at = k * 8 + 4 * i + c
-                                done[at, rows] = done[at, rows] + (turn * (1.0 / 12.0)) * acc[i]
-
-                on_sides(nb_work)
-
-            lax.fori_loop(0, nx // 16, lambda chunk, carry: (chunk_work(chunk), carry)[1], 0)
-            send(layer).start()
-
-        for cross in (False, True):
-            for step in range(2):
-                face_layer(cross, step)
+        for step in range(2):
+            send(face_place(False, step)[1]).start()
+
+        for step in range(2):
+            faces(done, mean_ref, mode_ref, pert_ref, nb_refs, None, second_ref, None, relay_refs, step)
+            send(face_place(True, step)[1]).start()
         for layer in range(nz):
             send(layer).wait()
 
@@ -701,7 +715,7 @@
             ],
             compiler_params=roomy,
         )(
-            flat(pert), flat(mean), flat(mode), inner, first_got, second_got, near_got,
+            flat(pert), flat(mean), flat(mode), inner, second_got,
             *relay_got, *[flat(b) for b in nb_got],
         )
     return jnp.swapaxes(out.reshape(per, 2, 4, nz, nx, ny), 3, 4)

time: 34.1 us -> 32.8 us (0.962)
  waiting for transfers between devices: 2.56 us -> 0.89 us
  Pallas kernels: 19.7 us -> 20.2 us
    ppermute x1, waiting for transfers between devices: 1.97 us -> 0.01 us  [shards(): second_got = lax.ppermute(second, 'gz', cross_pairs)]
    pallas_call x1, Pallas kernels: 4.87 us -> 6.63 us  [shards(): pl.pallas_call(neighbours, out_shape=jax.ShapeDtypeStruct((n_pert, own, n...]
    pallas_call x1, Pallas kernels: 3.68 us -> 2.32 us  [shards(): pl.pallas_call(finish, out_shape=jax.ShapeDtypeStruct((n_pert, own, ny),...]
    ppermute x1, waiting for transfers between devices: 0.01 us -> 0.7 us  [shards(): near_got = lax.ppermute(near, 'gz', near_pairs)]
    ppermute x1, waiting for transfers between devices: 0.58 us -> 0.17 us  [shards(): relay_got = [lax.ppermute(b, 'harm', p) for b, p in zip(relay, harm_perms)]]
  transfers between devices with their start and end apart: 7 -> 7, of which waited for: 2 -> 2; matrix products, arithmetic and copies ran while one was open for 0% -> 0% of each run, Pallas kernels for 38% -> 45%
where the time goes in v5:
time: 32.8 us; the launch traced here: 32.6 us
  Pallas kernels  20.2 us (62%)
  starting transfers between devices  9.49 us (29%)
  local copies, waits for them, and re-layouts  1.99 us (6%)
  waiting for transfers between devices  0.89 us (3%)
    pallas_call x1, Pallas kernels, shards(): pl.pallas_call(resident, out_shape=jax.ShapeDtypeStruct((n_pert, own, ny)...  8.12 us
    pallas_call x1, Pallas kernels, shards(): pl.pallas_call(neighbours, out_shape=jax.ShapeDtypeStruct((n_pert, own, n...  6.63 us
    ppermute x1, starting transfers between devices, shards(): nb_got = [lax.ppermute(b, 'harm', p) for b, p in zip(nb_send, harm_perms)]  3.03 us
    pallas_call x1, Pallas kernels, shards(): pl.pallas_call(pack, out_shape=(face(n_pert), face(n_base), edge, edge) +...  2.98 us
    pallas_call x1, Pallas kernels, shards(): pl.pallas_call(finish, out_shape=jax.ShapeDtypeStruct((n_pert, own, ny),...  2.32 us
    ppermute x1, starting transfers between devices, shards(): xa_got = lax.ppermute(edge_lo, 'gx', down_x)  2.25 us
    unnamed x10, local copies, waits for them, and re-layouts  1.99 us
    ppermute x1, starting transfers between devices, shards(): xb_got = lax.ppermute(edge_hi, 'gx', up_x)  1.58 us
  transfers between devices with their start and end apart: 7, of which 2 were waited for; matrix products, arithmetic and copies ran while one was open for 0% of the time, Pallas kernels for 45%

profile of v5, /device:TPU:0, one launch (start us, length us, event | category | flops | bytes accessed | tf_op | source)
XLA Modules:
  0.0 32.6 jit_solution(447054492612530745)
XLA Ops:
  0.0 0.0 copy-start
  0.0 3.0 %pack.1 = (bf16[32,2,32,128]{3,2,1,0:T(8,128)(2,1)}, bf16[15,2,32,128]{3,2,1,0:T(8,128)(2,1)}, bf16[36,16,128]{2,1,0:T(8,128)(2,1)}, bf16[36,16,128]{2,1,0:T(8,128)(2,1)}, bf16[12,6,32,128]{3,2,1,0:T(8,128)(2,1)}) custom-call(bf16[32,6,32,128]{3,2,1,0:T(8,128)(2,1)} %bitcast.20, bf16[3,6,32,128]{3,2,1,0:T(8,128)(2,1)} %bitcast.32, ...), custom_call_target="tpu_custom_call" | custom-call | tf_op jit(solution)/shard_map/pack/pallas_call | solution.py:178
  3.0 3.0 %collective-permute-start.3 = (bf16[12,6,32,128]{3,2,1,0:T(8,128)(2,1)}, bf16[12,6,32,128]{3,2,1,0:T(8,128)(2,1)S(1)}, u32[]{:S(2)}, u32[]{:S(2)}) collective-permute-start(bf16[12,6,32,128]{3,2,1,0:T(8,128)(2,1)} %get-tuple-element.13), channel_id=1, source_target_pairs={{0,16},{16,0},{1,17},{17,1},{2,18},{18,2},{3,19},{19,3},{4,20},{20... | collective-permute-start | bytes 1769480 | tf_op jit(solution)/shard_map/ppermute | solution.py:195
  6.0 0.7 %collective-permute-start.2 = (bf16[32,2,32,128]{3,2,1,0:T(8,128)(2,1)}, bf16[32,2,32,128]{3,2,1,0:T(8,128)(2,1)S(1)}, u32[]{:S(2)}, u32[]{:S(2)}) collective-permute-start(bf16[32,2,32,128]{3,2,1,0:T(8,128)(2,1)} %get-tuple-element.12), channel_id=1, source_target_pairs={{0,3},{1,2},{2,1},{3,0},{4,7},{5,6},{6,5},{7,4},{8,11},{9,10},{10,... | collective-permute-start | bytes 1572872 | tf_op jit(solution)/shard_map/ppermute | solution.py:194
  6.7 1.6 %collective-permute-start = (bf16[36,16,128]{2,1,0:T(8,128)(2,1)}, bf16[36,16,128]{2,1,0:T(8,128)(2,1)S(1)}, u32[]{:S(2)}, u32[]{:S(2)}) collective-permute-start(bf16[36,16,128]{2,1,0:T(8,128)(2,1)} %get-tuple-element.10), channel_id=1, source_target_pairs={{0,4},{4,8},{8,12},{12,0},{1,5},{5,9},{9,13},{13,1},{2,6},{6,10},{... | collective-permute-start | bytes 442376 | tf_op jit(solution)/shard_map/ppermute | solution.py:196
  8.3 2.2 %collective-permute-start.1 = (bf16[36,16,128]{2,1,0:T(8,128)(2,1)}, bf16[36,16,128]{2,1,0:T(8,128)(2,1)S(1)}, u32[]{:S(2)}, u32[]{:S(2)}) collective-permute-start(bf16[36,16,128]{2,1,0:T(8,128)(2,1)} %get-tuple-element.11), channel_id=1, source_target_pairs={{4,0},{8,4},{12,8},{0,12},{5,1},{9,5},{13,9},{1,13},{6,2},{10,6},{... | collective-permute-start | bytes 442376 | tf_op jit(solution)/shard_map/ppermute | solution.py:197
  10.5 0.0 copy-done
  10.5 0.0 copy-start.1
  10.5 1.1 %copy-done.1 = bf16[2,2,3,32,6,128]{5,3,4,2,1,0:T(8,128)(2,1)S(1)} copy-done((bf16[2,2,3,32,6,128]{5,3,4,2,1,0:T(8,128)(2,1)S(1)}, bf16[2,2,3,32,6,128]{5,3,4,2,1,0:T(8,128)(2,1)}, u32[]{:S(2)}) %copy-start.1) | copy-done | bytes 589848
  11.6 0.0 copy-start.2
  11.6 0.9 %copy-done.2 = bf16[3,32,6,128]{3,1,2,0:T(8,128)(2,1)S(1)} copy-done((bf16[3,32,6,128]{3,1,2,0:T(8,128)(2,1)S(1)}, bf16[3,32,6,128]{3,1,2,0:T(8,128)(2,1)}, u32[]{:S(2)}) %copy-start.2) | copy-done | bytes 147480
  12.5 8.1 %resident.1._.whole_ref = f32[32,192,128]{2,1,0:T(8,128)S(1)} custom-call(bf16[32,192,128]{2,1,0:T(8,128)(2,1)S(1)} %bitcast.21, bf16[3,192,128]{2,1,0:T(8,128)(2,1)S(1)} %bitcast.33, bf16[12,192,128]{2,1,0:T(8,128)(2,1)S(1)} %bitcast.26), custom_call_target="tpu_custom_call" | custom-call | tf_op jit(solution)/shard_map/resident/pallas_call | solution.py:342
  20.6 0.0 collective-permute-done.xb_ref
  20.6 0.0 collective-permute-done.1.xa_ref
  20.6 0.0 collective-permute-done.2.first_ref
  20.7 0.0 copy-start.4
  20.7 0.0 copy-start.3
  20.7 0.0 collective-permute-done.3.rest_0_
  20.7 0.1 pack_near.1
  20.8 0.5 %collective-permute-start.4 = (bf16[59,2,32,128]{3,2,1,0:T(8,128)(2,1)S(1)}, bf16[59,2,32,128]{3,2,1,0:T(8,128)(2,1)S(1)}, u32[]{:S(2)}, u32[]{:S(2)}) collective-permute-start(bf16[59,2,32,128]{3,2,1,0:T(8,128)(2,1)S(1)} %pack_near.1), channel_id=1, source_target_pairs={{0,1},{1,0},{2,3},{3,2},{4,5},{5,4},{6,7},{7,6},{8,9},{9,8},{10,11... | collective-permute-start | bytes 2899976 | tf_op jit(solution)/shard_map/ppermute | solution.py:393
  21.3 0.5 %collective-permute-start.6 = (bf16[12,96,128]{2,1,0:T(8,128)(2,1)S(1)}, bf16[12,96,128]{2,1,0:T(8,128)(2,1)S(1)}, u32[]{:S(2)}, u32[]{:S(2)}) collective-permute-start(bf16[12,96,128]{2,1,0:T(8,128)(2,1)S(1)} %pack_relay.1.rest_1_), channel_id=1, source_target_pairs={{0,16},{16,0},{1,17},{17,1},{2,18},{18,2},{3,19},{19,3},{4,20},{20... | collective-permute-start | bytes 884744 | tf_op jit(solution)/shard_map/ppermute | solution.py:375
  21.8 0.0 copy-done.4
  21.8 1.0 %collective-permute-start.5 = (bf16[15,2,32,128]{3,2,1,0:T(8,128)(2,1)S(1)}, bf16[15,2,32,128]{3,2,1,0:T(8,128)(2,1)S(1)}, u32[]{:S(2)}, u32[]{:S(2)}) collective-permute-start(bf16[15,2,32,128]{3,2,1,0:T(8,128)(2,1)S(1)} %copy-done.4), channel_id=1, source_target_pairs={{0,3},{1,2},{2,1},{3,0},{4,7},{5,6},{6,5},{7,4},{8,11},{9,10},{10,... | collective-permute-start | bytes 737288 | tf_op jit(solution)/shard_map/ppermute | solution.py:198
  22.8 0.7 %collective-permute-done.4.near_ref = bf16[59,2,32,128]{3,2,1,0:T(8,128)(2,1)S(1)} collective-permute-done((bf16[59,2,32,128]{3,2,1,0:T(8,128)(2,1)S(1)}, bf16[59,2,32,128]{3,2,1,0:T(8,128)(2,1)S(1)}, u32[]{:S(2)}, u32[]{:S(2)}) %collective-permute-start.4) | collective-permute-done | bytes 966688 | tf_op jit(solution)/shard_map/ppermute | solution.py:393
  23.5 0.0 copy-done.3
  23.5 6.6 %neighbours.1.inner_ref = f32[32,192,128]{2,1,0:T(8,128)S(1)} custom-call(s32[192,128]{1,0:T(8,128)S(1)} %bitcast.37, bf16[32,192,128]{2,1,0:T(8,128)(2,1)S(1)} %bitcast.23, bf16[3,192,128]{2,1,0:T(8,128)(2,1)S(1)} %bitcast.35, bf16[12,192,128]{2,1,0:T(8,128)(2,1)S(1)} %bitcast.28, bf16[36,16,128]{2,1,0:T(8,128)(2,1)S(1)} %collective-permute-done.xb_ref, ...), custom_call_target="tpu_custom_call" | custom-call | tf_op jit(solution)/shard_map/neighbours/pallas_call | solution.py:637
  30.1 0.0 collective-permute-done.5.second_ref
  30.1 0.2 collective-permute-done.6.rest_0_
  30.3 2.3 %finish.1 = f32[32,192,128]{2,1,0:T(8,128)} custom-call(bf16[32,192,128]{2,1,0:T(8,128)(2,1)S(1)} %bitcast.24, bf16[3,192,128]{2,1,0:T(8,128)(2,1)S(1)} %bitcast.36, bf16[12,192,128]{2,1,0:T(8,128)(2,1)S(1)} %bitcast.29, f32[32,192,128]{2,1,0:T(8,128)S(1)} %neighbours.1.inner_ref, bf16[15,2,32,128]{3,2,1,0:T(8,128)(2,1)S(1)} %collective-permute-done.5.second_ref, ...), custom_call_target="tpu_custom_call" | custom-call | tf_op jit(solution)/shard_map/finish/pallas_call | solution.py:707
  (1 shorter events, 0.0 us)
Async XLA Ops:
  0.0 10.5 %copy-start = (bf16[4,2,4,32,6,128]{5,3,4,2,1,0:T(8,128)(2,1)S(1)}, bf16[4,2,4,32,6,128]{5,3,4,2,1,0:T(8,128)(2,1)}, u32[]{:S(2)}) copy-start(bf16[4,2,4,32,6,128]{5,3,4,2,1,0:T(8,128)(2,1)} %param.4) | copy-start | bytes 4718596
  3.0 17.7 %collective-permute-start.3 = (bf16[12,6,32,128]{3,2,1,0:T(8,128)(2,1)}, bf16[12,6,32,128]{3,2,1,0:T(8,128)(2,1)S(1)}, u32[]{:S(2)}, u32[]{:S(2)}) collective-permute-start(bf16[12,6,32,128]{3,2,1,0:T(8,128)(2,1)} %get-tuple-element.13), channel_id=1, source_target_pairs={{0,16},{16,0},{1,17},{17,1},{2,18},{18,2},{3,19},{19,3},{4,20},{20... | collective-permute-start | bytes 1769480 | tf_op jit(solution)/shard_map/ppermute | solution.py:195
  6.0 14.6 %collective-permute-start.2 = (bf16[32,2,32,128]{3,2,1,0:T(8,128)(2,1)}, bf16[32,2,32,128]{3,2,1,0:T(8,128)(2,1)S(1)}, u32[]{:S(2)}, u32[]{:S(2)}) collective-permute-start(bf16[32,2,32,128]{3,2,1,0:T(8,128)(2,1)} %get-tuple-element.12), channel_id=1, source_target_pairs={{0,3},{1,2},{2,1},{3,0},{4,7},{5,6},{6,5},{7,4},{8,11},{9,10},{10,... | collective-permute-start | bytes 1572872 | tf_op jit(solution)/shard_map/ppermute | solution.py:194
  6.7 13.9 %collective-permute-start = (bf16[36,16,128]{2,1,0:T(8,128)(2,1)}, bf16[36,16,128]{2,1,0:T(8,128)(2,1)S(1)}, u32[]{:S(2)}, u32[]{:S(2)}) collective-permute-start(bf16[36,16,128]{2,1,0:T(8,128)(2,1)} %get-tuple-element.10), channel_id=1, source_target_pairs={{0,4},{4,8},{8,12},{12,0},{1,5},{5,9},{9,13},{13,1},{2,6},{6,10},{... | collective-permute-start | bytes 442376 | tf_op jit(solution)/shard_map/ppermute | solution.py:196
  8.3 12.4 %collective-permute-start.1 = (bf16[36,16,128]{2,1,0:T(8,128)(2,1)}, bf16[36,16,128]{2,1,0:T(8,128)(2,1)S(1)}, u32[]{:S(2)}, u32[]{:S(2)}) collective-permute-start(bf16[36,16,128]{2,1,0:T(8,128)(2,1)} %get-tuple-element.11), channel_id=1, source_target_pairs={{4,0},{8,4},{12,8},{0,12},{5,1},{9,5},{13,9},{1,13},{6,2},{10,6},{... | collective-permute-start | bytes 442376 | tf_op jit(solution)/shard_map/ppermute | solution.py:197
  10.5 1.1 %copy-start.1 = (bf16[2,2,3,32,6,128]{5,3,4,2,1,0:T(8,128)(2,1)S(1)}, bf16[2,2,3,32,6,128]{5,3,4,2,1,0:T(8,128)(2,1)}, u32[]{:S(2)}) copy-start(bf16[2,2,3,32,6,128]{5,3,4,2,1,0:T(8,128)(2,1)} %param.6) | copy-start | bytes 1769476
  11.6 0.9 %copy-start.2 = (bf16[3,32,6,128]{3,1,2,0:T(8,128)(2,1)S(1)}, bf16[3,32,6,128]{3,1,2,0:T(8,128)(2,1)}, u32[]{:S(2)}) copy-start(bf16[3,32,6,128]{3,1,2,0:T(8,128)(2,1)} %param.5) | copy-start | bytes 442372
  20.7 1.1 %copy-start.4 = (bf16[15,2,32,128]{3,2,1,0:T(8,128)(2,1)S(1)}, bf16[15,2,32,128]{3,2,1,0:T(8,128)(2,1)}, u32[]{:S(2)}) copy-start(bf16[15,2,32,128]{3,2,1,0:T(8,128)(2,1)} %get-tuple-element.14) | copy-start | bytes 737284
  20.7 2.8 %copy-start.3 = (s32[32,6,128]{2,0,1:T(8,128)S(1)}, s32[32,6,128]{2,0,1:T(8,128)}, u32[]{:S(2)}) copy-start(s32[32,6,128]{2,0,1:T(8,128)} %param.7) | copy-start | bytes 294916
  20.8 2.7 %collective-permute-start.4 = (bf16[59,2,32,128]{3,2,1,0:T(8,128)(2,1)S(1)}, bf16[59,2,32,128]{3,2,1,0:T(8,128)(2,1)S(1)}, u32[]{:S(2)}, u32[]{:S(2)}) collective-permute-start(bf16[59,2,32,128]{3,2,1,0:T(8,128)(2,1)S(1)} %pack_near.1), channel_id=1, source_target_pairs={{0,1},{1,0},{2,3},{3,2},{4,5},{5,4},{6,7},{7,6},{8,9},{9,8},{10,11... | collective-permute-start | bytes 2899976 | tf_op jit(solution)/shard_map/ppermute | solution.py:393
  21.3 9.0 %collective-permute-start.6 = (bf16[12,96,128]{2,1,0:T(8,128)(2,1)S(1)}, bf16[12,96,128]{2,1,0:T(8,128)(2,1)S(1)}, u32[]{:S(2)}, u32[]{:S(2)}) collective-permute-start(bf16[12,96,128]{2,1,0:T(8,128)(2,1)S(1)} %pack_relay.1.rest_1_), channel_id=1, source_target_pairs={{0,16},{16,0},{1,17},{17,1},{2,18},{18,2},{3,19},{19,3},{4,20},{20... | collective-permute-start | bytes 884744 | tf_op jit(solution)/shard_map/ppermute | solution.py:375
  21.8 8.3 %collective-permute-start.5 = (bf16[15,2,32,128]{3,2,1,0:T(8,128)(2,1)S(1)}, bf16[15,2,32,128]{3,2,1,0:T(8,128)(2,1)S(1)}, u32[]{:S(2)}, u32[]{:S(2)}) collective-permute-start(bf16[15,2,32,128]{3,2,1,0:T(8,128)(2,1)S(1)} %copy-done.4), channel_id=1, source_target_pairs={{0,3},{1,2},{2,1},{3,0},{4,7},{5,6},{6,5},{7,4},{8,11},{9,10},{10,... | collective-permute-start | bytes 737288 | tf_op jit(solution)/shard_map/ppermute | solution.py:198

commit v6 on v5

--- a/solution.py
+++ b/solution.py
@@ -233,7 +233,14 @@
             out += [(lr + hr, li + hi_), (hi_ - li, lr - hr)]
         return out
 
-    def resident(pert_ref, mean_ref, mode_ref, out_ref, grads, plain, ents, lin, rows_ref, walls_ref):
+    def rhs(ref, fields):
+        cols = [ref[f] for f in fields]
+        return cols[0] if len(cols) == 1 else jnp.concatenate(cols, axis=1)
+
+    def dot(a, b):
+        return jnp.dot(a, b, preferred_element_type=f32)
+
+    def resident_slopes(pert_ref, grads, plain, lin, rows_ref, walls_ref):
         me_h = place()[0]
         row, column = iotas(own, own)
         to_z, to_x = column_cells(column, nz, nx)
@@ -241,13 +248,6 @@
             rows_ref[i * own : (i + 1) * own] = slope_matrix(i, row >> nx.bit_length() - 1, row & (nx - 1), to_z, to_x).astype(bf16)
         store_walls(walls_ref, ny)
         mean_freq = 12.0 * FREQUENCY_STEP * (me_h * per + 1.5 - per * harms / 2).astype(f32)
-
-        def rhs(ref, fields):
-            cols = [ref[f] for f in fields]
-            return cols[0] if len(cols) == 1 else jnp.concatenate(cols, axis=1)
-
-        def dot(a, b):
-            return jnp.dot(a, b, preferred_element_type=f32)
 
         for at, (lo, hi) in enumerate(PAIRS):
             for i in range(2):
@@ -296,14 +296,21 @@
                     lin[2 * at + 1, 1 - i, c] = lin[2 * at + 1, 1 - i, c] - sign * VISCOSITY * ld
                     lin[2 * at, 1 - i, c] = lin[2 * at, 1 - i, c] + sign * (mean_freq * total + drift * diff)
                     lin[2 * at + 1, i, c] = lin[2 * at + 1, i, c] - (mean_freq * diff + drift * total)
+
+    def resident(mean_ref, mode_ref, grads, plain, lin, out_ref, ents, rows_ref, walls_ref):
+        row, column = iotas(own, own)
+        to_z, to_x = column_cells(column, nz, nx)
+        for i in range(2):
+            rows_ref[i * own : (i + 1) * own] = slope_matrix(i, row >> nx.bit_length() - 1, row & (nx - 1), to_z, to_x).astype(bf16)
+        store_walls(walls_ref, ny)
         for c in range(3):
             picked = [mean_ref[c].astype(f32)] + [mode_ref[3 * i + c].astype(f32) for i in range(4)]
             for n, ent in enumerate(entries(*picked)):
                 ents[c, n] = ent
-            mean_at = dot(rows_ref[: 2 * own], rhs(mean_ref, (c,)))
+            mean_at = dot(rows_ref[...], rhs(mean_ref, (c,)))
             mean_wall = dot(mean_ref[c], walls_ref[:ny, :ny])
-            real = dot(rows_ref[: 2 * own], rhs(mode_ref, (c, 6 + c)))
-            imag = dot(rows_ref[: 2 * own], rhs(mode_ref, (3 + c, 9 + c)))
+            real = dot(rows_ref[...], rhs(mode_ref, (c, 6 + c)))
+            imag = dot(rows_ref[...], rhs(mode_ref, (3 + c, 9 + c)))
             wall_real = dot(rhs(mode_ref, (c, 6 + c)), walls_ref[:, : 2 * ny])
             wall_imag = dot(rhs(mode_ref, (3 + c, 9 + c)), walls_ref[:, : 2 * ny])
             for d in range(3):
@@ -338,20 +345,24 @@
         lax.fori_loop(0, own // 8, block, 0, unroll=2)
 
     flat = lambda a: a.reshape(a.shape[0], -1, ny)
+    with jax.named_scope("resident_slopes"):
+        slopes = pl.pallas_call(
+            resident_slopes,
+            out_shape=tuple(jax.ShapeDtypeStruct(n + (own, ny), f32) for n in ((4, 2, 3, 3), (4, 2, 3), (4, 2, 4))),
+            scratch_shapes=[pltpu.VMEM((3 * own, own), bf16), pltpu.VMEM((2 * ny, 4 * ny), bf16)],
+            compiler_params=pltpu.CompilerParams(vmem_limit_bytes=20 * 1024 * 1024),
+        )(flat(pert))
     with jax.named_scope("resident"):
         whole = pl.pallas_call(
             resident,
             out_shape=jax.ShapeDtypeStruct((n_pert, own, ny), f32),
             scratch_shapes=[
-                pltpu.VMEM((4, 2, 3, 3, own, ny), f32),
-                pltpu.VMEM((4, 2, 3, own, ny), f32),
                 pltpu.VMEM((12, 8, own, ny), f32),
-                pltpu.VMEM((4, 2, 4, own, ny), f32),
-                pltpu.VMEM((3 * own, own), bf16),
-                pltpu.VMEM((2 * ny, 4 * ny), bf16),
+                pltpu.VMEM((2 * own, own), bf16),
+                pltpu.VMEM((2 * ny, 2 * ny), bf16),
             ],
             compiler_params=roomy,
-        )(flat(pert), flat(mean), flat(mode))
+        )(flat(mean), flat(mode), *slopes)
 
     deep = 2 * nx + 2 * HALO_X
 
@@ -429,7 +440,7 @@
         before = (odd == 0) if cross else (odd == 1)
         return before, jnp.where(before, step, nz - 1 - step), jnp.where(before, 1, 0)
 
-    def faces(out_ref, mean_ref, mode_ref, pert_ref, nb_refs, first_ref, second_ref, near_ref, relay_refs, step):
+    def faces(out_ref, mean_ref, mode_ref, pert_ref, nb_refs, first_ref, second_ref, near_ref, relay_refs, step, lowest=0):
         cross = near_ref is None
         before, layer, near_at = face_place(cross, step)
         turn = jnp.where(before, 1.0, -1.0)
@@ -442,6 +453,7 @@
 
         def chunk_work(chunk, carry):
             rows = pl.ds(pl.multiple_of(layer * nx + chunk * 16, 16), 16)
+            out_rows = pl.ds(pl.multiple_of((layer - lowest) * nx + chunk * 16, 16), 16)
             strip = pl.ds(pl.multiple_of(chunk * 16, 16), 16)
 
             def halos(f):
@@ -485,7 +497,7 @@
                 for k, parts in enumerate(harmonics_of(acc, 1.0 / 24.0)):
                     for i in range(2):
                         at = k * 8 + 4 * i + c
-                        out_ref[at, rows] = out_ref[at, rows] + parts[i]
+                        out_ref[at, out_rows] = out_ref[at, out_rows] + parts[i]
 
             def nb_work(pairs):
                 for k in sorted({p[0] for p in pairs}):
@@ -501,7 +513,7 @@
                             acc = product(acc, bent, carried, m)
                         for i in range(2):
                             at = k * 8 + 4 * i + c
-                            out_ref[at, rows] = out_ref[at, rows] + (turn * (1.0 / 12.0)) * acc[i]
+                            out_ref[at, out_rows] = out_ref[at, out_rows] + (turn * (1.0 / 12.0)) * acc[i]
 
             if base:
                 on_sides(nb_work)
@@ -511,7 +523,7 @@
 
     def neighbours(mask_ref, pert_ref, mean_ref, mode_ref, xb_ref, xa_ref, whole_ref, first_ref, near_ref, *rest):
         nb_refs = rest[:sides]
-        out_ref, grads, plain, stencil_ref, walls_ref, vecs, lins, bends = rest[-8:]
+        out_any, out_ref, grads, plain, stencil_ref, walls_ref, vecs, lins, bends, sems = rest[-10:]
         row, column = iotas(own, own + 2 * HALO_X)
         to_z, to_x = column_cells(column, nz, nx)
         for i in range(2):
@@ -628,15 +640,29 @@
             lax.fori_loop(0, own // 8, block, 0)
 
         on_sides(work)
+        sends = []
+
+        def send(layer):
+            rows = pl.ds(pl.multiple_of(layer * nx, nx), nx)
+            sends.append(pltpu.make_async_copy(out_ref.at[:, rows], out_any.at[:, rows], sems.at[len(sends)]))
+            sends[-1].start()
+
+        for layer in range(2, nz - 2):
+            send(layer)
+        for step in range(2):
+            faces(out_ref, mean_ref, mode_ref, pert_ref, nb_refs, None, None, near_ref, None, step)
+            send(face_place(False, step)[1])
         for step in range(2):
             faces(out_ref, mean_ref, mode_ref, pert_ref, nb_refs, first_ref, None, None, None, step)
-            faces(out_ref, mean_ref, mode_ref, pert_ref, nb_refs, None, None, near_ref, None, step)
+        for copy in sends:
+            copy.wait()
 
     n_ext = n_modes + sides * n_nb
     with jax.named_scope("neighbours"):
-        inner = pl.pallas_call(
+        result, inner = pl.pallas_call(
             neighbours,
-            out_shape=jax.ShapeDtypeStruct((n_pert, own, ny), f32),
+            out_shape=(jax.ShapeDtypeStruct((n_pert, own, ny), f32),) * 2,
+            out_specs=(HBM, VMEM),
             scratch_shapes=[
                 pltpu.VMEM((n_ext, 3, own, ny), f32),
                 pltpu.VMEM((n_ext, own, ny), f32),
@@ -645,20 +671,25 @@
                 pltpu.VMEM((4, 2, 3, ends, ny), f32),
                 pltpu.VMEM((4, 2, 3, ends, ny), f32),
                 pltpu.VMEM((3, 8, ends, ny), f32),
+                pltpu.SemaphoreType.DMA((nz - 2,)),
             ],
             compiler_params=roomy,
         )(mask, flat(pert), flat(mean), flat(mode), xb_got, xa_got, whole, first_got, near_got, *[flat(b) for b in nb_got])
 
-    def finish(pert_ref, mean_ref, mode_ref, inner_ref, second_ref, *rest):
+    n_keys = n_pert // 2 if swap else n_pert
+
+    def finish(pert_ref, mean_ref, mode_ref, inner_ref, second_ref, _, *rest):
         relay_refs, nb_refs = rest[:sides], rest[sides : 2 * sides]
-        out_any, done, bends, sems = rest[2 * sides :]
+        out_any, done, fringe, bends, sems = rest[2 * sides :]
         half = nx // 2
-        done[...] = inner_ref[...]
+        keys = jnp.where(lax.axis_index("harm") == 0, n_pert - n_keys, 0) if swap else 0
+        inner_layer = jnp.where(face_place(True, 0)[0], 2, 0)
         taps_of = edge_taps((FIRST,))
-
-        def send(layer):
-            rows = pl.ds(pl.multiple_of(layer * nx, nx), nx)
-            return pltpu.make_async_copy(done.at[:, rows], out_any.at[:, rows], sems.at[layer])
+        sends = []
+
+        def send(src, dst):
+            sends.append(pltpu.make_async_copy(src, dst, sems.at[len(sends)]))
+            sends[-1].start()
 
         for s in range(sides):
             for f in range(0, n_nb, 2):
@@ -667,55 +698,89 @@
                 for i in range(2):
                     bends[s * n_nb + f + i] = got[:, i * ny : (i + 1) * ny]
 
-        def edge_work(pairs):
-            def layer_edges(z, carry):
+        def edge_terms(pairs, z, end, add):
+            strip = pl.ds(pl.multiple_of(z * nx + end * half, 16), 16)
+            keep = slice(8 * end, 8 * end + 8)
+            bent = pl.ds(pl.multiple_of((end * nz + z) * 8, 8), 8)
+            for k in sorted({p[0] for p in pairs}):
+                zero = jnp.zeros((8, ny), f32)
+                acc = [(zero, zero)] * 3
+                for _, m, s, f in [p for p in pairs if p[0] == k]:
+                    base = (abs(m) - 1) * 6
+                    flow = tuple(mode_ref[base + 3 * i, strip].astype(f32)[keep] for i in range(2))
+                    for c in range(3):
+                        at = s * n_nb + f + c
+                        acc[c] = product(acc[c], flow, (bends[at, bent], bends[at + 3, bent]), m)
+                for c in range(3):
+                    for i in range(2):
+                        add(k, 4 * i + c, acc[c][i] * (1.0 / 12.0))
+
+        def end_rows(z, end):
+            return pl.ds(pl.multiple_of(z * nx + end * (nx - 8), 8), 8)
+
+        first_row = pl.multiple_of(jnp.where(face_place(True, 0)[0], 0, (nz - 2) * nx), nx)
+        done[...] = inner_ref[:, pl.ds(first_row, 2 * nx)]
+        cross_layer = first_row // nx
+
+        def cross_edges(pairs):
+            def at_layer(j, carry):
                 for end in range(2):
-                    strip = pl.ds(pl.multiple_of(z * nx + end * half, 16), 16)
-                    keep = slice(8 * end, 8 * end + 8)
-                    rows = pl.ds(pl.multiple_of(z * nx + end * (nx - 8), 8), 8)
-                    bent = pl.ds(pl.multiple_of((end * nz + z) * 8, 8), 8)
-                    for k in sorted({p[0] for p in pairs}):
-                        zero = jnp.zeros((8, ny), f32)
-                        acc = [(zero, zero)] * 3
-                        for _, m, s, f in [p for p in pairs if p[0] == k]:
-                            base = (abs(m) - 1) * 6
-                            flow = tuple(mode_ref[base + 3 * i, strip].astype(f32)[keep] for i in range(2))
-                            for c in range(3):
-                                at = s * n_nb + f + c
-                                acc[c] = product(acc[c], flow, (bends[at, bent], bends[at + 3, bent]), m)
-                        for c in range(3):
-                            for i in range(2):
-                                at = k * 8 + 4 * i + c
-                                done[at, rows] = done[at, rows] + acc[c][i] * (1.0 / 12.0)
+                    rows = end_rows(j, end)
+
+                    def add(k, part, value):
+                        done[k * 8 + part, rows] = done[k * 8 + part, rows] + value
+
+                    edge_terms(pairs, cross_layer + j, end, add)
                 return carry
 
-            lax.fori_loop(0, nz, layer_edges, 0)
-
-        on_sides(edge_work)
-        for layer in range(2, nz - 2):
-            send(layer).start()
+            lax.fori_loop(0, 2, at_layer, 0)
+
+        on_sides(cross_edges)
         for step in range(2):
-            send(face_place(False, step)[1]).start()
-
-        for step in range(2):
-            faces(done, mean_ref, mode_ref, pert_ref, nb_refs, None, second_ref, None, relay_refs, step)
-            send(face_place(True, step)[1]).start()
-        for layer in range(nz):
-            send(layer).wait()
+            faces(done, mean_ref, mode_ref, pert_ref, nb_refs, None, second_ref, None, relay_refs, step, cross_layer)
+        send(done, out_any.at[:, pl.ds(first_row, 2 * nx)])
+
+        def other_edges(pairs):
+            lowest = min(p[0] for p in pairs) * 8 if swap else 0
+
+            def at_layer(j, carry):
+                for end in range(2):
+
+                    def add(k, part, value):
+                        at = k * 8 + part - lowest
+                        fringe[end, at, j] = fringe[end, at, j] + value
+
+                    edge_terms(pairs, inner_layer + j, end, add)
+                return carry
+
+            lax.fori_loop(0, nz - 2, at_layer, 0)
+
+        for j in range(nz - 2):
+            for end in range(2):
+                fringe[end, :, j] = inner_ref[pl.ds(keys, n_keys), end_rows(inner_layer + j, end)]
+        on_sides(other_edges)
+        for j in range(nz - 2):
+            for end in range(2):
+                send(fringe.at[end, :, j], out_any.at[pl.ds(keys, n_keys), end_rows(inner_layer + j, end)])
+        for copy in sends:
+            copy.wait()
 
     with jax.named_scope("finish"):
         out = pl.pallas_call(
             finish,
             out_shape=jax.ShapeDtypeStruct((n_pert, own, ny), f32),
+            in_specs=[VMEM] * 5 + [HBM] + [VMEM] * (2 * sides),
             out_specs=HBM,
+            input_output_aliases={5: 0},
             scratch_shapes=[
-                pltpu.VMEM((n_pert, own, ny), f32),
+                pltpu.VMEM((n_pert, 2 * nx, ny), f32),
+                pltpu.VMEM((2, n_keys, nz - 2, 8, ny), f32),
                 pltpu.VMEM((sides * n_nb, ends, ny), f32),
-                pltpu.SemaphoreType.DMA((nz,)),
+                pltpu.SemaphoreType.DMA((1 + 2 * (nz - 2),)),
             ],
             compiler_params=roomy,
         )(
-            flat(pert), flat(mean), flat(mode), inner, second_got,
+            flat(pert), flat(mean), flat(mode), inner, second_got, result,
             *relay_got, *[flat(b) for b in nb_got],
         )
     return jnp.swapaxes(out.reshape(per, 2, 4, nz, nx, ny), 3, 4)

time: 32.8 us -> 32.4 us (0.988)
  local copies, waits for them, and re-layouts: 1.99 us -> 0.02 us
  waiting for transfers between devices: 0.89 us -> 2.11 us
    pallas_call x1 -> x2, Pallas kernels: 6.63 us -> 9.17 us  [the longest x1 6.8 us: shards(): pl.pallas_call(neighbours, out_shape=(jax.ShapeDtypeStruct((n_pert, own,...]
    pallas_call x1, Pallas kernels: 8.12 us -> 5.83 us  [shards(): pl.pallas_call(resident, out_shape=jax.ShapeDtypeStruct((n_pert, own, ny)...]
    unnamed x10, local copies, waits for them, and re-layouts: 1.99 us -> 0.02 us
    ppermute x1, waiting for transfers between devices: 0.01 us -> 1.65 us  [shards(): first_got = lax.ppermute(first, 'gz', cross_pairs)]
    ppermute x1, starting transfers between devices: 0.52 us -> 0.18 us  [shards(): near_got = lax.ppermute(near, 'gz', near_pairs)]
  transfers between devices with their start and end apart: 7 -> 7, of which waited for: 2 -> 3; matrix products, arithmetic and copies ran while one was open for 0% -> 0% of each run, Pallas kernels for 45% -> 47%
where the time goes in v6:
time: 32.4 us; the launch traced here: 32.3 us
  Pallas kernels  20.3 us (63%)
  starting transfers between devices  9.73 us (30%)
  waiting for transfers between devices  2.11 us (7%)
    pallas_call x1, Pallas kernels, shards(): pl.pallas_call(neighbours, out_shape=(jax.ShapeDtypeStruct((n_pert, own,...  6.8 us
    pallas_call x1, Pallas kernels, shards(): pl.pallas_call(resident, out_shape=jax.ShapeDtypeStruct((n_pert, own, ny)...  5.83 us
    ppermute x1, starting transfers between devices, shards(): nb_got = [lax.ppermute(b, 'harm', p) for b, p in zip(nb_send, harm_perms)]  3.04 us
    pallas_call x1, Pallas kernels, shards(): pl.pallas_call(pack, out_shape=(face(n_pert), face(n_base), edge, edge) +...  3.02 us
    pallas_call x1, Pallas kernels, shards(): pl.pallas_call(resident_slopes, out_shape=tuple((jax.ShapeDtypeStruct(n +...  2.37 us
    ppermute x1, starting transfers between devices, shards(): xa_got = lax.ppermute(edge_lo, 'gx', down_x)  2.25 us
    pallas_call x1, Pallas kernels, shards(): pl.pallas_call(finish, out_shape=jax.ShapeDtypeStruct((n_pert, own, ny),...  2.18 us
    ppermute x1, waiting for transfers between devices, shards(): first_got = lax.ppermute(first, 'gz', cross_pairs)  1.65 us
  transfers between devices with their start and end apart: 7, of which 3 were waited for; matrix products, arithmetic and copies ran while one was open for 0% of the time, Pallas kernels for 47%

profile of v6, /device:TPU:0, one launch (start us, length us, event | category | flops | bytes accessed | tf_op | source)
XLA Modules:
  0.0 32.3 jit_solution(7014430961637747919)
XLA Ops:
  0.0 0.0 copy-start
  0.0 0.0 copy-start.1
  0.0 0.0 copy-start.2
  0.0 3.0 %pack.1 = (bf16[32,2,32,128]{3,2,1,0:T(8,128)(2,1)}, bf16[15,2,32,128]{3,2,1,0:T(8,128)(2,1)}, bf16[36,16,128]{2,1,0:T(8,128)(2,1)}, bf16[36,16,128]{2,1,0:T(8,128)(2,1)}, bf16[12,6,32,128]{3,2,1,0:T(8,128)(2,1)}) custom-call(bf16[32,6,32,128]{3,2,1,0:T(8,128)(2,1)} %bitcast.20, bf16[3,6,32,128]{3,2,1,0:T(8,128)(2,1)} %bitcast.32, ...), custom_call_target="tpu_custom_call" | custom-call | tf_op jit(solution)/shard_map/pack/pallas_call | solution.py:178
  3.0 3.0 %collective-permute-start.3 = (bf16[12,6,32,128]{3,2,1,0:T(8,128)(2,1)}, bf16[12,6,32,128]{3,2,1,0:T(8,128)(2,1)S(1)}, u32[]{:S(2)}, u32[]{:S(2)}) collective-permute-start(bf16[12,6,32,128]{3,2,1,0:T(8,128)(2,1)} %get-tuple-element.21), channel_id=1, source_target_pairs={{0,16},{16,0},{1,17},{17,1},{2,18},{18,2},{3,19},{19,3},{4,20},{20... | collective-permute-start | bytes 1769480 | tf_op jit(solution)/shard_map/ppermute | solution.py:195
  6.1 0.7 %collective-permute-start.2 = (bf16[32,2,32,128]{3,2,1,0:T(8,128)(2,1)}, bf16[32,2,32,128]{3,2,1,0:T(8,128)(2,1)S(1)}, u32[]{:S(2)}, u32[]{:S(2)}) collective-permute-start(bf16[32,2,32,128]{3,2,1,0:T(8,128)(2,1)} %get-tuple-element.20), channel_id=1, source_target_pairs={{0,3},{1,2},{2,1},{3,0},{4,7},{5,6},{6,5},{7,4},{8,11},{9,10},{10,... | collective-permute-start | bytes 1572872 | tf_op jit(solution)/shard_map/ppermute | solution.py:194
  6.7 1.6 %collective-permute-start = (bf16[36,16,128]{2,1,0:T(8,128)(2,1)}, bf16[36,16,128]{2,1,0:T(8,128)(2,1)S(1)}, u32[]{:S(2)}, u32[]{:S(2)}) collective-permute-start(bf16[36,16,128]{2,1,0:T(8,128)(2,1)} %get-tuple-element.15), channel_id=1, source_target_pairs={{0,4},{4,8},{8,12},{12,0},{1,5},{5,9},{9,13},{13,1},{2,6},{6,10},{... | collective-permute-start | bytes 442376 | tf_op jit(solution)/shard_map/ppermute | solution.py:196
  8.3 2.2 %collective-permute-start.1 = (bf16[36,16,128]{2,1,0:T(8,128)(2,1)}, bf16[36,16,128]{2,1,0:T(8,128)(2,1)S(1)}, u32[]{:S(2)}, u32[]{:S(2)}) collective-permute-start(bf16[36,16,128]{2,1,0:T(8,128)(2,1)} %get-tuple-element.16), channel_id=1, source_target_pairs={{4,0},{8,4},{12,8},{0,12},{5,1},{9,5},{13,9},{1,13},{6,2},{10,6},{... | collective-permute-start | bytes 442376 | tf_op jit(solution)/shard_map/ppermute | solution.py:197
  10.6 0.0 copy-done
  10.6 2.4 %resident_slopes.1 = (f32[4,2,3,3,192,128]{5,4,3,2,1,0:T(8,128)S(1)}, f32[4,2,3,192,128]{4,3,2,1,0:T(8,128)S(1)}, f32[4,2,4,192,128]{4,3,2,1,0:T(8,128)S(1)}) custom-call(bf16[32,192,128]{2,1,0:T(8,128)(2,1)S(1)} %bitcast.21), custom_call_target="tpu_custom_call" | custom-call | tf_op jit(solution)/shard_map/resident_slopes/pallas_call | solution.py:349
  12.9 0.0 copy-done.1
  12.9 0.0 copy-done.2
  13.0 5.8 %resident.1._.whole_ref = f32[32,192,128]{2,1,0:T(8,128)S(1)} custom-call(bf16[3,192,128]{2,1,0:T(8,128)(2,1)S(1)} %bitcast.33, bf16[12,192,128]{2,1,0:T(8,128)(2,1)S(1)} %bitcast.26, f32[4,2,3,3,192,128]{5,4,3,2,1,0:T(8,128)S(1)} %get-tuple-element.17.grads, f32[4,2,3,192,128]{4,3,2,1,0:T(8,128)S(1)} %get-tuple-element.18.plain, ...), custom_call_target="tpu_custom_call" | custom-call | tf_op jit(solution)/shard_map/resident/pallas_call | solution.py:356
  18.8 0.0 collective-permute-done.xb_ref
  18.8 0.0 collective-permute-done.1.xa_ref
  18.8 1.7 %collective-permute-done.2.first_ref = bf16[32,2,32,128]{3,2,1,0:T(8,128)(2,1)S(1)} collective-permute-done((bf16[32,2,32,128]{3,2,1,0:T(8,128)(2,1)}, bf16[32,2,32,128]{3,2,1,0:T(8,128)(2,1)S(1)}, u32[]{:S(2)}, u32[]{:S(2)}) %collective-permute-start.2) | collective-permute-done | bytes 524320 | tf_op jit(solution)/shard_map/ppermute | solution.py:194
  20.5 0.0 copy-start.4
  20.5 0.0 copy-start.3
  20.5 0.0 collective-permute-done.3.rest_0_
  20.5 0.1 pack_near.1
  20.6 0.2 collective-permute-start.4
  20.8 0.8 %collective-permute-start.6 = (bf16[12,96,128]{2,1,0:T(8,128)(2,1)S(1)}, bf16[12,96,128]{2,1,0:T(8,128)(2,1)S(1)}, u32[]{:S(2)}, u32[]{:S(2)}) collective-permute-start(bf16[12,96,128]{2,1,0:T(8,128)(2,1)S(1)} %pack_relay.1.rest_1_), channel_id=1, source_target_pairs={{0,16},{16,0},{1,17},{17,1},{2,18},{18,2},{3,19},{19,3},{4,20},{20... | collective-permute-start | bytes 884744 | tf_op jit(solution)/shard_map/ppermute | solution.py:386
  21.6 0.0 copy-done.4
  21.6 1.3 %collective-permute-start.5 = (bf16[15,2,32,128]{3,2,1,0:T(8,128)(2,1)S(1)}, bf16[15,2,32,128]{3,2,1,0:T(8,128)(2,1)S(1)}, u32[]{:S(2)}, u32[]{:S(2)}) collective-permute-start(bf16[15,2,32,128]{3,2,1,0:T(8,128)(2,1)S(1)} %copy-done.4), channel_id=1, source_target_pairs={{0,3},{1,2},{2,1},{3,0},{4,7},{5,6},{6,5},{7,4},{8,11},{9,10},{10,... | collective-permute-start | bytes 737288 | tf_op jit(solution)/shard_map/ppermute | solution.py:198
  22.8 0.4 %collective-permute-done.4.near_ref = bf16[59,2,32,128]{3,2,1,0:T(8,128)(2,1)S(1)} collective-permute-done((bf16[59,2,32,128]{3,2,1,0:T(8,128)(2,1)S(1)}, bf16[59,2,32,128]{3,2,1,0:T(8,128)(2,1)S(1)}, u32[]{:S(2)}, u32[]{:S(2)}) %collective-permute-start.4) | collective-permute-done | bytes 966688 | tf_op jit(solution)/shard_map/ppermute | solution.py:404
  23.2 0.0 copy-done.3
  23.2 6.8 %neighbours.1 = (f32[32,192,128]{2,1,0:T(8,128)}, f32[32,192,128]{2,1,0:T(8,128)S(1)}) custom-call(s32[192,128]{1,0:T(8,128)S(1)} %bitcast.37, bf16[32,192,128]{2,1,0:T(8,128)(2,1)S(1)} %bitcast.23, bf16[3,192,128]{2,1,0:T(8,128)(2,1)S(1)} %bitcast.35, bf16[12,192,128]{2,1,0:T(8,128)(2,1)S(1)} %bitcast.28, ...), custom_call_target="tpu_custom_call" | custom-call | tf_op jit(solution)/shard_map/neighbours/pallas_call | solution.py:662
  30.0 0.0 collective-permute-done.5.second_ref
  30.0 0.1 collective-permute-done.6.rest_0_
  30.1 2.2 %finish.1 = f32[32,192,128]{2,1,0:T(8,128)} custom-call(bf16[32,192,128]{2,1,0:T(8,128)(2,1)S(1)} %bitcast.24, bf16[3,192,128]{2,1,0:T(8,128)(2,1)S(1)} %bitcast.36, bf16[12,192,128]{2,1,0:T(8,128)(2,1)S(1)} %bitcast.29, f32[32,192,128]{2,1,0:T(8,128)S(1)} %get-tuple-element.22.inner_ref, ...), custom_call_target="tpu_custom_call", output_to_operand_aliasing={{}: (5, {})} | custom-call | tf_op jit(solution)/shard_map/finish/pallas_call | solution.py:769
  (1 shorter events, 0.0 us)
Async XLA Ops:
  0.0 10.6 %copy-start = (bf16[4,2,4,32,6,128]{5,3,4,2,1,0:T(8,128)(2,1)S(1)}, bf16[4,2,4,32,6,128]{5,3,4,2,1,0:T(8,128)(2,1)}, u32[]{:S(2)}) copy-start(bf16[4,2,4,32,6,128]{5,3,4,2,1,0:T(8,128)(2,1)} %param.4) | copy-start | bytes 4718596
  0.0 12.9 %copy-start.1 = (bf16[2,2,3,32,6,128]{5,3,4,2,1,0:T(8,128)(2,1)S(1)}, bf16[2,2,3,32,6,128]{5,3,4,2,1,0:T(8,128)(2,1)}, u32[]{:S(2)}) copy-start(bf16[2,2,3,32,6,128]{5,3,4,2,1,0:T(8,128)(2,1)} %param.6) | copy-start | bytes 1769476
  0.0 12.9 %copy-start.2 = (bf16[3,32,6,128]{3,1,2,0:T(8,128)(2,1)S(1)}, bf16[3,32,6,128]{3,1,2,0:T(8,128)(2,1)}, u32[]{:S(2)}) copy-start(bf16[3,32,6,128]{3,1,2,0:T(8,128)(2,1)} %param.5) | copy-start | bytes 442372
  3.0 17.5 %collective-permute-start.3 = (bf16[12,6,32,128]{3,2,1,0:T(8,128)(2,1)}, bf16[12,6,32,128]{3,2,1,0:T(8,128)(2,1)S(1)}, u32[]{:S(2)}, u32[]{:S(2)}) collective-permute-start(bf16[12,6,32,128]{3,2,1,0:T(8,128)(2,1)} %get-tuple-element.21), channel_id=1, source_target_pairs={{0,16},{16,0},{1,17},{17,1},{2,18},{18,2},{3,19},{19,3},{4,20},{20... | collective-permute-start | bytes 1769480 | tf_op jit(solution)/shard_map/ppermute | solution.py:195
  6.1 14.4 %collective-permute-start.2 = (bf16[32,2,32,128]{3,2,1,0:T(8,128)(2,1)}, bf16[32,2,32,128]{3,2,1,0:T(8,128)(2,1)S(1)}, u32[]{:S(2)}, u32[]{:S(2)}) collective-permute-start(bf16[32,2,32,128]{3,2,1,0:T(8,128)(2,1)} %get-tuple-element.20), channel_id=1, source_target_pairs={{0,3},{1,2},{2,1},{3,0},{4,7},{5,6},{6,5},{7,4},{8,11},{9,10},{10,... | collective-permute-start | bytes 1572872 | tf_op jit(solution)/shard_map/ppermute | solution.py:194
  6.7 12.1 %collective-permute-start = (bf16[36,16,128]{2,1,0:T(8,128)(2,1)}, bf16[36,16,128]{2,1,0:T(8,128)(2,1)S(1)}, u32[]{:S(2)}, u32[]{:S(2)}) collective-permute-start(bf16[36,16,128]{2,1,0:T(8,128)(2,1)} %get-tuple-element.15), channel_id=1, source_target_pairs={{0,4},{4,8},{8,12},{12,0},{1,5},{5,9},{9,13},{13,1},{2,6},{6,10},{... | collective-permute-start | bytes 442376 | tf_op jit(solution)/shard_map/ppermute | solution.py:196
  8.3 10.5 %collective-permute-start.1 = (bf16[36,16,128]{2,1,0:T(8,128)(2,1)}, bf16[36,16,128]{2,1,0:T(8,128)(2,1)S(1)}, u32[]{:S(2)}, u32[]{:S(2)}) collective-permute-start(bf16[36,16,128]{2,1,0:T(8,128)(2,1)} %get-tuple-element.16), channel_id=1, source_target_pairs={{4,0},{8,4},{12,8},{0,12},{5,1},{9,5},{13,9},{1,13},{6,2},{10,6},{... | collective-permute-start | bytes 442376 | tf_op jit(solution)/shard_map/ppermute | solution.py:197
  20.5 1.1 %copy-start.4 = (bf16[15,2,32,128]{3,2,1,0:T(8,128)(2,1)S(1)}, bf16[15,2,32,128]{3,2,1,0:T(8,128)(2,1)}, u32[]{:S(2)}) copy-start(bf16[15,2,32,128]{3,2,1,0:T(8,128)(2,1)} %get-tuple-element.23) | copy-start | bytes 737284
  20.5 2.7 %copy-start.3 = (s32[32,6,128]{2,0,1:T(8,128)S(1)}, s32[32,6,128]{2,0,1:T(8,128)}, u32[]{:S(2)}) copy-start(s32[32,6,128]{2,0,1:T(8,128)} %param.7) | copy-start | bytes 294916
  20.6 2.6 %collective-permute-start.4 = (bf16[59,2,32,128]{3,2,1,0:T(8,128)(2,1)S(1)}, bf16[59,2,32,128]{3,2,1,0:T(8,128)(2,1)S(1)}, u32[]{:S(2)}, u32[]{:S(2)}) collective-permute-start(bf16[59,2,32,128]{3,2,1,0:T(8,128)(2,1)S(1)} %pack_near.1), channel_id=1, source_target_pairs={{0,1},{1,0},{2,3},{3,2},{4,5},{5,4},{6,7},{7,6},{8,9},{9,8},{10,11... | collective-permute-start | bytes 2899976 | tf_op jit(solution)/shard_map/ppermute | solution.py:404
  20.8 9.3 %collective-permute-start.6 = (bf16[12,96,128]{2,1,0:T(8,128)(2,1)S(1)}, bf16[12,96,128]{2,1,0:T(8,128)(2,1)S(1)}, u32[]{:S(2)}, u32[]{:S(2)}) collective-permute-start(bf16[12,96,128]{2,1,0:T(8,128)(2,1)S(1)} %pack_relay.1.rest_1_), channel_id=1, source_target_pairs={{0,16},{16,0},{1,17},{17,1},{2,18},{18,2},{3,19},{19,3},{4,20},{20... | collective-permute-start | bytes 884744 | tf_op jit(solution)/shard_map/ppermute | solution.py:386
  21.6 8.5 %collective-permute-start.5 = (bf16[15,2,32,128]{3,2,1,0:T(8,128)(2,1)S(1)}, bf16[15,2,32,128]{3,2,1,0:T(8,128)(2,1)S(1)}, u32[]{:S(2)}, u32[]{:S(2)}) collective-permute-start(bf16[15,2,32,128]{3,2,1,0:T(8,128)(2,1)S(1)} %copy-done.4), channel_id=1, source_target_pairs={{0,3},{1,2},{2,1},{3,0},{4,7},{5,6},{6,5},{7,4},{8,11},{9,10},{10,... | collective-permute-start | bytes 737288 | tf_op jit(solution)/shard_map/ppermute | solution.py:198

commit v7 on v6

--- a/solution.py
+++ b/solution.py
@@ -364,7 +364,106 @@
             compiler_params=roomy,
         )(flat(mean), flat(mode), *slopes)
 
-    deep = 2 * nx + 2 * HALO_X
+    base_modes_at = n_pert + n_mean
+    ends = 16 * nz
+
+    def edge_taps(tables):
+        row, column = iotas(ends, own + 2 * HALO_X)
+        last = row >= 8 * nz
+        row = jnp.where(last, row - 8 * nz, row)
+        to_z, to_x = column_cells(column, nz, nx)
+        dz, dx = to_z - (row >> 3), to_x - (row & 7) - jnp.where(last, nx - 8, 0)
+        return jnp.concatenate([jnp.where(dz == 0, taps(dx, table), 0.0)[:, own:] for table in tables], axis=0).astype(bf16)
+
+    def add_edges(mask_ref, pert_ref, mean_ref, mode_ref, xb_ref, xa_ref, whole_ref, out_ref, vecs, lins, bends):
+        taps_of = edge_taps((FIRST, SECOND))
+
+        def bent(fields, lap):
+            cols = [jnp.concatenate([edge_tile(xb_ref, f), edge_tile(xa_ref, f)], axis=0) for f in fields]
+            both = cols[0] if len(cols) == 1 else jnp.concatenate(cols, axis=1)
+            got = jnp.dot(taps_of if lap else taps_of[:ends], both, preferred_element_type=f32)
+            return [(got[:ends, i * ny : (i + 1) * ny], got[ends:, i * ny : (i + 1) * ny]) for i in range(len(fields))]
+
+        for at, (lo, hi) in enumerate(PAIRS):
+            for i in range(2):
+                sign = 1.0 if i == 0 else -1.0
+                for c in range(4):
+                    (gl, ll), (gr, lr) = bent((lo * 8 + 4 * i + c, hi * 8 + 4 * i + c), c < 3)
+                    if c < 3:
+                        vecs[2 * at, i, c] = gl + gr
+                        vecs[2 * at + 1, 1 - i, c] = sign * (gl - gr)
+                        lins[2 * at, i, c] = -VISCOSITY * (ll + lr)
+                        lins[2 * at + 1, 1 - i, c] = (-VISCOSITY * sign) * (ll - lr)
+                    else:
+                        lins[2 * at, i, 0] = lins[2 * at, i, 0] + (gl + gr)
+                        lins[2 * at + 1, 1 - i, 0] = lins[2 * at + 1, 1 - i, 0] + sign * (gl - gr)
+        for c in range(3):
+            at = base_modes_at + c
+            (t, _), = bent((n_pert + c,), False)
+            (p, _), (r, _) = bent((at, at + 6), False)
+            (q, _), (s_, _) = bent((at + 3, at + 9), False)
+            for n, ent in enumerate(entries(t, p, q, r, s_)):
+                bends[c, n] = ent
+
+        for z in range(nz):
+            rows = slice(z * nx, (z + 1) * nx)
+            solid = PENALTY * mask_ref[rows].astype(f32)
+            for f in range(n_pert):
+                if f % 4 < 3:
+                    out_ref[f, rows] = whole_ref[f, rows] + solid * pert_ref[f, rows].astype(f32)
+                else:
+                    out_ref[f, rows] = whole_ref[f, rows]
+
+        def layer_ends(z, carry):
+            for end in range(2):
+                strip = pl.ds(pl.multiple_of(z * nx + end * (nx // 2), 16), 16)
+                keep = slice(8 * end, 8 * end + 8)
+                rows = pl.ds(pl.multiple_of(z * nx + end * (nx - 8), 8), 8)
+                mine = pl.ds(pl.multiple_of((end * nz + z) * 8, 8), 8)
+
+                def read(ref, f):
+                    return ref[f, strip].astype(f32)[keep]
+
+                flow = entries(read(mean_ref, 0), *[read(mode_ref, 3 * i) for i in range(4)])
+                along = basis_of([(read(pert_ref, l * 8), read(pert_ref, l * 8 + 4)) for l in range(per)])
+                for c in range(4):
+                    if c < 3:
+                        acc = [(lins[j, 0, c, mine], lins[j, 1, c, mine]) for j in range(4)]
+                        acc = couple(acc, flow, [(vecs[j, 0, c, mine], vecs[j, 1, c, mine]) for j in range(4)])
+                        acc = couple(acc, [bends[c, n, mine] for n in range(8)], along)
+                    else:
+                        acc = [(vecs[j, 0, 0, mine], vecs[j, 1, 0, mine]) for j in range(4)]
+                    for k, parts in enumerate(harmonics_of(acc, 1.0 / 24.0)):
+                        for i in range(2):
+                            at = k * 8 + 4 * i + c
+                            out_ref[at, rows] = out_ref[at, rows] + parts[i]
+            return carry
+
+        lax.fori_loop(0, nz, layer_ends, 0)
+
+    with jax.named_scope("edges"):
+        edged = pl.pallas_call(
+            add_edges,
+            out_shape=jax.ShapeDtypeStruct((n_pert, own, ny), f32),
+            scratch_shapes=[
+                pltpu.VMEM((4, 2, 3, ends, ny), f32),
+                pltpu.VMEM((4, 2, 3, ends, ny), f32),
+                pltpu.VMEM((3, 8, ends, ny), f32),
+            ],
+            compiler_params=roomy,
+        )(mask, flat(pert), flat(mean), flat(mode), xb_got, xa_got, whole)
+
+    faces_deep = n_nb * 2 * nx
+    nb_tiles = 3 * n_nb // 4
+    deep = faces_deep + 2 * nb_tiles * HALO_X
+
+    def nb_tile(ref, after, f):
+        group, i = divmod(f, 4)
+        at = [faces_deep + (after * nb_tiles + 3 * group + j) * HALO_X for j in range(3)]
+        if i < 3:
+            return ref[at[i] : at[i] + HALO_X]
+        parts = [ref[row : row + HALO_X].astype(f32)[used:] for row in at]
+        return jnp.concatenate(parts + [jnp.zeros((spare, ny), f32)], axis=0).astype(bf16)
 
     def pack_relay(first_ref, xb_ref, xa_ref, _, *outs):
         scal = place()
@@ -372,17 +471,25 @@
             for i in range(modes * 2):
                 group = sent(s, scal) * 2 + i
                 for c in range(3):
-                    out[3 * i + c, : 2 * nx] = first_ref[group * 4 + c].reshape(2 * nx, ny)
-                    out[3 * i + c, 2 * nx : 2 * nx + HALO_X] = xb_ref[group * 3 + c]
-                    out[3 * i + c, 2 * nx + HALO_X :] = xa_ref[group * 3 + c]
+                    at = (3 * i + c) * 2 * nx
+                    out[at : at + 2 * nx] = first_ref[group * 4 + c].reshape(2 * nx, ny)
+            for after, ref in enumerate((xb_ref, xa_ref)):
+                for group in range(n_nb // 4):
+                    rows = []
+                    for f in range(4 * group, 4 * group + 4):
+                        rows.append(ref[(sent(s, scal) * 2 + f // 3) * 3 + f % 3].astype(f32))
+                    for i in range(3):
+                        at = faces_deep + (after * nb_tiles + 3 * group + i) * HALO_X
+                        tile = jnp.concatenate([rows[i][:used], rows[3][spare * i : spare * (i + 1)]], axis=0)
+                        out[at : at + HALO_X] = tile.astype(bf16)
 
     with jax.named_scope("pack_relay"):
         relay = pl.pallas_call(
             pack_relay,
-            out_shape=tuple(jax.ShapeDtypeStruct((n_nb, deep, ny), bf16) for _ in range(sides)),
+            out_shape=tuple(jax.ShapeDtypeStruct((deep, ny), bf16) for _ in range(sides)),
             in_specs=[VMEM] * 3 + [ANY],
             compiler_params=roomy,
-        )(first_got, xb_got, xa_got, whole)
+        )(first_got, xb_got, xa_got, edged)
     relay_got = [lax.ppermute(b, "harm", p) for b, p in zip(relay, harm_perms)]
 
     def pack_near(pert_ref, mean_ref, mode_ref, *rest):
@@ -412,16 +519,6 @@
             elif l >= per:
                 above.append((k, m, sides - 1, (l - per) * 6))
 
-    ends = 16 * nz
-
-    def edge_taps(tables):
-        row, column = iotas(ends, own + 2 * HALO_X)
-        last = row >= 8 * nz
-        row = jnp.where(last, row - 8 * nz, row)
-        to_z, to_x = column_cells(column, nz, nx)
-        dz, dx = to_z - (row >> 3), to_x - (row & 7) - jnp.where(last, nx - 8, 0)
-        return jnp.concatenate([jnp.where(dz == 0, taps(dx, table), 0.0)[:, own:] for table in tables], axis=0).astype(bf16)
-
     def on_sides(work):
         me_h = lax.axis_index("harm")
         pl.when(me_h > 0)(lambda: work(below))
@@ -433,7 +530,6 @@
             return acc[0] + fr * vr - fi * vi, acc[1] + fr * vi + fi * vr
         return acc[0] + fr * vr + fi * vi, acc[1] + fr * vi - fi * vr
 
-    base_modes_at = n_pert + n_mean
 
     def face_place(cross, step):
         odd = place()[1]
@@ -468,8 +564,8 @@
             def nb_halos(s, f):
                 if not cross:
                     return halos(n_res + s * n_nb + f)
-                at = [pl.ds(pl.multiple_of(j * nx + chunk * 16, 16), 16) for j in (near_at, 1 - near_at)]
-                return tuple(relay_refs[s][f, r].astype(f32) for r in at)
+                at = [pl.ds(pl.multiple_of((2 * f + j) * nx + chunk * 16, 16), 16) for j in (near_at, 1 - near_at)]
+                return tuple(relay_refs[s][r].astype(f32) for r in at)
 
             velocity, base = first_ref is not None or not cross, second_ref is not None or not cross
             if velocity:
@@ -521,9 +617,9 @@
 
         lax.fori_loop(0, nx // 16, chunk_work, 0)
 
-    def neighbours(mask_ref, pert_ref, mean_ref, mode_ref, xb_ref, xa_ref, whole_ref, first_ref, near_ref, *rest):
+    def neighbours(pert_ref, mean_ref, mode_ref, xb_ref, xa_ref, edged_ref, first_ref, near_ref, *rest):
         nb_refs = rest[:sides]
-        out_any, out_ref, grads, plain, stencil_ref, walls_ref, vecs, lins, bends, sems = rest[-10:]
+        out_any, out_ref, grads, plain, stencil_ref, walls_ref, sems = rest[-7:]
         row, column = iotas(own, own + 2 * HALO_X)
         to_z, to_x = column_cells(column, nz, nx)
         for i in range(2):
@@ -550,70 +646,7 @@
             for f in range(0, n_nb, 2):
                 slopes(n_modes + s * n_nb + f, [nb_refs[s][f], nb_refs[s][f + 1]], None)
 
-        taps_of = edge_taps((FIRST, SECOND))
-
-        def bent(fields, lap):
-            cols = [jnp.concatenate([edge_tile(xb_ref, f), edge_tile(xa_ref, f)], axis=0) for f in fields]
-            both = cols[0] if len(cols) == 1 else jnp.concatenate(cols, axis=1)
-            got = jnp.dot(taps_of if lap else taps_of[:ends], both, preferred_element_type=f32)
-            return [(got[:ends, i * ny : (i + 1) * ny], got[ends:, i * ny : (i + 1) * ny]) for i in range(len(fields))]
-
-        for at, (lo, hi) in enumerate(PAIRS):
-            for i in range(2):
-                sign = 1.0 if i == 0 else -1.0
-                for c in range(4):
-                    (gl, ll), (gr, lr) = bent((lo * 8 + 4 * i + c, hi * 8 + 4 * i + c), c < 3)
-                    if c < 3:
-                        vecs[2 * at, i, c] = gl + gr
-                        vecs[2 * at + 1, 1 - i, c] = sign * (gl - gr)
-                        lins[2 * at, i, c] = -VISCOSITY * (ll + lr)
-                        lins[2 * at + 1, 1 - i, c] = (-VISCOSITY * sign) * (ll - lr)
-                    else:
-                        lins[2 * at, i, 0] = lins[2 * at, i, 0] + (gl + gr)
-                        lins[2 * at + 1, 1 - i, 0] = lins[2 * at + 1, 1 - i, 0] + sign * (gl - gr)
-        for c in range(3):
-            at = base_modes_at + c
-            (t, _), = bent((n_pert + c,), False)
-            (p, _), (r, _) = bent((at, at + 6), False)
-            (q, _), (s_, _) = bent((at + 3, at + 9), False)
-            for n, ent in enumerate(entries(t, p, q, r, s_)):
-                bends[c, n] = ent
-
-        for z in range(nz):
-            rows = slice(z * nx, (z + 1) * nx)
-            solid = PENALTY * mask_ref[rows].astype(f32)
-            for f in range(n_pert):
-                if f % 4 < 3:
-                    out_ref[f, rows] = whole_ref[f, rows] + solid * pert_ref[f, rows].astype(f32)
-                else:
-                    out_ref[f, rows] = whole_ref[f, rows]
-
-        def layer_ends(z, carry):
-            for end in range(2):
-                strip = pl.ds(pl.multiple_of(z * nx + end * (nx // 2), 16), 16)
-                keep = slice(8 * end, 8 * end + 8)
-                rows = pl.ds(pl.multiple_of(z * nx + end * (nx - 8), 8), 8)
-                mine = pl.ds(pl.multiple_of((end * nz + z) * 8, 8), 8)
-
-                def read(ref, f):
-                    return ref[f, strip].astype(f32)[keep]
-
-                flow = entries(read(mean_ref, 0), *[read(mode_ref, 3 * i) for i in range(4)])
-                along = basis_of([(read(pert_ref, l * 8), read(pert_ref, l * 8 + 4)) for l in range(per)])
-                for c in range(4):
-                    if c < 3:
-                        acc = [(lins[j, 0, c, mine], lins[j, 1, c, mine]) for j in range(4)]
-                        acc = couple(acc, flow, [(vecs[j, 0, c, mine], vecs[j, 1, c, mine]) for j in range(4)])
-                        acc = couple(acc, [bends[c, n, mine] for n in range(8)], along)
-                    else:
-                        acc = [(vecs[j, 0, 0, mine], vecs[j, 1, 0, mine]) for j in range(4)]
-                    for k, parts in enumerate(harmonics_of(acc, 1.0 / 24.0)):
-                        for i in range(2):
-                            at = k * 8 + 4 * i + c
-                            out_ref[at, rows] = out_ref[at, rows] + parts[i]
-            return carry
-
-        lax.fori_loop(0, nz, layer_ends, 0)
+        out_ref[...] = edged_ref[...]
 
         def work(pairs):
             def block(b, carry):
@@ -668,13 +701,10 @@
                 pltpu.VMEM((n_ext, own, ny), f32),
                 pltpu.VMEM((2 * own, own + 2 * HALO_X), bf16),
                 pltpu.VMEM((ny, ny), bf16),
-                pltpu.VMEM((4, 2, 3, ends, ny), f32),
-                pltpu.VMEM((4, 2, 3, ends, ny), f32),
-                pltpu.VMEM((3, 8, ends, ny), f32),
                 pltpu.SemaphoreType.DMA((nz - 2,)),
             ],
             compiler_params=roomy,
-        )(mask, flat(pert), flat(mean), flat(mode), xb_got, xa_got, whole, first_got, near_got, *[flat(b) for b in nb_got])
+        )(flat(pert), flat(mean), flat(mode), xb_got, xa_got, edged, first_got, near_got, *[flat(b) for b in nb_got])
 
     n_keys = n_pert // 2 if swap else n_pert
 
@@ -693,7 +723,8 @@
 
         for s in range(sides):
             for f in range(0, n_nb, 2):
-                both = jnp.concatenate([relay_refs[s][f + i, 2 * nx :] for i in range(2)], axis=1)
+                both = [jnp.concatenate([nb_tile(relay_refs[s], after, f + i) for after in range(2)], axis=0) for i in range(2)]
+                both = jnp.concatenate(both, axis=1)
                 got = jnp.dot(taps_of, both, preferred_element_type=f32)
                 for i in range(2):
                     bends[s * n_nb + f + i] = got[:, i * ny : (i + 1) * ny]
@@ -738,7 +769,9 @@
         on_sides(cross_edges)
         for step in range(2):
             faces(done, mean_ref, mode_ref, pert_ref, nb_refs, None, second_ref, None, relay_refs, step, cross_layer)
-        send(done, out_any.at[:, pl.ds(first_row, 2 * nx)])
+            layer = face_place(True, step)[1]
+            here = pl.ds(pl.multiple_of((layer - cross_layer) * nx, nx), nx)
+            send(done.at[:, here], out_any.at[:, pl.ds(pl.multiple_of(layer * nx, nx), nx)])
 
         def other_edges(pairs):
             lowest = min(p[0] for p in pairs) * 8 if swap else 0
@@ -776,7 +809,7 @@
                 pltpu.VMEM((n_pert, 2 * nx, ny), f32),
                 pltpu.VMEM((2, n_keys, nz - 2, 8, ny), f32),
                 pltpu.VMEM((sides * n_nb, ends, ny), f32),
-                pltpu.SemaphoreType.DMA((1 + 2 * (nz - 2),)),
+                pltpu.SemaphoreType.DMA((2 + 2 * (nz - 2),)),
             ],
             compiler_params=roomy,
         )(

time: 32.4 us -> 32.1 us (level)
  waiting for transfers between devices: 2.11 us -> 1.63 us
  Pallas kernels: 20.3 us -> 20.7 us
    pallas_call x1 -> x2, Pallas kernels: 0.02 us -> 1.79 us  [the longest x1 1.75 us: shards(): pl.pallas_call(add_edges, out_shape=jax.ShapeDtypeStruct((n_pert, own, ny...]
    ppermute x1, waiting for transfers between devices: 1.65 us -> 0.01 us  [shards(): first_got = lax.ppermute(first, 'gz', cross_pairs)]
    pallas_call x1, Pallas kernels: 6.8 us -> 5.42 us  [shards(): pl.pallas_call(neighbours, out_shape=(jax.ShapeDtypeStruct((n_pert, own,...]
    ppermute x1, waiting for transfers between devices: 0.01 us -> 0.86 us  [shards(): second_got = lax.ppermute(second, 'gz', cross_pairs)]
    ppermute x1, waiting for transfers between devices: 0.39 us -> 0.75 us  [shards(): near_got = lax.ppermute(near, 'gz', near_pairs)]
    ppermute x1, starting transfers between devices: 1.26 us -> 0.91 us  [shards(): second_got = lax.ppermute(second, 'gz', cross_pairs)]
    ppermute x1, starting transfers between devices: 0.18 us -> 0.52 us  [shards(): near_got = lax.ppermute(near, 'gz', near_pairs)]
  transfers between devices with their start and end apart: 7 -> 7, of which waited for: 3 -> 2; matrix products, arithmetic and copies ran while one was open for 0% -> 0% of each run, Pallas kernels for 47% -> 49%
where the time goes in v7:
time: 32.1 us; the launch traced here: 32 us
  Pallas kernels  20.7 us (64%)
  starting transfers between devices  9.45 us (29%)
  waiting for transfers between devices  1.63 us (5%)
    pallas_call x1, Pallas kernels, shards(): pl.pallas_call(resident, out_shape=jax.ShapeDtypeStruct((n_pert, own, ny)...  5.96 us
    pallas_call x1, Pallas kernels, shards(): pl.pallas_call(neighbours, out_shape=(jax.ShapeDtypeStruct((n_pert, own,...  5.42 us
    ppermute x1, starting transfers between devices, shards(): nb_got = [lax.ppermute(b, 'harm', p) for b, p in zip(nb_send, harm_perms)]  3.04 us
    pallas_call x1, Pallas kernels, shards(): pl.pallas_call(pack, out_shape=(face(n_pert), face(n_base), edge, edge) +...  3.02 us
    pallas_call x1, Pallas kernels, shards(): pl.pallas_call(resident_slopes, out_shape=tuple((jax.ShapeDtypeStruct(n +...  2.37 us
    ppermute x1, starting transfers between devices, shards(): xa_got = lax.ppermute(edge_lo, 'gx', down_x)  2.25 us
    pallas_call x1, Pallas kernels, shards(): pl.pallas_call(finish, out_shape=jax.ShapeDtypeStruct((n_pert, own, ny),...  2.1 us
    pallas_call x1, Pallas kernels, shards(): pl.pallas_call(add_edges, out_shape=jax.ShapeDtypeStruct((n_pert, own, ny...  1.75 us
  transfers between devices with their start and end apart: 7, of which 2 were waited for; matrix products, arithmetic and copies ran while one was open for 0% of the time, Pallas kernels for 49%

profile of v7, /device:TPU:0, one launch (start us, length us, event | category | flops | bytes accessed | tf_op | source)
XLA Modules:
  0.0 32.0 jit_solution(13187906401827002320)
XLA Ops:
  0.0 0.0 copy-start.1
  0.0 0.0 copy-start.2
  0.0 0.0 copy-start
  0.0 3.0 %pack.1 = (bf16[32,2,32,128]{3,2,1,0:T(8,128)(2,1)}, bf16[15,2,32,128]{3,2,1,0:T(8,128)(2,1)}, bf16[36,16,128]{2,1,0:T(8,128)(2,1)}, bf16[36,16,128]{2,1,0:T(8,128)(2,1)}, bf16[12,6,32,128]{3,2,1,0:T(8,128)(2,1)}) custom-call(bf16[32,6,32,128]{3,2,1,0:T(8,128)(2,1)} %bitcast.20, bf16[3,6,32,128]{3,2,1,0:T(8,128)(2,1)} %bitcast.34, ...), custom_call_target="tpu_custom_call" | custom-call | tf_op jit(solution)/shard_map/pack/pallas_call | solution.py:178
  3.0 3.0 %collective-permute-start.3 = (bf16[12,6,32,128]{3,2,1,0:T(8,128)(2,1)}, bf16[12,6,32,128]{3,2,1,0:T(8,128)(2,1)S(1)}, u32[]{:S(2)}, u32[]{:S(2)}) collective-permute-start(bf16[12,6,32,128]{3,2,1,0:T(8,128)(2,1)} %get-tuple-element.21), channel_id=1, source_target_pairs={{0,16},{16,0},{1,17},{17,1},{2,18},{18,2},{3,19},{19,3},{4,20},{20... | collective-permute-start | bytes 1769480 | tf_op jit(solution)/shard_map/ppermute | solution.py:195
  6.1 0.7 %collective-permute-start.2 = (bf16[32,2,32,128]{3,2,1,0:T(8,128)(2,1)}, bf16[32,2,32,128]{3,2,1,0:T(8,128)(2,1)S(1)}, u32[]{:S(2)}, u32[]{:S(2)}) collective-permute-start(bf16[32,2,32,128]{3,2,1,0:T(8,128)(2,1)} %get-tuple-element.20), channel_id=1, source_target_pairs={{0,3},{1,2},{2,1},{3,0},{4,7},{5,6},{6,5},{7,4},{8,11},{9,10},{10,... | collective-permute-start | bytes 1572872 | tf_op jit(solution)/shard_map/ppermute | solution.py:194
  6.7 1.6 %collective-permute-start = (bf16[36,16,128]{2,1,0:T(8,128)(2,1)}, bf16[36,16,128]{2,1,0:T(8,128)(2,1)S(1)}, u32[]{:S(2)}, u32[]{:S(2)}) collective-permute-start(bf16[36,16,128]{2,1,0:T(8,128)(2,1)} %get-tuple-element.15), channel_id=1, source_target_pairs={{0,4},{4,8},{8,12},{12,0},{1,5},{5,9},{9,13},{13,1},{2,6},{6,10},{... | collective-permute-start | bytes 442376 | tf_op jit(solution)/shard_map/ppermute | solution.py:196
  8.3 2.2 %collective-permute-start.1 = (bf16[36,16,128]{2,1,0:T(8,128)(2,1)}, bf16[36,16,128]{2,1,0:T(8,128)(2,1)S(1)}, u32[]{:S(2)}, u32[]{:S(2)}) collective-permute-start(bf16[36,16,128]{2,1,0:T(8,128)(2,1)} %get-tuple-element.16), channel_id=1, source_target_pairs={{4,0},{8,4},{12,8},{0,12},{5,1},{9,5},{13,9},{1,13},{6,2},{10,6},{... | collective-permute-start | bytes 442376 | tf_op jit(solution)/shard_map/ppermute | solution.py:197
  10.6 0.0 copy-done
  10.6 2.4 %resident_slopes.1 = (f32[4,2,3,3,192,128]{5,4,3,2,1,0:T(8,128)S(1)}, f32[4,2,3,192,128]{4,3,2,1,0:T(8,128)S(1)}, f32[4,2,4,192,128]{4,3,2,1,0:T(8,128)S(1)}) custom-call(bf16[32,192,128]{2,1,0:T(8,128)(2,1)S(1)} %bitcast.21), custom_call_target="tpu_custom_call" | custom-call | tf_op jit(solution)/shard_map/resident_slopes/pallas_call | solution.py:349
  12.9 0.0 copy-done.1
  12.9 0.0 copy-done.2
  13.0 0.0 copy-start.3
  13.0 6.0 %resident.1.whole_ref = f32[32,192,128]{2,1,0:T(8,128)S(1)} custom-call(bf16[3,192,128]{2,1,0:T(8,128)(2,1)S(1)} %bitcast.35, bf16[12,192,128]{2,1,0:T(8,128)(2,1)S(1)} %bitcast.27, f32[4,2,3,3,192,128]{5,4,3,2,1,0:T(8,128)S(1)} %get-tuple-element.17.grads, f32[4,2,3,192,128]{4,3,2,1,0:T(8,128)S(1)} %get-tuple-element.18.plain, ...), custom_call_target="tpu_custom_call" | custom-call | tf_op jit(solution)/shard_map/resident/pallas_call | solution.py:356
  18.9 0.0 collective-permute-done.xb_ref
  18.9 0.0 collective-permute-done.1.xa_ref
  19.0 0.0 copy-done.3
  19.0 1.8 %edges.1._.edged_ref = f32[32,192,128]{2,1,0:T(8,128)S(1)} custom-call(s32[192,128]{1,0:T(8,128)S(1)} %bitcast.40, bf16[32,192,128]{2,1,0:T(8,128)(2,1)S(1)} %bitcast.22, bf16[3,192,128]{2,1,0:T(8,128)(2,1)S(1)} %bitcast.36, bf16[12,192,128]{2,1,0:T(8,128)(2,1)S(1)} %bitcast.28, bf16[36,16,128]{2,1,0:T(8,128)(2,1)S(1)} %collective-permute-done.xb_ref, ...), custom_call_target="tpu_custom_call" | custom-call | tf_op jit(solution)/shard_map/edges/pallas_call | solution.py:445
  20.7 0.0 copy-start.4
  20.7 0.0 collective-permute-done.2.first_ref
  20.8 0.0 collective-permute-done.3.rest_0_
  20.8 0.1 pack_near.1
  20.9 0.5 %collective-permute-start.4 = (bf16[59,2,32,128]{3,2,1,0:T(8,128)(2,1)S(1)}, bf16[59,2,32,128]{3,2,1,0:T(8,128)(2,1)S(1)}, u32[]{:S(2)}, u32[]{:S(2)}) collective-permute-start(bf16[59,2,32,128]{3,2,1,0:T(8,128)(2,1)S(1)} %pack_near.1), channel_id=1, source_target_pairs={{0,1},{1,0},{2,3},{3,2},{4,5},{5,4},{6,7},{7,6},{8,9},{9,8},{10,11... | collective-permute-start | bytes 2899976 | tf_op jit(solution)/shard_map/ppermute | solution.py:511
  21.4 0.5 %collective-permute-start.6 = (bf16[1056,128]{1,0:T(8,128)(2,1)S(1)}, bf16[1056,128]{1,0:T(8,128)(2,1)S(1)}, u32[]{:S(2)}, u32[]{:S(2)}) collective-permute-start(bf16[1056,128]{1,0:T(8,128)(2,1)S(1)} %pack_relay.1.rest_1_), channel_id=1, source_target_pairs={{0,16},{16,0},{1,17},{17,1},{2,18},{18,2},{3,19},{19,3},{4,20},{20... | collective-permute-start | bytes 811016 | tf_op jit(solution)/shard_map/ppermute | solution.py:493
  21.9 0.0 copy-done.4
  21.9 0.9 %collective-permute-start.5 = (bf16[15,2,32,128]{3,2,1,0:T(8,128)(2,1)S(1)}, bf16[15,2,32,128]{3,2,1,0:T(8,128)(2,1)S(1)}, u32[]{:S(2)}, u32[]{:S(2)}) collective-permute-start(bf16[15,2,32,128]{3,2,1,0:T(8,128)(2,1)S(1)} %copy-done.4), channel_id=1, source_target_pairs={{0,3},{1,2},{2,1},{3,0},{4,7},{5,6},{6,5},{7,4},{8,11},{9,10},{10,... | collective-permute-start | bytes 737288 | tf_op jit(solution)/shard_map/ppermute | solution.py:198
  22.8 0.7 %collective-permute-done.4.near_ref = bf16[59,2,32,128]{3,2,1,0:T(8,128)(2,1)S(1)} collective-permute-done((bf16[59,2,32,128]{3,2,1,0:T(8,128)(2,1)S(1)}, bf16[59,2,32,128]{3,2,1,0:T(8,128)(2,1)S(1)}, u32[]{:S(2)}, u32[]{:S(2)}) %collective-permute-start.4) | collective-permute-done | bytes 966688 | tf_op jit(solution)/shard_map/ppermute | solution.py:511
  23.6 5.4 %neighbours.1 = (f32[32,192,128]{2,1,0:T(8,128)}, f32[32,192,128]{2,1,0:T(8,128)S(1)}) custom-call(bf16[32,192,128]{2,1,0:T(8,128)(2,1)S(1)} %bitcast.24, bf16[3,192,128]{2,1,0:T(8,128)(2,1)S(1)} %bitcast.38, bf16[12,192,128]{2,1,0:T(8,128)(2,1)S(1)} %bitcast.30, bf16[36,16,128]{2,1,0:T(8,128)(2,1)S(1)} %collective-permute-done.xb_ref, ...), custom_call_target="tpu_custom_call" | custom-call | tf_op jit(solution)/shard_map/neighbours/pallas_call | solution.py:695
  29.0 0.9 %collective-permute-done.5.second_ref = bf16[15,2,32,128]{3,2,1,0:T(8,128)(2,1)S(1)} collective-permute-done((bf16[15,2,32,128]{3,2,1,0:T(8,128)(2,1)S(1)}, bf16[15,2,32,128]{3,2,1,0:T(8,128)(2,1)S(1)}, u32[]{:S(2)}, u32[]{:S(2)}) %collective-permute-start.5) | collective-permute-done | bytes 245792 | tf_op jit(solution)/shard_map/ppermute | solution.py:198
  29.9 0.0 collective-permute-done.6.rest_0_
  29.9 2.1 %finish.1 = f32[32,192,128]{2,1,0:T(8,128)} custom-call(bf16[32,192,128]{2,1,0:T(8,128)(2,1)S(1)} %bitcast.25, bf16[3,192,128]{2,1,0:T(8,128)(2,1)S(1)} %bitcast.39, bf16[12,192,128]{2,1,0:T(8,128)(2,1)S(1)} %bitcast.31, f32[32,192,128]{2,1,0:T(8,128)S(1)} %get-tuple-element.22.inner_ref, ...), custom_call_target="tpu_custom_call", output_to_operand_aliasing={{}: (5, {})} | custom-call | tf_op jit(solution)/shard_map/finish/pallas_call | solution.py:802
  (1 shorter events, 0.0 us)
Async XLA Ops:
  0.0 12.9 %copy-start.1 = (bf16[2,2,3,32,6,128]{5,3,4,2,1,0:T(8,128)(2,1)S(1)}, bf16[2,2,3,32,6,128]{5,3,4,2,1,0:T(8,128)(2,1)}, u32[]{:S(2)}) copy-start(bf16[2,2,3,32,6,128]{5,3,4,2,1,0:T(8,128)(2,1)} %param.6) | copy-start | bytes 1769476
  0.0 12.9 %copy-start.2 = (bf16[3,32,6,128]{3,1,2,0:T(8,128)(2,1)S(1)}, bf16[3,32,6,128]{3,1,2,0:T(8,128)(2,1)}, u32[]{:S(2)}) copy-start(bf16[3,32,6,128]{3,1,2,0:T(8,128)(2,1)} %param.5) | copy-start | bytes 442372
  0.0 10.5 %copy-start = (bf16[4,2,4,32,6,128]{5,3,4,2,1,0:T(8,128)(2,1)S(1)}, bf16[4,2,4,32,6,128]{5,3,4,2,1,0:T(8,128)(2,1)}, u32[]{:S(2)}) copy-start(bf16[4,2,4,32,6,128]{5,3,4,2,1,0:T(8,128)(2,1)} %param.4) | copy-start | bytes 4718596
  3.0 17.8 %collective-permute-start.3 = (bf16[12,6,32,128]{3,2,1,0:T(8,128)(2,1)}, bf16[12,6,32,128]{3,2,1,0:T(8,128)(2,1)S(1)}, u32[]{:S(2)}, u32[]{:S(2)}) collective-permute-start(bf16[12,6,32,128]{3,2,1,0:T(8,128)(2,1)} %get-tuple-element.21), channel_id=1, source_target_pairs={{0,16},{16,0},{1,17},{17,1},{2,18},{18,2},{3,19},{19,3},{4,20},{20... | collective-permute-start | bytes 1769480 | tf_op jit(solution)/shard_map/ppermute | solution.py:195
  6.1 14.7 %collective-permute-start.2 = (bf16[32,2,32,128]{3,2,1,0:T(8,128)(2,1)}, bf16[32,2,32,128]{3,2,1,0:T(8,128)(2,1)S(1)}, u32[]{:S(2)}, u32[]{:S(2)}) collective-permute-start(bf16[32,2,32,128]{3,2,1,0:T(8,128)(2,1)} %get-tuple-element.20), channel_id=1, source_target_pairs={{0,3},{1,2},{2,1},{3,0},{4,7},{5,6},{6,5},{7,4},{8,11},{9,10},{10,... | collective-permute-start | bytes 1572872 | tf_op jit(solution)/shard_map/ppermute | solution.py:194
  6.7 12.2 %collective-permute-start = (bf16[36,16,128]{2,1,0:T(8,128)(2,1)}, bf16[36,16,128]{2,1,0:T(8,128)(2,1)S(1)}, u32[]{:S(2)}, u32[]{:S(2)}) collective-permute-start(bf16[36,16,128]{2,1,0:T(8,128)(2,1)} %get-tuple-element.15), channel_id=1, source_target_pairs={{0,4},{4,8},{8,12},{12,0},{1,5},{5,9},{9,13},{13,1},{2,6},{6,10},{... | collective-permute-start | bytes 442376 | tf_op jit(solution)/shard_map/ppermute | solution.py:196
  8.3 10.6 %collective-permute-start.1 = (bf16[36,16,128]{2,1,0:T(8,128)(2,1)}, bf16[36,16,128]{2,1,0:T(8,128)(2,1)S(1)}, u32[]{:S(2)}, u32[]{:S(2)}) collective-permute-start(bf16[36,16,128]{2,1,0:T(8,128)(2,1)} %get-tuple-element.16), channel_id=1, source_target_pairs={{4,0},{8,4},{12,8},{0,12},{5,1},{9,5},{13,9},{1,13},{6,2},{10,6},{... | collective-permute-start | bytes 442376 | tf_op jit(solution)/shard_map/ppermute | solution.py:197
  13.0 6.0 %copy-start.3 = (s32[32,6,128]{2,0,1:T(8,128)S(1)}, s32[32,6,128]{2,0,1:T(8,128)}, u32[]{:S(2)}) copy-start(s32[32,6,128]{2,0,1:T(8,128)} %param.7) | copy-start | bytes 294916
  20.7 1.2 %copy-start.4 = (bf16[15,2,32,128]{3,2,1,0:T(8,128)(2,1)S(1)}, bf16[15,2,32,128]{3,2,1,0:T(8,128)(2,1)}, u32[]{:S(2)}) copy-start(bf16[15,2,32,128]{3,2,1,0:T(8,128)(2,1)} %get-tuple-element.23) | copy-start | bytes 737284
  20.9 2.7 %collective-permute-start.4 = (bf16[59,2,32,128]{3,2,1,0:T(8,128)(2,1)S(1)}, bf16[59,2,32,128]{3,2,1,0:T(8,128)(2,1)S(1)}, u32[]{:S(2)}, u32[]{:S(2)}) collective-permute-start(bf16[59,2,32,128]{3,2,1,0:T(8,128)(2,1)S(1)} %pack_near.1), channel_id=1, source_target_pairs={{0,1},{1,0},{2,3},{3,2},{4,5},{5,4},{6,7},{7,6},{8,9},{9,8},{10,11... | collective-permute-start | bytes 2899976 | tf_op jit(solution)/shard_map/ppermute | solution.py:511
  21.4 8.5 %collective-permute-start.6 = (bf16[1056,128]{1,0:T(8,128)(2,1)S(1)}, bf16[1056,128]{1,0:T(8,128)(2,1)S(1)}, u32[]{:S(2)}, u32[]{:S(2)}) collective-permute-start(bf16[1056,128]{1,0:T(8,128)(2,1)S(1)} %pack_relay.1.rest_1_), channel_id=1, source_target_pairs={{0,16},{16,0},{1,17},{17,1},{2,18},{18,2},{3,19},{19,3},{4,20},{20... | collective-permute-start | bytes 811016 | tf_op jit(solution)/shard_map/ppermute | solution.py:493
  21.9 8.0 %collective-permute-start.5 = (bf16[15,2,32,128]{3,2,1,0:T(8,128)(2,1)S(1)}, bf16[15,2,32,128]{3,2,1,0:T(8,128)(2,1)S(1)}, u32[]{:S(2)}, u32[]{:S(2)}) collective-permute-start(bf16[15,2,32,128]{3,2,1,0:T(8,128)(2,1)S(1)} %copy-done.4), channel_id=1, source_target_pairs={{0,3},{1,2},{2,1},{3,0},{4,7},{5,6},{6,5},{7,4},{8,11},{9,10},{10,... | collective-permute-start | bytes 737288 | tf_op jit(solution)/shard_map/ppermute | solution.py:198

commit v8 on v7

--- a/solution.py
+++ b/solution.py
@@ -375,7 +375,7 @@
         dz, dx = to_z - (row >> 3), to_x - (row & 7) - jnp.where(last, nx - 8, 0)
         return jnp.concatenate([jnp.where(dz == 0, taps(dx, table), 0.0)[:, own:] for table in tables], axis=0).astype(bf16)
 
-    def add_edges(mask_ref, pert_ref, mean_ref, mode_ref, xb_ref, xa_ref, whole_ref, out_ref, vecs, lins, bends):
+    def add_edges(pert_ref, mean_ref, mode_ref, xb_ref, xa_ref, _, out_ref, vecs, lins, bends):
         taps_of = edge_taps((FIRST, SECOND))
 
         def bent(fields, lap):
@@ -405,20 +405,10 @@
             for n, ent in enumerate(entries(t, p, q, r, s_)):
                 bends[c, n] = ent
 
-        for z in range(nz):
-            rows = slice(z * nx, (z + 1) * nx)
-            solid = PENALTY * mask_ref[rows].astype(f32)
-            for f in range(n_pert):
-                if f % 4 < 3:
-                    out_ref[f, rows] = whole_ref[f, rows] + solid * pert_ref[f, rows].astype(f32)
-                else:
-                    out_ref[f, rows] = whole_ref[f, rows]
-
         def layer_ends(z, carry):
             for end in range(2):
                 strip = pl.ds(pl.multiple_of(z * nx + end * (nx // 2), 16), 16)
                 keep = slice(8 * end, 8 * end + 8)
-                rows = pl.ds(pl.multiple_of(z * nx + end * (nx - 8), 8), 8)
                 mine = pl.ds(pl.multiple_of((end * nz + z) * 8, 8), 8)
 
                 def read(ref, f):
@@ -435,8 +425,7 @@
                         acc = [(vecs[j, 0, 0, mine], vecs[j, 1, 0, mine]) for j in range(4)]
                     for k, parts in enumerate(harmonics_of(acc, 1.0 / 24.0)):
                         for i in range(2):
-                            at = k * 8 + 4 * i + c
-                            out_ref[at, rows] = out_ref[at, rows] + parts[i]
+                            out_ref[k * 8 + 4 * i + c, mine] = parts[i]
             return carry
 
         lax.fori_loop(0, nz, layer_ends, 0)
@@ -444,14 +433,15 @@
     with jax.named_scope("edges"):
         edged = pl.pallas_call(
             add_edges,
-            out_shape=jax.ShapeDtypeStruct((n_pert, own, ny), f32),
+            out_shape=jax.ShapeDtypeStruct((n_pert, ends, ny), f32),
+            in_specs=[VMEM] * 5 + [ANY],
             scratch_shapes=[
                 pltpu.VMEM((4, 2, 3, ends, ny), f32),
                 pltpu.VMEM((4, 2, 3, ends, ny), f32),
                 pltpu.VMEM((3, 8, ends, ny), f32),
             ],
             compiler_params=roomy,
-        )(mask, flat(pert), flat(mean), flat(mode), xb_got, xa_got, whole)
+        )(flat(pert), flat(mean), flat(mode), xb_got, xa_got, whole)
 
     faces_deep = n_nb * 2 * nx
     nb_tiles = 3 * n_nb // 4
@@ -617,7 +607,7 @@
 
         lax.fori_loop(0, nx // 16, chunk_work, 0)
 
-    def neighbours(pert_ref, mean_ref, mode_ref, xb_ref, xa_ref, edged_ref, first_ref, near_ref, *rest):
+    def neighbours(mask_ref, pert_ref, mean_ref, mode_ref, xb_ref, xa_ref, whole_ref, edged_ref, first_ref, near_ref, *rest):
         nb_refs = rest[:sides]
         out_any, out_ref, grads, plain, stencil_ref, walls_ref, sems = rest[-7:]
         row, column = iotas(own, own + 2 * HALO_X)
@@ -646,7 +636,18 @@
             for f in range(0, n_nb, 2):
                 slopes(n_modes + s * n_nb + f, [nb_refs[s][f], nb_refs[s][f + 1]], None)
 
-        out_ref[...] = edged_ref[...]
+        for z in range(nz):
+            rows = slice(z * nx, (z + 1) * nx)
+            solid = PENALTY * mask_ref[rows].astype(f32)
+            for f in range(n_pert):
+                if f % 4 < 3:
+                    out_ref[f, rows] = whole_ref[f, rows] + solid * pert_ref[f, rows].astype(f32)
+                else:
+                    out_ref[f, rows] = whole_ref[f, rows]
+            for end in range(2):
+                rows = slice(z * nx + end * (nx - 8), z * nx + end * (nx - 8) + 8)
+                mine = slice((end * nz + z) * 8, (end * nz + z + 1) * 8)
+                out_ref[:, rows] = out_ref[:, rows] + edged_ref[:, mine]
 
         def work(pairs):
             def block(b, carry):
@@ -704,7 +705,7 @@
                 pltpu.SemaphoreType.DMA((nz - 2,)),
             ],
             compiler_params=roomy,
-        )(flat(pert), flat(mean), flat(mode), xb_got, xa_got, edged, first_got, near_got, *[flat(b) for b in nb_got])
+        )(mask, flat(pert), flat(mean), flat(mode), xb_got, xa_got, whole, edged, first_got, near_got, *[flat(b) for b in nb_got])
 
     n_keys = n_pert // 2 if swap else n_pert
 
@@ -749,30 +750,6 @@
         def end_rows(z, end):
             return pl.ds(pl.multiple_of(z * nx + end * (nx - 8), 8), 8)
 
-        first_row = pl.multiple_of(jnp.where(face_place(True, 0)[0], 0, (nz - 2) * nx), nx)
-        done[...] = inner_ref[:, pl.ds(first_row, 2 * nx)]
-        cross_layer = first_row // nx
-
-        def cross_edges(pairs):
-            def at_layer(j, carry):
-                for end in range(2):
-                    rows = end_rows(j, end)
-
-                    def add(k, part, value):
-                        done[k * 8 + part, rows] = done[k * 8 + part, rows] + value
-
-                    edge_terms(pairs, cross_layer + j, end, add)
-                return carry
-
-            lax.fori_loop(0, 2, at_layer, 0)
-
-        on_sides(cross_edges)
-        for step in range(2):
-            faces(done, mean_ref, mode_ref, pert_ref, nb_refs, None, second_ref, None, relay_refs, step, cross_layer)
-            layer = face_place(True, step)[1]
-            here = pl.ds(pl.multiple_of((layer - cross_layer) * nx, nx), nx)
-            send(done.at[:, here], out_any.at[:, pl.ds(pl.multiple_of(layer * nx, nx), nx)])
-
         def other_edges(pairs):
             lowest = min(p[0] for p in pairs) * 8 if swap else 0
 
@@ -795,6 +772,30 @@
         for j in range(nz - 2):
             for end in range(2):
                 send(fringe.at[end, :, j], out_any.at[pl.ds(keys, n_keys), end_rows(inner_layer + j, end)])
+
+        first_row = pl.multiple_of(jnp.where(face_place(True, 0)[0], 0, (nz - 2) * nx), nx)
+        done[...] = inner_ref[:, pl.ds(first_row, 2 * nx)]
+        cross_layer = first_row // nx
+
+        def cross_edges(pairs):
+            def at_layer(j, carry):
+                for end in range(2):
+                    rows = end_rows(j, end)
+
+                    def add(k, part, value):
+                        done[k * 8 + part, rows] = done[k * 8 + part, rows] + value
+
+                    edge_terms(pairs, cross_layer + j, end, add)
+                return carry
+
+            lax.fori_loop(0, 2, at_layer, 0)
+
+        on_sides(cross_edges)
+        for step in range(2):
+            faces(done, mean_ref, mode_ref, pert_ref, nb_refs, None, second_ref, None, relay_refs, step, cross_layer)
+            layer = face_place(True, step)[1]
+            here = pl.ds(pl.multiple_of((layer - cross_layer) * nx, nx), nx)
+            send(done.at[:, here], out_any.at[:, pl.ds(pl.multiple_of(layer * nx, nx), nx)])
         for copy in sends:
             copy.wait()
 

time: 32.1 us -> 31.8 us (level)
  waiting for transfers between devices: 1.63 us -> 1.15 us
    ppermute x1, waiting for transfers between devices: 0.75 us -> 0.37 us  [shards(): near_got = lax.ppermute(near, 'gz', near_pairs)]
    ppermute x1, waiting for transfers between devices: 0.86 us -> 0.51 us  [shards(): second_got = lax.ppermute(second, 'gz', cross_pairs)]
    ppermute x1, starting transfers between devices: 0.91 us -> 1.26 us  [shards(): second_got = lax.ppermute(second, 'gz', cross_pairs)]
    pallas_call x1, Pallas kernels: 5.42 us -> 5.76 us  [shards(): pl.pallas_call(neighbours, out_shape=(jax.ShapeDtypeStruct((n_pert, own,...]
  transfers between devices with their start and end apart: 7 -> 7, of which waited for: 2 -> 4; matrix products, arithmetic and copies ran while one was open for 0% -> 0% of each run, Pallas kernels for 49% -> 49%
where the time goes in v8:
time: 31.8 us; the launch traced here: 31.7 us
  Pallas kernels  20.6 us (65%)
  starting transfers between devices  9.74 us (31%)
  waiting for transfers between devices  1.15 us (4%)
    pallas_call x1, Pallas kernels, shards(): pl.pallas_call(resident, out_shape=jax.ShapeDtypeStruct((n_pert, own, ny)...  5.82 us
    pallas_call x1, Pallas kernels, shards(): pl.pallas_call(neighbours, out_shape=(jax.ShapeDtypeStruct((n_pert, own,...  5.76 us
    ppermute x1, starting transfers between devices, shards(): nb_got = [lax.ppermute(b, 'harm', p) for b, p in zip(nb_send, harm_perms)]  3.04 us
    pallas_call x1, Pallas kernels, shards(): pl.pallas_call(pack, out_shape=(face(n_pert), face(n_base), edge, edge) +...  3.02 us
    pallas_call x1, Pallas kernels, shards(): pl.pallas_call(resident_slopes, out_shape=tuple((jax.ShapeDtypeStruct(n +...  2.38 us
    ppermute x1, starting transfers between devices, shards(): xa_got = lax.ppermute(edge_lo, 'gx', down_x)  2.25 us
    pallas_call x1, Pallas kernels, shards(): pl.pallas_call(finish, out_shape=jax.ShapeDtypeStruct((n_pert, own, ny),...  2.12 us
    ppermute x1, starting transfers between devices, shards(): xb_got = lax.ppermute(edge_hi, 'gx', up_x)  1.58 us
  transfers between devices with their start and end apart: 7, of which 4 were waited for; matrix products, arithmetic and copies ran while one was open for 0% of the time, Pallas kernels for 49%

profile of v8, /device:TPU:0, one launch (start us, length us, event | category | flops | bytes accessed | tf_op | source)
XLA Modules:
  0.0 31.7 jit_solution(291359863115476217)
XLA Ops:
  0.0 0.0 copy-start
  0.0 0.0 copy-start.1
  0.0 0.0 copy-start.2
  0.0 3.0 %pack.1 = (bf16[32,2,32,128]{3,2,1,0:T(8,128)(2,1)}, bf16[15,2,32,128]{3,2,1,0:T(8,128)(2,1)}, bf16[36,16,128]{2,1,0:T(8,128)(2,1)}, bf16[36,16,128]{2,1,0:T(8,128)(2,1)}, bf16[12,6,32,128]{3,2,1,0:T(8,128)(2,1)}) custom-call(bf16[32,6,32,128]{3,2,1,0:T(8,128)(2,1)} %bitcast.20, bf16[3,6,32,128]{3,2,1,0:T(8,128)(2,1)} %bitcast.34, ...), custom_call_target="tpu_custom_call" | custom-call | tf_op jit(solution)/shard_map/pack/pallas_call | solution.py:178
  3.0 3.0 %collective-permute-start.3 = (bf16[12,6,32,128]{3,2,1,0:T(8,128)(2,1)}, bf16[12,6,32,128]{3,2,1,0:T(8,128)(2,1)S(1)}, u32[]{:S(2)}, u32[]{:S(2)}) collective-permute-start(bf16[12,6,32,128]{3,2,1,0:T(8,128)(2,1)} %get-tuple-element.21), channel_id=1, source_target_pairs={{0,16},{16,0},{1,17},{17,1},{2,18},{18,2},{3,19},{19,3},{4,20},{20... | collective-permute-start | bytes 1769480 | tf_op jit(solution)/shard_map/ppermute | solution.py:195
  6.1 0.7 %collective-permute-start.2 = (bf16[32,2,32,128]{3,2,1,0:T(8,128)(2,1)}, bf16[32,2,32,128]{3,2,1,0:T(8,128)(2,1)S(1)}, u32[]{:S(2)}, u32[]{:S(2)}) collective-permute-start(bf16[32,2,32,128]{3,2,1,0:T(8,128)(2,1)} %get-tuple-element.20), channel_id=1, source_target_pairs={{0,3},{1,2},{2,1},{3,0},{4,7},{5,6},{6,5},{7,4},{8,11},{9,10},{10,... | collective-permute-start | bytes 1572872 | tf_op jit(solution)/shard_map/ppermute | solution.py:194
  6.7 1.6 %collective-permute-start = (bf16[36,16,128]{2,1,0:T(8,128)(2,1)}, bf16[36,16,128]{2,1,0:T(8,128)(2,1)S(1)}, u32[]{:S(2)}, u32[]{:S(2)}) collective-permute-start(bf16[36,16,128]{2,1,0:T(8,128)(2,1)} %get-tuple-element.15), channel_id=1, source_target_pairs={{0,4},{4,8},{8,12},{12,0},{1,5},{5,9},{9,13},{13,1},{2,6},{6,10},{... | collective-permute-start | bytes 442376 | tf_op jit(solution)/shard_map/ppermute | solution.py:196
  8.3 2.2 %collective-permute-start.1 = (bf16[36,16,128]{2,1,0:T(8,128)(2,1)}, bf16[36,16,128]{2,1,0:T(8,128)(2,1)S(1)}, u32[]{:S(2)}, u32[]{:S(2)}) collective-permute-start(bf16[36,16,128]{2,1,0:T(8,128)(2,1)} %get-tuple-element.16), channel_id=1, source_target_pairs={{4,0},{8,4},{12,8},{0,12},{5,1},{9,5},{13,9},{1,13},{6,2},{10,6},{... | collective-permute-start | bytes 442376 | tf_op jit(solution)/shard_map/ppermute | solution.py:197
  10.6 0.0 copy-done
  10.6 2.4 %resident_slopes.1 = (f32[4,2,3,3,192,128]{5,4,3,2,1,0:T(8,128)S(1)}, f32[4,2,3,192,128]{4,3,2,1,0:T(8,128)S(1)}, f32[4,2,4,192,128]{4,3,2,1,0:T(8,128)S(1)}) custom-call(bf16[32,192,128]{2,1,0:T(8,128)(2,1)S(1)} %bitcast.21), custom_call_target="tpu_custom_call" | custom-call | tf_op jit(solution)/shard_map/resident_slopes/pallas_call | solution.py:349
  12.9 0.0 copy-done.1
  12.9 0.0 copy-done.2
  13.0 5.8 %resident.1._.whole_ref = f32[32,192,128]{2,1,0:T(8,128)S(1)} custom-call(bf16[3,192,128]{2,1,0:T(8,128)(2,1)S(1)} %bitcast.35, bf16[12,192,128]{2,1,0:T(8,128)(2,1)S(1)} %bitcast.27, f32[4,2,3,3,192,128]{5,4,3,2,1,0:T(8,128)S(1)} %get-tuple-element.17.grads, f32[4,2,3,192,128]{4,3,2,1,0:T(8,128)S(1)} %get-tuple-element.18.plain, ...), custom_call_target="tpu_custom_call" | custom-call | tf_op jit(solution)/shard_map/resident/pallas_call | solution.py:356
  18.8 0.0 collective-permute-done.xb_ref
  18.8 0.0 collective-permute-done.1.xa_ref
  18.8 1.4 %edges.1._.edged_ref = f32[32,96,128]{2,1,0:T(8,128)S(1)} custom-call(bf16[32,192,128]{2,1,0:T(8,128)(2,1)S(1)} %bitcast.22, bf16[3,192,128]{2,1,0:T(8,128)(2,1)S(1)} %bitcast.36, bf16[12,192,128]{2,1,0:T(8,128)(2,1)S(1)} %bitcast.28, bf16[36,16,128]{2,1,0:T(8,128)(2,1)S(1)} %collective-permute-done.xb_ref, ...), custom_call_target="tpu_custom_call" | custom-call | tf_op jit(solution)/shard_map/edges/pallas_call | solution.py:434
  20.3 0.0 copy-start.4
  20.3 0.0 copy-start.3
  20.3 0.2 collective-permute-done.2.first_ref
  20.5 0.0 collective-permute-done.3.rest_0_
  20.5 0.1 pack_near.1
  20.6 0.4 %collective-permute-start.4 = (bf16[59,2,32,128]{3,2,1,0:T(8,128)(2,1)S(1)}, bf16[59,2,32,128]{3,2,1,0:T(8,128)(2,1)S(1)}, u32[]{:S(2)}, u32[]{:S(2)}) collective-permute-start(bf16[59,2,32,128]{3,2,1,0:T(8,128)(2,1)S(1)} %pack_near.1), channel_id=1, source_target_pairs={{0,1},{1,0},{2,3},{3,2},{4,5},{5,4},{6,7},{7,6},{8,9},{9,8},{10,11... | collective-permute-start | bytes 2899976 | tf_op jit(solution)/shard_map/ppermute | solution.py:501
  21.0 0.6 %collective-permute-start.6 = (bf16[1056,128]{1,0:T(8,128)(2,1)S(1)}, bf16[1056,128]{1,0:T(8,128)(2,1)S(1)}, u32[]{:S(2)}, u32[]{:S(2)}) collective-permute-start(bf16[1056,128]{1,0:T(8,128)(2,1)S(1)} %pack_relay.1.rest_1_), channel_id=1, source_target_pairs={{0,16},{16,0},{1,17},{17,1},{2,18},{18,2},{3,19},{19,3},{4,20},{20... | collective-permute-start | bytes 811016 | tf_op jit(solution)/shard_map/ppermute | solution.py:483
  21.6 0.0 copy-done.4
  21.6 1.3 %collective-permute-start.5 = (bf16[15,2,32,128]{3,2,1,0:T(8,128)(2,1)S(1)}, bf16[15,2,32,128]{3,2,1,0:T(8,128)(2,1)S(1)}, u32[]{:S(2)}, u32[]{:S(2)}) collective-permute-start(bf16[15,2,32,128]{3,2,1,0:T(8,128)(2,1)S(1)} %copy-done.4), channel_id=1, source_target_pairs={{0,3},{1,2},{2,1},{3,0},{4,7},{5,6},{6,5},{7,4},{8,11},{9,10},{10,... | collective-permute-start | bytes 737288 | tf_op jit(solution)/shard_map/ppermute | solution.py:198
  22.8 0.4 %collective-permute-done.4.near_ref = bf16[59,2,32,128]{3,2,1,0:T(8,128)(2,1)S(1)} collective-permute-done((bf16[59,2,32,128]{3,2,1,0:T(8,128)(2,1)S(1)}, bf16[59,2,32,128]{3,2,1,0:T(8,128)(2,1)S(1)}, u32[]{:S(2)}, u32[]{:S(2)}) %collective-permute-start.4) | collective-permute-done | bytes 966688 | tf_op jit(solution)/shard_map/ppermute | solution.py:501
  23.2 0.0 copy-done.3
  23.2 5.8 %neighbours.1 = (f32[32,192,128]{2,1,0:T(8,128)}, f32[32,192,128]{2,1,0:T(8,128)S(1)}) custom-call(s32[192,128]{1,0:T(8,128)S(1)} %bitcast.40, bf16[32,192,128]{2,1,0:T(8,128)(2,1)S(1)} %bitcast.24, bf16[3,192,128]{2,1,0:T(8,128)(2,1)S(1)} %bitcast.38, bf16[12,192,128]{2,1,0:T(8,128)(2,1)S(1)} %bitcast.30, ...), custom_call_target="tpu_custom_call" | custom-call | tf_op jit(solution)/shard_map/neighbours/pallas_call | solution.py:696
  29.0 0.5 %collective-permute-done.5.second_ref = bf16[15,2,32,128]{3,2,1,0:T(8,128)(2,1)S(1)} collective-permute-done((bf16[15,2,32,128]{3,2,1,0:T(8,128)(2,1)S(1)}, bf16[15,2,32,128]{3,2,1,0:T(8,128)(2,1)S(1)}, u32[]{:S(2)}, u32[]{:S(2)}) %collective-permute-start.5) | collective-permute-done | bytes 245792 | tf_op jit(solution)/shard_map/ppermute | solution.py:198
  29.5 0.1 collective-permute-done.6.rest_0_
  29.6 2.1 %finish.1 = f32[32,192,128]{2,1,0:T(8,128)} custom-call(bf16[32,192,128]{2,1,0:T(8,128)(2,1)S(1)} %bitcast.25, bf16[3,192,128]{2,1,0:T(8,128)(2,1)S(1)} %bitcast.39, bf16[12,192,128]{2,1,0:T(8,128)(2,1)S(1)} %bitcast.31, f32[32,192,128]{2,1,0:T(8,128)S(1)} %get-tuple-element.22.inner_ref, ...), custom_call_target="tpu_custom_call", output_to_operand_aliasing={{}: (5, {})} | custom-call | tf_op jit(solution)/shard_map/finish/pallas_call | solution.py:803
  (1 shorter events, 0.0 us)
Async XLA Ops:
  0.0 10.6 %copy-start = (bf16[4,2,4,32,6,128]{5,3,4,2,1,0:T(8,128)(2,1)S(1)}, bf16[4,2,4,32,6,128]{5,3,4,2,1,0:T(8,128)(2,1)}, u32[]{:S(2)}) copy-start(bf16[4,2,4,32,6,128]{5,3,4,2,1,0:T(8,128)(2,1)} %param.4) | copy-start | bytes 4718596
  0.0 12.9 %copy-start.1 = (bf16[2,2,3,32,6,128]{5,3,4,2,1,0:T(8,128)(2,1)S(1)}, bf16[2,2,3,32,6,128]{5,3,4,2,1,0:T(8,128)(2,1)}, u32[]{:S(2)}) copy-start(bf16[2,2,3,32,6,128]{5,3,4,2,1,0:T(8,128)(2,1)} %param.6) | copy-start | bytes 1769476
  0.0 12.9 %copy-start.2 = (bf16[3,32,6,128]{3,1,2,0:T(8,128)(2,1)S(1)}, bf16[3,32,6,128]{3,1,2,0:T(8,128)(2,1)}, u32[]{:S(2)}) copy-start(bf16[3,32,6,128]{3,1,2,0:T(8,128)(2,1)} %param.5) | copy-start | bytes 442372
  3.0 17.5 %collective-permute-start.3 = (bf16[12,6,32,128]{3,2,1,0:T(8,128)(2,1)}, bf16[12,6,32,128]{3,2,1,0:T(8,128)(2,1)S(1)}, u32[]{:S(2)}, u32[]{:S(2)}) collective-permute-start(bf16[12,6,32,128]{3,2,1,0:T(8,128)(2,1)} %get-tuple-element.21), channel_id=1, source_target_pairs={{0,16},{16,0},{1,17},{17,1},{2,18},{18,2},{3,19},{19,3},{4,20},{20... | collective-permute-start | bytes 1769480 | tf_op jit(solution)/shard_map/ppermute | solution.py:195
  6.1 14.4 %collective-permute-start.2 = (bf16[32,2,32,128]{3,2,1,0:T(8,128)(2,1)}, bf16[32,2,32,128]{3,2,1,0:T(8,128)(2,1)S(1)}, u32[]{:S(2)}, u32[]{:S(2)}) collective-permute-start(bf16[32,2,32,128]{3,2,1,0:T(8,128)(2,1)} %get-tuple-element.20), channel_id=1, source_target_pairs={{0,3},{1,2},{2,1},{3,0},{4,7},{5,6},{6,5},{7,4},{8,11},{9,10},{10,... | collective-permute-start | bytes 1572872 | tf_op jit(solution)/shard_map/ppermute | solution.py:194
  6.7 12.1 %collective-permute-start = (bf16[36,16,128]{2,1,0:T(8,128)(2,1)}, bf16[36,16,128]{2,1,0:T(8,128)(2,1)S(1)}, u32[]{:S(2)}, u32[]{:S(2)}) collective-permute-start(bf16[36,16,128]{2,1,0:T(8,128)(2,1)} %get-tuple-element.15), channel_id=1, source_target_pairs={{0,4},{4,8},{8,12},{12,0},{1,5},{5,9},{9,13},{13,1},{2,6},{6,10},{... | collective-permute-start | bytes 442376 | tf_op jit(solution)/shard_map/ppermute | solution.py:196
  8.3 10.5 %collective-permute-start.1 = (bf16[36,16,128]{2,1,0:T(8,128)(2,1)}, bf16[36,16,128]{2,1,0:T(8,128)(2,1)S(1)}, u32[]{:S(2)}, u32[]{:S(2)}) collective-permute-start(bf16[36,16,128]{2,1,0:T(8,128)(2,1)} %get-tuple-element.16), channel_id=1, source_target_pairs={{4,0},{8,4},{12,8},{0,12},{5,1},{9,5},{13,9},{1,13},{6,2},{10,6},{... | collective-permute-start | bytes 442376 | tf_op jit(solution)/shard_map/ppermute | solution.py:197
  20.3 1.3 %copy-start.4 = (bf16[15,2,32,128]{3,2,1,0:T(8,128)(2,1)S(1)}, bf16[15,2,32,128]{3,2,1,0:T(8,128)(2,1)}, u32[]{:S(2)}) copy-start(bf16[15,2,32,128]{3,2,1,0:T(8,128)(2,1)} %get-tuple-element.23) | copy-start | bytes 737284
  20.3 2.9 %copy-start.3 = (s32[32,6,128]{2,0,1:T(8,128)S(1)}, s32[32,6,128]{2,0,1:T(8,128)}, u32[]{:S(2)}) copy-start(s32[32,6,128]{2,0,1:T(8,128)} %param.7) | copy-start | bytes 294916
  20.6 2.6 %collective-permute-start.4 = (bf16[59,2,32,128]{3,2,1,0:T(8,128)(2,1)S(1)}, bf16[59,2,32,128]{3,2,1,0:T(8,128)(2,1)S(1)}, u32[]{:S(2)}, u32[]{:S(2)}) collective-permute-start(bf16[59,2,32,128]{3,2,1,0:T(8,128)(2,1)S(1)} %pack_near.1), channel_id=1, source_target_pairs={{0,1},{1,0},{2,3},{3,2},{4,5},{5,4},{6,7},{7,6},{8,9},{9,8},{10,11... | collective-permute-start | bytes 2899976 | tf_op jit(solution)/shard_map/ppermute | solution.py:501
  21.0 8.6 %collective-permute-start.6 = (bf16[1056,128]{1,0:T(8,128)(2,1)S(1)}, bf16[1056,128]{1,0:T(8,128)(2,1)S(1)}, u32[]{:S(2)}, u32[]{:S(2)}) collective-permute-start(bf16[1056,128]{1,0:T(8,128)(2,1)S(1)} %pack_relay.1.rest_1_), channel_id=1, source_target_pairs={{0,16},{16,0},{1,17},{17,1},{2,18},{18,2},{3,19},{19,3},{4,20},{20... | collective-permute-start | bytes 811016 | tf_op jit(solution)/shard_map/ppermute | solution.py:483
  21.6 7.9 %collective-permute-start.5 = (bf16[15,2,32,128]{3,2,1,0:T(8,128)(2,1)S(1)}, bf16[15,2,32,128]{3,2,1,0:T(8,128)(2,1)S(1)}, u32[]{:S(2)}, u32[]{:S(2)}) collective-permute-start(bf16[15,2,32,128]{3,2,1,0:T(8,128)(2,1)S(1)} %copy-done.4), channel_id=1, source_target_pairs={{0,3},{1,2},{2,1},{3,0},{4,7},{5,6},{6,5},{7,4},{8,11},{9,10},{10,... | collective-permute-start | bytes 737288 | tf_op jit(solution)/shard_map/ppermute | solution.py:198

commit v9 on v8

--- a/solution.py
+++ b/solution.py
@@ -342,7 +342,7 @@
                     out_ref[k * 8 + 4 + c, rows] = im
             return carry
 
-        lax.fori_loop(0, own // 8, block, 0, unroll=2)
+        lax.fori_loop(0, own // 8, block, 0, unroll=4)
 
     flat = lambda a: a.reshape(a.shape[0], -1, ny)
     with jax.named_scope("resident_slopes"):
@@ -428,7 +428,7 @@
                             out_ref[k * 8 + 4 * i + c, mine] = parts[i]
             return carry
 
-        lax.fori_loop(0, nz, layer_ends, 0)
+        lax.fori_loop(0, nz, layer_ends, 0, unroll=2)
 
     with jax.named_scope("edges"):
         edged = pl.pallas_call(
@@ -605,7 +605,7 @@
                 on_sides(nb_work)
             return carry
 
-        lax.fori_loop(0, nx // 16, chunk_work, 0)
+        lax.fori_loop(0, nx // 16, chunk_work, 0, unroll=True)
 
     def neighbours(mask_ref, pert_ref, mean_ref, mode_ref, xb_ref, xa_ref, whole_ref, edged_ref, first_ref, near_ref, *rest):
         nb_refs = rest[:sides]
@@ -671,7 +671,7 @@
                             out_ref[at, rows] = out_ref[at, rows] + acc[c][i] * (1.0 / 12.0)
                 return carry
 
-            lax.fori_loop(0, own // 8, block, 0)
+            lax.fori_loop(0, own // 8, block, 0, unroll=2)
 
         on_sides(work)
         sends = []
@@ -763,7 +763,7 @@
                     edge_terms(pairs, inner_layer + j, end, add)
                 return carry
 
-            lax.fori_loop(0, nz - 2, at_layer, 0)
+            lax.fori_loop(0, nz - 2, at_layer, 0, unroll=2)
 
         for j in range(nz - 2):
             for end in range(2):
@@ -788,7 +788,7 @@
                     edge_terms(pairs, cross_layer + j, end, add)
                 return carry
 
-            lax.fori_loop(0, 2, at_layer, 0)
+            lax.fori_loop(0, 2, at_layer, 0, unroll=True)
 
         on_sides(cross_edges)
         for step in range(2):

time: 31.8 us -> 31.7 us (level)
  Pallas kernels: 20.6 us -> 20.2 us
  waiting for transfers between devices: 1.15 us -> 1.53 us
  transfers between devices with their start and end apart: 7 -> 7, of which waited for: 4 -> 4; matrix products, arithmetic and copies ran while one was open for 0% -> 0% of each run, Pallas kernels for 49% -> 48%
where the time goes in v9:
time: 31.7 us; the launch traced here: 31.6 us
  Pallas kernels  20.2 us (64%)
  starting transfers between devices  9.74 us (31%)
  waiting for transfers between devices  1.53 us (5%)
    pallas_call x1, Pallas kernels, shards(): pl.pallas_call(resident, out_shape=jax.ShapeDtypeStruct((n_pert, own, ny)...  5.66 us
    pallas_call x1, Pallas kernels, shards(): pl.pallas_call(neighbours, out_shape=(jax.ShapeDtypeStruct((n_pert, own,...  5.56 us
    ppermute x1, starting transfers between devices, shards(): nb_got = [lax.ppermute(b, 'harm', p) for b, p in zip(nb_send, harm_perms)]  3.04 us
    pallas_call x1, Pallas kernels, shards(): pl.pallas_call(pack, out_shape=(face(n_pert), face(n_base), edge, edge) +...  3.02 us
    pallas_call x1, Pallas kernels, shards(): pl.pallas_call(resident_slopes, out_shape=tuple((jax.ShapeDtypeStruct(n +...  2.38 us
    ppermute x1, starting transfers between devices, shards(): xa_got = lax.ppermute(edge_lo, 'gx', down_x)  2.25 us
    pallas_call x1, Pallas kernels, shards(): pl.pallas_call(finish, out_shape=jax.ShapeDtypeStruct((n_pert, own, ny),...  2.05 us
    ppermute x1, starting transfers between devices, shards(): xb_got = lax.ppermute(edge_hi, 'gx', up_x)  1.58 us
  transfers between devices with their start and end apart: 7, of which 4 were waited for; matrix products, arithmetic and copies ran while one was open for 0% of the time, Pallas kernels for 48%

profile of v9, /device:TPU:0, one launch (start us, length us, event | category | flops | bytes accessed | tf_op | source)
XLA Modules:
  0.0 31.6 jit_solution(17949536459844988242)
XLA Ops:
  0.0 0.0 copy-start
  0.0 0.0 copy-start.1
  0.0 0.0 copy-start.2
  0.0 3.0 %pack.1 = (bf16[32,2,32,128]{3,2,1,0:T(8,128)(2,1)}, bf16[15,2,32,128]{3,2,1,0:T(8,128)(2,1)}, bf16[36,16,128]{2,1,0:T(8,128)(2,1)}, bf16[36,16,128]{2,1,0:T(8,128)(2,1)}, bf16[12,6,32,128]{3,2,1,0:T(8,128)(2,1)}) custom-call(bf16[32,6,32,128]{3,2,1,0:T(8,128)(2,1)} %bitcast.20, bf16[3,6,32,128]{3,2,1,0:T(8,128)(2,1)} %bitcast.34, ...), custom_call_target="tpu_custom_call" | custom-call | tf_op jit(solution)/shard_map/pack/pallas_call | solution.py:178
  3.0 3.0 %collective-permute-start.3 = (bf16[12,6,32,128]{3,2,1,0:T(8,128)(2,1)}, bf16[12,6,32,128]{3,2,1,0:T(8,128)(2,1)S(1)}, u32[]{:S(2)}, u32[]{:S(2)}) collective-permute-start(bf16[12,6,32,128]{3,2,1,0:T(8,128)(2,1)} %get-tuple-element.21), channel_id=1, source_target_pairs={{0,16},{16,0},{1,17},{17,1},{2,18},{18,2},{3,19},{19,3},{4,20},{20... | collective-permute-start | bytes 1769480 | tf_op jit(solution)/shard_map/ppermute | solution.py:195
  6.1 0.7 %collective-permute-start.2 = (bf16[32,2,32,128]{3,2,1,0:T(8,128)(2,1)}, bf16[32,2,32,128]{3,2,1,0:T(8,128)(2,1)S(1)}, u32[]{:S(2)}, u32[]{:S(2)}) collective-permute-start(bf16[32,2,32,128]{3,2,1,0:T(8,128)(2,1)} %get-tuple-element.20), channel_id=1, source_target_pairs={{0,3},{1,2},{2,1},{3,0},{4,7},{5,6},{6,5},{7,4},{8,11},{9,10},{10,... | collective-permute-start | bytes 1572872 | tf_op jit(solution)/shard_map/ppermute | solution.py:194
  6.7 1.6 %collective-permute-start = (bf16[36,16,128]{2,1,0:T(8,128)(2,1)}, bf16[36,16,128]{2,1,0:T(8,128)(2,1)S(1)}, u32[]{:S(2)}, u32[]{:S(2)}) collective-permute-start(bf16[36,16,128]{2,1,0:T(8,128)(2,1)} %get-tuple-element.15), channel_id=1, source_target_pairs={{0,4},{4,8},{8,12},{12,0},{1,5},{5,9},{9,13},{13,1},{2,6},{6,10},{... | collective-permute-start | bytes 442376 | tf_op jit(solution)/shard_map/ppermute | solution.py:196
  8.3 2.2 %collective-permute-start.1 = (bf16[36,16,128]{2,1,0:T(8,128)(2,1)}, bf16[36,16,128]{2,1,0:T(8,128)(2,1)S(1)}, u32[]{:S(2)}, u32[]{:S(2)}) collective-permute-start(bf16[36,16,128]{2,1,0:T(8,128)(2,1)} %get-tuple-element.16), channel_id=1, source_target_pairs={{4,0},{8,4},{12,8},{0,12},{5,1},{9,5},{13,9},{1,13},{6,2},{10,6},{... | collective-permute-start | bytes 442376 | tf_op jit(solution)/shard_map/ppermute | solution.py:197
  10.6 0.0 copy-done
  10.6 2.4 %resident_slopes.1 = (f32[4,2,3,3,192,128]{5,4,3,2,1,0:T(8,128)S(1)}, f32[4,2,3,192,128]{4,3,2,1,0:T(8,128)S(1)}, f32[4,2,4,192,128]{4,3,2,1,0:T(8,128)S(1)}) custom-call(bf16[32,192,128]{2,1,0:T(8,128)(2,1)S(1)} %bitcast.21), custom_call_target="tpu_custom_call" | custom-call | tf_op jit(solution)/shard_map/resident_slopes/pallas_call | solution.py:349
  12.9 0.0 copy-done.1
  12.9 0.0 copy-done.2
  13.0 5.7 %resident.1._.whole_ref = f32[32,192,128]{2,1,0:T(8,128)S(1)} custom-call(bf16[3,192,128]{2,1,0:T(8,128)(2,1)S(1)} %bitcast.35, bf16[12,192,128]{2,1,0:T(8,128)(2,1)S(1)} %bitcast.27, f32[4,2,3,3,192,128]{5,4,3,2,1,0:T(8,128)S(1)} %get-tuple-element.17.grads, f32[4,2,3,192,128]{4,3,2,1,0:T(8,128)S(1)} %get-tuple-element.18.plain, ...), custom_call_target="tpu_custom_call" | custom-call | tf_op jit(solution)/shard_map/resident/pallas_call | solution.py:356
  18.6 0.0 collective-permute-done.xb_ref
  18.6 0.0 collective-permute-done.1.xa_ref
  18.6 1.4 %edges.1._.edged_ref = f32[32,96,128]{2,1,0:T(8,128)S(1)} custom-call(bf16[32,192,128]{2,1,0:T(8,128)(2,1)S(1)} %bitcast.22, bf16[3,192,128]{2,1,0:T(8,128)(2,1)S(1)} %bitcast.36, bf16[12,192,128]{2,1,0:T(8,128)(2,1)S(1)} %bitcast.28, bf16[36,16,128]{2,1,0:T(8,128)(2,1)S(1)} %collective-permute-done.xb_ref, ...), custom_call_target="tpu_custom_call" | custom-call | tf_op jit(solution)/shard_map/edges/pallas_call | solution.py:434
  20.1 0.0 copy-start.4
  20.1 0.0 copy-start.3
  20.1 0.4 %collective-permute-done.2.first_ref = bf16[32,2,32,128]{3,2,1,0:T(8,128)(2,1)S(1)} collective-permute-done((bf16[32,2,32,128]{3,2,1,0:T(8,128)(2,1)}, bf16[32,2,32,128]{3,2,1,0:T(8,128)(2,1)S(1)}, u32[]{:S(2)}, u32[]{:S(2)}) %collective-permute-start.2) | collective-permute-done | bytes 524320 | tf_op jit(solution)/shard_map/ppermute | solution.py:194
  20.5 0.0 collective-permute-done.3.rest_0_
  20.5 0.1 pack_near.1
  20.6 0.2 collective-permute-start.4
  20.8 0.8 %collective-permute-start.6 = (bf16[1056,128]{1,0:T(8,128)(2,1)S(1)}, bf16[1056,128]{1,0:T(8,128)(2,1)S(1)}, u32[]{:S(2)}, u32[]{:S(2)}) collective-permute-start(bf16[1056,128]{1,0:T(8,128)(2,1)S(1)} %pack_relay.1.rest_1_), channel_id=1, source_target_pairs={{0,16},{16,0},{1,17},{17,1},{2,18},{18,2},{3,19},{19,3},{4,20},{20... | collective-permute-start | bytes 811016 | tf_op jit(solution)/shard_map/ppermute | solution.py:483
  21.6 0.0 copy-done.4
  21.6 1.3 %collective-permute-start.5 = (bf16[15,2,32,128]{3,2,1,0:T(8,128)(2,1)S(1)}, bf16[15,2,32,128]{3,2,1,0:T(8,128)(2,1)S(1)}, u32[]{:S(2)}, u32[]{:S(2)}) collective-permute-start(bf16[15,2,32,128]{3,2,1,0:T(8,128)(2,1)S(1)} %copy-done.4), channel_id=1, source_target_pairs={{0,3},{1,2},{2,1},{3,0},{4,7},{5,6},{6,5},{7,4},{8,11},{9,10},{10,... | collective-permute-start | bytes 737288 | tf_op jit(solution)/shard_map/ppermute | solution.py:198
  22.8 0.4 %collective-permute-done.4.near_ref = bf16[59,2,32,128]{3,2,1,0:T(8,128)(2,1)S(1)} collective-permute-done((bf16[59,2,32,128]{3,2,1,0:T(8,128)(2,1)S(1)}, bf16[59,2,32,128]{3,2,1,0:T(8,128)(2,1)S(1)}, u32[]{:S(2)}, u32[]{:S(2)}) %collective-permute-start.4) | collective-permute-done | bytes 966688 | tf_op jit(solution)/shard_map/ppermute | solution.py:501
  23.2 0.0 copy-done.3
  23.2 5.6 %neighbours.1 = (f32[32,192,128]{2,1,0:T(8,128)}, f32[32,192,128]{2,1,0:T(8,128)S(1)}) custom-call(s32[192,128]{1,0:T(8,128)S(1)} %bitcast.40, bf16[32,192,128]{2,1,0:T(8,128)(2,1)S(1)} %bitcast.24, bf16[3,192,128]{2,1,0:T(8,128)(2,1)S(1)} %bitcast.38, bf16[12,192,128]{2,1,0:T(8,128)(2,1)S(1)} %bitcast.30, ...), custom_call_target="tpu_custom_call" | custom-call | tf_op jit(solution)/shard_map/neighbours/pallas_call | solution.py:696
  28.8 0.7 %collective-permute-done.5.second_ref = bf16[15,2,32,128]{3,2,1,0:T(8,128)(2,1)S(1)} collective-permute-done((bf16[15,2,32,128]{3,2,1,0:T(8,128)(2,1)S(1)}, bf16[15,2,32,128]{3,2,1,0:T(8,128)(2,1)S(1)}, u32[]{:S(2)}, u32[]{:S(2)}) %collective-permute-start.5) | collective-permute-done | bytes 245792 | tf_op jit(solution)/shard_map/ppermute | solution.py:198
  29.5 0.1 collective-permute-done.6.rest_0_
  29.6 2.0 %finish.1 = f32[32,192,128]{2,1,0:T(8,128)} custom-call(bf16[32,192,128]{2,1,0:T(8,128)(2,1)S(1)} %bitcast.25, bf16[3,192,128]{2,1,0:T(8,128)(2,1)S(1)} %bitcast.39, bf16[12,192,128]{2,1,0:T(8,128)(2,1)S(1)} %bitcast.31, f32[32,192,128]{2,1,0:T(8,128)S(1)} %get-tuple-element.22.inner_ref, ...), custom_call_target="tpu_custom_call", output_to_operand_aliasing={{}: (5, {})} | custom-call | tf_op jit(solution)/shard_map/finish/pallas_call | solution.py:803
  (1 shorter events, 0.0 us)
Async XLA Ops:
  0.0 10.6 %copy-start = (bf16[4,2,4,32,6,128]{5,3,4,2,1,0:T(8,128)(2,1)S(1)}, bf16[4,2,4,32,6,128]{5,3,4,2,1,0:T(8,128)(2,1)}, u32[]{:S(2)}) copy-start(bf16[4,2,4,32,6,128]{5,3,4,2,1,0:T(8,128)(2,1)} %param.4) | copy-start | bytes 4718596
  0.0 12.9 %copy-start.1 = (bf16[2,2,3,32,6,128]{5,3,4,2,1,0:T(8,128)(2,1)S(1)}, bf16[2,2,3,32,6,128]{5,3,4,2,1,0:T(8,128)(2,1)}, u32[]{:S(2)}) copy-start(bf16[2,2,3,32,6,128]{5,3,4,2,1,0:T(8,128)(2,1)} %param.6) | copy-start | bytes 1769476
  0.0 12.9 %copy-start.2 = (bf16[3,32,6,128]{3,1,2,0:T(8,128)(2,1)S(1)}, bf16[3,32,6,128]{3,1,2,0:T(8,128)(2,1)}, u32[]{:S(2)}) copy-start(bf16[3,32,6,128]{3,1,2,0:T(8,128)(2,1)} %param.5) | copy-start | bytes 442372
  3.0 17.5 %collective-permute-start.3 = (bf16[12,6,32,128]{3,2,1,0:T(8,128)(2,1)}, bf16[12,6,32,128]{3,2,1,0:T(8,128)(2,1)S(1)}, u32[]{:S(2)}, u32[]{:S(2)}) collective-permute-start(bf16[12,6,32,128]{3,2,1,0:T(8,128)(2,1)} %get-tuple-element.21), channel_id=1, source_target_pairs={{0,16},{16,0},{1,17},{17,1},{2,18},{18,2},{3,19},{19,3},{4,20},{20... | collective-permute-start | bytes 1769480 | tf_op jit(solution)/shard_map/ppermute | solution.py:195
  6.1 14.4 %collective-permute-start.2 = (bf16[32,2,32,128]{3,2,1,0:T(8,128)(2,1)}, bf16[32,2,32,128]{3,2,1,0:T(8,128)(2,1)S(1)}, u32[]{:S(2)}, u32[]{:S(2)}) collective-permute-start(bf16[32,2,32,128]{3,2,1,0:T(8,128)(2,1)} %get-tuple-element.20), channel_id=1, source_target_pairs={{0,3},{1,2},{2,1},{3,0},{4,7},{5,6},{6,5},{7,4},{8,11},{9,10},{10,... | collective-permute-start | bytes 1572872 | tf_op jit(solution)/shard_map/ppermute | solution.py:194
  6.7 11.9 %collective-permute-start = (bf16[36,16,128]{2,1,0:T(8,128)(2,1)}, bf16[36,16,128]{2,1,0:T(8,128)(2,1)S(1)}, u32[]{:S(2)}, u32[]{:S(2)}) collective-permute-start(bf16[36,16,128]{2,1,0:T(8,128)(2,1)} %get-tuple-element.15), channel_id=1, source_target_pairs={{0,4},{4,8},{8,12},{12,0},{1,5},{5,9},{9,13},{13,1},{2,6},{6,10},{... | collective-permute-start | bytes 442376 | tf_op jit(solution)/shard_map/ppermute | solution.py:196
  8.3 10.3 %collective-permute-start.1 = (bf16[36,16,128]{2,1,0:T(8,128)(2,1)}, bf16[36,16,128]{2,1,0:T(8,128)(2,1)S(1)}, u32[]{:S(2)}, u32[]{:S(2)}) collective-permute-start(bf16[36,16,128]{2,1,0:T(8,128)(2,1)} %get-tuple-element.16), channel_id=1, source_target_pairs={{4,0},{8,4},{12,8},{0,12},{5,1},{9,5},{13,9},{1,13},{6,2},{10,6},{... | collective-permute-start | bytes 442376 | tf_op jit(solution)/shard_map/ppermute | solution.py:197
  20.1 1.5 %copy-start.4 = (bf16[15,2,32,128]{3,2,1,0:T(8,128)(2,1)S(1)}, bf16[15,2,32,128]{3,2,1,0:T(8,128)(2,1)}, u32[]{:S(2)}) copy-start(bf16[15,2,32,128]{3,2,1,0:T(8,128)(2,1)} %get-tuple-element.23) | copy-start | bytes 737284
  20.1 3.1 %copy-start.3 = (s32[32,6,128]{2,0,1:T(8,128)S(1)}, s32[32,6,128]{2,0,1:T(8,128)}, u32[]{:S(2)}) copy-start(s32[32,6,128]{2,0,1:T(8,128)} %param.7) | copy-start | bytes 294916
  20.6 2.6 %collective-permute-start.4 = (bf16[59,2,32,128]{3,2,1,0:T(8,128)(2,1)S(1)}, bf16[59,2,32,128]{3,2,1,0:T(8,128)(2,1)S(1)}, u32[]{:S(2)}, u32[]{:S(2)}) collective-permute-start(bf16[59,2,32,128]{3,2,1,0:T(8,128)(2,1)S(1)} %pack_near.1), channel_id=1, source_target_pairs={{0,1},{1,0},{2,3},{3,2},{4,5},{5,4},{6,7},{7,6},{8,9},{9,8},{10,11... | collective-permute-start | bytes 2899976 | tf_op jit(solution)/shard_map/ppermute | solution.py:501
  20.8 8.8 %collective-permute-start.6 = (bf16[1056,128]{1,0:T(8,128)(2,1)S(1)}, bf16[1056,128]{1,0:T(8,128)(2,1)S(1)}, u32[]{:S(2)}, u32[]{:S(2)}) collective-permute-start(bf16[1056,128]{1,0:T(8,128)(2,1)S(1)} %pack_relay.1.rest_1_), channel_id=1, source_target_pairs={{0,16},{16,0},{1,17},{17,1},{2,18},{18,2},{3,19},{19,3},{4,20},{20... | collective-permute-start | bytes 811016 | tf_op jit(solution)/shard_map/ppermute | solution.py:483
  21.6 7.9 %collective-permute-start.5 = (bf16[15,2,32,128]{3,2,1,0:T(8,128)(2,1)S(1)}, bf16[15,2,32,128]{3,2,1,0:T(8,128)(2,1)S(1)}, u32[]{:S(2)}, u32[]{:S(2)}) collective-permute-start(bf16[15,2,32,128]{3,2,1,0:T(8,128)(2,1)S(1)} %copy-done.4), channel_id=1, source_target_pairs={{0,3},{1,2},{2,1},{3,0},{4,7},{5,6},{6,5},{7,4},{8,11},{9,10},{10,... | collective-permute-start | bytes 737288 | tf_op jit(solution)/shard_map/ppermute | solution.py:198

commit v10 on v9

--- a/solution.py
+++ b/solution.py
@@ -526,7 +526,7 @@
         before = (odd == 0) if cross else (odd == 1)
         return before, jnp.where(before, step, nz - 1 - step), jnp.where(before, 1, 0)
 
-    def faces(out_ref, mean_ref, mode_ref, pert_ref, nb_refs, first_ref, second_ref, near_ref, relay_refs, step, lowest=0):
+    def faces(out_ref, mean_ref, mode_ref, pert_ref, nb_refs, first_ref, second_ref, near_ref, relay_refs, step, lowest=0, after=None):
         cross = near_ref is None
         before, layer, near_at = face_place(cross, step)
         turn = jnp.where(before, 1.0, -1.0)
@@ -540,7 +540,7 @@
         def chunk_work(chunk, carry):
             rows = pl.ds(pl.multiple_of(layer * nx + chunk * 16, 16), 16)
             out_rows = pl.ds(pl.multiple_of((layer - lowest) * nx + chunk * 16, 16), 16)
-            strip = pl.ds(pl.multiple_of(chunk * 16, 16), 16)
+            strip = pl.ds(chunk * 16 if isinstance(chunk, int) else pl.multiple_of(chunk * 16, 16), 16)
 
             def halos(f):
                 if not cross:
@@ -605,7 +605,12 @@
                 on_sides(nb_work)
             return carry
 
-        lax.fori_loop(0, nx // 16, chunk_work, 0, unroll=True)
+        if after is None:
+            lax.fori_loop(0, nx // 16, chunk_work, 0, unroll=True)
+        else:
+            for chunk in range(nx // 16):
+                chunk_work(chunk, 0)
+                after(layer, chunk)
 
     def neighbours(mask_ref, pert_ref, mean_ref, mode_ref, xb_ref, xa_ref, whole_ref, edged_ref, first_ref, near_ref, *rest):
         nb_refs = rest[:sides]
@@ -791,11 +796,12 @@
             lax.fori_loop(0, 2, at_layer, 0, unroll=True)
 
         on_sides(cross_edges)
+        def send_chunk(layer, chunk):
+            here = pl.ds(pl.multiple_of((layer - cross_layer) * nx + chunk * 16, 16), 16)
+            send(done.at[:, here], out_any.at[:, pl.ds(pl.multiple_of(layer * nx + chunk * 16, 16), 16)])
+
         for step in range(2):
-            faces(done, mean_ref, mode_ref, pert_ref, nb_refs, None, second_ref, None, relay_refs, step, cross_layer)
-            layer = face_place(True, step)[1]
-            here = pl.ds(pl.multiple_of((layer - cross_layer) * nx, nx), nx)
-            send(done.at[:, here], out_any.at[:, pl.ds(pl.multiple_of(layer * nx, nx), nx)])
+            faces(done, mean_ref, mode_ref, pert_ref, nb_refs, None, second_ref, None, relay_refs, step, cross_layer, send_chunk)
         for copy in sends:
             copy.wait()
 
@@ -810,7 +816,7 @@
                 pltpu.VMEM((n_pert, 2 * nx, ny), f32),
                 pltpu.VMEM((2, n_keys, nz - 2, 8, ny), f32),
                 pltpu.VMEM((sides * n_nb, ends, ny), f32),
-                pltpu.SemaphoreType.DMA((2 + 2 * (nz - 2),)),
+                pltpu.SemaphoreType.DMA((nx // 8 + 2 * (nz - 2),)),
             ],
             compiler_params=roomy,
         )(

time: 31.7 us -> 31.7 us (level)
  no operation moved by 1% of the time
where the time goes in v10:
time: 31.7 us; the launch traced here: 31.5 us
  Pallas kernels  20.1 us (63%)
  starting transfers between devices  9.74 us (31%)
  waiting for transfers between devices  1.53 us (5%)
    pallas_call x1, Pallas kernels, shards(): pl.pallas_call(resident, out_shape=jax.ShapeDtypeStruct((n_pert, own, ny)...  5.66 us
    pallas_call x1, Pallas kernels, shards(): pl.pallas_call(neighbours, out_shape=(jax.ShapeDtypeStruct((n_pert, own,...  5.56 us
    ppermute x1, starting transfers between devices, shards(): nb_got = [lax.ppermute(b, 'harm', p) for b, p in zip(nb_send, harm_perms)]  3.04 us
    pallas_call x1, Pallas kernels, shards(): pl.pallas_call(pack, out_shape=(face(n_pert), face(n_base), edge, edge) +...  3.02 us
    pallas_call x1, Pallas kernels, shards(): pl.pallas_call(resident_slopes, out_shape=tuple((jax.ShapeDtypeStruct(n +...  2.38 us
    ppermute x1, starting transfers between devices, shards(): xa_got = lax.ppermute(edge_lo, 'gx', down_x)  2.25 us
    pallas_call x1, Pallas kernels, shards(): pl.pallas_call(finish, out_shape=jax.ShapeDtypeStruct((n_pert, own, ny),...  1.98 us
    ppermute x1, starting transfers between devices, shards(): xb_got = lax.ppermute(edge_hi, 'gx', up_x)  1.58 us
  transfers between devices with their start and end apart: 7, of which 4 were waited for; matrix products, arithmetic and copies ran while one was open for 0% of the time, Pallas kernels for 48%

profile of v10, /device:TPU:0, one launch (start us, length us, event | category | flops | bytes accessed | tf_op | source)
XLA Modules:
  0.0 31.5 jit_solution(4123588509445229420)
XLA Ops:
  0.0 0.0 copy-start
  0.0 0.0 copy-start.1
  0.0 0.0 copy-start.2
  0.0 3.0 %pack.1 = (bf16[32,2,32,128]{3,2,1,0:T(8,128)(2,1)}, bf16[15,2,32,128]{3,2,1,0:T(8,128)(2,1)}, bf16[36,16,128]{2,1,0:T(8,128)(2,1)}, bf16[36,16,128]{2,1,0:T(8,128)(2,1)}, bf16[12,6,32,128]{3,2,1,0:T(8,128)(2,1)}) custom-call(bf16[32,6,32,128]{3,2,1,0:T(8,128)(2,1)} %bitcast.20, bf16[3,6,32,128]{3,2,1,0:T(8,128)(2,1)} %bitcast.34, ...), custom_call_target="tpu_custom_call" | custom-call | tf_op jit(solution)/shard_map/pack/pallas_call | solution.py:178
  3.0 3.0 %collective-permute-start.3 = (bf16[12,6,32,128]{3,2,1,0:T(8,128)(2,1)}, bf16[12,6,32,128]{3,2,1,0:T(8,128)(2,1)S(1)}, u32[]{:S(2)}, u32[]{:S(2)}) collective-permute-start(bf16[12,6,32,128]{3,2,1,0:T(8,128)(2,1)} %get-tuple-element.21), channel_id=1, source_target_pairs={{0,16},{16,0},{1,17},{17,1},{2,18},{18,2},{3,19},{19,3},{4,20},{20... | collective-permute-start | bytes 1769480 | tf_op jit(solution)/shard_map/ppermute | solution.py:195
  6.1 0.7 %collective-permute-start.2 = (bf16[32,2,32,128]{3,2,1,0:T(8,128)(2,1)}, bf16[32,2,32,128]{3,2,1,0:T(8,128)(2,1)S(1)}, u32[]{:S(2)}, u32[]{:S(2)}) collective-permute-start(bf16[32,2,32,128]{3,2,1,0:T(8,128)(2,1)} %get-tuple-element.20), channel_id=1, source_target_pairs={{0,3},{1,2},{2,1},{3,0},{4,7},{5,6},{6,5},{7,4},{8,11},{9,10},{10,... | collective-permute-start | bytes 1572872 | tf_op jit(solution)/shard_map/ppermute | solution.py:194
  6.7 1.6 %collective-permute-start = (bf16[36,16,128]{2,1,0:T(8,128)(2,1)}, bf16[36,16,128]{2,1,0:T(8,128)(2,1)S(1)}, u32[]{:S(2)}, u32[]{:S(2)}) collective-permute-start(bf16[36,16,128]{2,1,0:T(8,128)(2,1)} %get-tuple-element.15), channel_id=1, source_target_pairs={{0,4},{4,8},{8,12},{12,0},{1,5},{5,9},{9,13},{13,1},{2,6},{6,10},{... | collective-permute-start | bytes 442376 | tf_op jit(solution)/shard_map/ppermute | solution.py:196
  8.3 2.2 %collective-permute-start.1 = (bf16[36,16,128]{2,1,0:T(8,128)(2,1)}, bf16[36,16,128]{2,1,0:T(8,128)(2,1)S(1)}, u32[]{:S(2)}, u32[]{:S(2)}) collective-permute-start(bf16[36,16,128]{2,1,0:T(8,128)(2,1)} %get-tuple-element.16), channel_id=1, source_target_pairs={{4,0},{8,4},{12,8},{0,12},{5,1},{9,5},{13,9},{1,13},{6,2},{10,6},{... | collective-permute-start | bytes 442376 | tf_op jit(solution)/shard_map/ppermute | solution.py:197
  10.6 0.0 copy-done
  10.6 2.4 %resident_slopes.1 = (f32[4,2,3,3,192,128]{5,4,3,2,1,0:T(8,128)S(1)}, f32[4,2,3,192,128]{4,3,2,1,0:T(8,128)S(1)}, f32[4,2,4,192,128]{4,3,2,1,0:T(8,128)S(1)}) custom-call(bf16[32,192,128]{2,1,0:T(8,128)(2,1)S(1)} %bitcast.21), custom_call_target="tpu_custom_call" | custom-call | tf_op jit(solution)/shard_map/resident_slopes/pallas_call | solution.py:349
  12.9 0.0 copy-done.1
  12.9 0.0 copy-done.2
  13.0 5.7 %resident.1._.whole_ref = f32[32,192,128]{2,1,0:T(8,128)S(1)} custom-call(bf16[3,192,128]{2,1,0:T(8,128)(2,1)S(1)} %bitcast.35, bf16[12,192,128]{2,1,0:T(8,128)(2,1)S(1)} %bitcast.27, f32[4,2,3,3,192,128]{5,4,3,2,1,0:T(8,128)S(1)} %get-tuple-element.17.grads, f32[4,2,3,192,128]{4,3,2,1,0:T(8,128)S(1)} %get-tuple-element.18.plain, ...), custom_call_target="tpu_custom_call" | custom-call | tf_op jit(solution)/shard_map/resident/pallas_call | solution.py:356
  18.6 0.0 collective-permute-done.xb_ref
  18.6 0.0 collective-permute-done.1.xa_ref
  18.6 1.4 %edges.1._.edged_ref = f32[32,96,128]{2,1,0:T(8,128)S(1)} custom-call(bf16[32,192,128]{2,1,0:T(8,128)(2,1)S(1)} %bitcast.22, bf16[3,192,128]{2,1,0:T(8,128)(2,1)S(1)} %bitcast.36, bf16[12,192,128]{2,1,0:T(8,128)(2,1)S(1)} %bitcast.28, bf16[36,16,128]{2,1,0:T(8,128)(2,1)S(1)} %collective-permute-done.xb_ref, ...), custom_call_target="tpu_custom_call" | custom-call | tf_op jit(solution)/shard_map/edges/pallas_call | solution.py:434
  20.1 0.0 copy-start.4
  20.1 0.0 copy-start.3
  20.1 0.4 %collective-permute-done.2.first_ref = bf16[32,2,32,128]{3,2,1,0:T(8,128)(2,1)S(1)} collective-permute-done((bf16[32,2,32,128]{3,2,1,0:T(8,128)(2,1)}, bf16[32,2,32,128]{3,2,1,0:T(8,128)(2,1)S(1)}, u32[]{:S(2)}, u32[]{:S(2)}) %collective-permute-start.2) | collective-permute-done | bytes 524320 | tf_op jit(solution)/shard_map/ppermute | solution.py:194
  20.5 0.0 collective-permute-done.3.rest_0_
  20.5 0.1 pack_near.1
  20.6 0.2 collective-permute-start.4
  20.8 0.8 %collective-permute-start.6 = (bf16[1056,128]{1,0:T(8,128)(2,1)S(1)}, bf16[1056,128]{1,0:T(8,128)(2,1)S(1)}, u32[]{:S(2)}, u32[]{:S(2)}) collective-permute-start(bf16[1056,128]{1,0:T(8,128)(2,1)S(1)} %pack_relay.1.rest_1_), channel_id=1, source_target_pairs={{0,16},{16,0},{1,17},{17,1},{2,18},{18,2},{3,19},{19,3},{4,20},{20... | collective-permute-start | bytes 811016 | tf_op jit(solution)/shard_map/ppermute | solution.py:483
  21.6 0.0 copy-done.4
  21.6 1.3 %collective-permute-start.5 = (bf16[15,2,32,128]{3,2,1,0:T(8,128)(2,1)S(1)}, bf16[15,2,32,128]{3,2,1,0:T(8,128)(2,1)S(1)}, u32[]{:S(2)}, u32[]{:S(2)}) collective-permute-start(bf16[15,2,32,128]{3,2,1,0:T(8,128)(2,1)S(1)} %copy-done.4), channel_id=1, source_target_pairs={{0,3},{1,2},{2,1},{3,0},{4,7},{5,6},{6,5},{7,4},{8,11},{9,10},{10,... | collective-permute-start | bytes 737288 | tf_op jit(solution)/shard_map/ppermute | solution.py:198
  22.8 0.4 %collective-permute-done.4.near_ref = bf16[59,2,32,128]{3,2,1,0:T(8,128)(2,1)S(1)} collective-permute-done((bf16[59,2,32,128]{3,2,1,0:T(8,128)(2,1)S(1)}, bf16[59,2,32,128]{3,2,1,0:T(8,128)(2,1)S(1)}, u32[]{:S(2)}, u32[]{:S(2)}) %collective-permute-start.4) | collective-permute-done | bytes 966688 | tf_op jit(solution)/shard_map/ppermute | solution.py:501
  23.2 0.0 copy-done.3
  23.2 5.6 %neighbours.1 = (f32[32,192,128]{2,1,0:T(8,128)}, f32[32,192,128]{2,1,0:T(8,128)S(1)}) custom-call(s32[192,128]{1,0:T(8,128)S(1)} %bitcast.40, bf16[32,192,128]{2,1,0:T(8,128)(2,1)S(1)} %bitcast.24, bf16[3,192,128]{2,1,0:T(8,128)(2,1)S(1)} %bitcast.38, bf16[12,192,128]{2,1,0:T(8,128)(2,1)S(1)} %bitcast.30, ...), custom_call_target="tpu_custom_call" | custom-call | tf_op jit(solution)/shard_map/neighbours/pallas_call | solution.py:701
  28.8 0.7 %collective-permute-done.5.second_ref = bf16[15,2,32,128]{3,2,1,0:T(8,128)(2,1)S(1)} collective-permute-done((bf16[15,2,32,128]{3,2,1,0:T(8,128)(2,1)S(1)}, bf16[15,2,32,128]{3,2,1,0:T(8,128)(2,1)S(1)}, u32[]{:S(2)}, u32[]{:S(2)}) %collective-permute-start.5) | collective-permute-done | bytes 245792 | tf_op jit(solution)/shard_map/ppermute | solution.py:198
  29.5 0.1 collective-permute-done.6.rest_0_
  29.6 2.0 %finish.1 = f32[32,192,128]{2,1,0:T(8,128)} custom-call(bf16[32,192,128]{2,1,0:T(8,128)(2,1)S(1)} %bitcast.25, bf16[3,192,128]{2,1,0:T(8,128)(2,1)S(1)} %bitcast.39, bf16[12,192,128]{2,1,0:T(8,128)(2,1)S(1)} %bitcast.31, f32[32,192,128]{2,1,0:T(8,128)S(1)} %get-tuple-element.22.inner_ref, ...), custom_call_target="tpu_custom_call", output_to_operand_aliasing={{}: (5, {})} | custom-call | tf_op jit(solution)/shard_map/finish/pallas_call | solution.py:809
  (1 shorter events, 0.0 us)
Async XLA Ops:
  0.0 10.6 %copy-start = (bf16[4,2,4,32,6,128]{5,3,4,2,1,0:T(8,128)(2,1)S(1)}, bf16[4,2,4,32,6,128]{5,3,4,2,1,0:T(8,128)(2,1)}, u32[]{:S(2)}) copy-start(bf16[4,2,4,32,6,128]{5,3,4,2,1,0:T(8,128)(2,1)} %param.4) | copy-start | bytes 4718596
  0.0 12.9 %copy-start.1 = (bf16[2,2,3,32,6,128]{5,3,4,2,1,0:T(8,128)(2,1)S(1)}, bf16[2,2,3,32,6,128]{5,3,4,2,1,0:T(8,128)(2,1)}, u32[]{:S(2)}) copy-start(bf16[2,2,3,32,6,128]{5,3,4,2,1,0:T(8,128)(2,1)} %param.6) | copy-start | bytes 1769476
  0.0 12.9 %copy-start.2 = (bf16[3,32,6,128]{3,1,2,0:T(8,128)(2,1)S(1)}, bf16[3,32,6,128]{3,1,2,0:T(8,128)(2,1)}, u32[]{:S(2)}) copy-start(bf16[3,32,6,128]{3,1,2,0:T(8,128)(2,1)} %param.5) | copy-start | bytes 442372
  3.0 17.5 %collective-permute-start.3 = (bf16[12,6,32,128]{3,2,1,0:T(8,128)(2,1)}, bf16[12,6,32,128]{3,2,1,0:T(8,128)(2,1)S(1)}, u32[]{:S(2)}, u32[]{:S(2)}) collective-permute-start(bf16[12,6,32,128]{3,2,1,0:T(8,128)(2,1)} %get-tuple-element.21), channel_id=1, source_target_pairs={{0,16},{16,0},{1,17},{17,1},{2,18},{18,2},{3,19},{19,3},{4,20},{20... | collective-permute-start | bytes 1769480 | tf_op jit(solution)/shard_map/ppermute | solution.py:195
  6.1 14.4 %collective-permute-start.2 = (bf16[32,2,32,128]{3,2,1,0:T(8,128)(2,1)}, bf16[32,2,32,128]{3,2,1,0:T(8,128)(2,1)S(1)}, u32[]{:S(2)}, u32[]{:S(2)}) collective-permute-start(bf16[32,2,32,128]{3,2,1,0:T(8,128)(2,1)} %get-tuple-element.20), channel_id=1, source_target_pairs={{0,3},{1,2},{2,1},{3,0},{4,7},{5,6},{6,5},{7,4},{8,11},{9,10},{10,... | collective-permute-start | bytes 1572872 | tf_op jit(solution)/shard_map/ppermute | solution.py:194
  6.7 11.9 %collective-permute-start = (bf16[36,16,128]{2,1,0:T(8,128)(2,1)}, bf16[36,16,128]{2,1,0:T(8,128)(2,1)S(1)}, u32[]{:S(2)}, u32[]{:S(2)}) collective-permute-start(bf16[36,16,128]{2,1,0:T(8,128)(2,1)} %get-tuple-element.15), channel_id=1, source_target_pairs={{0,4},{4,8},{8,12},{12,0},{1,5},{5,9},{9,13},{13,1},{2,6},{6,10},{... | collective-permute-start | bytes 442376 | tf_op jit(solution)/shard_map/ppermute | solution.py:196
  8.3 10.3 %collective-permute-start.1 = (bf16[36,16,128]{2,1,0:T(8,128)(2,1)}, bf16[36,16,128]{2,1,0:T(8,128)(2,1)S(1)}, u32[]{:S(2)}, u32[]{:S(2)}) collective-permute-start(bf16[36,16,128]{2,1,0:T(8,128)(2,1)} %get-tuple-element.16), channel_id=1, source_target_pairs={{4,0},{8,4},{12,8},{0,12},{5,1},{9,5},{13,9},{1,13},{6,2},{10,6},{... | collective-permute-start | bytes 442376 | tf_op jit(solution)/shard_map/ppermute | solution.py:197
  20.1 1.5 %copy-start.4 = (bf16[15,2,32,128]{3,2,1,0:T(8,128)(2,1)S(1)}, bf16[15,2,32,128]{3,2,1,0:T(8,128)(2,1)}, u32[]{:S(2)}) copy-start(bf16[15,2,32,128]{3,2,1,0:T(8,128)(2,1)} %get-tuple-element.23) | copy-start | bytes 737284
  20.1 3.1 %copy-start.3 = (s32[32,6,128]{2,0,1:T(8,128)S(1)}, s32[32,6,128]{2,0,1:T(8,128)}, u32[]{:S(2)}) copy-start(s32[32,6,128]{2,0,1:T(8,128)} %param.7) | copy-start | bytes 294916
  20.6 2.6 %collective-permute-start.4 = (bf16[59,2,32,128]{3,2,1,0:T(8,128)(2,1)S(1)}, bf16[59,2,32,128]{3,2,1,0:T(8,128)(2,1)S(1)}, u32[]{:S(2)}, u32[]{:S(2)}) collective-permute-start(bf16[59,2,32,128]{3,2,1,0:T(8,128)(2,1)S(1)} %pack_near.1), channel_id=1, source_target_pairs={{0,1},{1,0},{2,3},{3,2},{4,5},{5,4},{6,7},{7,6},{8,9},{9,8},{10,11... | collective-permute-start | bytes 2899976 | tf_op jit(solution)/shard_map/ppermute | solution.py:501
  20.8 8.8 %collective-permute-start.6 = (bf16[1056,128]{1,0:T(8,128)(2,1)S(1)}, bf16[1056,128]{1,0:T(8,128)(2,1)S(1)}, u32[]{:S(2)}, u32[]{:S(2)}) collective-permute-start(bf16[1056,128]{1,0:T(8,128)(2,1)S(1)} %pack_relay.1.rest_1_), channel_id=1, source_target_pairs={{0,16},{16,0},{1,17},{17,1},{2,18},{18,2},{3,19},{19,3},{4,20},{20... | collective-permute-start | bytes 811016 | tf_op jit(solution)/shard_map/ppermute | solution.py:483
  21.6 7.9 %collective-permute-start.5 = (bf16[15,2,32,128]{3,2,1,0:T(8,128)(2,1)S(1)}, bf16[15,2,32,128]{3,2,1,0:T(8,128)(2,1)S(1)}, u32[]{:S(2)}, u32[]{:S(2)}) collective-permute-start(bf16[15,2,32,128]{3,2,1,0:T(8,128)(2,1)S(1)} %copy-done.4), channel_id=1, source_target_pairs={{0,3},{1,2},{2,1},{3,0},{4,7},{5,6},{6,5},{7,4},{8,11},{9,10},{10,... | collective-permute-start | bytes 737288 | tf_op jit(solution)/shard_map/ppermute | solution.py:198

commit v11 on v10

--- a/solution.py
+++ b/solution.py
@@ -162,14 +162,18 @@
                 send(pert_ref.at[pl.ds(sent(s, scal) * 8 + 4 * i, 3)], nb_any.at[pl.ds(3 * i, 3)])
         for group in range(n_pert // 4):
             edges(group)
+        early = pl.ds(0, 3 * n_pert // 4)
+        send(lo_ref.at[early], lo_any.at[early])
+        send(hi_ref.at[early], hi_any.at[early])
         loads[per].wait()
         loads[per + 1].wait()
         send(mean_ref.at[:, z], second_any.at[pl.ds(0, n_mean)])
         send(mode_ref.at[:, z], second_any.at[pl.ds(n_mean, n_modes)])
         for group in range(n_pert // 4, tiles // 3):
             edges(group)
-        send(lo_ref, lo_any)
-        send(hi_ref, hi_any)
+        late = pl.ds(3 * n_pert // 4, tiles - 3 * n_pert // 4)
+        send(lo_ref.at[late], lo_any.at[late])
+        send(hi_ref.at[late], hi_any.at[late])
         for copy in out:
             copy.wait()
 
@@ -187,7 +191,7 @@
                 pltpu.VMEM((tiles, HALO_X, ny), bf16),
                 pltpu.VMEM((tiles, HALO_X, ny), bf16),
                 pltpu.SemaphoreType.DMA((per + 2,)),
-                pltpu.SemaphoreType.DMA((per + sides * modes * 2 + 4,)),
+                pltpu.SemaphoreType.DMA((per + sides * modes * 2 + 6,)),
             ],
             compiler_params=pltpu.CompilerParams(vmem_limit_bytes=VMEM_BYTES),
         )(pert, mean, mode)

time: 31.7 us -> 31.6 us (level)
  no operation moved by 1% of the time
where the time goes in v11:
time: 31.6 us; the launch traced here: 31.5 us
  Pallas kernels  20.1 us (64%)
  starting transfers between devices  9.74 us (31%)
  waiting for transfers between devices  1.53 us (5%)
    pallas_call x1, Pallas kernels, shards(): pl.pallas_call(resident, out_shape=jax.ShapeDtypeStruct((n_pert, own, ny)...  5.66 us
    pallas_call x1, Pallas kernels, shards(): pl.pallas_call(neighbours, out_shape=(jax.ShapeDtypeStruct((n_pert, own,...  5.56 us
    ppermute x1, starting transfers between devices, shards(): nb_got = [lax.ppermute(b, 'harm', p) for b, p in zip(nb_send, harm_perms)]  3.04 us
    pallas_call x1, Pallas kernels, shards(): pl.pallas_call(pack, out_shape=(face(n_pert), face(n_base), edge, edge) +...  2.96 us
    pallas_call x1, Pallas kernels, shards(): pl.pallas_call(resident_slopes, out_shape=tuple((jax.ShapeDtypeStruct(n +...  2.38 us
    ppermute x1, starting transfers between devices, shards(): xa_got = lax.ppermute(edge_lo, 'gx', down_x)  2.25 us
    pallas_call x1, Pallas kernels, shards(): pl.pallas_call(finish, out_shape=jax.ShapeDtypeStruct((n_pert, own, ny),...  1.98 us
    ppermute x1, starting transfers between devices, shards(): xb_got = lax.ppermute(edge_hi, 'gx', up_x)  1.58 us
  transfers between devices with their start and end apart: 7, of which 4 were waited for; matrix products, arithmetic and copies ran while one was open for 0% of the time, Pallas kernels for 48%

profile of v11, /device:TPU:0, one launch (start us, length us, event | category | flops | bytes accessed | tf_op | source)
XLA Modules:
  0.0 31.5 jit_solution(2341207584009335628)
XLA Ops:
  0.0 0.0 copy-start
  0.0 0.0 copy-start.1
  0.0 0.0 copy-start.2
  0.0 3.0 %pack.1 = (bf16[32,2,32,128]{3,2,1,0:T(8,128)(2,1)}, bf16[15,2,32,128]{3,2,1,0:T(8,128)(2,1)}, bf16[36,16,128]{2,1,0:T(8,128)(2,1)}, bf16[36,16,128]{2,1,0:T(8,128)(2,1)}, bf16[12,6,32,128]{3,2,1,0:T(8,128)(2,1)}) custom-call(bf16[32,6,32,128]{3,2,1,0:T(8,128)(2,1)} %bitcast.20, bf16[3,6,32,128]{3,2,1,0:T(8,128)(2,1)} %bitcast.34, ...), custom_call_target="tpu_custom_call" | custom-call | tf_op jit(solution)/shard_map/pack/pallas_call | solution.py:182
  3.0 3.0 %collective-permute-start.3 = (bf16[12,6,32,128]{3,2,1,0:T(8,128)(2,1)}, bf16[12,6,32,128]{3,2,1,0:T(8,128)(2,1)S(1)}, u32[]{:S(2)}, u32[]{:S(2)}) collective-permute-start(bf16[12,6,32,128]{3,2,1,0:T(8,128)(2,1)} %get-tuple-element.21), channel_id=1, source_target_pairs={{0,16},{16,0},{1,17},{17,1},{2,18},{18,2},{3,19},{19,3},{4,20},{20... | collective-permute-start | bytes 1769480 | tf_op jit(solution)/shard_map/ppermute | solution.py:199
  6.0 0.7 %collective-permute-start.2 = (bf16[32,2,32,128]{3,2,1,0:T(8,128)(2,1)}, bf16[32,2,32,128]{3,2,1,0:T(8,128)(2,1)S(1)}, u32[]{:S(2)}, u32[]{:S(2)}) collective-permute-start(bf16[32,2,32,128]{3,2,1,0:T(8,128)(2,1)} %get-tuple-element.20), channel_id=1, source_target_pairs={{0,3},{1,2},{2,1},{3,0},{4,7},{5,6},{6,5},{7,4},{8,11},{9,10},{10,... | collective-permute-start | bytes 1572872 | tf_op jit(solution)/shard_map/ppermute | solution.py:198
  6.7 1.6 %collective-permute-start = (bf16[36,16,128]{2,1,0:T(8,128)(2,1)}, bf16[36,16,128]{2,1,0:T(8,128)(2,1)S(1)}, u32[]{:S(2)}, u32[]{:S(2)}) collective-permute-start(bf16[36,16,128]{2,1,0:T(8,128)(2,1)} %get-tuple-element.15), channel_id=1, source_target_pairs={{0,4},{4,8},{8,12},{12,0},{1,5},{5,9},{9,13},{13,1},{2,6},{6,10},{... | collective-permute-start | bytes 442376 | tf_op jit(solution)/shard_map/ppermute | solution.py:200
  8.2 2.2 %collective-permute-start.1 = (bf16[36,16,128]{2,1,0:T(8,128)(2,1)}, bf16[36,16,128]{2,1,0:T(8,128)(2,1)S(1)}, u32[]{:S(2)}, u32[]{:S(2)}) collective-permute-start(bf16[36,16,128]{2,1,0:T(8,128)(2,1)} %get-tuple-element.16), channel_id=1, source_target_pairs={{4,0},{8,4},{12,8},{0,12},{5,1},{9,5},{13,9},{1,13},{6,2},{10,6},{... | collective-permute-start | bytes 442376 | tf_op jit(solution)/shard_map/ppermute | solution.py:201
  10.5 0.0 copy-done
  10.5 2.4 %resident_slopes.1 = (f32[4,2,3,3,192,128]{5,4,3,2,1,0:T(8,128)S(1)}, f32[4,2,3,192,128]{4,3,2,1,0:T(8,128)S(1)}, f32[4,2,4,192,128]{4,3,2,1,0:T(8,128)S(1)}) custom-call(bf16[32,192,128]{2,1,0:T(8,128)(2,1)S(1)} %bitcast.21), custom_call_target="tpu_custom_call" | custom-call | tf_op jit(solution)/shard_map/resident_slopes/pallas_call | solution.py:353
  12.9 0.0 copy-done.1
  12.9 0.0 copy-done.2
  12.9 5.7 %resident.1._.whole_ref = f32[32,192,128]{2,1,0:T(8,128)S(1)} custom-call(bf16[3,192,128]{2,1,0:T(8,128)(2,1)S(1)} %bitcast.35, bf16[12,192,128]{2,1,0:T(8,128)(2,1)S(1)} %bitcast.27, f32[4,2,3,3,192,128]{5,4,3,2,1,0:T(8,128)S(1)} %get-tuple-element.17.grads, f32[4,2,3,192,128]{4,3,2,1,0:T(8,128)S(1)} %get-tuple-element.18.plain, ...), custom_call_target="tpu_custom_call" | custom-call | tf_op jit(solution)/shard_map/resident/pallas_call | solution.py:360
  18.6 0.0 collective-permute-done.xb_ref
  18.6 0.0 collective-permute-done.1.xa_ref
  18.6 1.4 %edges.1._.edged_ref = f32[32,96,128]{2,1,0:T(8,128)S(1)} custom-call(bf16[32,192,128]{2,1,0:T(8,128)(2,1)S(1)} %bitcast.22, bf16[3,192,128]{2,1,0:T(8,128)(2,1)S(1)} %bitcast.36, bf16[12,192,128]{2,1,0:T(8,128)(2,1)S(1)} %bitcast.28, bf16[36,16,128]{2,1,0:T(8,128)(2,1)S(1)} %collective-permute-done.xb_ref, ...), custom_call_target="tpu_custom_call" | custom-call | tf_op jit(solution)/shard_map/edges/pallas_call | solution.py:438
  20.0 0.0 copy-start.4
  20.0 0.0 copy-start.3
  20.0 0.4 %collective-permute-done.2.first_ref = bf16[32,2,32,128]{3,2,1,0:T(8,128)(2,1)S(1)} collective-permute-done((bf16[32,2,32,128]{3,2,1,0:T(8,128)(2,1)}, bf16[32,2,32,128]{3,2,1,0:T(8,128)(2,1)S(1)}, u32[]{:S(2)}, u32[]{:S(2)}) %collective-permute-start.2) | collective-permute-done | bytes 524320 | tf_op jit(solution)/shard_map/ppermute | solution.py:198
  20.4 0.0 collective-permute-done.3.rest_0_
  20.4 0.1 pack_near.1
  20.5 0.2 collective-permute-start.4
  20.7 0.8 %collective-permute-start.6 = (bf16[1056,128]{1,0:T(8,128)(2,1)S(1)}, bf16[1056,128]{1,0:T(8,128)(2,1)S(1)}, u32[]{:S(2)}, u32[]{:S(2)}) collective-permute-start(bf16[1056,128]{1,0:T(8,128)(2,1)S(1)} %pack_relay.1.rest_1_), channel_id=1, source_target_pairs={{0,16},{16,0},{1,17},{17,1},{2,18},{18,2},{3,19},{19,3},{4,20},{20... | collective-permute-start | bytes 811016 | tf_op jit(solution)/shard_map/ppermute | solution.py:487
  21.5 0.0 copy-done.4
  21.5 1.3 %collective-permute-start.5 = (bf16[15,2,32,128]{3,2,1,0:T(8,128)(2,1)S(1)}, bf16[15,2,32,128]{3,2,1,0:T(8,128)(2,1)S(1)}, u32[]{:S(2)}, u32[]{:S(2)}) collective-permute-start(bf16[15,2,32,128]{3,2,1,0:T(8,128)(2,1)S(1)} %copy-done.4), channel_id=1, source_target_pairs={{0,3},{1,2},{2,1},{3,0},{4,7},{5,6},{6,5},{7,4},{8,11},{9,10},{10,... | collective-permute-start | bytes 737288 | tf_op jit(solution)/shard_map/ppermute | solution.py:202
  22.8 0.4 %collective-permute-done.4.near_ref = bf16[59,2,32,128]{3,2,1,0:T(8,128)(2,1)S(1)} collective-permute-done((bf16[59,2,32,128]{3,2,1,0:T(8,128)(2,1)S(1)}, bf16[59,2,32,128]{3,2,1,0:T(8,128)(2,1)S(1)}, u32[]{:S(2)}, u32[]{:S(2)}) %collective-permute-start.4) | collective-permute-done | bytes 966688 | tf_op jit(solution)/shard_map/ppermute | solution.py:505
  23.1 0.0 copy-done.3
  23.1 5.6 %neighbours.1 = (f32[32,192,128]{2,1,0:T(8,128)}, f32[32,192,128]{2,1,0:T(8,128)S(1)}) custom-call(s32[192,128]{1,0:T(8,128)S(1)} %bitcast.40, bf16[32,192,128]{2,1,0:T(8,128)(2,1)S(1)} %bitcast.24, bf16[3,192,128]{2,1,0:T(8,128)(2,1)S(1)} %bitcast.38, bf16[12,192,128]{2,1,0:T(8,128)(2,1)S(1)} %bitcast.30, ...), custom_call_target="tpu_custom_call" | custom-call | tf_op jit(solution)/shard_map/neighbours/pallas_call | solution.py:705
  28.7 0.7 %collective-permute-done.5.second_ref = bf16[15,2,32,128]{3,2,1,0:T(8,128)(2,1)S(1)} collective-permute-done((bf16[15,2,32,128]{3,2,1,0:T(8,128)(2,1)S(1)}, bf16[15,2,32,128]{3,2,1,0:T(8,128)(2,1)S(1)}, u32[]{:S(2)}, u32[]{:S(2)}) %collective-permute-start.5) | collective-permute-done | bytes 245792 | tf_op jit(solution)/shard_map/ppermute | solution.py:202
  29.4 0.1 collective-permute-done.6.rest_0_
  29.5 2.0 %finish.1 = f32[32,192,128]{2,1,0:T(8,128)} custom-call(bf16[32,192,128]{2,1,0:T(8,128)(2,1)S(1)} %bitcast.25, bf16[3,192,128]{2,1,0:T(8,128)(2,1)S(1)} %bitcast.39, bf16[12,192,128]{2,1,0:T(8,128)(2,1)S(1)} %bitcast.31, f32[32,192,128]{2,1,0:T(8,128)S(1)} %get-tuple-element.22.inner_ref, ...), custom_call_target="tpu_custom_call", output_to_operand_aliasing={{}: (5, {})} | custom-call | tf_op jit(solution)/shard_map/finish/pallas_call | solution.py:813
  (1 shorter events, 0.0 us)
Async XLA Ops:
  0.0 10.5 %copy-start = (bf16[4,2,4,32,6,128]{5,3,4,2,1,0:T(8,128)(2,1)S(1)}, bf16[4,2,4,32,6,128]{5,3,4,2,1,0:T(8,128)(2,1)}, u32[]{:S(2)}) copy-start(bf16[4,2,4,32,6,128]{5,3,4,2,1,0:T(8,128)(2,1)} %param.4) | copy-start | bytes 4718596
  0.0 12.9 %copy-start.1 = (bf16[2,2,3,32,6,128]{5,3,4,2,1,0:T(8,128)(2,1)S(1)}, bf16[2,2,3,32,6,128]{5,3,4,2,1,0:T(8,128)(2,1)}, u32[]{:S(2)}) copy-start(bf16[2,2,3,32,6,128]{5,3,4,2,1,0:T(8,128)(2,1)} %param.6) | copy-start | bytes 1769476
  0.0 12.9 %copy-start.2 = (bf16[3,32,6,128]{3,1,2,0:T(8,128)(2,1)S(1)}, bf16[3,32,6,128]{3,1,2,0:T(8,128)(2,1)}, u32[]{:S(2)}) copy-start(bf16[3,32,6,128]{3,1,2,0:T(8,128)(2,1)} %param.5) | copy-start | bytes 442372
  3.0 17.5 %collective-permute-start.3 = (bf16[12,6,32,128]{3,2,1,0:T(8,128)(2,1)}, bf16[12,6,32,128]{3,2,1,0:T(8,128)(2,1)S(1)}, u32[]{:S(2)}, u32[]{:S(2)}) collective-permute-start(bf16[12,6,32,128]{3,2,1,0:T(8,128)(2,1)} %get-tuple-element.21), channel_id=1, source_target_pairs={{0,16},{16,0},{1,17},{17,1},{2,18},{18,2},{3,19},{19,3},{4,20},{20... | collective-permute-start | bytes 1769480 | tf_op jit(solution)/shard_map/ppermute | solution.py:199
  6.0 14.4 %collective-permute-start.2 = (bf16[32,2,32,128]{3,2,1,0:T(8,128)(2,1)}, bf16[32,2,32,128]{3,2,1,0:T(8,128)(2,1)S(1)}, u32[]{:S(2)}, u32[]{:S(2)}) collective-permute-start(bf16[32,2,32,128]{3,2,1,0:T(8,128)(2,1)} %get-tuple-element.20), channel_id=1, source_target_pairs={{0,3},{1,2},{2,1},{3,0},{4,7},{5,6},{6,5},{7,4},{8,11},{9,10},{10,... | collective-permute-start | bytes 1572872 | tf_op jit(solution)/shard_map/ppermute | solution.py:198
  6.7 11.9 %collective-permute-start = (bf16[36,16,128]{2,1,0:T(8,128)(2,1)}, bf16[36,16,128]{2,1,0:T(8,128)(2,1)S(1)}, u32[]{:S(2)}, u32[]{:S(2)}) collective-permute-start(bf16[36,16,128]{2,1,0:T(8,128)(2,1)} %get-tuple-element.15), channel_id=1, source_target_pairs={{0,4},{4,8},{8,12},{12,0},{1,5},{5,9},{9,13},{13,1},{2,6},{6,10},{... | collective-permute-start | bytes 442376 | tf_op jit(solution)/shard_map/ppermute | solution.py:200
  8.2 10.3 %collective-permute-start.1 = (bf16[36,16,128]{2,1,0:T(8,128)(2,1)}, bf16[36,16,128]{2,1,0:T(8,128)(2,1)S(1)}, u32[]{:S(2)}, u32[]{:S(2)}) collective-permute-start(bf16[36,16,128]{2,1,0:T(8,128)(2,1)} %get-tuple-element.16), channel_id=1, source_target_pairs={{4,0},{8,4},{12,8},{0,12},{5,1},{9,5},{13,9},{1,13},{6,2},{10,6},{... | collective-permute-start | bytes 442376 | tf_op jit(solution)/shard_map/ppermute | solution.py:201
  20.0 1.5 %copy-start.4 = (bf16[15,2,32,128]{3,2,1,0:T(8,128)(2,1)S(1)}, bf16[15,2,32,128]{3,2,1,0:T(8,128)(2,1)}, u32[]{:S(2)}) copy-start(bf16[15,2,32,128]{3,2,1,0:T(8,128)(2,1)} %get-tuple-element.23) | copy-start | bytes 737284
  20.0 3.1 %copy-start.3 = (s32[32,6,128]{2,0,1:T(8,128)S(1)}, s32[32,6,128]{2,0,1:T(8,128)}, u32[]{:S(2)}) copy-start(s32[32,6,128]{2,0,1:T(8,128)} %param.7) | copy-start | bytes 294916
  20.5 2.6 %collective-permute-start.4 = (bf16[59,2,32,128]{3,2,1,0:T(8,128)(2,1)S(1)}, bf16[59,2,32,128]{3,2,1,0:T(8,128)(2,1)S(1)}, u32[]{:S(2)}, u32[]{:S(2)}) collective-permute-start(bf16[59,2,32,128]{3,2,1,0:T(8,128)(2,1)S(1)} %pack_near.1), channel_id=1, source_target_pairs={{0,1},{1,0},{2,3},{3,2},{4,5},{5,4},{6,7},{7,6},{8,9},{9,8},{10,11... | collective-permute-start | bytes 2899976 | tf_op jit(solution)/shard_map/ppermute | solution.py:505
  20.7 8.8 %collective-permute-start.6 = (bf16[1056,128]{1,0:T(8,128)(2,1)S(1)}, bf16[1056,128]{1,0:T(8,128)(2,1)S(1)}, u32[]{:S(2)}, u32[]{:S(2)}) collective-permute-start(bf16[1056,128]{1,0:T(8,128)(2,1)S(1)} %pack_relay.1.rest_1_), channel_id=1, source_target_pairs={{0,16},{16,0},{1,17},{17,1},{2,18},{18,2},{3,19},{19,3},{4,20},{20... | collective-permute-start | bytes 811016 | tf_op jit(solution)/shard_map/ppermute | solution.py:487
  21.5 7.9 %collective-permute-start.5 = (bf16[15,2,32,128]{3,2,1,0:T(8,128)(2,1)S(1)}, bf16[15,2,32,128]{3,2,1,0:T(8,128)(2,1)S(1)}, u32[]{:S(2)}, u32[]{:S(2)}) collective-permute-start(bf16[15,2,32,128]{3,2,1,0:T(8,128)(2,1)S(1)} %copy-done.4), channel_id=1, source_target_pairs={{0,3},{1,2},{2,1},{3,0},{4,7},{5,6},{6,5},{7,4},{8,11},{9,10},{10,... | collective-permute-start | bytes 737288 | tf_op jit(solution)/shard_map/ppermute | solution.py:202
